TPU v7x, 256 devices: a whole 4x4x8 slice. The times are simulated.
256 devices in a mesh: ctx: 32 (over y, z), fsdp: 8 (over x, core).
Axes of the slice: x: 4, y: 4, z: 8, core: 2. Of those that a mesh axis runs over, the one named last changes fastest.
Arguments:
- tokens: bfloat16 [8, 4096, 2560], P('fsdp', 'ctx'), may hold values from -10 to 10
- gate_input: bfloat16 [8, 4096, 3456], P('fsdp', 'ctx'), may hold values from -6 to 6
- segment_ids: int32 [8, 4096], P('fsdp', 'ctx'), may hold values from 0 to 7, never falling along the last dimension, each value on 1 to 1024 neighbouring positions
- in_weight: bfloat16 [2560, 3456], P('ctx', 'fsdp'), may hold values from -0.125 to 0.125
- conv_weight: float32 [4, 3456], replicated, may hold values from -3 to 3
- conv_bias: float32 [3456], replicated, may hold values from -3 to 3
- gate_a: bfloat16 [27, 128, 128], replicated, may hold values from -0.5 to 0.5
- gate_i: bfloat16 [27, 128, 128], replicated, may hold values from -0.5 to 0.5
- bias_a: float32 [3456], replicated, may hold values from -4 to -2
- bias_i: float32 [3456], replicated, may hold values from -4 to 4
- decay_rate: float32 [3456], replicated, as said below
Outputs:
- gated: bfloat16 [8, 4096, 3456], P('fsdp', 'ctx')
Inputs may be any that keep to these rules, and one draw needn't show every extreme that they name: `decay_rate`: positive.
All inputs are finite; a program needn't handle non-finite values.
Results may differ from a plain program's by a relative error of at most 0.0075.
Values may be sent and summed in bfloat16 or wider, within the bound.
No kernel may reach another device: no remote copies, remote signals or barrier semaphores. Data moves between devices by JAX's collectives and lax.ppermute only.
A program may use at most 128 MiB of HBM per device.

v0:
```python
import jax
import jax.numpy as jnp
from jax import lax
from jax.sharding import PartitionSpec as P


def passed_along(value, axis, by):
    count = lax.axis_size(axis)
    pairs = [(i, i + by) for i in range(count) if 0 <= i + by < count]
    return lax.ppermute(value, axis, pairs)


def prefix(part, axis, combine, identity):
    place = lax.axis_index(axis)
    gathered = jax.tree.map(lambda a: lax.all_gather(a, axis), part)
    state = jax.tree.map(lambda a, e: jnp.zeros_like(a) + jnp.asarray(e, a.dtype), part, identity)

    def one(turn, state):
        return combine(
            state, jax.tree.map(lambda a: lax.dynamic_index_in_dim(a, turn, 0, False), gathered)
        )

    return lax.fori_loop(0, place, one, state)


def combine_pairs(earlier, later):
    return (earlier[0] * later[0], later[0] * earlier[1] + later[1])


def blocked_scan(keep, inflow):
    length = keep.shape[0]
    width = keep.shape[1]
    span = 16
    groups = length // span
    keep_three = keep.reshape(groups, span, width)
    inflow_three = inflow.reshape(groups, span, width)
    run_prod = keep_three[:, 0]
    run_state = inflow_three[:, 0]
    prod_list = [run_prod]
    state_list = [run_state]
    for step in range(1, span):
        factor = keep_three[:, step]
        run_prod = factor * run_prod
        run_state = factor * run_state + inflow_three[:, step]
        prod_list.append(run_prod)
        state_list.append(run_state)
    within_prod = jnp.stack(prod_list, axis=1)
    within_state = jnp.stack(state_list, axis=1)
    group_prod, group_state = lax.associative_scan(combine_pairs, (run_prod, run_state), axis=0)
    before_prod = jnp.concatenate([jnp.ones((1, width), jnp.float32), group_prod[:-1]], axis=0)
    before_state = jnp.concatenate([jnp.zeros((1, width), jnp.float32), group_state[:-1]], axis=0)
    products = (within_prod * before_prod[:, None, :]).reshape(length, width)
    states = (within_state + within_prod * before_state[:, None, :]).reshape(length, width)
    return (products, states, group_prod[-1], group_state[-1])


def body(
    tokens,
    gate_input,
    segment_ids,
    in_weight,
    conv_weight,
    conv_bias,
    gate_a,
    gate_i,
    bias_a,
    bias_i,
    decay_rate,
):
    inputs = tokens[0]
    seg_row = segment_ids[0]
    length = inputs.shape[0]
    wide_rows = lax.all_gather(in_weight, "fsdp", axis=1, tiled=True)
    projected_sum = jnp.dot(
        inputs,
        lax.all_gather(wide_rows, "ctx", axis=0, tiled=True),
        preferred_element_type=jnp.float32,
    )
    projected = projected_sum.astype(jnp.bfloat16)
    width = projected.shape[1]
    rim_ids = (seg_row[-3:] + 1).astype(jnp.bfloat16)
    prior_rows, prior_ids = passed_along((projected[-3:], rim_ids), "ctx", 1)
    prior_ids = prior_ids.astype(jnp.float32).astype(jnp.int32) - 1
    extended = jnp.concatenate([prior_rows, projected], axis=0).astype(jnp.float32)
    extended_ids = jnp.concatenate([prior_ids, seg_row], axis=0)
    conv = conv_weight[0][None, :] * extended[3:] + conv_bias[None, :]
    for back in range(1, 4):
        shifted = extended[3 - back : 3 - back + length]
        shifted_ids = extended_ids[3 - back : 3 - back + length]
        valid = (shifted_ids == seg_row)[:, None]
        conv = conv + conv_weight[back][None, :] * jnp.where(valid, shifted, jnp.float32(0.0))
    conv = conv.astype(jnp.bfloat16)
    blocked = conv.reshape(length, gate_a.shape[0], gate_a.shape[1])
    rgate = jax.nn.sigmoid(
        jnp.einsum("thi,hij->thj", blocked, gate_a, preferred_element_type=jnp.float32).reshape(
            length, width
        )
        + bias_a[None, :]
    )
    igate = jax.nn.sigmoid(
        jnp.einsum("thi,hij->thj", blocked, gate_i, preferred_element_type=jnp.float32).reshape(
            length, width
        )
        + bias_i[None, :]
    )
    logdecay = -8.0 * decay_rate[None, :] * rgate
    decay = jnp.exp(logdecay)
    reset = (seg_row != extended_ids[2 : 2 + length])[:, None]
    factor = jnp.where(reset, jnp.float32(1.0), jnp.sqrt(-jnp.expm1(2.0 * logdecay)))
    inflow = factor * igate * conv.astype(jnp.float32)
    keep = jnp.where(reset, jnp.float32(0.0), decay)
    products, local_state, end_product, end_state = blocked_scan(keep, inflow)
    identity = (jnp.ones((width,), jnp.float32), jnp.zeros((width,), jnp.float32))
    carried = prefix((end_product, end_state), "ctx", combine_pairs, identity)
    incoming = carried[1]
    state = local_state + products * incoming[None, :]
    gelu_gate = jax.nn.gelu(gate_input[0].astype(jnp.float32), approximate=True)
    return (state * gelu_gate).astype(jnp.bfloat16)[None]


def solution(mesh):
    placed = (
        P("fsdp", "ctx", None),
        P("fsdp", "ctx", None),
        P("fsdp", "ctx"),
        P("ctx", "fsdp"),
        P(),
        P(),
        P(),
        P(),
        P(),
        P(),
        P(),
    )
    return jax.shard_map(
        body, mesh=mesh, in_specs=placed, out_specs=P("fsdp", "ctx", None), check_vma=False
    )
```

profile of v0, /device:TPU:24, one launch (start us, length us, event | category | flops | bytes accessed | tf_op | source)
XLA Modules:
  0.0 380.8 jit_solution(14813031237158210726)
XLA Ops:
  6.5 13.9 %all-gather = bf16[8,432,80]{1,2,0:T(8,128)(2,1)S(1)} all-gather(bf16[1,432,80]{1,2,0:T(8,128)(2,1)} %bitcast.138), channel_id=1, replica_groups=mesh['ctx'=32,'fsdp'=8] {'fsdp'}, dimensions={0}, use_global_device_ids=true | all-gather | bytes 622080 | tf_op jit(solution)/shard_map/all_gather | solution.py:73
  20.9 1.7 reshape.151
  22.7 3.8 %collective-permute-start = (bf16[3]{0:T(256)(128)(2,1)S(1)}, bf16[3]{0:T(256)(128)(2,1)S(1)}, u32[]{:S(2)}, u32[]{:S(2)}) collective-permute-start(bf16[3]{0:T(256)(128)(2,1)S(1)} %convert_bitcast_fusion), channel_id=1, source_target_pairs={{0,8},{8,16},{16,24},{24,32},{32,40},{40,48},{48,56},{56,64},{64,7... | collective-permute-start | bytes 26 | tf_op jit(solution)/shard_map/ppermute | solution.py:10
  27.9 4.2 %collective-permute-done = bf16[3]{0:T(256)(128)(2,1)S(1)} collective-permute-done((bf16[3]{0:T(256)(128)(2,1)S(1)}, bf16[3]{0:T(256)(128)(2,1)S(1)}, u32[]{:S(2)}, u32[]{:S(2)}) %collective-permute-start) | collective-permute-done | bytes 38 | tf_op jit(solution)/shard_map/ppermute | solution.py:10
  32.2 135.7 %all-gather.5.cloned.1.call-done = bf16[2560,3456]{1,0:T(8,128)(2,1)} async-done(((bf16[80,3456]{1,0:T(8,128)(2,1)}), bf16[2560,3456]{1,0:T(8,128)(2,1)}) %all-gather.5.cloned.1.call-update) | async-done | bytes 17694736 | tf_op jit(solution)/shard_map/all_gather | solution.py:76
  168.0 8.6 %convolution_convert_fusion = bf16[128,3456]{1,0:T(8,128)(2,1)S(1)} fusion(bf16[2560,3456]{1,0:T(8,128)(2,1)} %all-gather.5.cloned.1.call-done, bf16[1,128,2560]{2,1,0:T(8,128)(2,1)S(1)} %copy-done.4), kind=kOutput, calls=%fused_computation.3 | convolution fusion | flops 2265366528 | bytes 19234816 | tf_op jit(solution)/shard_map/dot_general | solution.py:74
  176.6 0.9 copy-done.3
  177.5 2.1 collective-permute-start.1
  180.4 4.9 %collective-permute-done.1 = bf16[3,3456]{1,0:T(4,128)(2,1)S(1)} collective-permute-done((bf16[3,3456]{1,0:T(4,128)(2,1)S(1)}, bf16[3,3456]{1,0:T(4,128)(2,1)S(1)}, u32[]{:S(2)}, u32[]{:S(2)}) %collective-permute-start.1) | collective-permute-done | bytes 20768 | tf_op jit(solution)/shard_map/ppermute | solution.py:10
  185.3 1.4 maximum_convert_fusion
  186.7 2.3 fusion.9
  189.0 2.2 copy.110
  191.2 2.9 fusion.39
  194.1 2.7 copy.116
  196.9 3.2 fusion.38
  200.0 2.8 copy.113
  202.8 4.5 %convert_multiply_fusion.3 = f32[128,3456]{1,0:T(8,128)S(1)} fusion(f32[128,3456]{1,0:T(8,128)} %copy.116, f32[128,3456]{1,0:T(8,128)} %copy.113, f32[3456]{0:T(1024)S(1)} %copy-done.44, f32[3456]{0:T(1024)S(1)} %copy-done.42, f32[3456]{0:T(1024)S(1)} %broadcast_multiply_fusion.1, pred[128]{0:T(512)(128)(4,1)S(1)} %get-tuple-element.155, ...), kind=kLoop, calls=%fused_computation.31 | loop fusion | flops 11943936 | bytes 12497408 | tf_op jit(solution)/shard_map/mul | solution.py:110
  207.3 2.1 fusion.34
  209.7 2.3 copy.118
  212.0 1.7 reshape.137
  214.5 1.2 fusion.35
  215.8 1.1 bitcast_add_fusion
  216.9 1.5 slice.281
  218.5 1.5 slice.280
  220.0 1.0 fusion.22
  221.0 0.9 slice.279
  221.9 0.9 slice.283
  222.8 0.9 multiply_add_fusion.8
  224.2 0.8 copy.157
  224.9 2.2 copy_multiply_fusion.10
  229.1 47.6 %all-gather.1 = f32[32,1,3456]{2,1,0:T(1,128)S(1)} all-gather(f32[1,1,3456]{2,1,0:T(1,128)S(1)} %get-tuple-element.154), channel_id=1, replica_groups=mesh['ctx'=32,'fsdp'=8] {'ctx'}, dimensions={0}, use_global_device_ids=true | all-gather | bytes 456192 | tf_op jit(solution)/shard_map/all_gather | solution.py:15
  276.8 48.7 %all-gather.2 = f32[32,1,3456]{2,1,0:T(1,128)S(1)} all-gather(f32[1,1,3456]{2,1,0:T(1,128)S(1)} %get-tuple-element.153), channel_id=1, replica_groups=mesh['ctx'=32,'fsdp'=8] {'ctx'}, dimensions={0}, use_global_device_ids=true | all-gather | bytes 456192 | tf_op jit(solution)/shard_map/all_gather | solution.py:15
  325.5 3.0 while.12
  331.2 1.7 copy.155
  332.8 1.7 copy.156
  334.5 1.7 copy.158
  336.2 1.7 copy.159
  337.9 1.7 copy.160
  339.6 1.7 copy.161
  341.3 1.7 copy.162
  343.0 1.7 copy.163
  344.7 2.0 copy_add_fusion.8
  346.7 0.8 copy.165
  355.0 0.8 copy.177
  357.6 5.3 %stack.4 = f32[8,16,3456]{2,1,0:T(8,128)S(1)} concatenate(f32[8,1,3456]{2,1,0:T(1,128)S(1)} %get-tuple-element.113, f32[8,1,3456]{2,1,0:T(1,128)S(1)} %copy.150, f32[8,1,3456]{2,1,0:T(1,128)S(1)} %copy.151, f32[8,1,3456]{2,1,0:T(1,128)} %copy.152, f32[8,1,3456]{2,1,0:T(1,128)} %copy.153, f32[8,1,3456]{2,1,0:T(1,128)} %copy.154, f32[8,1,3456]{2,1,0:T(1,128)} %copy.155, ...), dimensions={1} | concatenate | bytes 3538944 | tf_op jit(solution)/shard_map/stack | solution.py:48
  363.0 7.4 %stack.5 = f32[8,16,3456]{2,1,0:T(8,128)} concatenate(f32[8,1,3456]{2,1,0:T(1,128)S(1)} %get-tuple-element.130, f32[8,1,3456]{2,1,0:T(1,128)} %copy.165, f32[8,1,3456]{2,1,0:T(1,128)} %copy.166, f32[8,1,3456]{2,1,0:T(1,128)} %copy.167, f32[8,1,3456]{2,1,0:T(1,128)} %copy.168, f32[8,1,3456]{2,1,0:T(1,128)} %copy.169, f32[8,1,3456]{2,1,0:T(1,128)} %copy.170, f32[8,1,3456]{2,1,0:T(1,128)} %copy.171, ...), dimensions={1} | concatenate | bytes 3538944 | tf_op jit(solution)/shard_map/stack | solution.py:47
  370.4 1.9 multiply_add_fusion.1
  372.3 1.7 fusion.6
  (214 shorter events, 20.3 us)
Async XLA Ops:
  6.5 184.7 %copy-start = (bf16[27,128,128]{2,1,0:T(8,128)(2,1)S(1)}, bf16[27,128,128]{2,1,0:T(8,128)(2,1)}, u32[]{:S(2)}) copy-start(bf16[27,128,128]{2,1,0:T(8,128)(2,1)} %param.20) | copy-start | bytes 2654212
  6.5 161.4 %all-gather.5.cloned.1.call-start = ((), (), s32[]{:S(2)}) async-start(), calls=%async_computation | async-start | bytes 18247680 | tf_op jit(solution)/shard_map/all_gather | solution.py:76
  6.5 16.1 %copy-start.47 = (s32[1,128]{1,0:T(1,128)S(1)}, s32[1,128]{1,0:T(1,128)}, u32[]{:S(2)}) copy-start(s32[1,128]{1,0:T(1,128)} %param.15) | copy-start | bytes 1540
  6.5 21.2 %copy-start.43 = (f32[4,3456]{1,0:T(4,128)S(1)}, f32[4,3456]{1,0:T(4,128)}, u32[]{:S(2)}) copy-start(f32[4,3456]{1,0:T(4,128)} %param.17) | copy-start | bytes 165892
  20.5 7.4 %copy-start.45 = (f32[3456]{0:T(1024)S(1)}, f32[3456]{0:T(1024)}, u32[]{:S(2)}) copy-start(f32[3456]{0:T(1024)} %param.23) | copy-start | bytes 41476
  20.5 147.5 %copy-start.4 = (bf16[1,128,2560]{2,1,0:T(8,128)(2,1)S(1)}, bf16[1,128,2560]{2,1,0:T(8,128)(2,1)}, u32[]{:S(2)}) copy-start(bf16[1,128,2560]{2,1,0:T(8,128)(2,1)} %param.13) | copy-start | bytes 1966084
  22.7 9.4 %collective-permute-start = (bf16[3]{0:T(256)(128)(2,1)S(1)}, bf16[3]{0:T(256)(128)(2,1)S(1)}, u32[]{:S(2)}, u32[]{:S(2)}) collective-permute-start(bf16[3]{0:T(256)(128)(2,1)S(1)} %convert_bitcast_fusion), channel_id=1, source_target_pairs={{0,8},{8,16},{16,24},{24,32},{32,40},{40,48},{48,56},{56,64},{64,7... | collective-permute-start | bytes 26 | tf_op jit(solution)/shard_map/ppermute | solution.py:10
  177.5 9.3 %copy-start.41 = (f32[3456]{0:T(1024)S(1)}, f32[3456]{0:T(1024)}, u32[]{:S(2)}) copy-start(f32[3456]{0:T(1024)} %param.18) | copy-start | bytes 41476
  177.5 7.9 %collective-permute-start.1 = (bf16[3,3456]{1,0:T(4,128)(2,1)S(1)}, bf16[3,3456]{1,0:T(4,128)(2,1)S(1)}, u32[]{:S(2)}, u32[]{:S(2)}) collective-permute-start(bf16[3,3456]{1,0:T(4,128)(2,1)S(1)} %slice.305), channel_id=1, source_target_pairs={{0,8},{8,16},{16,24},{24,32},{32,40},{40,48},{48,56},{56,64},{64,7... | collective-permute-start | bytes 62216 | tf_op jit(solution)/shard_map/ppermute | solution.py:10
  200.0 2.8 copy-start.42
  200.0 2.8 copy-start.44
  207.3 2.1 copy-start.2
  207.3 2.4 copy-start.1
  212.0 1.7 copy-start.46
  214.4 1.3 copy-start.10
  214.4 1.3 copy-start.11
  214.4 1.3 copy-start.12
  214.5 1.3 copy-start.13
  214.5 1.3 copy-start.14
  214.5 1.3 copy-start.15
  214.5 1.3 copy-start.16
  224.1 3.0 copy-start.5
  224.9 2.6 copy-start.7
  224.9 3.2 copy-start.8
  229.1 99.5 %copy-start.30 = (f32[8,1,3456]{2,0,1:T(8,128)S(1)}, f32[8,1,3456]{2,0,1:T(8,128)}, u32[]{:S(2)}) copy-start(f32[8,1,3456]{2,0,1:T(8,128)} %get-tuple-element.72) | copy-start | bytes 331780
  276.7 52.0 %copy-start.29 = (f32[8,1,3456]{2,0,1:T(8,128)S(1)}, f32[8,1,3456]{2,0,1:T(8,128)}, u32[]{:S(2)}) copy-start(f32[8,1,3456]{2,0,1:T(8,128)} %get-tuple-element.71) | copy-start | bytes 331780
  276.7 52.2 %copy-start.28 = (f32[8,1,3456]{2,0,1:T(8,128)S(1)}, f32[8,1,3456]{2,0,1:T(8,128)}, u32[]{:S(2)}) copy-start(f32[8,1,3456]{2,0,1:T(8,128)} %get-tuple-element.70) | copy-start | bytes 331780
  276.7 52.9 %copy-start.27 = (f32[8,1,3456]{2,0,1:T(8,128)S(1)}, f32[8,1,3456]{2,0,1:T(8,128)}, u32[]{:S(2)}) copy-start(f32[8,1,3456]{2,0,1:T(8,128)} %get-tuple-element.69) | copy-start | bytes 331780
  276.8 53.6 %copy-start.26 = (f32[8,1,3456]{2,0,1:T(8,128)S(1)}, f32[8,1,3456]{2,0,1:T(8,128)}, u32[]{:S(2)}) copy-start(f32[8,1,3456]{2,0,1:T(8,128)} %get-tuple-element.68) | copy-start | bytes 331780
  328.6 16.1 %copy-start.38 = (f32[8,1,3456]{2,0,1:T(8,128)S(1)}, f32[8,1,3456]{2,0,1:T(8,128)}, u32[]{:S(2)}) copy-start(f32[8,1,3456]{2,0,1:T(8,128)} %get-tuple-element.73) | copy-start | bytes 331780
  328.6 18.1 %copy-start.25 = (f32[8,1,3456]{2,0,1:T(8,128)S(1)}, f32[8,1,3456]{2,0,1:T(8,128)}, u32[]{:S(2)}) copy-start(f32[8,1,3456]{2,0,1:T(8,128)} %get-tuple-element.88) | copy-start | bytes 331780
  328.6 18.9 %copy-start.24 = (f32[8,1,3456]{2,0,1:T(8,128)S(1)}, f32[8,1,3456]{2,0,1:T(8,128)}, u32[]{:S(2)}) copy-start(f32[8,1,3456]{2,0,1:T(8,128)} %get-tuple-element.87) | copy-start | bytes 331780
  328.7 19.5 %copy-start.23 = (f32[8,1,3456]{2,0,1:T(8,128)S(1)}, f32[8,1,3456]{2,0,1:T(8,128)}, u32[]{:S(2)}) copy-start(f32[8,1,3456]{2,0,1:T(8,128)} %get-tuple-element.86) | copy-start | bytes 331780
  328.9 20.1 %copy-start.22 = (f32[8,1,3456]{2,0,1:T(8,128)S(1)}, f32[8,1,3456]{2,0,1:T(8,128)}, u32[]{:S(2)}) copy-start(f32[8,1,3456]{2,0,1:T(8,128)} %get-tuple-element.85) | copy-start | bytes 331780
  329.6 20.1 %copy-start.21 = (f32[8,1,3456]{2,0,1:T(8,128)S(1)}, f32[8,1,3456]{2,0,1:T(8,128)}, u32[]{:S(2)}) copy-start(f32[8,1,3456]{2,0,1:T(8,128)} %get-tuple-element.84) | copy-start | bytes 331780
  330.4 20.1 %copy-start.20 = (f32[8,1,3456]{2,0,1:T(8,128)S(1)}, f32[8,1,3456]{2,0,1:T(8,128)}, u32[]{:S(2)}) copy-start(f32[8,1,3456]{2,0,1:T(8,128)} %get-tuple-element.83) | copy-start | bytes 331780
  331.2 20.1 %copy-start.19 = (f32[8,1,3456]{2,0,1:T(8,128)S(1)}, f32[8,1,3456]{2,0,1:T(8,128)}, u32[]{:S(2)}) copy-start(f32[8,1,3456]{2,0,1:T(8,128)} %get-tuple-element.82) | copy-start | bytes 331780
  332.8 19.2 %copy-start.37 = (f32[8,1,3456]{2,0,1:T(8,128)S(1)}, f32[8,1,3456]{2,0,1:T(8,128)}, u32[]{:S(2)}) copy-start(f32[8,1,3456]{2,0,1:T(8,128)} %get-tuple-element.138) | copy-start | bytes 331780
  334.5 18.2 %copy-start.36 = (f32[8,1,3456]{2,0,1:T(8,128)S(1)}, f32[8,1,3456]{2,0,1:T(8,128)}, u32[]{:S(2)}) copy-start(f32[8,1,3456]{2,0,1:T(8,128)} %get-tuple-element.137) | copy-start | bytes 331780
  336.2 17.3 %copy-start.35 = (f32[8,1,3456]{2,0,1:T(8,128)S(1)}, f32[8,1,3456]{2,0,1:T(8,128)}, u32[]{:S(2)}) copy-start(f32[8,1,3456]{2,0,1:T(8,128)} %get-tuple-element.136) | copy-start | bytes 331780
  337.9 16.4 %copy-start.34 = (f32[8,1,3456]{2,0,1:T(8,128)S(1)}, f32[8,1,3456]{2,0,1:T(8,128)}, u32[]{:S(2)}) copy-start(f32[8,1,3456]{2,0,1:T(8,128)} %get-tuple-element.135) | copy-start | bytes 331780
  339.6 15.4 %copy-start.33 = (f32[8,1,3456]{2,0,1:T(8,128)S(1)}, f32[8,1,3456]{2,0,1:T(8,128)}, u32[]{:S(2)}) copy-start(f32[8,1,3456]{2,0,1:T(8,128)} %get-tuple-element.134) | copy-start | bytes 331780
  341.3 14.5 %copy-start.32 = (f32[8,1,3456]{2,0,1:T(8,128)S(1)}, f32[8,1,3456]{2,0,1:T(8,128)}, u32[]{:S(2)}) copy-start(f32[8,1,3456]{2,0,1:T(8,128)} %get-tuple-element.133) | copy-start | bytes 331780
  343.0 13.6 %copy-start.31 = (f32[8,1,3456]{2,0,1:T(8,128)S(1)}, f32[8,1,3456]{2,0,1:T(8,128)}, u32[]{:S(2)}) copy-start(f32[8,1,3456]{2,0,1:T(8,128)} %get-tuple-element.132) | copy-start | bytes 331780
  344.7 12.7 %copy-start.39 = (f32[3,3456]{1,0:T(4,128)S(1)}, f32[3,3456]{1,0:T(4,128)}, u32[]{:S(2)}) copy-start(f32[3,3456]{1,0:T(4,128)} %slice.295) | copy-start | bytes 124420
  344.7 12.7 %copy-start.40 = (f32[3,3456]{1,0:T(4,128)S(1)}, f32[3,3456]{1,0:T(4,128)}, u32[]{:S(2)}) copy-start(f32[3,3456]{1,0:T(4,128)} %slice.278) | copy-start | bytes 124420
  352.8 4.9 %copy-start.9 = (f32[8,1,3456]{2,1,0:T(1,128)S(1)}, f32[8,1,3456]{2,1,0:T(1,128)}, u32[]{:S(2)}) copy-start(f32[8,1,3456]{2,1,0:T(1,128)} %copy.157) | copy-start | bytes 331780
  370.4 1.9 copy-start.6
  (3 other events, 3.5 us)
Sparse Core Ops, SparseCore 0:
  22.7 145.1 all-gather.4
where the time goes:
time: 383 us; the launch traced here: 381 us
  waiting for transfers between devices  145 us (38%)
  blocking collectives  110 us (29%)
  local copies, waits for them, and re-layouts  68.4 us (18%)
  other arithmetic  21.7 us (6%)
  matrix products  14.6 us (4%)
  between operations  14.1 us (4%)
  starting transfers between devices  5.92 us (2%)
    all_gather x1, waiting for transfers between devices, body(): lax.all_gather(wide_rows, 'ctx', axis=0, tiled=True)  136 us
    all_gather x2, blocking collectives, prefix(): gathered = jax.tree.map(lambda a: lax.all_gather(a, axis), part)  96.3 us
    add x14, local copies, waits for them, and re-layouts, blocked_scan(): run_state = factor * run_state + inflow_three[:, step]  16.8 us
    all_gather x1, blocking collectives, body(): wide_rows = lax.all_gather(in_weight, 'fsdp', axis=1, tiled=True)  13.9 us
    mul x15, local copies, waits for them, and re-layouts, blocked_scan(): run_prod = factor * run_prod  10.7 us
    ppermute x2, waiting for transfers between devices, passed_along(): return lax.ppermute(value, axis, pairs)  9.14 us
    dot_general x1, matrix products, body(): jnp.dot(inputs, lax.all_gather(wide_rows, 'ctx', axis=0, tiled=True), pre...  8.58 us
  transfers between devices with their start and end apart: 3, of which 3 were waited for; matrix products, arithmetic and copies ran while one was open for 1% of the time, Pallas kernels for 0%

commit v1 on v0

v1 whole, which is shorter than its diff:
```python
import functools

import jax
import jax.numpy as jnp
from jax import lax
from jax.experimental import pallas as pl
from jax.experimental.pallas import tpu as pltpu
from jax.sharding import Mesh
from jax.sharding import PartitionSpec as P

F32 = jnp.float32
BF16 = jnp.bfloat16
VMEM = pl.BlockSpec(memory_space=pltpu.VMEM)
SMEM = pl.BlockSpec(memory_space=pltpu.SMEM)

LENGTH = 128
WIDTH = 3456
DEPTH = 2560
COLS = 432
HEAD = 128
HEADS = 27
SPAN = 16
HALO = 8
PACK = COLS + 32
CUT = 256


def shift(value, axis, by):
    count = lax.axis_size(axis)
    return lax.ppermute(value, axis, [(i, (i + by) % count) for i in range(count)])


def flip(value):
    return lax.ppermute(value, "c", [(0, 1), (1, 0)])


def ring(value, axis, cut):
    back = shift(value, axis, 1)
    ahead = shift(value, axis, -1)
    first = shift(back[:cut], axis, 1)
    second = shift(ahead[cut:], axis, -1)
    return value, back, ahead, first, second


def prepare_kernel(gate_ref, ids_ref, gelu_ref, mask_ref, ids_scr):
    def head(h, carry):
        lanes = pl.ds(pl.multiple_of(h * HEAD, HEAD), HEAD)
        gelu_ref[h] = jax.nn.gelu(gate_ref[:, lanes].astype(F32), approximate=True)
        return carry

    lax.fori_loop(0, HEADS, head, 0)
    prior = jnp.broadcast_to(ids_ref[0:1, :], (LENGTH, LENGTH)).T
    own = jnp.broadcast_to(ids_ref[1:2, :], (LENGTH, LENGTH)).T
    ids_scr[0:HALO, :] = prior[LENGTH - HALO :, :]
    ids_scr[HALO:, :] = own
    for k in range(SPAN):
        here = ids_scr[pl.ds(HALO + k, 8, stride=SPAN), :]
        for back in range(1, 4):
            there = ids_scr[pl.ds(HALO + k - back, 8, stride=SPAN), :]
            same = (here == there).astype(F32)
            mask_ref[back, 8 * k : 8 * k + 8, :] = same
            if back == 1:
                mask_ref[0, 8 * k : 8 * k + 8, :] = same


def project_kernel(at_ref, t0, t1, t2, t3, w0, w1, w2, w3, w4, out_ref, acc_ref, wide_ref):
    x, c, y = at_ref[0], at_ref[1], at_ref[2]
    steps = (
        (lax.rem(y, 4) * 640, 640, w0),
        (lax.rem(y + 3, 4) * 640, 640, w1),
        (lax.rem(y + 1, 4) * 640, 640, w2),
        (lax.rem(y + 2, 4) * 640, CUT, w3),
        (lax.rem(y + 2, 4) * 640 + CUT, 640 - CUT, w4),
    )
    for back, t_ref in ((0, t0), (1, t1), (3, t2), (2, t3)):
        total = None
        for start, size, w_ref in steps:
            part = jnp.dot(
                t_ref[:, pl.ds(pl.multiple_of(start, 128), size)],
                w_ref[...],
                preferred_element_type=F32,
            )
            total = part if total is None else total + part
        acc_ref[...] = total
        for other in range(2):
            stream = lax.rem(x + 4 - back, 4) * 2 + (c if other == 0 else 1 - c)
            top = other * (LENGTH + HALO)
            wide_ref[:, 0:COLS] = acc_ref[top : top + LENGTH + HALO, :]
            for j in range(4):
                block = wide_ref[0:LENGTH, j * 128 : (j + 1) * 128].T.astype(BF16)
                size = min(128, COLS - j * 128)
                out_ref[stream, j * 128 : j * 128 + size, :] = block[:size]
            for j in range(2):
                pair = [
                    wide_ref[LENGTH : LENGTH + HALO, (2 * j + i) * 128 : (2 * j + i + 1) * 128]
                    for i in range(2)
                ]
                out_ref[stream, COLS + 16 * j : COLS + 16 * j + 16, :] = jnp.concatenate(
                    pair, axis=0
                ).astype(BF16)


def recur_kernel(
    got_ref, mask_ref, gelu_ref, par_ref, gates_ref, state_ref, prod_ref, end_ref, x_scr
):
    ahead = []
    for f in range(8):
        packed = got_ref[f, COLS:PACK, :].astype(F32)
        ahead += [packed[8 * j : 8 * j + 8, : min(128, COLS - 128 * j)] for j in range(4)]
    ahead = jnp.concatenate(ahead, axis=1)
    for h in range(HEADS):
        f, low = (h * HEAD) // COLS, (h * HEAD) % COLS
        size = min(HEAD, COLS - low)
        block = got_ref[f, low : low + size, :].astype(F32)
        if size < HEAD:
            rest = got_ref[f + 1, 0 : HEAD - size, :].astype(F32)
            block = jnp.concatenate([block, rest], axis=0)
        x_scr[h, 0:HALO, :] = ahead[:, h * HEAD : (h + 1) * HEAD]
        x_scr[h, HALO:, :] = block.T

    row = lax.broadcasted_iota(jnp.int32, (8, HEAD), 0)

    def head(h, carry):
        lanes = pl.ds(pl.multiple_of(h * HEAD, HEAD), HEAD)
        par = [par_ref[i : i + 1, lanes] for i in range(8)]
        shifted = {
            off: x_scr[h, pl.ds(HALO + off, 8, stride=SPAN), :] for off in range(-3, SPAN)
        }
        conv = []
        for k in range(SPAN):
            total = par[0] * shifted[k] + par[4]
            for back in range(1, 4):
                valid = mask_ref[back, 8 * k : 8 * k + 8, :]
                total = total + par[back] * (shifted[k - back] * valid)
            conv.append(total)
        conv = jnp.concatenate(conv, axis=0).astype(BF16)
        both = jnp.dot(conv, gates_ref[h], preferred_element_type=F32)
        rgate = jax.nn.sigmoid(both[:, :HEAD] + par[5])
        igate = jax.nn.sigmoid(both[:, HEAD:] + par[6])
        logdecay = par[7] * rgate
        decay = jnp.exp(logdecay)
        same = mask_ref[0]
        twice = 2.0 * logdecay
        series = 1.0 + twice * (
            1 / 2
            + twice
            * (1 / 6 + twice * (1 / 24 + twice * (1 / 120 + twice * (1 / 720 + twice * (1 / 5040)))))
        )
        lost = jnp.where(twice > -0.5, -twice * series, 1.0 - decay * decay)
        factor = jnp.where(same > 0.5, jnp.sqrt(lost), 1.0)
        inflow = factor * igate * conv.astype(F32)
        keep = decay * same
        prods, states = [keep[0:8]], [inflow[0:8]]
        for k in range(1, SPAN):
            part = keep[8 * k : 8 * k + 8]
            prods.append(part * prods[-1])
            states.append(part * states[-1] + inflow[8 * k : 8 * k + 8])
        prod, state = prods[-1], states[-1]
        for by in (1, 2, 4):
            before_prod = jnp.where(row >= by, pltpu.roll(prod, by, 0), 1.0)
            before_state = jnp.where(row >= by, pltpu.roll(state, by, 0), 0.0)
            state = prod * before_state + state
            prod = prod * before_prod
        end_ref[0:1, lanes] = prod[7:8]
        end_ref[1:2, lanes] = state[7:8]
        in_prod = jnp.where(row >= 1, pltpu.roll(prod, 1, 0), 1.0)
        in_state = jnp.where(row >= 1, pltpu.roll(state, 1, 0), 0.0)
        for k in range(SPAN):
            at = pl.ds(k, 8, stride=SPAN)
            gelu = gelu_ref[h, at, :]
            state_ref[h, at, :] = (states[k] + prods[k] * in_state) * gelu
            prod_ref[h, at, :] = (prods[k] * in_prod) * gelu
        return carry

    lax.fori_loop(0, HEADS, head, 0)


def finish_kernel(state_ref, prod_ref, in_ref, out_ref):
    def head(h, carry):
        lanes = pl.ds(pl.multiple_of(h * HEAD, HEAD), HEAD)
        out_ref[:, lanes] = (state_ref[h] + prod_ref[h] * in_ref[:, lanes]).astype(BF16)
        return carry

    lax.fori_loop(0, HEADS, head, 0)


def call(kernel, outs, ins, scratch=(), flops=0, moved=0):
    return pl.pallas_call(
        kernel,
        out_shape=outs,
        in_specs=ins,
        out_specs=jax.tree.map(lambda _: VMEM, outs),
        scratch_shapes=list(scratch),
        compiler_params=pltpu.CompilerParams(vmem_limit_bytes=48 * 2**20),
        cost_estimate=pl.CostEstimate(flops=flops, bytes_accessed=moved, transcendentals=0),
    )


def joined(earlier, later):
    return jnp.concatenate(
        [earlier[:1] * later[:1], later[:1] * earlier[1:] + later[1:]], axis=0
    )


def body(
    tokens,
    gate_input,
    segment_ids,
    in_weight,
    conv_weight,
    conv_bias,
    gate_a,
    gate_i,
    bias_a,
    bias_i,
    decay_rate,
):
    ctx = ("y", "z")
    own = tokens[0]
    at = jnp.stack([lax.axis_index("x"), lax.axis_index("c"), lax.axis_index("y")]).astype(
        jnp.int32
    )

    column = lax.all_to_all(
        jnp.broadcast_to(in_weight[None], (8,) + in_weight.shape), "z", 0, 0, tiled=True
    ).reshape(-1, in_weight.shape[1])
    weights = ring(column, "y", CUT)

    rows = jnp.concatenate([own, shift(own[-HALO:], ctx, 1)], axis=0)
    here, back, ahead, first, second = ring(rows, "x", 64)
    far = jnp.concatenate([first, second], axis=0)
    streams = [jnp.concatenate([t, flip(t)], axis=0) for t in (here, back, ahead, far)]

    ids = segment_ids.astype(BF16)
    prior = shift(ids, ctx, 1).astype(F32)
    prior = jnp.where(lax.axis_index(ctx) == 0, F32(-1.0), prior)
    ids = jnp.concatenate([prior, segment_ids.astype(F32)], axis=0)
    gelu, masks = call(
        prepare_kernel,
        (
            jax.ShapeDtypeStruct((HEADS, LENGTH, HEAD), F32),
            jax.ShapeDtypeStruct((4, LENGTH, HEAD), F32),
        ),
        [VMEM] * 2,
        [pltpu.VMEM((LENGTH + HALO, HEAD), F32)],
        moved=2_700_000,
    )(gate_input[0], ids)
    params = jnp.concatenate(
        [
            conv_weight,
            conv_bias[None],
            bias_a[None],
            bias_i[None],
            -8.0 * decay_rate[None],
        ],
        axis=0,
    )
    gates = jnp.concatenate([gate_a, gate_i], axis=2)

    sent = call(
        project_kernel,
        jax.ShapeDtypeStruct((8, PACK, 128), BF16),
        [SMEM] + [VMEM] * 9,
        [
            pltpu.VMEM((2 * (LENGTH + HALO), COLS), F32),
            pltpu.VMEM((LENGTH + HALO, 512), F32),
        ],
        flops=2 * 1088 * 2560 * 432,
        moved=8_000_000,
    )(at, *streams, *weights)
    got = lax.all_to_all(sent, ("x", "c"), 0, 0, tiled=True)
    states, prods, ends = call(
        recur_kernel,
        (
            jax.ShapeDtypeStruct((HEADS, LENGTH, HEAD), F32),
            jax.ShapeDtypeStruct((HEADS, LENGTH, HEAD), F32),
            jax.ShapeDtypeStruct((2, WIDTH), F32),
        ),
        [VMEM] * 5,
        [pltpu.VMEM((HEADS, LENGTH + HALO, HEAD), F32)],
        flops=2 * 128 * 3456 * 256,
        moved=8_000_000,
    )(got, masks, gelu, params, gates)

    two = joined(shift(ends, ctx, 1), ends)
    pairs = [shift(two, ctx, by) for by in (7, 5, 3, 1)]
    incoming = functools.reduce(joined, pairs)[1:]
    out = call(
        finish_kernel,
        jax.ShapeDtypeStruct((LENGTH, WIDTH), BF16),
        [VMEM] * 3,
        moved=4_400_000,
    )(states, prods, incoming)
    return out[None]


def solution(mesh):
    fine = Mesh(mesh.devices.reshape(4, 8, 4, 2), ("y", "z", "x", "c"))
    ctx, fsdp = ("y", "z"), ("x", "c")
    placed = (
        P(fsdp, ctx, None),
        P(fsdp, ctx, None),
        P(fsdp, ctx),
        P(ctx, fsdp),
        P(),
        P(),
        P(),
        P(),
        P(),
        P(),
        P(),
    )
    return jax.shard_map(
        body, mesh=fine, in_specs=placed, out_specs=P(fsdp, ctx, None), check_vma=False
    )
```

time: 383 us -> 130 us (0.34)
  blocking collectives: 110 us -> 0 us
  waiting for transfers between devices: 145 us -> 49.5 us
  local copies, waits for them, and re-layouts: 68.4 us -> 12.9 us
  starting transfers between devices: 5.92 us -> 33.5 us
  Pallas kernels: 0 us -> 19.3 us
  matrix products: 14.6 us -> 0 us
  between operations: 14.1 us -> 0.29 us
  other arithmetic: 21.7 us -> 13.7 us
    all_gather x1 -> x0, waiting for transfers between devices: 136 us -> none  [body(): lax.all_gather(wide_rows, 'ctx', axis=0, tiled=True)]
    all_gather x3 -> x0, blocking collectives: 110 us -> none  [the longest x2 96.3 us: prefix(): gathered = jax.tree.map(lambda a: lax.all_gather(a, axis), part)]
    ppermute x2 -> x19, waiting for transfers between devices: 9.14 us -> 37.2 us  [the longest x15 37.2 us: shift(): lax.ppermute(value, axis, [(i, (i + by) % count) for i in range(count)])]
    pallas_call x0 -> x4, Pallas kernels: none -> 19.3 us  [the longest x1 11 us: body(): call(recur_kernel, (jax.ShapeDtypeStruct((HEADS, LENGTH, HEAD), F32), jax...]
    ppermute x2 -> x19, starting transfers between devices: 5.92 us -> 23.2 us  [the longest x15 22.7 us: shift(): lax.ppermute(value, axis, [(i, (i + by) % count) for i in range(count)])]
    add x14 -> x0, local copies, waits for them, and re-layouts: 16.8 us -> none  [blocked_scan(): run_state = factor * run_state + inflow_three[:, step]]
    dot_general x3 -> x0, matrix products: 14.6 us -> none  [the longest x1 8.58 us: body(): jnp.dot(inputs, lax.all_gather(wide_rows, 'ctx', axis=0, tiled=True), pre...]
    concatenate x4 -> x9, other arithmetic: 0.19 us -> 13.5 us  [the longest x4 8.69 us: body(): jnp.concatenate([t, flip(t)], axis=0)]
  transfers between devices with their start and end apart: 3 -> 21, of which waited for: 3 -> 12; matrix products, arithmetic and copies ran while one was open for 1% -> 17% of each run, Pallas kernels for 0% -> 1%
where the time goes in v1:
time: 130 us; the launch traced here: 129 us
  waiting for transfers between devices  49.5 us (38%)
  starting transfers between devices  33.5 us (26%)
  Pallas kernels  19.3 us (15%)
  other arithmetic  13.7 us (11%)
  local copies, waits for them, and re-layouts  12.9 us (10%)
    ppermute x15, waiting for transfers between devices, shift(): lax.ppermute(value, axis, [(i, (i + by) % count) for i in range(count)])  37.2 us
    ppermute x15, starting transfers between devices, shift(): lax.ppermute(value, axis, [(i, (i + by) % count) for i in range(count)])  22.7 us
    pallas_call x1, Pallas kernels, body(): call(recur_kernel, (jax.ShapeDtypeStruct((HEADS, LENGTH, HEAD), F32), jax...  11 us
    concatenate x4, other arithmetic, body(): jnp.concatenate([t, flip(t)], axis=0)  8.69 us
    all_to_all x1, waiting for transfers between devices, body(): got = lax.all_to_all(sent, ('x', 'c'), 0, 0, tiled=True)  6.91 us
    pallas_call x1, Pallas kernels, body(): call(project_kernel, jax.ShapeDtypeStruct((8, PACK, 128), BF16), [SMEM] +...  6.13 us
    all_to_all x1, starting transfers between devices, body(): lax.all_to_all(jnp.broadcast_to(in_weight[None], (8,) + in_weight.shape),...  5.66 us
    all_to_all x1, waiting for transfers between devices, body(): lax.all_to_all(jnp.broadcast_to(in_weight[None], (8,) + in_weight.shape),...  5.42 us
  transfers between devices with their start and end apart: 21, of which 12 were waited for; matrix products, arithmetic and copies ran while one was open for 17% of the time, Pallas kernels for 1%

profile of v1, /device:TPU:24, one launch (start us, length us, event | category | flops | bytes accessed | tf_op | source)
XLA Modules:
  0.0 129.2 jit_solution(2491268382855297462)
XLA Ops:
  0.0 0.8 slice_bitcast_fusion
  0.8 1.9 %collective-permute-start = (bf16[8,2560]{1,0:T(8,128)(2,1)S(1)}, bf16[8,2560]{1,0:T(8,128)(2,1)S(1)}, u32[]{:S(2)}, u32[]{:S(2)}) collective-permute-start(bf16[8,2560]{1,0:T(8,128)(2,1)S(1)} %slice_bitcast_fusion), channel_id=1, source_target_pairs={{0,8},{8,16},{16,24},{24,32},{32,40},{40,48},{48,56},{56,64},{64,7... | collective-permute-start | bytes 122888 | tf_op jit(solution)/shard_map/ppermute | solution.py:30
  2.7 6.1 %collective-permute-done = bf16[8,2560]{1,0:T(8,128)(2,1)S(1)} collective-permute-done((bf16[8,2560]{1,0:T(8,128)(2,1)S(1)}, bf16[8,2560]{1,0:T(8,128)(2,1)S(1)}, u32[]{:S(2)}, u32[]{:S(2)}) %collective-permute-start) | collective-permute-done | bytes 40992 | tf_op jit(solution)/shard_map/ppermute | solution.py:30
  8.8 1.1 pad_maximum_fusion.5
  9.9 2.8 %collective-permute-start.4 = (bf16[136,2560]{1,0:T(8,128)(2,1)S(1)}, bf16[136,2560]{1,0:T(8,128)(2,1)}, u32[]{:S(2)}, u32[]{:S(2)}) collective-permute-start(bf16[136,2560]{1,0:T(8,128)(2,1)S(1)} %pad_maximum_fusion.5), channel_id=1, source_target_pairs={{0,6},{2,0},{4,2},{6,4},{1,7},{3,1},{5,3},{7,5},{8,14},{10,8},{12,... | collective-permute-start | bytes 2088968 | tf_op jit(solution)/shard_map/ppermute | solution.py:30
  12.8 1.8 %broadcast_in_dim.23 = bf16[8,80,432]{2,1,0:T(8,128)(2,1)} broadcast(bf16[80,432]{1,0:T(8,128)(2,1)} %param.14), dimensions={1,2} | broadcast | bytes 622080 | tf_op jit(solution)/shard_map/broadcast_in_dim | solution.py:225
  14.6 5.7 %all-to-all-start = ((bf16[8,80,432]{2,1,0:T(8,128)(2,1)}), bf16[8,80,432]{2,1,0:T(8,128)(2,1)S(1)}, u32[]{:S(2)}, u32[]{:S(2)}) async-start(bf16[8,80,432]{2,1,0:T(8,128)(2,1)} %broadcast_in_dim.23), calls=%async_computation | async-start | bytes 1310720 | tf_op jit(solution)/shard_map/all_to_all | solution.py:224
  20.3 6.5 %collective-permute-done.4 = bf16[136,2560]{1,0:T(8,128)(2,1)} collective-permute-done((bf16[136,2560]{1,0:T(8,128)(2,1)S(1)}, bf16[136,2560]{1,0:T(8,128)(2,1)}, u32[]{:S(2)}, u32[]{:S(2)}) %collective-permute-start.4) | collective-permute-done | bytes 696352 | tf_op jit(solution)/shard_map/ppermute | solution.py:30
  26.8 1.8 %slice.70 = bf16[72,2560]{1,0:T(8,128)(2,1)} slice(bf16[136,2560]{1,0:T(8,128)(2,1)} %collective-permute-done.4), slice={[64:136], [0:2560]} | slice | bytes 737280 | tf_op jit(solution)/shard_map/slice | solution.py:41
  28.5 3.8 %collective-permute-start.7 = (bf16[72,2560]{1,0:T(8,128)(2,1)}, bf16[72,2560]{1,0:T(8,128)(2,1)S(1)}, u32[]{:S(2)}, u32[]{:S(2)}) collective-permute-start(bf16[72,2560]{1,0:T(8,128)(2,1)} %slice.70), channel_id=1, source_target_pairs={{0,6},{2,0},{4,2},{6,4},{1,7},{3,1},{5,3},{7,5},{8,14},{10,8},{12,... | collective-permute-start | bytes 1105928 | tf_op jit(solution)/shard_map/ppermute | solution.py:30
  32.3 1.7 %slice.69 = bf16[64,2560]{1,0:T(8,128)(2,1)} slice(bf16[136,2560]{1,0:T(8,128)(2,1)} %collective-permute-done.2), slice={[0:64], [0:2560]} | slice | bytes 655360 | tf_op jit(solution)/shard_map/slice | solution.py:40
  34.1 0.5 collective-permute-start.5
  34.6 1.2 pad_maximum_fusion.1.t0
  35.8 5.4 %all-to-all-done = bf16[8,80,432]{2,1,0:T(8,128)(2,1)S(1)} async-done(((bf16[8,80,432]{2,1,0:T(8,128)(2,1)}), bf16[8,80,432]{2,1,0:T(8,128)(2,1)S(1)}, u32[]{:S(2)}, u32[]{:S(2)}) %all-to-all-start) | async-done | bytes 552992 | tf_op jit(solution)/shard_map/all_to_all | solution.py:224
  41.2 1.1 copy.12
  42.3 0.7 collective-permute-start.10
  43.0 2.5 %collective-permute-start.9 = (bf16[640,432]{0,1:T(8,128)(2,1)}, bf16[640,432]{0,1:T(8,128)(2,1)}, u32[]{:S(2)}, u32[]{:S(2)}) collective-permute-start(bf16[640,432]{0,1:T(8,128)(2,1)} %copy.12), channel_id=1, source_target_pairs={{0,64},{64,128},{128,192},{192,0},{1,65},{65,129},{129,193},{193,1... | collective-permute-start | bytes 1658888 | tf_op jit(solution)/shard_map/ppermute | solution.py:30
  45.5 1.0 pad_maximum_fusion.6
  46.5 2.5 %pad_maximum_fusion.2.t1 = bf16[272,2560]{1,0:T(8,128)(2,1)} fusion(bf16[136,2560]{1,0:T(8,128)(2,1)} %collective-permute-done.3, bf16[136,2560]{1,0:T(8,128)(2,1)} %collective-permute-done.2), kind=kLoop, calls=%fused_computation.2 | loop fusion | flops 2785280 | bytes 2785280 | tf_op jit(solution)/shard_map/concatenate | solution.py:232
  49.0 2.5 %pad_maximum_fusion.3.t2 = bf16[272,2560]{1,0:T(8,128)(2,1)} fusion(bf16[136,2560]{1,0:T(8,128)(2,1)} %collective-permute-done.5, bf16[136,2560]{1,0:T(8,128)(2,1)} %collective-permute-done.4), kind=kLoop, calls=%fused_computation.3 | loop fusion | flops 2785280 | bytes 2785280 | tf_op jit(solution)/shard_map/concatenate | solution.py:232
  51.5 6.8 %collective-permute-done.10 = bf16[640,432]{0,1:T(8,128)(2,1)} collective-permute-done((bf16[640,432]{0,1:T(8,128)(2,1)}, bf16[640,432]{0,1:T(8,128)(2,1)}, u32[]{:S(2)}, u32[]{:S(2)}) %collective-permute-start.10) | collective-permute-done | bytes 552992 | tf_op jit(solution)/shard_map/ppermute | solution.py:30
  58.3 1.3 copy.17.w2
  59.6 0.8 slice.72
  60.4 1.3 copy.16.w1
  61.7 3.5 %collective-permute-start.11 = (bf16[256,432]{1,0:T(8,128)(2,1)S(1)}, bf16[256,432]{1,0:T(8,128)(2,1)S(1)}, u32[]{:S(2)}, u32[]{:S(2)}) collective-permute-start(bf16[256,432]{1,0:T(8,128)(2,1)S(1)} %slice.71), channel_id=1, source_target_pairs={{0,64},{64,128},{128,192},{192,0},{1,65},{65,129},{129,193},{193,1... | collective-permute-start | bytes 663560 | tf_op jit(solution)/shard_map/ppermute | solution.py:30
  65.2 2.5 %pad_maximum_fusion.4.t3 = bf16[272,2560]{1,0:T(8,128)(2,1)} fusion(bf16[136,2560]{1,0:T(8,128)(2,1)} %collective-permute-done.8, bf16[72,2560]{1,0:T(8,128)(2,1)} %copy-done.4, bf16[64,2560]{1,0:T(8,128)(2,1)} %copy-done.5), kind=kLoop, calls=%fused_computation.4 | loop fusion | flops 4177920 | bytes 2785280 | tf_op jit(solution)/shard_map/concatenate | solution.py:232
  67.7 2.2 %collective-permute-done.11.w3 = bf16[256,432]{1,0:T(8,128)(2,1)S(1)} collective-permute-done((bf16[256,432]{1,0:T(8,128)(2,1)S(1)}, bf16[256,432]{1,0:T(8,128)(2,1)S(1)}, u32[]{:S(2)}, u32[]{:S(2)}) %collective-permute-start.11) | collective-permute-done | bytes 221216 | tf_op jit(solution)/shard_map/ppermute | solution.py:30
  69.8 2.3 %collective-permute-done.12.w4 = bf16[384,432]{1,0:T(8,128)(2,1)} collective-permute-done((bf16[384,432]{1,0:T(8,128)(2,1)}, bf16[384,432]{1,0:T(8,128)(2,1)}, u32[]{:S(2)}, u32[]{:S(2)}) %collective-permute-start.12) | collective-permute-done | bytes 331808 | tf_op jit(solution)/shard_map/ppermute | solution.py:30
  72.1 6.1 %shard_map.109 = bf16[8,464,128]{2,1,0:T(8,128)(2,1)S(1)} custom-call(s32[3]{0:T(128)S(1)} %pad_add_fusion.at_ref, bf16[272,2560]{1,0:T(8,128)(2,1)S(1)} %pad_maximum_fusion.1.t0, bf16[272,2560]{1,0:T(8,128)(2,1)} %pad_maximum_fusion.2.t1, bf16[272,2560]{1,0:T(8,128)(2,1)} %pad_maximum_fusion.3.t2, bf16[272,2560]{1,0:T(8,128)(2,1)} %pad_maximum_fusion.4.t3, ...), custom_call_target="tpu_custom_call" | custom-call | flops 2406481920 | bytes 8000000 | tf_op jit(solution)/shard_map/pallas_call | solution.py:260
  78.2 0.9 copy-done
  79.2 4.7 %all-to-all-start.1 = ((bf16[8,464,128]{2,1,0:T(8,128)(2,1)}), bf16[8,464,128]{2,1,0:T(8,128)(2,1)S(1)}, u32[]{:S(2)}, u32[]{:S(2)}) async-start(bf16[8,464,128]{2,1,0:T(8,128)(2,1)} %copy-done), calls=%async_computation.1 | async-start | bytes 1900544 | tf_op jit(solution)/shard_map/all_to_all | solution.py:271
  83.9 0.1 collective-permute-start.13
  84.1 2.7 %pad_maximum_fusion.gates_ref = bf16[27,128,256]{2,1,0:T(8,128)(2,1)} fusion(bf16[27,128,128]{2,1,0:T(8,128)(2,1)S(1)} %copy-done.6, bf16[27,128,128]{2,1,0:T(8,128)(2,1)} %param.17), kind=kLoop, calls=%fused_computation | loop fusion | flops 3538944 | bytes 3538944 | tf_op jit(solution)/shard_map/concatenate | solution.py:258
  86.8 0.1 concatenate.39.par_ref
  86.9 2.7 %collective-permute-done.13 = bf16[1,128]{1,0:T(2,128)(2,1)S(1)} collective-permute-done((bf16[1,128]{1,0:T(2,128)(2,1)S(1)}, bf16[1,128]{1,0:T(2,128)(2,1)S(1)}, u32[]{:S(2)}, u32[]{:S(2)}) %collective-permute-start.13) | collective-permute-done | bytes 288 | tf_op jit(solution)/shard_map/ppermute | solution.py:30
  89.6 1.0 shard_map.110
  90.6 1.2 copy-done.1
  91.9 6.9 %all-to-all-done.1.got_ref = bf16[8,464,128]{2,1,0:T(8,128)(2,1)S(1)} async-done(((bf16[8,464,128]{2,1,0:T(8,128)(2,1)}), bf16[8,464,128]{2,1,0:T(8,128)(2,1)S(1)}, u32[]{:S(2)}, u32[]{:S(2)}) %all-to-all-start.1) | async-done | bytes 950304 | tf_op jit(solution)/shard_map/all_to_all | solution.py:271
  98.8 11.0 %shard_map.111 = (f32[27,128,128]{2,1,0:T(8,128)S(1)}, f32[27,128,128]{2,1,0:T(8,128)S(1)}, f32[2,3456]{1,0:T(2,128)S(1)}) custom-call(bf16[8,464,128]{2,1,0:T(8,128)(2,1)S(1)} %all-to-all-done.1.got_ref, f32[4,128,128]{2,1,0:T(8,128)S(1)} %get-tuple-element.10.mask_ref, f32[27,128,128]{2,1,0:T(8,128)} %copy-done.1, f32[8,3456]{1,0:T(8,128)S(1)} %concatenate.39.par_ref, ...), custom_call_target="tpu_custom_call" | custom-call | flops 226492416 | bytes 8000000 | tf_op jit(solution)/shard_map/pallas_call | solution.py:272
  109.7 0.1 collective-permute-start.14
  109.8 6.0 %collective-permute-done.14 = f32[2,3456]{1,0:T(2,128)S(1)} collective-permute-done((f32[2,3456]{1,0:T(2,128)S(1)}, f32[2,3456]{1,0:T(2,128)S(1)}, u32[]{:S(2)}, u32[]{:S(2)}) %collective-permute-start.14) | collective-permute-done | bytes 27680 | tf_op jit(solution)/shard_map/ppermute | solution.py:30
  115.9 0.1 collective-permute-start.15
  115.9 0.1 collective-permute-start.16
  116.0 7.1 %collective-permute-start.17 = (f32[2,3456]{1,0:T(2,128)S(1)}, f32[2,3456]{1,0:T(2,128)S(1)}, u32[]{:S(2)}, u32[]{:S(2)}) collective-permute-start(f32[2,3456]{1,0:T(2,128)S(1)} %pad_maximum_fusion.7), channel_id=1, source_target_pairs={{0,40},{8,48},{16,56},{24,64},{32,72},{40,80},{48,88},{56,96},{64,... | collective-permute-start | bytes 82952 | tf_op jit(solution)/shard_map/ppermute | solution.py:30
  123.1 0.7 collective-permute-done.16
  123.8 1.0 collective-permute-done.17
  124.8 3.1 %collective-permute-done.18 = f32[2,3456]{1,0:T(2,128)S(1)} collective-permute-done((f32[2,3456]{1,0:T(2,128)S(1)}, f32[2,3456]{1,0:T(2,128)S(1)}, u32[]{:S(2)}, u32[]{:S(2)}) %collective-permute-start.18) | collective-permute-done | bytes 27680 | tf_op jit(solution)/shard_map/ppermute | solution.py:30
  128.0 1.2 shard_map.112
  (53 shorter events, 0.4 us)
Async XLA Ops:
  0.8 8.0 %collective-permute-start = (bf16[8,2560]{1,0:T(8,128)(2,1)S(1)}, bf16[8,2560]{1,0:T(8,128)(2,1)S(1)}, u32[]{:S(2)}, u32[]{:S(2)}) collective-permute-start(bf16[8,2560]{1,0:T(8,128)(2,1)S(1)} %slice_bitcast_fusion), channel_id=1, source_target_pairs={{0,8},{8,16},{16,24},{24,32},{32,40},{40,48},{48,56},{56,64},{64,7... | collective-permute-start | bytes 122888 | tf_op jit(solution)/shard_map/ppermute | solution.py:30
  9.9 24.7 %copy-start.3 = (bf16[1,128,2560]{2,1,0:T(8,128)(2,1)S(1)}, bf16[1,128,2560]{2,1,0:T(8,128)(2,1)}, u32[]{:S(2)}) copy-start(bf16[1,128,2560]{2,1,0:T(8,128)(2,1)} %param.11) | copy-start | bytes 1966084
  9.9 16.8 %collective-permute-start.4 = (bf16[136,2560]{1,0:T(8,128)(2,1)S(1)}, bf16[136,2560]{1,0:T(8,128)(2,1)}, u32[]{:S(2)}, u32[]{:S(2)}) collective-permute-start(bf16[136,2560]{1,0:T(8,128)(2,1)S(1)} %pad_maximum_fusion.5), channel_id=1, source_target_pairs={{0,6},{2,0},{4,2},{6,4},{1,7},{3,1},{5,3},{7,5},{8,14},{10,8},{12,... | collective-permute-start | bytes 2088968 | tf_op jit(solution)/shard_map/ppermute | solution.py:30
  12.8 19.6 %collective-permute-start.2 = (bf16[136,2560]{1,0:T(8,128)(2,1)S(1)}, bf16[136,2560]{1,0:T(8,128)(2,1)}, u32[]{:S(2)}, u32[]{:S(2)}) collective-permute-start(bf16[136,2560]{1,0:T(8,128)(2,1)S(1)} %pad_maximum_fusion.5), channel_id=1, source_target_pairs={{0,2},{2,4},{4,6},{6,0},{1,3},{3,5},{5,7},{7,1},{8,10},{10,12},{12... | collective-permute-start | bytes 2088968 | tf_op jit(solution)/shard_map/ppermute | solution.py:30
  12.8 21.8 %collective-permute-start.1 = (bf16[136,2560]{1,0:T(8,128)(2,1)S(1)}, bf16[136,2560]{1,0:T(8,128)(2,1)}, u32[]{:S(2)}, u32[]{:S(2)}) collective-permute-start(bf16[136,2560]{1,0:T(8,128)(2,1)S(1)} %pad_maximum_fusion.5), channel_id=1, source_target_pairs={{0,1},{1,0},{2,3},{3,2},{4,5},{5,4},{6,7},{7,6},{8,9},{9,8},{10,11... | collective-permute-start | bytes 2088968 | tf_op jit(solution)/shard_map/ppermute | solution.py:34
  14.6 26.6 %all-to-all-start = ((bf16[8,80,432]{2,1,0:T(8,128)(2,1)}), bf16[8,80,432]{2,1,0:T(8,128)(2,1)S(1)}, u32[]{:S(2)}, u32[]{:S(2)}) async-start(bf16[8,80,432]{2,1,0:T(8,128)(2,1)} %broadcast_in_dim.23), calls=%async_computation | async-start | bytes 1310720 | tf_op jit(solution)/shard_map/all_to_all | solution.py:224
  28.5 17.0 %collective-permute-start.7 = (bf16[72,2560]{1,0:T(8,128)(2,1)}, bf16[72,2560]{1,0:T(8,128)(2,1)S(1)}, u32[]{:S(2)}, u32[]{:S(2)}) collective-permute-start(bf16[72,2560]{1,0:T(8,128)(2,1)} %slice.70), channel_id=1, source_target_pairs={{0,6},{2,0},{4,2},{6,4},{1,7},{3,1},{5,3},{7,5},{8,14},{10,8},{12,... | collective-permute-start | bytes 1105928 | tf_op jit(solution)/shard_map/ppermute | solution.py:30
  34.1 9.0 %collective-permute-start.6 = (bf16[64,2560]{1,0:T(8,128)(2,1)}, bf16[64,2560]{1,0:T(8,128)(2,1)S(1)}, u32[]{:S(2)}, u32[]{:S(2)}) collective-permute-start(bf16[64,2560]{1,0:T(8,128)(2,1)} %slice.69), channel_id=1, source_target_pairs={{0,2},{2,4},{4,6},{6,0},{1,3},{3,5},{5,7},{7,1},{8,10},{10,12},{12... | collective-permute-start | bytes 983048 | tf_op jit(solution)/shard_map/ppermute | solution.py:30
  34.1 12.4 %collective-permute-start.3 = (bf16[136,2560]{1,0:T(8,128)(2,1)}, bf16[136,2560]{1,0:T(8,128)(2,1)}, u32[]{:S(2)}, u32[]{:S(2)}) collective-permute-start(bf16[136,2560]{1,0:T(8,128)(2,1)} %collective-permute-done.2), channel_id=1, source_target_pairs={{0,1},{1,0},{2,3},{3,2},{4,5},{5,4},{6,7},{7,6},{8,9},{9,8},{10,11... | collective-permute-start | bytes 2088968 | tf_op jit(solution)/shard_map/ppermute | solution.py:34
  34.1 15.0 %collective-permute-start.5 = (bf16[136,2560]{1,0:T(8,128)(2,1)}, bf16[136,2560]{1,0:T(8,128)(2,1)}, u32[]{:S(2)}, u32[]{:S(2)}) collective-permute-start(bf16[136,2560]{1,0:T(8,128)(2,1)} %collective-permute-done.4), channel_id=1, source_target_pairs={{0,1},{1,0},{2,3},{3,2},{4,5},{5,4},{6,7},{7,6},{8,9},{9,8},{10,11... | collective-permute-start | bytes 2088968 | tf_op jit(solution)/shard_map/ppermute | solution.py:34
  42.3 16.0 %collective-permute-start.10 = (bf16[640,432]{0,1:T(8,128)(2,1)}, bf16[640,432]{0,1:T(8,128)(2,1)}, u32[]{:S(2)}, u32[]{:S(2)}) collective-permute-start(bf16[640,432]{0,1:T(8,128)(2,1)} %copy.12), channel_id=1, source_target_pairs={{0,192},{64,0},{128,64},{192,128},{1,193},{65,1},{129,65},{193,129... | collective-permute-start | bytes 1658888 | tf_op jit(solution)/shard_map/ppermute | solution.py:30
  43.0 6.0 %copy-start.5 = (bf16[64,2560]{1,0:T(8,128)(2,1)}, bf16[64,2560]{1,0:T(8,128)(2,1)S(1)}, u32[]{:S(2)}) copy-start(bf16[64,2560]{1,0:T(8,128)(2,1)S(1)} %collective-permute-done.6) | copy-start | bytes 983044
  43.0 17.3 %collective-permute-start.9 = (bf16[640,432]{0,1:T(8,128)(2,1)}, bf16[640,432]{0,1:T(8,128)(2,1)}, u32[]{:S(2)}, u32[]{:S(2)}) collective-permute-start(bf16[640,432]{0,1:T(8,128)(2,1)} %copy.12), channel_id=1, source_target_pairs={{0,64},{64,128},{128,192},{192,0},{1,65},{65,129},{129,193},{193,1... | collective-permute-start | bytes 1658888 | tf_op jit(solution)/shard_map/ppermute | solution.py:30
  45.5 3.5 %copy-start.4 = (bf16[72,2560]{1,0:T(8,128)(2,1)}, bf16[72,2560]{1,0:T(8,128)(2,1)S(1)}, u32[]{:S(2)}) copy-start(bf16[72,2560]{1,0:T(8,128)(2,1)S(1)} %collective-permute-done.7) | copy-start | bytes 1105924
  46.5 18.7 %collective-permute-start.8 = (bf16[136,2560]{1,0:T(8,128)(2,1)}, bf16[136,2560]{1,0:T(8,128)(2,1)}, u32[]{:S(2)}, u32[]{:S(2)}) collective-permute-start(bf16[136,2560]{1,0:T(8,128)(2,1)} %pad_maximum_fusion.6), channel_id=1, source_target_pairs={{0,1},{1,0},{2,3},{3,2},{4,5},{5,4},{6,7},{7,6},{8,9},{9,8},{10,11... | collective-permute-start | bytes 2088968 | tf_op jit(solution)/shard_map/ppermute | solution.py:34
  60.4 11.7 %collective-permute-start.12 = (bf16[384,432]{1,0:T(8,128)(2,1)}, bf16[384,432]{1,0:T(8,128)(2,1)}, u32[]{:S(2)}, u32[]{:S(2)}) collective-permute-start(bf16[384,432]{1,0:T(8,128)(2,1)} %slice.72), channel_id=1, source_target_pairs={{0,192},{64,0},{128,64},{192,128},{1,193},{65,1},{129,65},{193,129... | collective-permute-start | bytes 995336 | tf_op jit(solution)/shard_map/ppermute | solution.py:30
  61.7 8.1 %collective-permute-start.11 = (bf16[256,432]{1,0:T(8,128)(2,1)S(1)}, bf16[256,432]{1,0:T(8,128)(2,1)S(1)}, u32[]{:S(2)}, u32[]{:S(2)}) collective-permute-start(bf16[256,432]{1,0:T(8,128)(2,1)S(1)} %slice.71), channel_id=1, source_target_pairs={{0,64},{64,128},{128,192},{192,0},{1,65},{65,129},{129,193},{193,1... | collective-permute-start | bytes 663560 | tf_op jit(solution)/shard_map/ppermute | solution.py:30
  78.2 0.9 copy-start
  79.2 4.7 %copy-start.12 = (s32[1,128]{1,0:T(1,128)S(1)}, s32[1,128]{1,0:T(1,128)}, u32[]{:S(2)}) copy-start(s32[1,128]{1,0:T(1,128)} %param.13) | copy-start | bytes 1540
  79.2 4.8 %copy-start.8 = (f32[3456]{0:T(1024)S(1)}, f32[3456]{0:T(1024)}, u32[]{:S(2)}) copy-start(f32[3456]{0:T(1024)} %param.21) | copy-start | bytes 41476
  79.2 4.8 %copy-start.9 = (f32[3456]{0:T(1024)S(1)}, f32[3456]{0:T(1024)}, u32[]{:S(2)}) copy-start(f32[3456]{0:T(1024)} %param.16) | copy-start | bytes 41476
  79.2 4.9 %copy-start.10 = (f32[3456]{0:T(1024)S(1)}, f32[3456]{0:T(1024)}, u32[]{:S(2)}) copy-start(f32[3456]{0:T(1024)} %param.19) | copy-start | bytes 41476
  79.2 4.9 %copy-start.11 = (f32[3456]{0:T(1024)S(1)}, f32[3456]{0:T(1024)}, u32[]{:S(2)}) copy-start(f32[3456]{0:T(1024)} %param.20) | copy-start | bytes 41476
  79.2 4.9 %copy-start.6 = (bf16[27,128,128]{2,1,0:T(8,128)(2,1)S(1)}, bf16[27,128,128]{2,1,0:T(8,128)(2,1)}, u32[]{:S(2)}) copy-start(bf16[27,128,128]{2,1,0:T(8,128)(2,1)} %param.18) | copy-start | bytes 2654212
  79.2 19.6 %all-to-all-start.1 = ((bf16[8,464,128]{2,1,0:T(8,128)(2,1)}), bf16[8,464,128]{2,1,0:T(8,128)(2,1)S(1)}, u32[]{:S(2)}, u32[]{:S(2)}) async-start(bf16[8,464,128]{2,1,0:T(8,128)(2,1)} %copy-done), calls=%async_computation.1 | async-start | bytes 1900544 | tf_op jit(solution)/shard_map/all_to_all | solution.py:271
  83.9 5.7 %collective-permute-start.13 = (bf16[1,128]{1,0:T(2,128)(2,1)S(1)}, bf16[1,128]{1,0:T(2,128)(2,1)S(1)}, u32[]{:S(2)}, u32[]{:S(2)}) collective-permute-start(bf16[1,128]{1,0:T(2,128)(2,1)S(1)} %get-tuple-element.17), channel_id=1, source_target_pairs={{0,8},{8,16},{16,24},{24,32},{32,40},{40,48},{48,56},{56,64},{64,7... | collective-permute-start | bytes 776 | tf_op jit(solution)/shard_map/ppermute | solution.py:30
  84.1 2.7 %copy-start.7 = (f32[4,3456]{1,0:T(4,128)S(1)}, f32[4,3456]{1,0:T(4,128)}, u32[]{:S(2)}) copy-start(f32[4,3456]{1,0:T(4,128)} %param.15) | copy-start | bytes 165892
  84.1 5.5 %copy-start.2 = (bf16[1,128,3456]{2,1,0:T(8,128)(2,1)S(1)}, bf16[1,128,3456]{2,1,0:T(8,128)(2,1)}, u32[]{:S(2)}) copy-start(bf16[1,128,3456]{2,1,0:T(8,128)(2,1)} %param.12) | copy-start | bytes 2654212
  90.6 1.2 copy-start.1
  109.7 6.0 %collective-permute-start.14 = (f32[2,3456]{1,0:T(2,128)S(1)}, f32[2,3456]{1,0:T(2,128)S(1)}, u32[]{:S(2)}, u32[]{:S(2)}) collective-permute-start(f32[2,3456]{1,0:T(2,128)S(1)} %get-tuple-element.14), channel_id=1, source_target_pairs={{0,8},{8,16},{16,24},{24,32},{32,40},{40,48},{48,56},{56,64},{64,7... | collective-permute-start | bytes 82952 | tf_op jit(solution)/shard_map/ppermute | solution.py:30
  115.9 7.3 %collective-permute-start.15 = (f32[2,3456]{1,0:T(2,128)S(1)}, f32[2,3456]{1,0:T(2,128)S(1)}, u32[]{:S(2)}, u32[]{:S(2)}) collective-permute-start(f32[2,3456]{1,0:T(2,128)S(1)} %pad_maximum_fusion.7), channel_id=1, source_target_pairs={{0,8},{8,16},{16,24},{24,32},{32,40},{40,48},{48,56},{56,64},{64,7... | collective-permute-start | bytes 82952 | tf_op jit(solution)/shard_map/ppermute | solution.py:30
  115.9 7.8 %collective-permute-start.16 = (f32[2,3456]{1,0:T(2,128)S(1)}, f32[2,3456]{1,0:T(2,128)S(1)}, u32[]{:S(2)}, u32[]{:S(2)}) collective-permute-start(f32[2,3456]{1,0:T(2,128)S(1)} %pad_maximum_fusion.7), channel_id=1, source_target_pairs={{0,24},{8,32},{16,40},{24,48},{32,56},{40,64},{48,72},{56,80},{64,... | collective-permute-start | bytes 82952 | tf_op jit(solution)/shard_map/ppermute | solution.py:30
  116.0 8.7 %collective-permute-start.17 = (f32[2,3456]{1,0:T(2,128)S(1)}, f32[2,3456]{1,0:T(2,128)S(1)}, u32[]{:S(2)}, u32[]{:S(2)}) collective-permute-start(f32[2,3456]{1,0:T(2,128)S(1)} %pad_maximum_fusion.7), channel_id=1, source_target_pairs={{0,40},{8,48},{16,56},{24,64},{32,72},{40,80},{48,88},{56,96},{64,... | collective-permute-start | bytes 82952 | tf_op jit(solution)/shard_map/ppermute | solution.py:30
  123.1 4.8 %collective-permute-start.18 = (f32[2,3456]{1,0:T(2,128)S(1)}, f32[2,3456]{1,0:T(2,128)S(1)}, u32[]{:S(2)}, u32[]{:S(2)}) collective-permute-start(f32[2,3456]{1,0:T(2,128)S(1)} %pad_maximum_fusion.7), channel_id=1, source_target_pairs={{0,56},{8,64},{16,72},{24,80},{32,88},{40,96},{48,104},{56,112},{6... | collective-permute-start | bytes 82952 | tf_op jit(solution)/shard_map/ppermute | solution.py:30

commit v2 on v1

--- a/solution.py
+++ b/solution.py
@@ -22,7 +22,9 @@
 SPAN = 16
 HALO = 8
 PACK = COLS + 32
+FULL = 512
 CUT = 256
+ROWS = LENGTH + HALO
 
 
 def shift(value, axis, by):
@@ -32,14 +34,6 @@
 
 def flip(value):
     return lax.ppermute(value, "c", [(0, 1), (1, 0)])
-
-
-def ring(value, axis, cut):
-    back = shift(value, axis, 1)
-    ahead = shift(value, axis, -1)
-    first = shift(back[:cut], axis, 1)
-    second = shift(ahead[cut:], axis, -1)
-    return value, back, ahead, first, second
 
 
 def prepare_kernel(gate_ref, ids_ref, gelu_ref, mask_ref, ids_scr):
@@ -63,46 +57,87 @@
                 mask_ref[0, 8 * k : 8 * k + 8, :] = same
 
 
-def project_kernel(at_ref, t0, t1, t2, t3, w0, w1, w2, w3, w4, out_ref, acc_ref, wide_ref):
-    x, c, y = at_ref[0], at_ref[1], at_ref[2]
-    steps = (
-        (lax.rem(y, 4) * 640, 640, w0),
-        (lax.rem(y + 3, 4) * 640, 640, w1),
-        (lax.rem(y + 1, 4) * 640, 640, w2),
-        (lax.rem(y + 2, 4) * 640, CUT, w3),
-        (lax.rem(y + 2, 4) * 640 + CUT, 640 - CUT, w4),
-    )
-    for back, t_ref in ((0, t0), (1, t1), (3, t2), (2, t3)):
-        total = None
-        for start, size, w_ref in steps:
-            part = jnp.dot(
-                t_ref[:, pl.ds(pl.multiple_of(start, 128), size)],
-                w_ref[...],
-                preferred_element_type=F32,
-            )
-            total = part if total is None else total + part
-        acc_ref[...] = total
-        for other in range(2):
-            stream = lax.rem(x + 4 - back, 4) * 2 + (c if other == 0 else 1 - c)
-            top = other * (LENGTH + HALO)
-            wide_ref[:, 0:COLS] = acc_ref[top : top + LENGTH + HALO, :]
+def copies(pairs, sems):
+    made = [
+        pltpu.make_async_copy(src, dst, sems.at[i]) for i, (src, dst) in enumerate(pairs)
+    ]
+    for copy in made:
+        copy.start()
+    return made
+
+
+def project_kernel(at_ref, t0, t1, t2, t3, *refs):
+    weights, part_ref = refs[:6], refs[6]
+    y = at_ref[2]
+    for i, t_ref in enumerate((t0, t1, t2, t3)):
+        for half in range(2):
+            total = None
+            for j, back in enumerate((0, 3, 1)):
+                start = pl.multiple_of(lax.rem(y + back, 4) * 640, 128)
+                part = jnp.dot(
+                    t_ref[:, pl.ds(start, 640)],
+                    weights[2 * j + half][...],
+                    preferred_element_type=F32,
+                )
+                total = part if total is None else total + part
+            part_ref[i, half] = total
+
+
+def pack_kernel(at_ref, part_ref, t0, t1, t2, t3, *refs):
+    weights, outs = refs[:4], refs[4:8]
+    wide_ref = refs[8]
+    c, y = at_ref[1], at_ref[2]
+    far = lax.rem(y + 2, 4) * 640
+    for i, t_ref in enumerate((t0, t1, t2, t3)):
+        for half in range(2):
+            total = part_ref[i, half]
+            for j, (start, size) in enumerate(((far, CUT), (far + CUT, 640 - CUT))):
+                total = total + jnp.dot(
+                    t_ref[:, pl.ds(pl.multiple_of(start, 128), size)],
+                    weights[2 * j + half][...],
+                    preferred_element_type=F32,
+                )
+            wide_ref[...] = total
+            place = c if half == 0 else 1 - c
+            out_ref = outs[i]
             for j in range(4):
                 block = wide_ref[0:LENGTH, j * 128 : (j + 1) * 128].T.astype(BF16)
                 size = min(128, COLS - j * 128)
-                out_ref[stream, j * 128 : j * 128 + size, :] = block[:size]
+                out_ref[place, j * 128 : j * 128 + size, :] = block[:size]
             for j in range(2):
                 pair = [
-                    wide_ref[LENGTH : LENGTH + HALO, (2 * j + i) * 128 : (2 * j + i + 1) * 128]
-                    for i in range(2)
+                    wide_ref[LENGTH:ROWS, (2 * j + n) * 128 : (2 * j + n + 1) * 128]
+                    for n in range(2)
                 ]
-                out_ref[stream, COLS + 16 * j : COLS + 16 * j + 16, :] = jnp.concatenate(
+                out_ref[place, COLS + 16 * j : COLS + 16 * j + 16, :] = jnp.concatenate(
                     pair, axis=0
                 ).astype(BF16)
 
 
 def recur_kernel(
-    got_ref, mask_ref, gelu_ref, par_ref, gates_ref, state_ref, prod_ref, end_ref, x_scr
+    at_ref,
+    g0,
+    g1,
+    g2,
+    g3,
+    mask_ref,
+    gelu_ref,
+    par_ref,
+    gates_ref,
+    state_ref,
+    prod_ref,
+    end_ref,
+    x_scr,
+    got_ref,
+    sems,
 ):
+    x = at_ref[0]
+    pairs = [
+        (ref, got_ref.at[pl.ds(lax.rem(x + 4 - back, 4) * 2, 2)])
+        for back, ref in ((0, g0), (1, g1), (3, g2), (2, g3))
+    ]
+    for copy in copies(pairs, sems):
+        copy.wait()
     ahead = []
     for f in range(8):
         packed = got_ref[f, COLS:PACK, :].astype(F32)
@@ -184,14 +219,14 @@
     lax.fori_loop(0, HEADS, head, 0)
 
 
-def call(kernel, outs, ins, scratch=(), flops=0, moved=0):
+def call(kernel, outs, ins, scratch=(), room=16, flops=0, moved=0):
     return pl.pallas_call(
         kernel,
         out_shape=outs,
         in_specs=ins,
         out_specs=jax.tree.map(lambda _: VMEM, outs),
         scratch_shapes=list(scratch),
-        compiler_params=pltpu.CompilerParams(vmem_limit_bytes=48 * 2**20),
+        compiler_params=pltpu.CompilerParams(vmem_limit_bytes=room * 2**20),
         cost_estimate=pl.CostEstimate(flops=flops, bytes_accessed=moved, transcendentals=0),
     )
 
@@ -221,15 +256,19 @@
         jnp.int32
     )
 
+    filled = jnp.pad(in_weight, ((0, 0), (0, FULL - COLS)))
     column = lax.all_to_all(
-        jnp.broadcast_to(in_weight[None], (8,) + in_weight.shape), "z", 0, 0, tiled=True
-    ).reshape(-1, in_weight.shape[1])
-    weights = ring(column, "y", CUT)
+        jnp.broadcast_to(filled[None], (8,) + filled.shape), "z", 0, 0, tiled=True
+    ).reshape(-1, FULL)
+    from_back = shift(column, "y", 1)
+    from_ahead = shift(column, "y", -1)
+    near = [column, flip(column), from_back, flip(from_back), from_ahead, flip(from_ahead)]
+    first = shift(from_back[:CUT], "y", 1)
+    second = shift(from_ahead[CUT:], "y", -1)
+    far = [first, flip(first), second, flip(second)]
 
     rows = jnp.concatenate([own, shift(own[-HALO:], ctx, 1)], axis=0)
-    here, back, ahead, first, second = ring(rows, "x", 64)
-    far = jnp.concatenate([first, second], axis=0)
-    streams = [jnp.concatenate([t, flip(t)], axis=0) for t in (here, back, ahead, far)]
+    streams = [rows, shift(rows, "x", 1), shift(rows, "x", -1), shift(rows, "x", 2)]
 
     ids = segment_ids.astype(BF16)
     prior = shift(ids, ctx, 1).astype(F32)
@@ -257,18 +296,27 @@
     )
     gates = jnp.concatenate([gate_a, gate_i], axis=2)
 
+    part = call(
+        project_kernel,
+        jax.ShapeDtypeStruct((4, 2, ROWS, FULL), F32),
+        [SMEM] + [VMEM] * 10,
+        flops=2 * 544 * 1920 * 1024,
+        moved=9_000_000,
+    )(at, *streams, *near)
     sent = call(
-        project_kernel,
-        jax.ShapeDtypeStruct((8, PACK, 128), BF16),
+        pack_kernel,
+        [jax.ShapeDtypeStruct((2, PACK, 128), BF16)] * 4,
         [SMEM] + [VMEM] * 9,
-        [
-            pltpu.VMEM((2 * (LENGTH + HALO), COLS), F32),
-            pltpu.VMEM((LENGTH + HALO, 512), F32),
-        ],
-        flops=2 * 1088 * 2560 * 432,
-        moved=8_000_000,
-    )(at, *streams, *weights)
-    got = lax.all_to_all(sent, ("x", "c"), 0, 0, tiled=True)
+        [pltpu.VMEM((ROWS, FULL), F32)],
+        flops=2 * 544 * 640 * 1024,
+        moved=7_000_000,
+    )(at, part, *streams, *far)
+    got = [
+        sent[0],
+        shift(sent[2], "x", 1),
+        shift(sent[1], "x", -1),
+        shift(sent[3], "x", 2),
+    ]
     states, prods, ends = call(
         recur_kernel,
         (
@@ -276,11 +324,15 @@
             jax.ShapeDtypeStruct((HEADS, LENGTH, HEAD), F32),
             jax.ShapeDtypeStruct((2, WIDTH), F32),
         ),
-        [VMEM] * 5,
-        [pltpu.VMEM((HEADS, LENGTH + HALO, HEAD), F32)],
+        [SMEM] + [pl.BlockSpec(memory_space=pl.ANY)] * 4 + [VMEM] * 4,
+        [
+            pltpu.VMEM((HEADS, LENGTH + HALO, HEAD), F32),
+            pltpu.VMEM((8, PACK, 128), BF16),
+            pltpu.SemaphoreType.DMA((4,)),
+        ],
         flops=2 * 128 * 3456 * 256,
         moved=8_000_000,
-    )(got, masks, gelu, params, gates)
+    )(at, *got, masks, gelu, params, gates)
 
     two = joined(shift(ends, ctx, 1), ends)
     pairs = [shift(two, ctx, by) for by in (7, 5, 3, 1)]

time: 130 us -> 128 us (0.985); the launches traced: 129 us -> 126 us
  other arithmetic: 13.7 us -> 2.51 us
  starting transfers between devices: 33.5 us -> 41.9 us
  local copies, waits for them, and re-layouts: 12.9 us -> 8.75 us
  waiting for transfers between devices: 49.5 us -> 52.2 us
    ppermute x15 -> x17, waiting for transfers between devices: 37.2 us -> 51.4 us  [shift(): lax.ppermute(value, axis, [(i, (i + by) % count) for i in range(count)])]
    all_to_all x2 -> x1, waiting for transfers between devices: 12.3 us -> 0.82 us  [body(): lax.all_to_all(jnp.broadcast_to(filled[None], (8,) + filled.shape), 'z',...]
    ppermute x15 -> x17, starting transfers between devices: 22.7 us -> 32.4 us  [shift(): lax.ppermute(value, axis, [(i, (i + by) % count) for i in range(count)])]
    concatenate x5 -> x0, other arithmetic: 9.65 us -> none  [the longest x4 8.69 us: body(): jnp.concatenate([t, flip(t)], axis=0)]
    ppermute x2 -> x0, local copies, waits for them, and re-layouts: 2.58 us -> none  [shift(): lax.ppermute(value, axis, [(i, (i + by) % count) for i in range(count)])]
    unnamed x26 -> x16, local copies, waits for them, and re-layouts: 2.21 us -> 0.04 us
    all_to_all x2 -> x1, starting transfers between devices: 10.3 us -> 8.6 us  [body(): lax.all_to_all(jnp.broadcast_to(filled[None], (8,) + filled.shape), 'z',...]
    pallas_call x1 -> x2, Pallas kernels: 6.13 us -> 7.27 us  [the longest x1 4.83 us: body(): call(project_kernel, jax.ShapeDtypeStruct((4, 2, ROWS, FULL), F32), [SMEM...]
  transfers between devices with their start and end apart: 21 -> 23, of which waited for: 12 -> 11; matrix products, arithmetic and copies ran while one was open for 17% -> 7% of each run, Pallas kernels for 1% -> 7%
where the time goes in v2:
time: 128 us; the launch traced here: 126 us
  waiting for transfers between devices  52.2 us (41%)
  starting transfers between devices  41.9 us (33%)
  Pallas kernels  20.2 us (16%)
  local copies, waits for them, and re-layouts  8.75 us (7%)
  other arithmetic  2.51 us (2%)
    ppermute x17, waiting for transfers between devices, shift(): lax.ppermute(value, axis, [(i, (i + by) % count) for i in range(count)])  51.4 us
    ppermute x17, starting transfers between devices, shift(): lax.ppermute(value, axis, [(i, (i + by) % count) for i in range(count)])  32.4 us
    pallas_call x1, Pallas kernels, body(): call(recur_kernel, (jax.ShapeDtypeStruct((HEADS, LENGTH, HEAD), F32), jax...  10.8 us
    all_to_all x1, starting transfers between devices, body(): lax.all_to_all(jnp.broadcast_to(filled[None], (8,) + filled.shape), 'z',...  8.6 us
    pallas_call x1, Pallas kernels, body(): call(project_kernel, jax.ShapeDtypeStruct((4, 2, ROWS, FULL), F32), [SMEM...  4.83 us
  transfers between devices with their start and end apart: 23, of which 11 were waited for; matrix products, arithmetic and copies ran while one was open for 7% of the time, Pallas kernels for 7%

profile of v2, /device:TPU:24, one launch (start us, length us, event | category | flops | bytes accessed | tf_op | source)
XLA Modules:
  0.0 125.8 jit_solution(8354127167838410532)
XLA Ops:
  0.0 1.0 pad.4
  1.0 0.9 broadcast_in_dim.23
  1.9 8.6 %all-to-all-start = ((bf16[8,80,512]{2,1,0:T(8,128)(2,1)}), bf16[8,80,512]{2,1,0:T(8,128)(2,1)S(1)}, u32[]{:S(2)}, u32[]{:S(2)}) async-start(bf16[8,80,512]{2,1,0:T(8,128)(2,1)} %broadcast_in_dim.23), calls=%async_computation | async-start | bytes 1310720 | tf_op jit(solution)/shard_map/all_to_all | solution.py:260
  10.5 2.1 %collective-permute-start = (bf16[8,2560]{1,0:T(8,128)(2,1)S(1)}, bf16[8,2560]{1,0:T(8,128)(2,1)S(1)}, u32[]{:S(2)}, u32[]{:S(2)}) collective-permute-start(bf16[8,2560]{1,0:T(8,128)(2,1)S(1)} %slice_bitcast_fusion), channel_id=1, source_target_pairs={{0,8},{8,16},{16,24},{24,32},{32,40},{40,48},{48,56},{56,64},{64,7... | collective-permute-start | bytes 122888 | tf_op jit(solution)/shard_map/ppermute | solution.py:32
  12.6 13.9 %collective-permute-done = bf16[8,2560]{1,0:T(8,128)(2,1)S(1)} collective-permute-done((bf16[8,2560]{1,0:T(8,128)(2,1)S(1)}, bf16[8,2560]{1,0:T(8,128)(2,1)S(1)}, u32[]{:S(2)}, u32[]{:S(2)}) %collective-permute-start) | collective-permute-done | bytes 40992 | tf_op jit(solution)/shard_map/ppermute | solution.py:32
  26.6 1.6 %collective-permute-start.1 = (bf16[136,2560]{1,0:T(8,128)(2,1)S(1)}, bf16[136,2560]{1,0:T(8,128)(2,1)S(1)}, u32[]{:S(2)}, u32[]{:S(2)}) collective-permute-start(bf16[136,2560]{1,0:T(8,128)(2,1)S(1)} %pad_maximum_fusion.1.t0), channel_id=1, source_target_pairs={{0,2},{2,4},{4,6},{6,0},{1,3},{3,5},{5,7},{7,1},{8,10},{10,12},{12... | collective-permute-start | bytes 2088968 | tf_op jit(solution)/shard_map/ppermute | solution.py:32
  28.1 1.7 %collective-permute-start.2 = (bf16[136,2560]{1,0:T(8,128)(2,1)S(1)}, bf16[136,2560]{1,0:T(8,128)(2,1)S(1)}, u32[]{:S(2)}, u32[]{:S(2)}) collective-permute-start(bf16[136,2560]{1,0:T(8,128)(2,1)S(1)} %pad_maximum_fusion.1.t0), channel_id=1, source_target_pairs={{0,6},{2,0},{4,2},{6,4},{1,7},{3,1},{5,3},{7,5},{8,14},{10,8},{12,... | collective-permute-start | bytes 2088968 | tf_op jit(solution)/shard_map/ppermute | solution.py:32
  29.9 0.8 all-to-all-done
  30.7 0.7 collective-permute-start.7
  31.4 2.5 %collective-permute-start.5 = (bf16[640,512]{1,0:T(8,128)(2,1)S(1)}, bf16[640,512]{1,0:T(8,128)(2,1)}, u32[]{:S(2)}, u32[]{:S(2)}) collective-permute-start(bf16[640,512]{1,0:T(8,128)(2,1)S(1)} %bitcast.10), channel_id=1, source_target_pairs={{0,64},{64,128},{128,192},{192,0},{1,65},{65,129},{129,193},{193,1... | collective-permute-start | bytes 1966088 | tf_op jit(solution)/shard_map/ppermute | solution.py:32
  33.9 3.0 %collective-permute-start.3 = (bf16[136,2560]{1,0:T(8,128)(2,1)S(1)}, bf16[136,2560]{1,0:T(8,128)(2,1)S(1)}, u32[]{:S(2)}, u32[]{:S(2)}) collective-permute-start(bf16[136,2560]{1,0:T(8,128)(2,1)S(1)} %pad_maximum_fusion.1.t0), channel_id=1, source_target_pairs={{0,4},{2,6},{4,0},{6,2},{1,5},{3,7},{5,1},{7,3},{8,12},{10,14},{12... | collective-permute-start | bytes 2088968 | tf_op jit(solution)/shard_map/ppermute | solution.py:32
  36.9 11.4 %collective-permute-done.7.refs_4_ = bf16[640,512]{1,0:T(8,128)(2,1)} collective-permute-done((bf16[640,512]{1,0:T(8,128)(2,1)S(1)}, bf16[640,512]{1,0:T(8,128)(2,1)}, u32[]{:S(2)}, u32[]{:S(2)}) %collective-permute-start.7) | collective-permute-done | bytes 655392 | tf_op jit(solution)/shard_map/ppermute | solution.py:32
  48.4 1.8 %slice.62 = bf16[384,512]{1,0:T(8,128)(2,1)} slice(bf16[640,512]{1,0:T(8,128)(2,1)} %collective-permute-done.7.refs_4_), slice={[256:640], [0:512]} | slice | bytes 786432 | tf_op jit(solution)/shard_map/slice | solution.py:267
  50.1 7.7 %collective-permute-done.2.t2 = bf16[136,2560]{1,0:T(8,128)(2,1)S(1)} collective-permute-done((bf16[136,2560]{1,0:T(8,128)(2,1)S(1)}, bf16[136,2560]{1,0:T(8,128)(2,1)S(1)}, u32[]{:S(2)}, u32[]{:S(2)}) %collective-permute-start.2) | collective-permute-done | bytes 696352 | tf_op jit(solution)/shard_map/ppermute | solution.py:32
  57.8 0.5 collective-permute-start.6
  58.3 1.7 %slice.61 = bf16[256,512]{1,0:T(8,128)(2,1)} slice(bf16[640,512]{1,0:T(8,128)(2,1)} %collective-permute-done.5.refs_2_), slice={[0:256], [0:512]} | slice | bytes 524288 | tf_op jit(solution)/shard_map/slice | solution.py:266
  60.0 2.5 %collective-permute-start.9 = (bf16[256,512]{1,0:T(8,128)(2,1)}, bf16[256,512]{1,0:T(8,128)(2,1)}, u32[]{:S(2)}, u32[]{:S(2)}) collective-permute-start(bf16[256,512]{1,0:T(8,128)(2,1)} %slice.61), channel_id=1, source_target_pairs={{0,64},{64,128},{128,192},{192,0},{1,65},{65,129},{129,193},{193,1... | collective-permute-start | bytes 786440 | tf_op jit(solution)/shard_map/ppermute | solution.py:32
  62.5 0.6 fusion.3
  63.1 0.6 mul.30
  63.7 0.6 broadcast_in_dim.25
  64.4 0.6 broadcast_in_dim.26
  65.0 0.6 broadcast_in_dim.27
  65.6 1.0 concatenate.17.par_ref
  66.5 0.1 collective-permute-start.12
  66.6 1.7 %pad_maximum_fusion.gates_ref = bf16[27,128,256]{2,1,0:T(8,128)(2,1)S(1)} fusion(bf16[27,128,128]{2,1,0:T(8,128)(2,1)} %param.18, bf16[27,128,128]{2,1,0:T(8,128)(2,1)} %param.17), kind=kLoop, calls=%fused_computation | loop fusion | flops 3538944 | bytes 3538944 | tf_op jit(solution)/shard_map/concatenate | solution.py:297
  68.3 0.3 collective-permute-done.9.refs_0_
  68.6 0.3 collective-permute-start.10
  68.9 0.1 pad_add_fusion.at_ref
  69.0 0.2 collective-permute-start.16
  69.3 4.8 %shard_map.109.part_ref = f32[4,2,136,512]{3,2,1,0:T(8,128)S(1)} custom-call(s32[3]{0:T(128)S(1)} %pad_add_fusion.at_ref, bf16[136,2560]{1,0:T(8,128)(2,1)S(1)} %pad_maximum_fusion.1.t0, bf16[136,2560]{1,0:T(8,128)(2,1)S(1)} %collective-permute-done.1.t1, bf16[136,2560]{1,0:T(8,128)(2,1)S(1)} %collective-permute-done.2.t2, ...), custom_call_target="tpu_custom_call" | custom-call | flops 2139095040 | bytes 9000000 | tf_op jit(solution)/shard_map/pallas_call | solution.py:299
  74.1 2.4 %shard_map.110 = (bf16[2,464,128]{2,1,0:T(8,128)(2,1)S(1)}, bf16[2,464,128]{2,1,0:T(8,128)(2,1)S(1)}, bf16[2,464,128]{2,1,0:T(8,128)(2,1)S(1)}, bf16[2,464,128]{2,1,0:T(8,128)(2,1)S(1)}) custom-call(s32[3]{0:T(128)S(1)} %pad_add_fusion.at_ref, f32[4,2,136,512]{3,2,1,0:T(8,128)S(1)} %shard_map.109.part_ref, bf16[136,2560]{1,0:T(8,128)(2,1)S(1)} %pad_maximum_fusion.1.t0, ...), custom_call_target="tpu_custom_call" | custom-call | flops 713031680 | bytes 7000000 | tf_op jit(solution)/shard_map/pallas_call | solution.py:306
  76.6 0.7 collective-permute-start.13
  77.3 3.1 %collective-permute-start.14 = (bf16[2,464,128]{2,1,0:T(8,128)(2,1)S(1)}, bf16[2,464,128]{2,1,0:T(8,128)(2,1)S(1)}, u32[]{:S(2)}, u32[]{:S(2)}) collective-permute-start(bf16[2,464,128]{2,1,0:T(8,128)(2,1)S(1)} %get-tuple-element.16), channel_id=1, source_target_pairs={{0,6},{2,0},{4,2},{6,4},{1,7},{3,1},{5,3},{7,5},{8,14},{10,8},{12,... | collective-permute-start | bytes 712712 | tf_op jit(solution)/shard_map/ppermute | solution.py:32
  80.4 1.4 %collective-permute-start.15 = (bf16[2,464,128]{2,1,0:T(8,128)(2,1)S(1)}, bf16[2,464,128]{2,1,0:T(8,128)(2,1)S(1)}, u32[]{:S(2)}, u32[]{:S(2)}) collective-permute-start(bf16[2,464,128]{2,1,0:T(8,128)(2,1)S(1)} %get-tuple-element.17), channel_id=1, source_target_pairs={{0,4},{2,6},{4,0},{6,2},{1,5},{3,7},{5,1},{7,3},{8,12},{10,14},{12... | collective-permute-start | bytes 712712 | tf_op jit(solution)/shard_map/ppermute | solution.py:32
  81.8 1.0 shard_map.111
  82.8 3.7 %collective-permute-done.13.g1 = bf16[2,464,128]{2,1,0:T(8,128)(2,1)S(1)} collective-permute-done((bf16[2,464,128]{2,1,0:T(8,128)(2,1)S(1)}, bf16[2,464,128]{2,1,0:T(8,128)(2,1)S(1)}, u32[]{:S(2)}, u32[]{:S(2)}) %collective-permute-start.13) | collective-permute-done | bytes 237600 | tf_op jit(solution)/shard_map/ppermute | solution.py:32
  86.5 4.4 %collective-permute-done.14.g2 = bf16[2,464,128]{2,1,0:T(8,128)(2,1)S(1)} collective-permute-done((bf16[2,464,128]{2,1,0:T(8,128)(2,1)S(1)}, bf16[2,464,128]{2,1,0:T(8,128)(2,1)S(1)}, u32[]{:S(2)}, u32[]{:S(2)}) %collective-permute-start.14) | collective-permute-done | bytes 237600 | tf_op jit(solution)/shard_map/ppermute | solution.py:32
  90.9 1.8 %collective-permute-done.15.g3 = bf16[2,464,128]{2,1,0:T(8,128)(2,1)S(1)} collective-permute-done((bf16[2,464,128]{2,1,0:T(8,128)(2,1)S(1)}, bf16[2,464,128]{2,1,0:T(8,128)(2,1)S(1)}, u32[]{:S(2)}, u32[]{:S(2)}) %collective-permute-start.15) | collective-permute-done | bytes 237600 | tf_op jit(solution)/shard_map/ppermute | solution.py:32
  92.7 10.8 %shard_map.112 = (f32[27,128,128]{2,1,0:T(8,128)S(1)}, f32[27,128,128]{2,1,0:T(8,128)S(1)}, f32[2,3456]{1,0:T(2,128)S(1)}) custom-call(s32[3]{0:T(128)S(1)} %pad_add_fusion.at_ref, bf16[2,464,128]{2,1,0:T(8,128)(2,1)S(1)} %get-tuple-element.14.g0, bf16[2,464,128]{2,1,0:T(8,128)(2,1)S(1)} %collective-permute-done.13.g1, ...), custom_call_target="tpu_custom_call" | custom-call | flops 226492416 | bytes 8000000 | tf_op jit(solution)/shard_map/pallas_call | solution.py:320
  103.5 3.3 %collective-permute-start.17 = (f32[2,3456]{1,0:T(2,128)S(1)}, f32[2,3456]{1,0:T(2,128)S(1)}, u32[]{:S(2)}, u32[]{:S(2)}) collective-permute-start(f32[2,3456]{1,0:T(2,128)S(1)} %get-tuple-element.22), channel_id=1, source_target_pairs={{0,8},{8,16},{16,24},{24,32},{32,40},{40,48},{48,56},{56,64},{64,7... | collective-permute-start | bytes 82952 | tf_op jit(solution)/shard_map/ppermute | solution.py:32
  106.8 2.8 %collective-permute-done.17 = f32[2,3456]{1,0:T(2,128)S(1)} collective-permute-done((f32[2,3456]{1,0:T(2,128)S(1)}, f32[2,3456]{1,0:T(2,128)S(1)}, u32[]{:S(2)}, u32[]{:S(2)}) %collective-permute-start.17) | collective-permute-done | bytes 27680 | tf_op jit(solution)/shard_map/ppermute | solution.py:32
  109.6 1.2 collective-permute-start.18
  110.8 7.2 %collective-permute-start.19 = (f32[2,3456]{1,0:T(2,128)S(1)}, f32[2,3456]{1,0:T(2,128)S(1)}, u32[]{:S(2)}, u32[]{:S(2)}) collective-permute-start(f32[2,3456]{1,0:T(2,128)S(1)} %pad_maximum_fusion.2), channel_id=1, source_target_pairs={{0,24},{8,32},{16,40},{24,48},{32,56},{40,64},{48,72},{56,80},{64,... | collective-permute-start | bytes 82952 | tf_op jit(solution)/shard_map/ppermute | solution.py:32
  118.0 1.1 collective-permute-start.20
  119.1 0.4 collective-permute-done.19
  119.5 5.0 %collective-permute-done.20 = f32[2,3456]{1,0:T(2,128)S(1)} collective-permute-done((f32[2,3456]{1,0:T(2,128)S(1)}, f32[2,3456]{1,0:T(2,128)S(1)}, u32[]{:S(2)}, u32[]{:S(2)}) %collective-permute-start.20) | collective-permute-done | bytes 27680 | tf_op jit(solution)/shard_map/ppermute | solution.py:32
  124.5 0.1 slice_add_fusion.in_ref
  124.6 1.2 shard_map.113
  (39 shorter events, 0.2 us)
Async XLA Ops:
  0.0 10.5 %copy-start.1 = (bf16[1,128,2560]{2,1,0:T(8,128)(2,1)S(1)}, bf16[1,128,2560]{2,1,0:T(8,128)(2,1)}, u32[]{:S(2)}) copy-start(bf16[1,128,2560]{2,1,0:T(8,128)(2,1)} %param.11) | copy-start | bytes 1966084
  1.9 56.5 %copy-start.2 = (f32[3456]{0:T(1024)S(1)}, f32[3456]{0:T(1024)}, u32[]{:S(2)}) copy-start(f32[3456]{0:T(1024)} %param.21) | copy-start | bytes 41476
  1.9 60.7 %copy-start.6 = (s32[1,128]{1,0:T(1,128)S(1)}, s32[1,128]{1,0:T(1,128)}, u32[]{:S(2)}) copy-start(s32[1,128]{1,0:T(1,128)} %param.13) | copy-start | bytes 1540
  1.9 61.9 %copy-start.3 = (f32[3456]{0:T(1024)S(1)}, f32[3456]{0:T(1024)}, u32[]{:S(2)}) copy-start(f32[3456]{0:T(1024)} %param.16) | copy-start | bytes 41476
  1.9 28.8 %all-to-all-start = ((bf16[8,80,512]{2,1,0:T(8,128)(2,1)}), bf16[8,80,512]{2,1,0:T(8,128)(2,1)S(1)}, u32[]{:S(2)}, u32[]{:S(2)}) async-start(bf16[8,80,512]{2,1,0:T(8,128)(2,1)} %broadcast_in_dim.23), calls=%async_computation | async-start | bytes 1310720 | tf_op jit(solution)/shard_map/all_to_all | solution.py:260
  10.5 53.9 %copy-start.4 = (f32[3456]{0:T(1024)S(1)}, f32[3456]{0:T(1024)}, u32[]{:S(2)}) copy-start(f32[3456]{0:T(1024)} %param.19) | copy-start | bytes 41476
  10.5 54.5 %copy-start.5 = (f32[3456]{0:T(1024)S(1)}, f32[3456]{0:T(1024)}, u32[]{:S(2)}) copy-start(f32[3456]{0:T(1024)} %param.20) | copy-start | bytes 41476
  10.5 16.0 %collective-permute-start = (bf16[8,2560]{1,0:T(8,128)(2,1)S(1)}, bf16[8,2560]{1,0:T(8,128)(2,1)S(1)}, u32[]{:S(2)}, u32[]{:S(2)}) collective-permute-start(bf16[8,2560]{1,0:T(8,128)(2,1)S(1)} %slice_bitcast_fusion), channel_id=1, source_target_pairs={{0,8},{8,16},{16,24},{24,32},{32,40},{40,48},{48,56},{56,64},{64,7... | collective-permute-start | bytes 122888 | tf_op jit(solution)/shard_map/ppermute | solution.py:32
  26.6 23.6 %collective-permute-start.1 = (bf16[136,2560]{1,0:T(8,128)(2,1)S(1)}, bf16[136,2560]{1,0:T(8,128)(2,1)S(1)}, u32[]{:S(2)}, u32[]{:S(2)}) collective-permute-start(bf16[136,2560]{1,0:T(8,128)(2,1)S(1)} %pad_maximum_fusion.1.t0), channel_id=1, source_target_pairs={{0,2},{2,4},{4,6},{6,0},{1,3},{3,5},{5,7},{7,1},{8,10},{10,12},{12... | collective-permute-start | bytes 2088968 | tf_op jit(solution)/shard_map/ppermute | solution.py:32
  28.1 29.7 %collective-permute-start.2 = (bf16[136,2560]{1,0:T(8,128)(2,1)S(1)}, bf16[136,2560]{1,0:T(8,128)(2,1)S(1)}, u32[]{:S(2)}, u32[]{:S(2)}) collective-permute-start(bf16[136,2560]{1,0:T(8,128)(2,1)S(1)} %pad_maximum_fusion.1.t0), channel_id=1, source_target_pairs={{0,6},{2,0},{4,2},{6,4},{1,7},{3,1},{5,3},{7,5},{8,14},{10,8},{12,... | collective-permute-start | bytes 2088968 | tf_op jit(solution)/shard_map/ppermute | solution.py:32
  30.7 17.7 %collective-permute-start.7 = (bf16[640,512]{1,0:T(8,128)(2,1)S(1)}, bf16[640,512]{1,0:T(8,128)(2,1)}, u32[]{:S(2)}, u32[]{:S(2)}) collective-permute-start(bf16[640,512]{1,0:T(8,128)(2,1)S(1)} %bitcast.9), channel_id=1, source_target_pairs={{0,192},{64,0},{128,64},{192,128},{1,193},{65,1},{129,65},{193,129... | collective-permute-start | bytes 1966088 | tf_op jit(solution)/shard_map/ppermute | solution.py:32
  31.4 26.4 %collective-permute-start.5 = (bf16[640,512]{1,0:T(8,128)(2,1)S(1)}, bf16[640,512]{1,0:T(8,128)(2,1)}, u32[]{:S(2)}, u32[]{:S(2)}) collective-permute-start(bf16[640,512]{1,0:T(8,128)(2,1)S(1)} %bitcast.10), channel_id=1, source_target_pairs={{0,64},{64,128},{128,192},{192,0},{1,65},{65,129},{129,193},{193,1... | collective-permute-start | bytes 1966088 | tf_op jit(solution)/shard_map/ppermute | solution.py:32
  33.9 26.1 %collective-permute-start.3 = (bf16[136,2560]{1,0:T(8,128)(2,1)S(1)}, bf16[136,2560]{1,0:T(8,128)(2,1)S(1)}, u32[]{:S(2)}, u32[]{:S(2)}) collective-permute-start(bf16[136,2560]{1,0:T(8,128)(2,1)S(1)} %pad_maximum_fusion.1.t0), channel_id=1, source_target_pairs={{0,4},{2,6},{4,0},{6,2},{1,5},{3,7},{5,1},{7,3},{8,12},{10,14},{12... | collective-permute-start | bytes 2088968 | tf_op jit(solution)/shard_map/ppermute | solution.py:32
  48.4 20.6 %collective-permute-start.4 = (bf16[640,512]{1,0:T(8,128)(2,1)S(1)}, bf16[640,512]{1,0:T(8,128)(2,1)}, u32[]{:S(2)}, u32[]{:S(2)}) collective-permute-start(bf16[640,512]{1,0:T(8,128)(2,1)S(1)} %bitcast.11), channel_id=1, source_target_pairs={{0,1},{1,0},{2,3},{3,2},{4,5},{5,4},{6,7},{7,6},{8,9},{9,8},{10,11... | collective-permute-start | bytes 1966088 | tf_op jit(solution)/shard_map/ppermute | solution.py:36
  50.1 16.4 %collective-permute-start.11 = (bf16[384,512]{1,0:T(8,128)(2,1)}, bf16[384,512]{1,0:T(8,128)(2,1)}, u32[]{:S(2)}, u32[]{:S(2)}) collective-permute-start(bf16[384,512]{1,0:T(8,128)(2,1)} %slice.62), channel_id=1, source_target_pairs={{0,192},{64,0},{128,64},{192,128},{1,193},{65,1},{129,65},{193,129... | collective-permute-start | bytes 1179656 | tf_op jit(solution)/shard_map/ppermute | solution.py:32
  57.8 11.4 %collective-permute-start.8 = (bf16[640,512]{1,0:T(8,128)(2,1)}, bf16[640,512]{1,0:T(8,128)(2,1)}, u32[]{:S(2)}, u32[]{:S(2)}) collective-permute-start(bf16[640,512]{1,0:T(8,128)(2,1)} %collective-permute-done.7.refs_4_), channel_id=1, source_target_pairs={{0,1},{1,0},{2,3},{3,2},{4,5},{5,4},{6,7},{7,6},{8,9},{9,8},{10,11... | collective-permute-start | bytes 1966088 | tf_op jit(solution)/shard_map/ppermute | solution.py:36
  57.8 11.4 %collective-permute-start.6 = (bf16[640,512]{1,0:T(8,128)(2,1)}, bf16[640,512]{1,0:T(8,128)(2,1)}, u32[]{:S(2)}, u32[]{:S(2)}) collective-permute-start(bf16[640,512]{1,0:T(8,128)(2,1)} %collective-permute-done.5.refs_2_), channel_id=1, source_target_pairs={{0,1},{1,0},{2,3},{3,2},{4,5},{5,4},{6,7},{7,6},{8,9},{9,8},{10,11... | collective-permute-start | bytes 1966088 | tf_op jit(solution)/shard_map/ppermute | solution.py:36
  60.0 8.6 %collective-permute-start.9 = (bf16[256,512]{1,0:T(8,128)(2,1)}, bf16[256,512]{1,0:T(8,128)(2,1)}, u32[]{:S(2)}, u32[]{:S(2)}) collective-permute-start(bf16[256,512]{1,0:T(8,128)(2,1)} %slice.61), channel_id=1, source_target_pairs={{0,64},{64,128},{128,192},{192,0},{1,65},{65,129},{129,193},{193,1... | collective-permute-start | bytes 786440 | tf_op jit(solution)/shard_map/ppermute | solution.py:32
  66.5 2.5 %copy-start.7 = (bf16[1,128]{1,0:T(2,128)(2,1)S(1)}, bf16[1,128]{1,0:T(2,128)(2,1)}, u32[]{:S(2)}) copy-start(bf16[1,128]{1,0:T(2,128)(2,1)} %get-tuple-element.25) | copy-start | bytes 772
  66.5 7.6 %collective-permute-start.12 = (bf16[384,512]{1,0:T(8,128)(2,1)}, bf16[384,512]{1,0:T(8,128)(2,1)S(1)}, u32[]{:S(2)}, u32[]{:S(2)}) collective-permute-start(bf16[384,512]{1,0:T(8,128)(2,1)} %collective-permute-done.11.refs_2_), channel_id=1, source_target_pairs={{0,1},{1,0},{2,3},{3,2},{4,5},{5,4},{6,7},{7,6},{8,9},{9,8},{10,11... | collective-permute-start | bytes 1179656 | tf_op jit(solution)/shard_map/ppermute | solution.py:36
  68.6 5.5 %collective-permute-start.10 = (bf16[256,512]{1,0:T(8,128)(2,1)}, bf16[256,512]{1,0:T(8,128)(2,1)S(1)}, u32[]{:S(2)}, u32[]{:S(2)}) collective-permute-start(bf16[256,512]{1,0:T(8,128)(2,1)} %collective-permute-done.9.refs_0_), channel_id=1, source_target_pairs={{0,1},{1,0},{2,3},{3,2},{4,5},{5,4},{6,7},{7,6},{8,9},{9,8},{10,11... | collective-permute-start | bytes 786440 | tf_op jit(solution)/shard_map/ppermute | solution.py:36
  69.0 12.8 %collective-permute-start.16 = (bf16[1,128]{1,0:T(2,128)(2,1)S(1)}, bf16[1,128]{1,0:T(2,128)(2,1)S(1)}, u32[]{:S(2)}, u32[]{:S(2)}) collective-permute-start(bf16[1,128]{1,0:T(2,128)(2,1)S(1)} %copy-done.7), channel_id=1, source_target_pairs={{0,8},{8,16},{16,24},{24,32},{32,40},{40,48},{48,56},{56,64},{64,7... | collective-permute-start | bytes 776 | tf_op jit(solution)/shard_map/ppermute | solution.py:32
  74.1 7.7 %copy-start = (bf16[1,128,3456]{2,1,0:T(8,128)(2,1)S(1)}, bf16[1,128,3456]{2,1,0:T(8,128)(2,1)}, u32[]{:S(2)}) copy-start(bf16[1,128,3456]{2,1,0:T(8,128)(2,1)} %param.12) | copy-start | bytes 2654212
  76.6 9.9 %collective-permute-start.13 = (bf16[2,464,128]{2,1,0:T(8,128)(2,1)S(1)}, bf16[2,464,128]{2,1,0:T(8,128)(2,1)S(1)}, u32[]{:S(2)}, u32[]{:S(2)}) collective-permute-start(bf16[2,464,128]{2,1,0:T(8,128)(2,1)S(1)} %get-tuple-element.15), channel_id=1, source_target_pairs={{0,2},{2,4},{4,6},{6,0},{1,3},{3,5},{5,7},{7,1},{8,10},{10,12},{12... | collective-permute-start | bytes 712712 | tf_op jit(solution)/shard_map/ppermute | solution.py:32
  77.3 13.6 %collective-permute-start.14 = (bf16[2,464,128]{2,1,0:T(8,128)(2,1)S(1)}, bf16[2,464,128]{2,1,0:T(8,128)(2,1)S(1)}, u32[]{:S(2)}, u32[]{:S(2)}) collective-permute-start(bf16[2,464,128]{2,1,0:T(8,128)(2,1)S(1)} %get-tuple-element.16), channel_id=1, source_target_pairs={{0,6},{2,0},{4,2},{6,4},{1,7},{3,1},{5,3},{7,5},{8,14},{10,8},{12,... | collective-permute-start | bytes 712712 | tf_op jit(solution)/shard_map/ppermute | solution.py:32
  80.4 12.3 %collective-permute-start.15 = (bf16[2,464,128]{2,1,0:T(8,128)(2,1)S(1)}, bf16[2,464,128]{2,1,0:T(8,128)(2,1)S(1)}, u32[]{:S(2)}, u32[]{:S(2)}) collective-permute-start(bf16[2,464,128]{2,1,0:T(8,128)(2,1)S(1)} %get-tuple-element.17), channel_id=1, source_target_pairs={{0,4},{2,6},{4,0},{6,2},{1,5},{3,7},{5,1},{7,3},{8,12},{10,14},{12... | collective-permute-start | bytes 712712 | tf_op jit(solution)/shard_map/ppermute | solution.py:32
  103.5 6.0 %collective-permute-start.17 = (f32[2,3456]{1,0:T(2,128)S(1)}, f32[2,3456]{1,0:T(2,128)S(1)}, u32[]{:S(2)}, u32[]{:S(2)}) collective-permute-start(f32[2,3456]{1,0:T(2,128)S(1)} %get-tuple-element.22), channel_id=1, source_target_pairs={{0,8},{8,16},{16,24},{24,32},{32,40},{40,48},{48,56},{56,64},{64,7... | collective-permute-start | bytes 82952 | tf_op jit(solution)/shard_map/ppermute | solution.py:32
  109.6 9.5 %collective-permute-start.18 = (f32[2,3456]{1,0:T(2,128)S(1)}, f32[2,3456]{1,0:T(2,128)S(1)}, u32[]{:S(2)}, u32[]{:S(2)}) collective-permute-start(f32[2,3456]{1,0:T(2,128)S(1)} %pad_maximum_fusion.2), channel_id=1, source_target_pairs={{0,8},{8,16},{16,24},{24,32},{32,40},{40,48},{48,56},{56,64},{64,7... | collective-permute-start | bytes 82952 | tf_op jit(solution)/shard_map/ppermute | solution.py:32
  110.8 8.7 %collective-permute-start.19 = (f32[2,3456]{1,0:T(2,128)S(1)}, f32[2,3456]{1,0:T(2,128)S(1)}, u32[]{:S(2)}, u32[]{:S(2)}) collective-permute-start(f32[2,3456]{1,0:T(2,128)S(1)} %pad_maximum_fusion.2), channel_id=1, source_target_pairs={{0,24},{8,32},{16,40},{24,48},{32,56},{40,64},{48,72},{56,80},{64,... | collective-permute-start | bytes 82952 | tf_op jit(solution)/shard_map/ppermute | solution.py:32
  118.0 6.6 %collective-permute-start.20 = (f32[2,3456]{1,0:T(2,128)S(1)}, f32[2,3456]{1,0:T(2,128)S(1)}, u32[]{:S(2)}, u32[]{:S(2)}) collective-permute-start(f32[2,3456]{1,0:T(2,128)S(1)} %pad_maximum_fusion.2), channel_id=1, source_target_pairs={{0,40},{8,48},{16,56},{24,64},{32,72},{40,80},{48,88},{56,96},{64,... | collective-permute-start | bytes 82952 | tf_op jit(solution)/shard_map/ppermute | solution.py:32
  119.1 5.4 %collective-permute-start.21 = (f32[2,3456]{1,0:T(2,128)S(1)}, f32[2,3456]{1,0:T(2,128)S(1)}, u32[]{:S(2)}, u32[]{:S(2)}) collective-permute-start(f32[2,3456]{1,0:T(2,128)S(1)} %pad_maximum_fusion.2), channel_id=1, source_target_pairs={{0,56},{8,64},{16,72},{24,80},{32,88},{40,96},{48,104},{56,112},{6... | collective-permute-start | bytes 82952 | tf_op jit(solution)/shard_map/ppermute | solution.py:32

commit v3 on v2

--- a/solution.py
+++ b/solution.py
@@ -11,6 +11,7 @@
 F32 = jnp.float32
 BF16 = jnp.bfloat16
 VMEM = pl.BlockSpec(memory_space=pltpu.VMEM)
+ANY = pl.BlockSpec(memory_space=pl.ANY)
 SMEM = pl.BlockSpec(memory_space=pltpu.SMEM)
 
 LENGTH = 128
@@ -22,9 +23,9 @@
 SPAN = 16
 HALO = 8
 PACK = COLS + 32
-FULL = 512
-CUT = 256
-ROWS = LENGTH + HALO
+CUT = 208
+AHEAD = 4 * HALO + 16
+ROWS = 4 * LENGTH + AHEAD
 
 
 def shift(value, axis, by):
@@ -36,15 +37,17 @@
     return lax.ppermute(value, "c", [(0, 1), (1, 0)])
 
 
-def prepare_kernel(gate_ref, ids_ref, gelu_ref, mask_ref, ids_scr):
+def prepare_kernel(at_ref, gate_ref, ids_ref, ahead_ref, gelu_ref, mask_ref, ids_scr):
     def head(h, carry):
         lanes = pl.ds(pl.multiple_of(h * HEAD, HEAD), HEAD)
         gelu_ref[h] = jax.nn.gelu(gate_ref[:, lanes].astype(F32), approximate=True)
         return carry
 
     lax.fori_loop(0, HEADS, head, 0)
-    prior = jnp.broadcast_to(ids_ref[0:1, :], (LENGTH, LENGTH)).T
-    own = jnp.broadcast_to(ids_ref[1:2, :], (LENGTH, LENGTH)).T
+    prior = ahead_ref[4 * HALO : AHEAD, 0:LENGTH].astype(F32)[0:1]
+    prior = jnp.where(at_ref[3] == 0, -1.0, prior)
+    prior = jnp.broadcast_to(prior, (LENGTH, LENGTH)).T
+    own = jnp.broadcast_to(ids_ref[...].astype(F32), (LENGTH, LENGTH)).T
     ids_scr[0:HALO, :] = prior[LENGTH - HALO :, :]
     ids_scr[HALO:, :] = own
     for k in range(SPAN):
@@ -66,49 +69,44 @@
     return made
 
 
-def project_kernel(at_ref, t0, t1, t2, t3, *refs):
-    weights, part_ref = refs[:6], refs[6]
+def across(weight, rows):
+    return lax.dot_general(
+        weight, rows, (((1,), (1,)), ((), ())), preferred_element_type=F32
+    )
+
+
+def project_kernel(at_ref, t0, t1, t2, t3, ahead, *refs):
+    weights, (part_ref, far_ref, rows_ref, sems) = refs[:6], refs[6:]
     y = at_ref[2]
-    for i, t_ref in enumerate((t0, t1, t2, t3)):
-        for half in range(2):
-            total = None
-            for j, back in enumerate((0, 3, 1)):
-                start = pl.multiple_of(lax.rem(y + back, 4) * 640, 128)
-                part = jnp.dot(
-                    t_ref[:, pl.ds(start, 640)],
-                    weights[2 * j + half][...],
-                    preferred_element_type=F32,
-                )
-                total = part if total is None else total + part
-            part_ref[i, half] = total
-
-
-def pack_kernel(at_ref, part_ref, t0, t1, t2, t3, *refs):
-    weights, outs = refs[:4], refs[4:8]
-    wide_ref = refs[8]
-    c, y = at_ref[1], at_ref[2]
-    far = lax.rem(y + 2, 4) * 640
-    for i, t_ref in enumerate((t0, t1, t2, t3)):
-        for half in range(2):
-            total = part_ref[i, half]
-            for j, (start, size) in enumerate(((far, CUT), (far + CUT, 640 - CUT))):
-                total = total + jnp.dot(
-                    t_ref[:, pl.ds(pl.multiple_of(start, 128), size)],
-                    weights[2 * j + half][...],
-                    preferred_element_type=F32,
-                )
-            wide_ref[...] = total
-            place = c if half == 0 else 1 - c
-            out_ref = outs[i]
-            for j in range(4):
-                block = wide_ref[0:LENGTH, j * 128 : (j + 1) * 128].T.astype(BF16)
-                size = min(128, COLS - j * 128)
-                out_ref[place, j * 128 : j * 128 + size, :] = block[:size]
+    pairs = [
+        (ref, rows_ref.at[pl.ds(i * LENGTH, LENGTH)]) for i, ref in enumerate((t0, t1, t2, t3))
+    ] + [(ahead, rows_ref.at[pl.ds(4 * LENGTH, AHEAD)])]
+    for copy in copies(pairs, sems):
+        copy.wait()
+    for half in range(2):
+        total = None
+        for j, back in enumerate((0, 3, 1)):
+            start = pl.multiple_of(lax.rem(y + back, 4) * 640, 128)
+            part = across(weights[2 * j + half][...], rows_ref[:, pl.ds(start, 640)])
+            total = part if total is None else total + part
+        part_ref[half] = total
+    far_ref[...] = rows_ref[:, pl.ds(pl.multiple_of(lax.rem(y + 2, 4) * 640, 128), 640)]
+
+
+def pack_kernel(at_ref, part_ref, far_ref, *refs):
+    weights, outs, (all_ref, wide_ref) = refs[:4], refs[4:8], refs[8:]
+    c = at_ref[1]
+    for half in range(2):
+        all_ref[0:CUT, :] = weights[half][...]
+        all_ref[CUT:COLS, :] = weights[2 + half][...]
+        total = part_ref[half] + across(all_ref[...], far_ref[...])
+        place = c if half == 0 else 1 - c
+        wide_ref[0:COLS, 0:AHEAD] = total[:, 4 * LENGTH :]
+        turned = [wide_ref[j * 128 : (j + 1) * 128, :].T for j in range(4)]
+        for i, out_ref in enumerate(outs):
+            out_ref[place, 0:COLS, :] = total[:, i * LENGTH : (i + 1) * LENGTH].astype(BF16)
             for j in range(2):
-                pair = [
-                    wide_ref[LENGTH:ROWS, (2 * j + n) * 128 : (2 * j + n + 1) * 128]
-                    for n in range(2)
-                ]
+                pair = [turned[2 * j + n][HALO * i : HALO * i + HALO, :] for n in range(2)]
                 out_ref[place, COLS + 16 * j : COLS + 16 * j + 16, :] = jnp.concatenate(
                     pair, axis=0
                 ).astype(BF16)
@@ -122,8 +120,13 @@
     g3,
     mask_ref,
     gelu_ref,
-    par_ref,
-    gates_ref,
+    taps_ref,
+    bias_ref,
+    bias_a_ref,
+    bias_i_ref,
+    rate_ref,
+    gate_a_ref,
+    gate_i_ref,
     state_ref,
     prod_ref,
     end_ref,
@@ -157,22 +160,24 @@
 
     def head(h, carry):
         lanes = pl.ds(pl.multiple_of(h * HEAD, HEAD), HEAD)
-        par = [par_ref[i : i + 1, lanes] for i in range(8)]
+        at_head = pl.ds(h, 1)
+        taps = [taps_ref[i : i + 1, lanes] for i in range(4)]
         shifted = {
             off: x_scr[h, pl.ds(HALO + off, 8, stride=SPAN), :] for off in range(-3, SPAN)
         }
         conv = []
         for k in range(SPAN):
-            total = par[0] * shifted[k] + par[4]
+            total = taps[0] * shifted[k] + bias_ref[at_head, :]
             for back in range(1, 4):
                 valid = mask_ref[back, 8 * k : 8 * k + 8, :]
-                total = total + par[back] * (shifted[k - back] * valid)
+                total = total + taps[back] * (shifted[k - back] * valid)
             conv.append(total)
         conv = jnp.concatenate(conv, axis=0).astype(BF16)
-        both = jnp.dot(conv, gates_ref[h], preferred_element_type=F32)
-        rgate = jax.nn.sigmoid(both[:, :HEAD] + par[5])
-        igate = jax.nn.sigmoid(both[:, HEAD:] + par[6])
-        logdecay = par[7] * rgate
+        gates = jnp.concatenate([gate_a_ref[h], gate_i_ref[h]], axis=1)
+        both = jnp.dot(conv, gates, preferred_element_type=F32)
+        rgate = jax.nn.sigmoid(both[:, :HEAD] + bias_a_ref[at_head, :])
+        igate = jax.nn.sigmoid(both[:, HEAD:] + bias_i_ref[at_head, :])
+        logdecay = (-8.0 * rate_ref[at_head, :]) * rgate
         decay = jnp.exp(logdecay)
         same = mask_ref[0]
         twice = 2.0 * logdecay
@@ -252,65 +257,55 @@
 ):
     ctx = ("y", "z")
     own = tokens[0]
-    at = jnp.stack([lax.axis_index("x"), lax.axis_index("c"), lax.axis_index("y")]).astype(
+    at = jnp.stack([lax.axis_index(a) for a in ("x", "c", "y")] + [lax.axis_index(ctx)]).astype(
         jnp.int32
     )
 
-    filled = jnp.pad(in_weight, ((0, 0), (0, FULL - COLS)))
+    streams = [own, shift(own, "x", 1), shift(own, "x", -1), shift(own, "x", 2)]
+    filled = jnp.pad(in_weight, ((0, 0), (0, 512 - COLS)))
     column = lax.all_to_all(
         jnp.broadcast_to(filled[None], (8,) + filled.shape), "z", 0, 0, tiled=True
-    ).reshape(-1, FULL)
+    ).reshape(-1, 512)[:, :COLS].T
     from_back = shift(column, "y", 1)
     from_ahead = shift(column, "y", -1)
     near = [column, flip(column), from_back, flip(from_back), from_ahead, flip(from_ahead)]
     first = shift(from_back[:CUT], "y", 1)
     second = shift(from_ahead[CUT:], "y", -1)
+
+    documents = jnp.pad(segment_ids.astype(BF16), ((0, 15), (0, DEPTH - LENGTH)))
+    ahead = shift(jnp.concatenate([t[-HALO:] for t in streams] + [documents], axis=0), ctx, 1)
+
+    part, rows_far = call(
+        project_kernel,
+        (
+            jax.ShapeDtypeStruct((2, COLS, ROWS), F32),
+            jax.ShapeDtypeStruct((ROWS, 640), BF16),
+        ),
+        [SMEM] + [ANY] * 5 + [VMEM] * 6,
+        [pltpu.VMEM((ROWS, DEPTH), BF16), pltpu.SemaphoreType.DMA((5,))],
+        flops=2 * 560 * 1920 * 864,
+        moved=9_000_000,
+    )(at, *streams, ahead, *near)
+    first, second, part = lax.optimization_barrier((first, second, part))
     far = [first, flip(first), second, flip(second)]
-
-    rows = jnp.concatenate([own, shift(own[-HALO:], ctx, 1)], axis=0)
-    streams = [rows, shift(rows, "x", 1), shift(rows, "x", -1), shift(rows, "x", 2)]
-
-    ids = segment_ids.astype(BF16)
-    prior = shift(ids, ctx, 1).astype(F32)
-    prior = jnp.where(lax.axis_index(ctx) == 0, F32(-1.0), prior)
-    ids = jnp.concatenate([prior, segment_ids.astype(F32)], axis=0)
+    sent = call(
+        pack_kernel,
+        [jax.ShapeDtypeStruct((2, PACK, 128), BF16)] * 4,
+        [SMEM] + [VMEM] * 6,
+        [pltpu.VMEM((COLS, 640), BF16), pltpu.VMEM((512, 128), F32)],
+        flops=2 * 560 * 640 * 864,
+        moved=5_000_000,
+    )(at, part, rows_far, *far)
     gelu, masks = call(
         prepare_kernel,
         (
             jax.ShapeDtypeStruct((HEADS, LENGTH, HEAD), F32),
             jax.ShapeDtypeStruct((4, LENGTH, HEAD), F32),
         ),
-        [VMEM] * 2,
+        [SMEM] + [VMEM] * 3,
         [pltpu.VMEM((LENGTH + HALO, HEAD), F32)],
         moved=2_700_000,
-    )(gate_input[0], ids)
-    params = jnp.concatenate(
-        [
-            conv_weight,
-            conv_bias[None],
-            bias_a[None],
-            bias_i[None],
-            -8.0 * decay_rate[None],
-        ],
-        axis=0,
-    )
-    gates = jnp.concatenate([gate_a, gate_i], axis=2)
-
-    part = call(
-        project_kernel,
-        jax.ShapeDtypeStruct((4, 2, ROWS, FULL), F32),
-        [SMEM] + [VMEM] * 10,
-        flops=2 * 544 * 1920 * 1024,
-        moved=9_000_000,
-    )(at, *streams, *near)
-    sent = call(
-        pack_kernel,
-        [jax.ShapeDtypeStruct((2, PACK, 128), BF16)] * 4,
-        [SMEM] + [VMEM] * 9,
-        [pltpu.VMEM((ROWS, FULL), F32)],
-        flops=2 * 544 * 640 * 1024,
-        moved=7_000_000,
-    )(at, part, *streams, *far)
+    )(at, gate_input[0], segment_ids, ahead)
     got = [
         sent[0],
         shift(sent[2], "x", 1),
@@ -324,7 +319,7 @@
             jax.ShapeDtypeStruct((HEADS, LENGTH, HEAD), F32),
             jax.ShapeDtypeStruct((2, WIDTH), F32),
         ),
-        [SMEM] + [pl.BlockSpec(memory_space=pl.ANY)] * 4 + [VMEM] * 4,
+        [SMEM] + [ANY] * 4 + [VMEM] * 9,
         [
             pltpu.VMEM((HEADS, LENGTH + HALO, HEAD), F32),
             pltpu.VMEM((8, PACK, 128), BF16),
@@ -332,7 +327,16 @@
         ],
         flops=2 * 128 * 3456 * 256,
         moved=8_000_000,
-    )(at, *got, masks, gelu, params, gates)
+    )(
+        at,
+        *got,
+        masks,
+        gelu,
+        conv_weight,
+        *(v.reshape(HEADS, HEAD) for v in (conv_bias, bias_a, bias_i, decay_rate)),
+        gate_a,
+        gate_i,
+    )
 
     two = joined(shift(ends, ctx, 1), ends)
     pairs = [shift(two, ctx, by) for by in (7, 5, 3, 1)]

time: 128 us -> 121 us (0.945); the launches traced: 126 us -> 120 us
  starting transfers between devices: 41.9 us -> 33.2 us
  waiting for transfers between devices: 52.2 us -> 59.5 us
  local copies, waits for them, and re-layouts: 8.75 us -> 4.93 us
  other arithmetic: 2.51 us -> 0.2 us
  Pallas kernels: 20.2 us -> 22 us
    ppermute x17 -> x16, starting transfers between devices: 32.4 us -> 23.7 us  [shift(): lax.ppermute(value, axis, [(i, (i + by) % count) for i in range(count)])]
    ppermute x17 -> x16, waiting for transfers between devices: 51.4 us -> 55.4 us  [shift(): lax.ppermute(value, axis, [(i, (i + by) % count) for i in range(count)])]
    unnamed x16 -> x29, local copies, waits for them, and re-layouts: 0.04 us -> 3.06 us
    broadcast_in_dim x3 -> x0, local copies, waits for them, and re-layouts: 1.83 us -> none  [the longest x1 0.61 us: body(): bias_i[None]]
    all_to_all x1, waiting for transfers between devices: 0.82 us -> 2.63 us  [body(): lax.all_to_all(jnp.broadcast_to(filled[None], (8,) + filled.shape), 'z',...]
    slice x1, local copies, waits for them, and re-layouts: 1.77 us -> 0.03 us  [body(): second = shift(from_ahead[CUT:], 'y', -1)]
    concatenate x3 -> x0, other arithmetic: 1.72 us -> none  [the longest x1 1.66 us: body(): gates = jnp.concatenate([gate_a, gate_i], axis=2)]
    slice x1, local copies, waits for them, and re-layouts: 1.7 us -> 0.02 us  [body(): first = shift(from_back[:CUT], 'y', 1)]
  transfers between devices with their start and end apart: 23 -> 22, of which waited for: 11 -> 11; matrix products, arithmetic and copies ran while one was open for 7% -> 3% of each run, Pallas kernels for 7% -> 7%
where the time goes in v3:
time: 121 us; the launch traced here: 120 us
  waiting for transfers between devices  59.5 us (49%)
  starting transfers between devices  33.2 us (27%)
  Pallas kernels  22 us (18%)
  local copies, waits for them, and re-layouts  4.93 us (4%)
    ppermute x16, waiting for transfers between devices, shift(): lax.ppermute(value, axis, [(i, (i + by) % count) for i in range(count)])  55.4 us
    ppermute x16, starting transfers between devices, shift(): lax.ppermute(value, axis, [(i, (i + by) % count) for i in range(count)])  23.7 us
    pallas_call x1, Pallas kernels, body(): call(recur_kernel, (jax.ShapeDtypeStruct((HEADS, LENGTH, HEAD), F32), jax...  10.8 us
    all_to_all x1, starting transfers between devices, body(): lax.all_to_all(jnp.broadcast_to(filled[None], (8,) + filled.shape), 'z',...  8.47 us
    pallas_call x1, Pallas kernels, body(): call(project_kernel, (jax.ShapeDtypeStruct((2, COLS, ROWS), F32), jax.Sha...  6.47 us
    unnamed x29, local copies, waits for them, and re-layouts  3.06 us
    all_to_all x1, waiting for transfers between devices, body(): lax.all_to_all(jnp.broadcast_to(filled[None], (8,) + filled.shape), 'z',...  2.63 us
  transfers between devices with their start and end apart: 22, of which 11 were waited for; matrix products, arithmetic and copies ran while one was open for 3% of the time, Pallas kernels for 7%

profile of v3, /device:TPU:24, one launch (start us, length us, event | category | flops | bytes accessed | tf_op | source)
XLA Modules:
  0.0 120.1 jit_solution(10426783849624497958)
XLA Ops:
  0.0 1.5 %collective-permute-start.4 = (bf16[128,2560]{1,0:T(8,128)(2,1)}, bf16[128,2560]{1,0:T(8,128)(2,1)S(1)}, u32[]{:S(2)}, u32[]{:S(2)}) collective-permute-start(bf16[128,2560]{1,0:T(8,128)(2,1)} %bitcast.25), channel_id=1, source_target_pairs={{0,2},{2,4},{4,6},{6,0},{1,3},{3,5},{5,7},{7,1},{8,10},{10,12},{12... | collective-permute-start | bytes 1966088 | tf_op jit(solution)/shard_map/ppermute | solution.py:33
  1.5 1.7 %collective-permute-start.5 = (bf16[128,2560]{1,0:T(8,128)(2,1)}, bf16[128,2560]{1,0:T(8,128)(2,1)S(1)}, u32[]{:S(2)}, u32[]{:S(2)}) collective-permute-start(bf16[128,2560]{1,0:T(8,128)(2,1)} %bitcast.26), channel_id=1, source_target_pairs={{0,6},{2,0},{4,2},{6,4},{1,7},{3,1},{5,3},{7,5},{8,14},{10,8},{12,... | collective-permute-start | bytes 1966088 | tf_op jit(solution)/shard_map/ppermute | solution.py:33
  3.2 1.8 %collective-permute-start.6 = (bf16[128,2560]{1,0:T(8,128)(2,1)}, bf16[128,2560]{1,0:T(8,128)(2,1)}, u32[]{:S(2)}, u32[]{:S(2)}) collective-permute-start(bf16[128,2560]{1,0:T(8,128)(2,1)} %bitcast.27), channel_id=1, source_target_pairs={{0,4},{2,6},{4,0},{6,2},{1,5},{3,7},{5,1},{7,3},{8,12},{10,14},{12... | collective-permute-start | bytes 1966088 | tf_op jit(solution)/shard_map/ppermute | solution.py:33
  5.1 0.9 pad.8
  6.0 0.9 broadcast_in_dim.4
  6.9 8.5 %all-to-all-start = ((bf16[8,80,512]{2,1,0:T(8,128)(2,1)}), bf16[8,80,512]{2,1,0:T(8,128)(2,1)S(1)}, u32[]{:S(2)}, u32[]{:S(2)}) async-start(bf16[8,80,512]{2,1,0:T(8,128)(2,1)} %broadcast_in_dim.4), calls=%async_computation | async-start | bytes 1310720 | tf_op jit(solution)/shard_map/all_to_all | solution.py:266
  15.4 2.7 %collective-permute-done.4.t1 = bf16[128,2560]{1,0:T(8,128)(2,1)S(1)} collective-permute-done((bf16[128,2560]{1,0:T(8,128)(2,1)}, bf16[128,2560]{1,0:T(8,128)(2,1)S(1)}, u32[]{:S(2)}, u32[]{:S(2)}) %collective-permute-start.4) | collective-permute-done | bytes 655392 | tf_op jit(solution)/shard_map/ppermute | solution.py:33
  18.1 13.3 %collective-permute-done.5.t2 = bf16[128,2560]{1,0:T(8,128)(2,1)S(1)} collective-permute-done((bf16[128,2560]{1,0:T(8,128)(2,1)}, bf16[128,2560]{1,0:T(8,128)(2,1)S(1)}, u32[]{:S(2)}, u32[]{:S(2)}) %collective-permute-start.5) | collective-permute-done | bytes 655392 | tf_op jit(solution)/shard_map/ppermute | solution.py:33
  31.3 0.8 copy-done.9
  32.2 2.6 %all-to-all-done = bf16[8,80,512]{2,1,0:T(8,128)(2,1)S(1)} async-done(((bf16[8,80,512]{2,1,0:T(8,128)(2,1)}), bf16[8,80,512]{2,1,0:T(8,128)(2,1)S(1)}, u32[]{:S(2)}, u32[]{:S(2)}) %all-to-all-start) | async-done | bytes 655392 | tf_op jit(solution)/shard_map/all_to_all | solution.py:266
  34.8 0.3 copy.14
  35.1 0.8 collective-permute-start.2
  35.9 2.5 %collective-permute-start = (bf16[432,640]{1,0:T(8,128)(2,1)S(1)}, bf16[432,640]{1,0:T(8,128)(2,1)S(1)}, u32[]{:S(2)}, u32[]{:S(2)}) collective-permute-start(bf16[432,640]{1,0:T(8,128)(2,1)S(1)} %bitcast.18), channel_id=1, source_target_pairs={{0,64},{64,128},{128,192},{192,0},{1,65},{65,129},{129,193},{193,1... | collective-permute-start | bytes 1658888 | tf_op jit(solution)/shard_map/ppermute | solution.py:33
  38.4 0.8 slice_dynamic-update-slice_fusion
  39.2 10.1 %collective-permute-done.2.refs_4_ = bf16[432,640]{1,0:T(8,128)(2,1)S(1)} collective-permute-done((bf16[432,640]{1,0:T(8,128)(2,1)S(1)}, bf16[432,640]{1,0:T(8,128)(2,1)S(1)}, u32[]{:S(2)}, u32[]{:S(2)}) %collective-permute-start.2) | collective-permute-done | bytes 552992 | tf_op jit(solution)/shard_map/ppermute | solution.py:33
  49.3 0.5 collective-permute-start.9
  49.8 0.1 collective-permute-start.3
  50.0 9.9 %collective-permute-done.7.ahead.ahead_ref = bf16[48,2560]{1,0:T(8,128)(2,1)S(1)} collective-permute-done((bf16[48,2560]{1,0:T(8,128)(2,1)S(1)}, bf16[48,2560]{1,0:T(8,128)(2,1)S(1)}, u32[]{:S(2)}, u32[]{:S(2)}) %collective-permute-start.7) | collective-permute-done | bytes 245792 | tf_op jit(solution)/shard_map/ppermute | solution.py:33
  59.8 4.1 %collective-permute-start.1 = (bf16[208,640]{1,0:T(8,128)(2,1)S(1)}, bf16[208,640]{1,0:T(8,128)(2,1)S(1)}, u32[]{:S(2)}, u32[]{:S(2)}) collective-permute-start(bf16[208,640]{1,0:T(8,128)(2,1)S(1)} %slice.78), channel_id=1, source_target_pairs={{0,64},{64,128},{128,192},{192,0},{1,65},{65,129},{129,193},{193,1... | collective-permute-start | bytes 798728 | tf_op jit(solution)/shard_map/ppermute | solution.py:33
  63.9 0.1 pad_add_fusion.at_ref
  64.0 0.0 copy-start.10
  64.0 1.1 copy-done.10
  65.1 6.5 %shard_map.109 = (f32[2,432,560]{2,1,0:T(8,128)S(1)}, bf16[560,640]{1,0:T(8,128)(2,1)S(1)}) custom-call(s32[4]{0:T(128)S(1)} %pad_add_fusion.at_ref, bf16[128,2560]{1,0:T(8,128)(2,1)S(1)} %bitcast.28, bf16[128,2560]{1,0:T(8,128)(2,1)S(1)} %collective-permute-done.4.t1, bf16[128,2560]{1,0:T(8,128)(2,1)S(1)} %copy-done.10, ...), custom_call_target="tpu_custom_call" | custom-call | flops 1857945600 | bytes 9000000 | tf_op jit(solution)/shard_map/pallas_call | solution.py:278
  71.6 0.1 collective-permute-start.12
  71.7 0.5 collective-permute-start.11
  72.2 1.4 %collective-permute-done.11.refs_1_ = bf16[208,640]{1,0:T(8,128)(2,1)S(1)} collective-permute-done((bf16[208,640]{1,0:T(8,128)(2,1)S(1)}, bf16[208,640]{1,0:T(8,128)(2,1)S(1)}, u32[]{:S(2)}, u32[]{:S(2)}) %collective-permute-start.11) | collective-permute-done | bytes 266272 | tf_op jit(solution)/shard_map/ppermute | solution.py:37
  73.7 0.0 copy-start.3
  73.7 0.0 copy-start.4
  73.7 0.0 copy-start.5
  73.7 0.0 copy-start.6
  73.7 0.0 copy-start.7
  73.7 1.9 %shard_map.110 = (bf16[2,464,128]{2,1,0:T(8,128)(2,1)S(1)}, bf16[2,464,128]{2,1,0:T(8,128)(2,1)S(1)}, bf16[2,464,128]{2,1,0:T(8,128)(2,1)S(1)}, bf16[2,464,128]{2,1,0:T(8,128)(2,1)S(1)}) custom-call(s32[4]{0:T(128)S(1)} %pad_add_fusion.at_ref, f32[2,432,560]{2,1,0:T(8,128)S(1)} %get-tuple-element.20.part_ref, ...), custom_call_target="tpu_custom_call" | custom-call | flops 619315200 | bytes 5000000 | tf_op jit(solution)/shard_map/pallas_call | solution.py:291
  75.7 0.6 collective-permute-start.13
  76.3 2.6 %collective-permute-start.14 = (bf16[2,464,128]{2,1,0:T(8,128)(2,1)S(1)}, bf16[2,464,128]{2,1,0:T(8,128)(2,1)S(1)}, u32[]{:S(2)}, u32[]{:S(2)}) collective-permute-start(bf16[2,464,128]{2,1,0:T(8,128)(2,1)S(1)} %get-tuple-element.26), channel_id=1, source_target_pairs={{0,6},{2,0},{4,2},{6,4},{1,7},{3,1},{5,3},{7,5},{8,14},{10,8},{12,... | collective-permute-start | bytes 712712 | tf_op jit(solution)/shard_map/ppermute | solution.py:33
  79.0 0.5 collective-permute-start.15
  79.5 1.5 %shard_map.111 = (f32[27,128,128]{2,1,0:T(8,128)S(1)}, f32[4,128,128]{2,1,0:T(8,128)S(1)}) custom-call(s32[4]{0:T(128)S(1)} %pad_add_fusion.at_ref, bf16[128,3456]{1,0:T(8,128)(2,1)S(1)} %bitcast.16, s32[1,128]{1,0:T(1,128)S(1)} %copy-done.11, bf16[48,2560]{1,0:T(8,128)(2,1)S(1)} %collective-permute-done.7.ahead.ahead_ref), custom_call_target="tpu_custom_call" | custom-call | bytes 2700000 | tf_op jit(solution)/shard_map/pallas_call | solution.py:299
  81.0 8.8 %collective-permute-done.13.g1 = bf16[2,464,128]{2,1,0:T(8,128)(2,1)S(1)} collective-permute-done((bf16[2,464,128]{2,1,0:T(8,128)(2,1)S(1)}, bf16[2,464,128]{2,1,0:T(8,128)(2,1)S(1)}, u32[]{:S(2)}, u32[]{:S(2)}) %collective-permute-start.13) | collective-permute-done | bytes 237600 | tf_op jit(solution)/shard_map/ppermute | solution.py:33
  89.9 10.8 %shard_map.112 = (f32[27,128,128]{2,1,0:T(8,128)S(1)}, f32[27,128,128]{2,1,0:T(8,128)S(1)}, f32[2,3456]{1,0:T(2,128)S(1)}) custom-call(s32[4]{0:T(128)S(1)} %pad_add_fusion.at_ref, bf16[2,464,128]{2,1,0:T(8,128)(2,1)S(1)} %get-tuple-element.24.g0, bf16[2,464,128]{2,1,0:T(8,128)(2,1)S(1)} %collective-permute-done.13.g1, ...), custom_call_target="tpu_custom_call" | custom-call | flops 226492416 | bytes 8000000 | tf_op jit(solution)/shard_map/pallas_call | solution.py:315
  100.7 0.1 collective-permute-start.16
  100.8 6.0 %collective-permute-done.16 = f32[2,3456]{1,0:T(2,128)S(1)} collective-permute-done((f32[2,3456]{1,0:T(2,128)S(1)}, f32[2,3456]{1,0:T(2,128)S(1)}, u32[]{:S(2)}, u32[]{:S(2)}) %collective-permute-start.16) | collective-permute-done | bytes 27680 | tf_op jit(solution)/shard_map/ppermute | solution.py:33
  106.8 0.1 collective-permute-start.17
  106.9 0.8 collective-permute-start.18
  107.7 6.4 %collective-permute-start.19 = (f32[2,3456]{1,0:T(2,128)S(1)}, f32[2,3456]{1,0:T(2,128)S(1)}, u32[]{:S(2)}, u32[]{:S(2)}) collective-permute-start(f32[2,3456]{1,0:T(2,128)S(1)} %pad_maximum_fusion), channel_id=1, source_target_pairs={{0,40},{8,48},{16,56},{24,64},{32,72},{40,80},{48,88},{56,96},{64,... | collective-permute-start | bytes 82952 | tf_op jit(solution)/shard_map/ppermute | solution.py:33
  114.1 0.9 collective-permute-done.18
  115.0 0.7 collective-permute-done.19
  115.7 3.1 %collective-permute-done.20 = f32[2,3456]{1,0:T(2,128)S(1)} collective-permute-done((f32[2,3456]{1,0:T(2,128)S(1)}, f32[2,3456]{1,0:T(2,128)S(1)}, u32[]{:S(2)}, u32[]{:S(2)}) %collective-permute-start.20) | collective-permute-done | bytes 27680 | tf_op jit(solution)/shard_map/ppermute | solution.py:33
  118.8 0.1 slice_add_fusion.in_ref
  118.9 1.2 %shard_map.113 = bf16[128,3456]{1,0:T(8,128)(2,1)} custom-call(f32[27,128,128]{2,1,0:T(8,128)S(1)} %get-tuple-element.30.state_ref, f32[27,128,128]{2,1,0:T(8,128)S(1)} %get-tuple-element.31.prod_ref, f32[1,3456]{1,0:T(1,128)S(1)} %slice_add_fusion.in_ref), custom_call_target="tpu_custom_call" | custom-call | bytes 4400000 | tf_op jit(solution)/shard_map/pallas_call | solution.py:344
  (40 shorter events, 0.2 us)
Async XLA Ops:
  0.0 15.4 %copy-start.8 = (bf16[1,128,2560]{2,1,0:T(8,128)(2,1)S(1)}, bf16[1,128,2560]{2,1,0:T(8,128)(2,1)}, u32[]{:S(2)}) copy-start(bf16[1,128,2560]{2,1,0:T(8,128)(2,1)} %param.11) | copy-start | bytes 1966084
  0.0 15.3 %copy-start.11 = (s32[1,128]{1,0:T(1,128)S(1)}, s32[1,128]{1,0:T(1,128)}, u32[]{:S(2)}) copy-start(s32[1,128]{1,0:T(1,128)} %ids_ref.1) | copy-start | bytes 1540
  0.0 18.1 %collective-permute-start.4 = (bf16[128,2560]{1,0:T(8,128)(2,1)}, bf16[128,2560]{1,0:T(8,128)(2,1)S(1)}, u32[]{:S(2)}, u32[]{:S(2)}) collective-permute-start(bf16[128,2560]{1,0:T(8,128)(2,1)} %bitcast.25), channel_id=1, source_target_pairs={{0,2},{2,4},{4,6},{6,0},{1,3},{3,5},{5,7},{7,1},{8,10},{10,12},{12... | collective-permute-start | bytes 1966088 | tf_op jit(solution)/shard_map/ppermute | solution.py:33
  1.5 29.8 %collective-permute-start.5 = (bf16[128,2560]{1,0:T(8,128)(2,1)}, bf16[128,2560]{1,0:T(8,128)(2,1)S(1)}, u32[]{:S(2)}, u32[]{:S(2)}) collective-permute-start(bf16[128,2560]{1,0:T(8,128)(2,1)} %bitcast.26), channel_id=1, source_target_pairs={{0,6},{2,0},{4,2},{6,4},{1,7},{3,1},{5,3},{7,5},{8,14},{10,8},{12,... | collective-permute-start | bytes 1966088 | tf_op jit(solution)/shard_map/ppermute | solution.py:33
  3.2 35.2 %collective-permute-start.6 = (bf16[128,2560]{1,0:T(8,128)(2,1)}, bf16[128,2560]{1,0:T(8,128)(2,1)}, u32[]{:S(2)}, u32[]{:S(2)}) collective-permute-start(bf16[128,2560]{1,0:T(8,128)(2,1)} %bitcast.27), channel_id=1, source_target_pairs={{0,4},{2,6},{4,0},{6,2},{1,5},{3,7},{5,1},{7,3},{8,12},{10,14},{12... | collective-permute-start | bytes 1966088 | tf_op jit(solution)/shard_map/ppermute | solution.py:33
  6.9 27.9 %all-to-all-start = ((bf16[8,80,512]{2,1,0:T(8,128)(2,1)}), bf16[8,80,512]{2,1,0:T(8,128)(2,1)S(1)}, u32[]{:S(2)}, u32[]{:S(2)}) async-start(bf16[8,80,512]{2,1,0:T(8,128)(2,1)} %broadcast_in_dim.4), calls=%async_computation | async-start | bytes 1310720 | tf_op jit(solution)/shard_map/all_to_all | solution.py:266
  31.3 0.8 copy-start.9
  35.1 14.2 %collective-permute-start.2 = (bf16[432,640]{1,0:T(8,128)(2,1)S(1)}, bf16[432,640]{1,0:T(8,128)(2,1)S(1)}, u32[]{:S(2)}, u32[]{:S(2)}) collective-permute-start(bf16[432,640]{1,0:T(8,128)(2,1)S(1)} %bitcast.17), channel_id=1, source_target_pairs={{0,192},{64,0},{128,64},{192,128},{1,193},{65,1},{129,65},{193,129... | collective-permute-start | bytes 1658888 | tf_op jit(solution)/shard_map/ppermute | solution.py:33
  35.9 13.3 %collective-permute-start = (bf16[432,640]{1,0:T(8,128)(2,1)S(1)}, bf16[432,640]{1,0:T(8,128)(2,1)S(1)}, u32[]{:S(2)}, u32[]{:S(2)}) collective-permute-start(bf16[432,640]{1,0:T(8,128)(2,1)S(1)} %bitcast.18), channel_id=1, source_target_pairs={{0,64},{64,128},{128,192},{192,0},{1,65},{65,129},{129,193},{193,1... | collective-permute-start | bytes 1658888 | tf_op jit(solution)/shard_map/ppermute | solution.py:33
  39.2 24.8 %collective-permute-start.8 = (bf16[432,640]{1,0:T(8,128)(2,1)S(1)}, bf16[432,640]{1,0:T(8,128)(2,1)}, u32[]{:S(2)}, u32[]{:S(2)}) collective-permute-start(bf16[432,640]{1,0:T(8,128)(2,1)S(1)} %bitcast.19), channel_id=1, source_target_pairs={{0,1},{1,0},{2,3},{3,2},{4,5},{5,4},{6,7},{7,6},{8,9},{9,8},{10,11... | collective-permute-start | bytes 1658888 | tf_op jit(solution)/shard_map/ppermute | solution.py:37
  49.3 14.8 %collective-permute-start.10 = (bf16[432,640]{1,0:T(8,128)(2,1)S(1)}, bf16[432,640]{1,0:T(8,128)(2,1)}, u32[]{:S(2)}, u32[]{:S(2)}) collective-permute-start(bf16[432,640]{1,0:T(8,128)(2,1)S(1)} %collective-permute-done.2.refs_4_), channel_id=1, source_target_pairs={{0,1},{1,0},{2,3},{3,2},{4,5},{5,4},{6,7},{7,6},{8,9},{9,8},{10,11... | collective-permute-start | bytes 1658888 | tf_op jit(solution)/shard_map/ppermute | solution.py:37
  49.3 14.7 %collective-permute-start.9 = (bf16[432,640]{1,0:T(8,128)(2,1)S(1)}, bf16[432,640]{1,0:T(8,128)(2,1)}, u32[]{:S(2)}, u32[]{:S(2)}) collective-permute-start(bf16[432,640]{1,0:T(8,128)(2,1)S(1)} %collective-permute-done.refs_2_), channel_id=1, source_target_pairs={{0,1},{1,0},{2,3},{3,2},{4,5},{5,4},{6,7},{7,6},{8,9},{9,8},{10,11... | collective-permute-start | bytes 1658888 | tf_op jit(solution)/shard_map/ppermute | solution.py:37
  49.8 10.1 %collective-permute-start.7 = (bf16[48,2560]{1,0:T(8,128)(2,1)S(1)}, bf16[48,2560]{1,0:T(8,128)(2,1)S(1)}, u32[]{:S(2)}, u32[]{:S(2)}) collective-permute-start(bf16[48,2560]{1,0:T(8,128)(2,1)S(1)} %pad_dynamic-update-slice_fusion), channel_id=1, source_target_pairs={{0,8},{8,16},{16,24},{24,32},{32,40},{40,48},{48,56},{56,64},{64,7... | collective-permute-start | bytes 737288 | tf_op jit(solution)/shard_map/ppermute | solution.py:33
  49.8 21.8 %collective-permute-start.3 = (bf16[224,640]{1,0:T(8,128)(2,1)S(1)}, bf16[224,640]{1,0:T(8,128)(2,1)S(1)}, u32[]{:S(2)}, u32[]{:S(2)}) collective-permute-start(bf16[224,640]{1,0:T(8,128)(2,1)S(1)} %slice.79), channel_id=1, source_target_pairs={{0,192},{64,0},{128,64},{192,128},{1,193},{65,1},{129,65},{193,129... | collective-permute-start | bytes 860168 | tf_op jit(solution)/shard_map/ppermute | solution.py:33
  59.8 11.8 %collective-permute-start.1 = (bf16[208,640]{1,0:T(8,128)(2,1)S(1)}, bf16[208,640]{1,0:T(8,128)(2,1)S(1)}, u32[]{:S(2)}, u32[]{:S(2)}) collective-permute-start(bf16[208,640]{1,0:T(8,128)(2,1)S(1)} %slice.78), channel_id=1, source_target_pairs={{0,64},{64,128},{128,192},{192,0},{1,65},{65,129},{129,193},{193,1... | collective-permute-start | bytes 798728 | tf_op jit(solution)/shard_map/ppermute | solution.py:33
  64.0 1.1 copy-start.10
  71.6 2.0 %collective-permute-start.12 = (bf16[224,640]{1,0:T(8,128)(2,1)S(1)}, bf16[224,640]{1,0:T(8,128)(2,1)S(1)}, u32[]{:S(2)}, u32[]{:S(2)}) collective-permute-start(bf16[224,640]{1,0:T(8,128)(2,1)S(1)} %collective-permute-done.3.refs_2_), channel_id=1, source_target_pairs={{0,1},{1,0},{2,3},{3,2},{4,5},{5,4},{6,7},{7,6},{8,9},{9,8},{10,11... | collective-permute-start | bytes 860168 | tf_op jit(solution)/shard_map/ppermute | solution.py:37
  71.7 1.9 %collective-permute-start.11 = (bf16[208,640]{1,0:T(8,128)(2,1)S(1)}, bf16[208,640]{1,0:T(8,128)(2,1)S(1)}, u32[]{:S(2)}, u32[]{:S(2)}) collective-permute-start(bf16[208,640]{1,0:T(8,128)(2,1)S(1)} %collective-permute-done.1.refs_0_), channel_id=1, source_target_pairs={{0,1},{1,0},{2,3},{3,2},{4,5},{5,4},{6,7},{7,6},{8,9},{9,8},{10,11... | collective-permute-start | bytes 798728 | tf_op jit(solution)/shard_map/ppermute | solution.py:37
  73.7 5.8 %copy-start = (bf16[1,128,3456]{2,1,0:T(8,128)(2,1)S(1)}, bf16[1,128,3456]{2,1,0:T(8,128)(2,1)}, u32[]{:S(2)}) copy-start(bf16[1,128,3456]{2,1,0:T(8,128)(2,1)} %param.12) | copy-start | bytes 2654212
  73.7 16.2 %copy-start.1 = (bf16[27,128,128]{2,1,0:T(8,128)(2,1)S(1)}, bf16[27,128,128]{2,1,0:T(8,128)(2,1)}, u32[]{:S(2)}) copy-start(bf16[27,128,128]{2,1,0:T(8,128)(2,1)} %gate_a_ref.1) | copy-start | bytes 2654212
  73.7 16.2 %copy-start.2 = (bf16[27,128,128]{2,1,0:T(8,128)(2,1)S(1)}, bf16[27,128,128]{2,1,0:T(8,128)(2,1)}, u32[]{:S(2)}) copy-start(bf16[27,128,128]{2,1,0:T(8,128)(2,1)} %gate_i_ref.1) | copy-start | bytes 2654212
  73.7 16.2 %copy-start.3 = (f32[4,3456]{1,0:T(4,128)S(1)}, f32[4,3456]{1,0:T(4,128)}, u32[]{:S(2)}) copy-start(f32[4,3456]{1,0:T(4,128)} %taps_ref.1) | copy-start | bytes 165892
  73.7 16.2 %copy-start.4 = (f32[3456]{0:T(1024)S(1)}, f32[3456]{0:T(1024)}, u32[]{:S(2)}) copy-start(f32[3456]{0:T(1024)} %param.16) | copy-start | bytes 41476
  73.7 16.2 %copy-start.5 = (f32[3456]{0:T(1024)S(1)}, f32[3456]{0:T(1024)}, u32[]{:S(2)}) copy-start(f32[3456]{0:T(1024)} %param.19) | copy-start | bytes 41476
  73.7 16.2 %copy-start.6 = (f32[3456]{0:T(1024)S(1)}, f32[3456]{0:T(1024)}, u32[]{:S(2)}) copy-start(f32[3456]{0:T(1024)} %param.20) | copy-start | bytes 41476
  73.7 16.2 %copy-start.7 = (f32[3456]{0:T(1024)S(1)}, f32[3456]{0:T(1024)}, u32[]{:S(2)}) copy-start(f32[3456]{0:T(1024)} %param.21) | copy-start | bytes 41476
  75.7 14.2 %collective-permute-start.13 = (bf16[2,464,128]{2,1,0:T(8,128)(2,1)S(1)}, bf16[2,464,128]{2,1,0:T(8,128)(2,1)S(1)}, u32[]{:S(2)}, u32[]{:S(2)}) collective-permute-start(bf16[2,464,128]{2,1,0:T(8,128)(2,1)S(1)} %get-tuple-element.25), channel_id=1, source_target_pairs={{0,2},{2,4},{4,6},{6,0},{1,3},{3,5},{5,7},{7,1},{8,10},{10,12},{12... | collective-permute-start | bytes 712712 | tf_op jit(solution)/shard_map/ppermute | solution.py:33
  76.3 13.5 %collective-permute-start.14 = (bf16[2,464,128]{2,1,0:T(8,128)(2,1)S(1)}, bf16[2,464,128]{2,1,0:T(8,128)(2,1)S(1)}, u32[]{:S(2)}, u32[]{:S(2)}) collective-permute-start(bf16[2,464,128]{2,1,0:T(8,128)(2,1)S(1)} %get-tuple-element.26), channel_id=1, source_target_pairs={{0,6},{2,0},{4,2},{6,4},{1,7},{3,1},{5,3},{7,5},{8,14},{10,8},{12,... | collective-permute-start | bytes 712712 | tf_op jit(solution)/shard_map/ppermute | solution.py:33
  79.0 10.9 %collective-permute-start.15 = (bf16[2,464,128]{2,1,0:T(8,128)(2,1)S(1)}, bf16[2,464,128]{2,1,0:T(8,128)(2,1)S(1)}, u32[]{:S(2)}, u32[]{:S(2)}) collective-permute-start(bf16[2,464,128]{2,1,0:T(8,128)(2,1)S(1)} %get-tuple-element.27), channel_id=1, source_target_pairs={{0,4},{2,6},{4,0},{6,2},{1,5},{3,7},{5,1},{7,3},{8,12},{10,14},{12... | collective-permute-start | bytes 712712 | tf_op jit(solution)/shard_map/ppermute | solution.py:33
  100.7 6.0 %collective-permute-start.16 = (f32[2,3456]{1,0:T(2,128)S(1)}, f32[2,3456]{1,0:T(2,128)S(1)}, u32[]{:S(2)}, u32[]{:S(2)}) collective-permute-start(f32[2,3456]{1,0:T(2,128)S(1)} %get-tuple-element.32), channel_id=1, source_target_pairs={{0,8},{8,16},{16,24},{24,32},{32,40},{40,48},{48,56},{56,64},{64,7... | collective-permute-start | bytes 82952 | tf_op jit(solution)/shard_map/ppermute | solution.py:33
  106.8 7.2 %collective-permute-start.17 = (f32[2,3456]{1,0:T(2,128)S(1)}, f32[2,3456]{1,0:T(2,128)S(1)}, u32[]{:S(2)}, u32[]{:S(2)}) collective-permute-start(f32[2,3456]{1,0:T(2,128)S(1)} %pad_maximum_fusion), channel_id=1, source_target_pairs={{0,8},{8,16},{16,24},{24,32},{32,40},{40,48},{48,56},{56,64},{64,7... | collective-permute-start | bytes 82952 | tf_op jit(solution)/shard_map/ppermute | solution.py:33
  106.9 8.1 %collective-permute-start.18 = (f32[2,3456]{1,0:T(2,128)S(1)}, f32[2,3456]{1,0:T(2,128)S(1)}, u32[]{:S(2)}, u32[]{:S(2)}) collective-permute-start(f32[2,3456]{1,0:T(2,128)S(1)} %pad_maximum_fusion), channel_id=1, source_target_pairs={{0,24},{8,32},{16,40},{24,48},{32,56},{40,64},{48,72},{56,80},{64,... | collective-permute-start | bytes 82952 | tf_op jit(solution)/shard_map/ppermute | solution.py:33
  107.7 8.0 %collective-permute-start.19 = (f32[2,3456]{1,0:T(2,128)S(1)}, f32[2,3456]{1,0:T(2,128)S(1)}, u32[]{:S(2)}, u32[]{:S(2)}) collective-permute-start(f32[2,3456]{1,0:T(2,128)S(1)} %pad_maximum_fusion), channel_id=1, source_target_pairs={{0,40},{8,48},{16,56},{24,64},{32,72},{40,80},{48,88},{56,96},{64,... | collective-permute-start | bytes 82952 | tf_op jit(solution)/shard_map/ppermute | solution.py:33
  114.1 4.8 %collective-permute-start.20 = (f32[2,3456]{1,0:T(2,128)S(1)}, f32[2,3456]{1,0:T(2,128)S(1)}, u32[]{:S(2)}, u32[]{:S(2)}) collective-permute-start(f32[2,3456]{1,0:T(2,128)S(1)} %pad_maximum_fusion), channel_id=1, source_target_pairs={{0,56},{8,64},{16,72},{24,80},{32,88},{40,96},{48,104},{56,112},{6... | collective-permute-start | bytes 82952 | tf_op jit(solution)/shard_map/ppermute | solution.py:33

commit v4 on v3

--- a/solution.py
+++ b/solution.py
@@ -24,7 +24,8 @@
 HALO = 8
 PACK = COLS + 32
 CUT = 208
-AHEAD = 4 * HALO + 16
+AHEAD = 16
+NEAR, FAR = 20, 8
 ROWS = 4 * LENGTH + AHEAD
 
 
@@ -44,7 +45,7 @@
         return carry
 
     lax.fori_loop(0, HEADS, head, 0)
-    prior = ahead_ref[4 * HALO : AHEAD, 0:LENGTH].astype(F32)[0:1]
+    prior = ahead_ref[:, 0:LENGTH].astype(F32)[0:1]
     prior = jnp.where(at_ref[3] == 0, -1.0, prior)
     prior = jnp.broadcast_to(prior, (LENGTH, LENGTH)).T
     own = jnp.broadcast_to(ids_ref[...].astype(F32), (LENGTH, LENGTH)).T
@@ -101,73 +102,69 @@
         all_ref[CUT:COLS, :] = weights[2 + half][...]
         total = part_ref[half] + across(all_ref[...], far_ref[...])
         place = c if half == 0 else 1 - c
+        main = pl.ds(pl.multiple_of(place * COLS, 16), COLS)
         wide_ref[0:COLS, 0:AHEAD] = total[:, 4 * LENGTH :]
         turned = [wide_ref[j * 128 : (j + 1) * 128, :].T for j in range(4)]
         for i, out_ref in enumerate(outs):
-            out_ref[place, 0:COLS, :] = total[:, i * LENGTH : (i + 1) * LENGTH].astype(BF16)
+            out_ref[main, :] = total[:, i * LENGTH : (i + 1) * LENGTH].astype(BF16)
+            group = [t[8 * (i // 2) : 8 * (i // 2) + 8, :] for t in turned]
+            if i % 2 == 0:
+                group = [pltpu.roll(g, 4, 0) for g in group]
             for j in range(2):
-                pair = [turned[2 * j + n][HALO * i : HALO * i + HALO, :] for n in range(2)]
-                out_ref[place, COLS + 16 * j : COLS + 16 * j + 16, :] = jnp.concatenate(
-                    pair, axis=0
-                ).astype(BF16)
-
-
-def recur_kernel(
-    at_ref,
-    g0,
-    g1,
-    g2,
-    g3,
-    mask_ref,
-    gelu_ref,
-    taps_ref,
-    bias_ref,
-    bias_a_ref,
-    bias_i_ref,
-    rate_ref,
-    gate_a_ref,
-    gate_i_ref,
-    state_ref,
-    prod_ref,
-    end_ref,
-    x_scr,
-    got_ref,
-    sems,
-):
+                rest = pl.ds(pl.multiple_of(2 * COLS + 32 * place + 16 * j, 16), 16)
+                out_ref[rest, :] = jnp.concatenate(group[2 * j : 2 * j + 2], axis=0).astype(BF16)
+
+
+def far_head(x):
+    return jnp.minimum((lax.rem(x + 2, 4) * HEADS) // 4, HEADS - FAR)
+
+
+def recur(at_ref, got, refs, far, state_ref, prod_ref, end_ref, scratch):
+    (
+        mask_ref,
+        gelu_ref,
+        taps_ref,
+        bias_ref,
+        bias_a_ref,
+        bias_i_ref,
+        rate_ref,
+        gate_a_ref,
+        gate_i_ref,
+    ) = refs
+    x_scr, main_ref, pack_ref, ahead_ref, sems = scratch
     x = at_ref[0]
-    pairs = [
-        (ref, got_ref.at[pl.ds(lax.rem(x + 4 - back, 4) * 2, 2)])
-        for back, ref in ((0, g0), (1, g1), (3, g2), (2, g3))
-    ]
+    pairs = []
+    for back, ref in zip((0, 1, 3, 2), got):
+        block = lax.rem(x + 4 - back, 4)
+        rows = pl.ds(pl.multiple_of(block * (2 * COLS), 16), 2 * COLS)
+        pairs.append((ref.at[pl.ds(0, 2 * COLS)], main_ref.at[rows]))
+        pairs.append((ref.at[pl.ds(2 * COLS, 64)], pack_ref.at[block]))
     for copy in copies(pairs, sems):
         copy.wait()
     ahead = []
     for f in range(8):
-        packed = got_ref[f, COLS:PACK, :].astype(F32)
+        packed = pack_ref[f // 2, 32 * (f % 2) : 32 * (f % 2) + 32, :].astype(F32)
         ahead += [packed[8 * j : 8 * j + 8, : min(128, COLS - 128 * j)] for j in range(4)]
-    ahead = jnp.concatenate(ahead, axis=1)
-    for h in range(HEADS):
-        f, low = (h * HEAD) // COLS, (h * HEAD) % COLS
-        size = min(HEAD, COLS - low)
-        block = got_ref[f, low : low + size, :].astype(F32)
-        if size < HEAD:
-            rest = got_ref[f + 1, 0 : HEAD - size, :].astype(F32)
-            block = jnp.concatenate([block, rest], axis=0)
-        x_scr[h, 0:HALO, :] = ahead[:, h * HEAD : (h + 1) * HEAD]
-        x_scr[h, HALO:, :] = block.T
+    ahead_ref[...] = jnp.concatenate(ahead, axis=1)
 
     row = lax.broadcasted_iota(jnp.int32, (8, HEAD), 0)
-
-    def head(h, carry):
+    start = far_head(x)
+
+    def head(i, slot):
+        h = start + i if far else lax.rem(start + FAR + i, HEADS)
+        out = i if far else h
         lanes = pl.ds(pl.multiple_of(h * HEAD, HEAD), HEAD)
         at_head = pl.ds(h, 1)
-        taps = [taps_ref[i : i + 1, lanes] for i in range(4)]
+        x_scr[slot, 0:HALO, :] = ahead_ref[:, lanes]
+        x_scr[slot, HALO:, :] = main_ref[lanes, :].astype(F32).T
+        taps = [taps_ref[n : n + 1, lanes] for n in range(4)]
+        bias = bias_ref[at_head, :]
         shifted = {
-            off: x_scr[h, pl.ds(HALO + off, 8, stride=SPAN), :] for off in range(-3, SPAN)
+            off: x_scr[slot, pl.ds(HALO + off, 8, stride=SPAN), :] for off in range(-3, SPAN)
         }
         conv = []
         for k in range(SPAN):
-            total = taps[0] * shifted[k] + bias_ref[at_head, :]
+            total = taps[0] * shifted[k] + bias
             for back in range(1, 4):
                 valid = mask_ref[back, 8 * k : 8 * k + 8, :]
                 total = total + taps[back] * (shifted[k - back] * valid)
@@ -208,20 +205,45 @@
         for k in range(SPAN):
             at = pl.ds(k, 8, stride=SPAN)
             gelu = gelu_ref[h, at, :]
-            state_ref[h, at, :] = (states[k] + prods[k] * in_state) * gelu
-            prod_ref[h, at, :] = (prods[k] * in_prod) * gelu
+            state_ref[out, at, :] = (states[k] + prods[k] * in_state) * gelu
+            prod_ref[out, at, :] = (prods[k] * in_prod) * gelu
+
+    def pair(i, carry):
+        for slot in range(2):
+            head(2 * i + slot, slot)
         return carry
 
-    lax.fori_loop(0, HEADS, head, 0)
-
-
-def finish_kernel(state_ref, prod_ref, in_ref, out_ref):
-    def head(h, carry):
+    lax.fori_loop(0, (FAR if far else NEAR) // 2, pair, 0)
+
+
+def near_kernel(at_ref, *refs):
+    state_ref, prod_ref, end_ref = refs[12:15]
+    recur(at_ref, refs[:3], refs[3:12], False, state_ref, prod_ref, end_ref, refs[15:])
+
+
+def far_kernel(at_ref, *refs):
+    ends_ref = refs[13]
+    state_ref, prod_ref, end_ref = refs[14:17]
+    end_ref[...] = ends_ref[...]
+    recur(at_ref, refs[:4], refs[4:13], True, state_ref, prod_ref, end_ref, refs[17:])
+
+
+def finish_kernel(at_ref, state_ref, prod_ref, far_state_ref, far_prod_ref, in_ref, out_ref):
+    start = far_head(at_ref[0])
+
+    def near(i, carry):
+        h = lax.rem(start + FAR + i, HEADS)
         lanes = pl.ds(pl.multiple_of(h * HEAD, HEAD), HEAD)
         out_ref[:, lanes] = (state_ref[h] + prod_ref[h] * in_ref[:, lanes]).astype(BF16)
         return carry
 
-    lax.fori_loop(0, HEADS, head, 0)
+    def far(i, carry):
+        lanes = pl.ds(pl.multiple_of((start + i) * HEAD, HEAD), HEAD)
+        out_ref[:, lanes] = (far_state_ref[i] + far_prod_ref[i] * in_ref[:, lanes]).astype(BF16)
+        return carry
+
+    lax.fori_loop(0, HEADS - FAR, near, 0)
+    lax.fori_loop(0, FAR, far, 0)
 
 
 def call(kernel, outs, ins, scratch=(), room=16, flops=0, moved=0):
@@ -261,19 +283,19 @@
         jnp.int32
     )
 
+    copied = jnp.broadcast_to(in_weight[None], (8,) + in_weight.shape)
+    column = lax.all_to_all(copied, "z", 0, 0, tiled=True).reshape(-1, COLS).T
     streams = [own, shift(own, "x", 1), shift(own, "x", -1), shift(own, "x", 2)]
-    filled = jnp.pad(in_weight, ((0, 0), (0, 512 - COLS)))
-    column = lax.all_to_all(
-        jnp.broadcast_to(filled[None], (8,) + filled.shape), "z", 0, 0, tiled=True
-    ).reshape(-1, 512)[:, :COLS].T
     from_back = shift(column, "y", 1)
     from_ahead = shift(column, "y", -1)
     near = [column, flip(column), from_back, flip(from_back), from_ahead, flip(from_ahead)]
     first = shift(from_back[:CUT], "y", 1)
     second = shift(from_ahead[CUT:], "y", -1)
 
-    documents = jnp.pad(segment_ids.astype(BF16), ((0, 15), (0, DEPTH - LENGTH)))
-    ahead = shift(jnp.concatenate([t[-HALO:] for t in streams] + [documents], axis=0), ctx, 1)
+    documents = jnp.pad(segment_ids.astype(BF16), ((0, 0), (0, DEPTH - LENGTH)))
+    ahead = shift(
+        jnp.concatenate([documents, own[-3:]] + [t[-4:] for t in streams[1:]], axis=0), ctx, 1
+    )
 
     part, rows_far = call(
         project_kernel,
@@ -290,7 +312,7 @@
     far = [first, flip(first), second, flip(second)]
     sent = call(
         pack_kernel,
-        [jax.ShapeDtypeStruct((2, PACK, 128), BF16)] * 4,
+        [jax.ShapeDtypeStruct((2 * PACK, 128), BF16)] * 4,
         [SMEM] + [VMEM] * 6,
         [pltpu.VMEM((COLS, 640), BF16), pltpu.VMEM((512, 128), F32)],
         flops=2 * 560 * 640 * 864,
@@ -312,24 +334,7 @@
         shift(sent[1], "x", -1),
         shift(sent[3], "x", 2),
     ]
-    states, prods, ends = call(
-        recur_kernel,
-        (
-            jax.ShapeDtypeStruct((HEADS, LENGTH, HEAD), F32),
-            jax.ShapeDtypeStruct((HEADS, LENGTH, HEAD), F32),
-            jax.ShapeDtypeStruct((2, WIDTH), F32),
-        ),
-        [SMEM] + [ANY] * 4 + [VMEM] * 9,
-        [
-            pltpu.VMEM((HEADS, LENGTH + HALO, HEAD), F32),
-            pltpu.VMEM((8, PACK, 128), BF16),
-            pltpu.SemaphoreType.DMA((4,)),
-        ],
-        flops=2 * 128 * 3456 * 256,
-        moved=8_000_000,
-    )(
-        at,
-        *got,
+    shared = (
         masks,
         gelu,
         conv_weight,
@@ -337,6 +342,37 @@
         gate_a,
         gate_i,
     )
+    scratch = [
+        pltpu.VMEM((2, LENGTH + HALO, HEAD), F32),
+        pltpu.VMEM((WIDTH, LENGTH), BF16),
+        pltpu.VMEM((4, 64, 128), BF16),
+        pltpu.VMEM((HALO, WIDTH), F32),
+        pltpu.SemaphoreType.DMA((8,)),
+    ]
+
+    def walked(heads):
+        return (
+            jax.ShapeDtypeStruct((heads, LENGTH, HEAD), F32),
+            jax.ShapeDtypeStruct((heads, LENGTH, HEAD), F32),
+            jax.ShapeDtypeStruct((2, WIDTH), F32),
+        )
+
+    states, prods, ends = call(
+        near_kernel,
+        walked(HEADS),
+        [SMEM] + [ANY] * 3 + [VMEM] * 9,
+        scratch,
+        flops=2 * 128 * 2560 * 256,
+        moved=20_000_000,
+    )(at, *got[:3], *shared)
+    far_states, far_prods, ends = call(
+        far_kernel,
+        walked(FAR),
+        [SMEM] + [ANY] * 4 + [VMEM] * 10,
+        scratch,
+        flops=2 * 128 * 1024 * 256,
+        moved=8_000_000,
+    )(at, *got, *shared, ends)
 
     two = joined(shift(ends, ctx, 1), ends)
     pairs = [shift(two, ctx, by) for by in (7, 5, 3, 1)]
@@ -344,9 +380,9 @@
     out = call(
         finish_kernel,
         jax.ShapeDtypeStruct((LENGTH, WIDTH), BF16),
-        [VMEM] * 3,
+        [SMEM] + [VMEM] * 5,
         moved=4_400_000,
-    )(states, prods, incoming)
+    )(at, states, prods, far_states, far_prods, incoming)
     return out[None]
 
 

time: 121 us -> 133 us (1.099)
  waiting for transfers between devices: 59.5 us -> 70.1 us
  starting transfers between devices: 33.2 us -> 31.8 us
    all_to_all x1, waiting for transfers between devices: 2.63 us -> 18.7 us  [body(): column = lax.all_to_all(copied, 'z', 0, 0, tiled=True).reshape(-1, COLS).T]
    ppermute x16, waiting for transfers between devices: 55.4 us -> 49.9 us  [shift(): lax.ppermute(value, axis, [(i, (i + by) % count) for i in range(count)])]
    pallas_call x3 -> x4, Pallas kernels: 13.9 us -> 15.6 us  [the longest x1 7.32 us: body(): call(near_kernel, walked(HEADS), [SMEM] + [ANY] * 3 + [VMEM] * 9, scratch...]
    ppermute x16, starting transfers between devices: 23.7 us -> 22.1 us  [shift(): lax.ppermute(value, axis, [(i, (i + by) % count) for i in range(count)])]
    unnamed x29 -> x28, local copies, waits for them, and re-layouts: 3.06 us -> 3.89 us
  transfers between devices with their start and end apart: 22 -> 22, of which waited for: 11 -> 10; matrix products, arithmetic and copies ran while one was open for 3% -> 0% of each run, Pallas kernels for 7% -> 11%
where the time goes in v4:
time: 133 us; the launch traced here: 131 us
  waiting for transfers between devices  70.1 us (53%)
  starting transfers between devices  31.8 us (24%)
  Pallas kernels  22.8 us (17%)
  local copies, waits for them, and re-layouts  6.23 us (5%)
    ppermute x16, waiting for transfers between devices, shift(): lax.ppermute(value, axis, [(i, (i + by) % count) for i in range(count)])  49.9 us
    ppermute x16, starting transfers between devices, shift(): lax.ppermute(value, axis, [(i, (i + by) % count) for i in range(count)])  22.1 us
    all_to_all x1, waiting for transfers between devices, body(): column = lax.all_to_all(copied, 'z', 0, 0, tiled=True).reshape(-1, COLS).T  18.7 us
    all_to_all x1, starting transfers between devices, body(): column = lax.all_to_all(copied, 'z', 0, 0, tiled=True).reshape(-1, COLS).T  8.47 us
    pallas_call x1, Pallas kernels, body(): call(near_kernel, walked(HEADS), [SMEM] + [ANY] * 3 + [VMEM] * 9, scratch...  7.32 us
    pallas_call x1, Pallas kernels, body(): call(project_kernel, (jax.ShapeDtypeStruct((2, COLS, ROWS), F32), jax.Sha...  5.71 us
    pallas_call x1, Pallas kernels, body(): call(far_kernel, walked(FAR), [SMEM] + [ANY] * 4 + [VMEM] * 10, scratch,...  4.35 us
    unnamed x28, local copies, waits for them, and re-layouts  3.89 us
  transfers between devices with their start and end apart: 22, of which 10 were waited for; matrix products, arithmetic and copies ran while one was open for 0% of the time, Pallas kernels for 11%

profile of v4, /device:TPU:24, one launch (start us, length us, event | category | flops | bytes accessed | tf_op | source)
XLA Modules:
  0.0 131.5 jit_solution(8226113525092376068)
XLA Ops:
  0.0 1.8 %broadcast_in_dim.4 = bf16[8,80,432]{2,1,0:T(8,128)(2,1)} broadcast(bf16[80,432]{1,0:T(8,128)(2,1)} %param.14), dimensions={1,2} | broadcast | bytes 622080 | tf_op jit(solution)/shard_map/broadcast_in_dim | solution.py:286
  1.8 8.5 %all-to-all-start = ((bf16[8,80,432]{2,1,0:T(8,128)(2,1)}), bf16[8,80,432]{2,1,0:T(8,128)(2,1)S(1)}, u32[]{:S(2)}, u32[]{:S(2)}) async-start(bf16[8,80,432]{2,1,0:T(8,128)(2,1)} %broadcast_in_dim.4), calls=%async_computation | async-start | bytes 1310720 | tf_op jit(solution)/shard_map/all_to_all | solution.py:287
  10.3 1.6 %collective-permute-start.4 = (bf16[128,2560]{1,0:T(8,128)(2,1)S(1)}, bf16[128,2560]{1,0:T(8,128)(2,1)S(1)}, u32[]{:S(2)}, u32[]{:S(2)}) collective-permute-start(bf16[128,2560]{1,0:T(8,128)(2,1)S(1)} %bitcast.28), channel_id=1, source_target_pairs={{0,2},{2,4},{4,6},{6,0},{1,3},{3,5},{5,7},{7,1},{8,10},{10,12},{12... | collective-permute-start | bytes 1966088 | tf_op jit(solution)/shard_map/ppermute | solution.py:34
  11.9 18.7 %all-to-all-done = bf16[8,80,432]{2,1,0:T(8,128)(2,1)S(1)} async-done(((bf16[8,80,432]{2,1,0:T(8,128)(2,1)}), bf16[8,80,432]{2,1,0:T(8,128)(2,1)S(1)}, u32[]{:S(2)}, u32[]{:S(2)}) %all-to-all-start) | async-done | bytes 552992 | tf_op jit(solution)/shard_map/all_to_all | solution.py:287
  30.6 0.3 copy.13
  30.9 0.8 collective-permute-start.2
  31.7 2.5 %collective-permute-start = (bf16[432,640]{1,0:T(8,128)(2,1)S(1)}, bf16[432,640]{1,0:T(8,128)(2,1)S(1)}, u32[]{:S(2)}, u32[]{:S(2)}) collective-permute-start(bf16[432,640]{1,0:T(8,128)(2,1)S(1)} %bitcast.17), channel_id=1, source_target_pairs={{0,64},{64,128},{128,192},{192,0},{1,65},{65,129},{129,193},{193,1... | collective-permute-start | bytes 1658888 | tf_op jit(solution)/shard_map/ppermute | solution.py:34
  34.2 2.8 %collective-permute-start.5 = (bf16[128,2560]{1,0:T(8,128)(2,1)S(1)}, bf16[128,2560]{1,0:T(8,128)(2,1)S(1)}, u32[]{:S(2)}, u32[]{:S(2)}) collective-permute-start(bf16[128,2560]{1,0:T(8,128)(2,1)S(1)} %bitcast.29), channel_id=1, source_target_pairs={{0,6},{2,0},{4,2},{6,4},{1,7},{3,1},{5,3},{7,5},{8,14},{10,8},{12,... | collective-permute-start | bytes 1966088 | tf_op jit(solution)/shard_map/ppermute | solution.py:34
  37.0 0.8 collective-permute-start.6
  37.8 0.1 collective-permute-start.8
  37.9 8.7 %collective-permute-done.2.refs_4_ = bf16[432,640]{1,0:T(8,128)(2,1)S(1)} collective-permute-done((bf16[432,640]{1,0:T(8,128)(2,1)S(1)}, bf16[432,640]{1,0:T(8,128)(2,1)S(1)}, u32[]{:S(2)}, u32[]{:S(2)}) %collective-permute-start.2) | collective-permute-done | bytes 552992 | tf_op jit(solution)/shard_map/ppermute | solution.py:34
  46.7 0.5 collective-permute-start.9
  47.2 17.5 %collective-permute-done.5.t2 = bf16[128,2560]{1,0:T(8,128)(2,1)S(1)} collective-permute-done((bf16[128,2560]{1,0:T(8,128)(2,1)S(1)}, bf16[128,2560]{1,0:T(8,128)(2,1)S(1)}, u32[]{:S(2)}, u32[]{:S(2)}) %collective-permute-start.5) | collective-permute-done | bytes 655392 | tf_op jit(solution)/shard_map/ppermute | solution.py:34
  64.7 0.8 copy-done.9
  65.6 0.8 copy-done.11
  66.4 0.1 concatenate.6
  66.5 0.1 collective-permute-start.7
  66.6 0.1 collective-permute-start.3
  66.7 6.4 %collective-permute-done.7.ahead.ahead_ref = bf16[16,2560]{1,0:T(8,128)(2,1)S(1)} collective-permute-done((bf16[16,2560]{1,0:T(8,128)(2,1)S(1)}, bf16[16,2560]{1,0:T(8,128)(2,1)S(1)}, u32[]{:S(2)}, u32[]{:S(2)}) %collective-permute-start.7) | collective-permute-done | bytes 81952 | tf_op jit(solution)/shard_map/ppermute | solution.py:34
  73.1 1.5 %collective-permute-start.1 = (bf16[208,640]{1,0:T(8,128)(2,1)S(1)}, bf16[208,640]{1,0:T(8,128)(2,1)S(1)}, u32[]{:S(2)}, u32[]{:S(2)}) collective-permute-start(bf16[208,640]{1,0:T(8,128)(2,1)S(1)} %slice.73), channel_id=1, source_target_pairs={{0,64},{64,128},{128,192},{192,0},{1,65},{65,129},{129,193},{193,1... | collective-permute-start | bytes 798728 | tf_op jit(solution)/shard_map/ppermute | solution.py:34
  74.6 0.1 pad_add_fusion.at_ref
  74.7 1.1 copy-done.10
  75.8 1.1 copy-done.12
  76.9 5.7 %shard_map.109 = (f32[2,432,528]{2,1,0:T(8,128)S(1)}, bf16[528,640]{1,0:T(8,128)(2,1)S(1)}) custom-call(s32[4]{0:T(128)S(1)} %pad_add_fusion.at_ref, bf16[128,2560]{1,0:T(8,128)(2,1)S(1)} %bitcast.31, bf16[128,2560]{1,0:T(8,128)(2,1)S(1)} %collective-permute-done.4.t1, bf16[128,2560]{1,0:T(8,128)(2,1)S(1)} %copy-done.10, bf16[128,2560]{1,0:T(8,128)(2,1)S(1)} %copy-done.12, ...), custom_call_target="tpu_custom_call" | custom-call | flops 1857945600 | bytes 9000000 | tf_op jit(solution)/shard_map/pallas_call | solution.py:300
  82.6 0.1 collective-permute-start.12
  82.7 0.5 collective-permute-start.11
  83.2 1.4 %collective-permute-done.11.refs_1_ = bf16[208,640]{1,0:T(8,128)(2,1)S(1)} collective-permute-done((bf16[208,640]{1,0:T(8,128)(2,1)S(1)}, bf16[208,640]{1,0:T(8,128)(2,1)S(1)}, u32[]{:S(2)}, u32[]{:S(2)}) %collective-permute-start.11) | collective-permute-done | bytes 266272 | tf_op jit(solution)/shard_map/ppermute | solution.py:38
  84.7 0.0 copy-start.5
  84.7 0.0 copy-start.6
  84.7 1.9 %shard_map.110 = (bf16[928,128]{1,0:T(8,128)(2,1)S(1)}, bf16[928,128]{1,0:T(8,128)(2,1)S(1)}, bf16[928,128]{1,0:T(8,128)(2,1)S(1)}, bf16[928,128]{1,0:T(8,128)(2,1)S(1)}) custom-call(s32[4]{0:T(128)S(1)} %pad_add_fusion.at_ref, f32[2,432,528]{2,1,0:T(8,128)S(1)} %get-tuple-element.23.part_ref, bf16[528,640]{1,0:T(8,128)(2,1)S(1)} %get-tuple-element.24.far_ref, ...), custom_call_target="tpu_custom_call" | custom-call | flops 619315200 | bytes 5000000 | tf_op jit(solution)/shard_map/pallas_call | solution.py:313
  86.7 1.3 collective-permute-start.13
  88.0 2.6 %collective-permute-start.14 = (bf16[928,128]{1,0:T(8,128)(2,1)S(1)}, bf16[928,128]{1,0:T(8,128)(2,1)S(1)}, u32[]{:S(2)}, u32[]{:S(2)}) collective-permute-start(bf16[928,128]{1,0:T(8,128)(2,1)S(1)} %get-tuple-element.29), channel_id=1, source_target_pairs={{0,6},{2,0},{4,2},{6,4},{1,7},{3,1},{5,3},{7,5},{8,14},{10,8},{12,... | collective-permute-start | bytes 712712 | tf_op jit(solution)/shard_map/ppermute | solution.py:34
  90.5 1.4 %collective-permute-start.15 = (bf16[928,128]{1,0:T(8,128)(2,1)S(1)}, bf16[928,128]{1,0:T(8,128)(2,1)S(1)}, u32[]{:S(2)}, u32[]{:S(2)}) collective-permute-start(bf16[928,128]{1,0:T(8,128)(2,1)S(1)} %get-tuple-element.34), channel_id=1, source_target_pairs={{0,4},{2,6},{4,0},{6,2},{1,5},{3,7},{5,1},{7,3},{8,12},{10,14},{12... | collective-permute-start | bytes 712712 | tf_op jit(solution)/shard_map/ppermute | solution.py:34
  91.9 1.5 %shard_map.111 = (f32[27,128,128]{2,1,0:T(8,128)S(1)}, f32[4,128,128]{2,1,0:T(8,128)S(1)}) custom-call(s32[4]{0:T(128)S(1)} %pad_add_fusion.at_ref, bf16[128,3456]{1,0:T(8,128)(2,1)S(1)} %bitcast.15, s32[1,128]{1,0:T(1,128)S(1)} %copy-done.13, bf16[16,2560]{1,0:T(8,128)(2,1)S(1)} %collective-permute-done.7.ahead.ahead_ref), custom_call_target="tpu_custom_call" | custom-call | bytes 2700000 | tf_op jit(solution)/shard_map/pallas_call | solution.py:321
  93.5 3.1 %collective-permute-done.13.refs_1_ = bf16[928,128]{1,0:T(8,128)(2,1)S(1)} collective-permute-done((bf16[928,128]{1,0:T(8,128)(2,1)S(1)}, bf16[928,128]{1,0:T(8,128)(2,1)S(1)}, u32[]{:S(2)}, u32[]{:S(2)}) %collective-permute-start.13) | collective-permute-done | bytes 237600 | tf_op jit(solution)/shard_map/ppermute | solution.py:34
  96.5 4.4 %collective-permute-done.14.refs_2_ = bf16[928,128]{1,0:T(8,128)(2,1)S(1)} collective-permute-done((bf16[928,128]{1,0:T(8,128)(2,1)S(1)}, bf16[928,128]{1,0:T(8,128)(2,1)S(1)}, u32[]{:S(2)}, u32[]{:S(2)}) %collective-permute-start.14) | collective-permute-done | bytes 237600 | tf_op jit(solution)/shard_map/ppermute | solution.py:34
  101.0 7.3 %shard_map.112 = (f32[27,128,128]{2,1,0:T(8,128)S(1)}, f32[27,128,128]{2,1,0:T(8,128)S(1)}, f32[2,3456]{1,0:T(2,128)S(1)}) custom-call(s32[4]{0:T(128)S(1)} %pad_add_fusion.at_ref, bf16[928,128]{1,0:T(8,128)(2,1)S(1)} %get-tuple-element.27.refs_0_, bf16[928,128]{1,0:T(8,128)(2,1)S(1)} %collective-permute-done.13.refs_1_, ...), custom_call_target="tpu_custom_call" | custom-call | flops 167772160 | bytes 20000000 | tf_op jit(solution)/shard_map/pallas_call | solution.py:360
  108.3 4.4 %shard_map.113 = (f32[8,128,128]{2,1,0:T(8,128)S(1)}, f32[8,128,128]{2,1,0:T(8,128)S(1)}, f32[2,3456]{1,0:T(2,128)S(1)}) custom-call(s32[4]{0:T(128)S(1)} %pad_add_fusion.at_ref, bf16[928,128]{1,0:T(8,128)(2,1)S(1)} %get-tuple-element.27.refs_0_, bf16[928,128]{1,0:T(8,128)(2,1)S(1)} %collective-permute-done.13.refs_1_, ...), custom_call_target="tpu_custom_call" | custom-call | flops 67108864 | bytes 8000000 | tf_op jit(solution)/shard_map/pallas_call | solution.py:368
  112.7 0.1 collective-permute-start.16
  112.8 6.0 %collective-permute-done.16 = f32[2,3456]{1,0:T(2,128)S(1)} collective-permute-done((f32[2,3456]{1,0:T(2,128)S(1)}, f32[2,3456]{1,0:T(2,128)S(1)}, u32[]{:S(2)}, u32[]{:S(2)}) %collective-permute-start.16) | collective-permute-done | bytes 27680 | tf_op jit(solution)/shard_map/ppermute | solution.py:34
  118.8 0.1 collective-permute-start.17
  118.9 0.1 collective-permute-start.18
  119.0 5.7 %collective-permute-start.19 = (f32[2,3456]{1,0:T(2,128)S(1)}, f32[2,3456]{1,0:T(2,128)S(1)}, u32[]{:S(2)}, u32[]{:S(2)}) collective-permute-start(f32[2,3456]{1,0:T(2,128)S(1)} %pad_maximum_fusion), channel_id=1, source_target_pairs={{0,40},{8,48},{16,56},{24,64},{32,72},{40,80},{48,88},{56,96},{64,... | collective-permute-start | bytes 82952 | tf_op jit(solution)/shard_map/ppermute | solution.py:34
  124.7 0.9 collective-permute-start.20
  125.5 1.2 collective-permute-done.18
  126.8 2.7 %collective-permute-done.20 = f32[2,3456]{1,0:T(2,128)S(1)} collective-permute-done((f32[2,3456]{1,0:T(2,128)S(1)}, f32[2,3456]{1,0:T(2,128)S(1)}, u32[]{:S(2)}, u32[]{:S(2)}) %collective-permute-start.20) | collective-permute-done | bytes 27680 | tf_op jit(solution)/shard_map/ppermute | solution.py:34
  129.4 0.1 slice_add_fusion.in_ref
  129.5 2.0 %shard_map.114 = bf16[128,3456]{1,0:T(8,128)(2,1)} custom-call(s32[4]{0:T(128)S(1)} %pad_add_fusion.at_ref, f32[27,128,128]{2,1,0:T(8,128)S(1)} %get-tuple-element.32.state_ref, f32[27,128,128]{2,1,0:T(8,128)S(1)} %get-tuple-element.33.prod_ref, f32[8,128,128]{2,1,0:T(8,128)S(1)} %get-tuple-element.36.far_state_ref, ...), custom_call_target="tpu_custom_call" | custom-call | bytes 4400000 | tf_op jit(solution)/shard_map/pallas_call | solution.py:380
  (45 shorter events, 0.3 us)
Async XLA Ops:
  0.0 10.3 %copy-start.8 = (bf16[1,128,2560]{2,1,0:T(8,128)(2,1)S(1)}, bf16[1,128,2560]{2,1,0:T(8,128)(2,1)}, u32[]{:S(2)}) copy-start(bf16[1,128,2560]{2,1,0:T(8,128)(2,1)} %param.11) | copy-start | bytes 1966084
  0.0 37.8 %copy-start.13 = (s32[1,128]{1,0:T(1,128)S(1)}, s32[1,128]{1,0:T(1,128)}, u32[]{:S(2)}) copy-start(s32[1,128]{1,0:T(1,128)} %ids_ref.1) | copy-start | bytes 1540
  1.8 28.8 %all-to-all-start = ((bf16[8,80,432]{2,1,0:T(8,128)(2,1)}), bf16[8,80,432]{2,1,0:T(8,128)(2,1)S(1)}, u32[]{:S(2)}, u32[]{:S(2)}) async-start(bf16[8,80,432]{2,1,0:T(8,128)(2,1)} %broadcast_in_dim.4), calls=%async_computation | async-start | bytes 1310720 | tf_op jit(solution)/shard_map/all_to_all | solution.py:287
  10.3 27.5 %collective-permute-start.4 = (bf16[128,2560]{1,0:T(8,128)(2,1)S(1)}, bf16[128,2560]{1,0:T(8,128)(2,1)S(1)}, u32[]{:S(2)}, u32[]{:S(2)}) collective-permute-start(bf16[128,2560]{1,0:T(8,128)(2,1)S(1)} %bitcast.28), channel_id=1, source_target_pairs={{0,2},{2,4},{4,6},{6,0},{1,3},{3,5},{5,7},{7,1},{8,10},{10,12},{12... | collective-permute-start | bytes 1966088 | tf_op jit(solution)/shard_map/ppermute | solution.py:34
  30.9 15.7 %collective-permute-start.2 = (bf16[432,640]{1,0:T(8,128)(2,1)S(1)}, bf16[432,640]{1,0:T(8,128)(2,1)S(1)}, u32[]{:S(2)}, u32[]{:S(2)}) collective-permute-start(bf16[432,640]{1,0:T(8,128)(2,1)S(1)} %bitcast.16), channel_id=1, source_target_pairs={{0,192},{64,0},{128,64},{192,128},{1,193},{65,1},{129,65},{193,129... | collective-permute-start | bytes 1658888 | tf_op jit(solution)/shard_map/ppermute | solution.py:34
  31.7 14.9 %collective-permute-start = (bf16[432,640]{1,0:T(8,128)(2,1)S(1)}, bf16[432,640]{1,0:T(8,128)(2,1)S(1)}, u32[]{:S(2)}, u32[]{:S(2)}) collective-permute-start(bf16[432,640]{1,0:T(8,128)(2,1)S(1)} %bitcast.17), channel_id=1, source_target_pairs={{0,64},{64,128},{128,192},{192,0},{1,65},{65,129},{129,193},{193,1... | collective-permute-start | bytes 1658888 | tf_op jit(solution)/shard_map/ppermute | solution.py:34
  34.2 30.4 %collective-permute-start.5 = (bf16[128,2560]{1,0:T(8,128)(2,1)S(1)}, bf16[128,2560]{1,0:T(8,128)(2,1)S(1)}, u32[]{:S(2)}, u32[]{:S(2)}) collective-permute-start(bf16[128,2560]{1,0:T(8,128)(2,1)S(1)} %bitcast.29), channel_id=1, source_target_pairs={{0,6},{2,0},{4,2},{6,4},{1,7},{3,1},{5,3},{7,5},{8,14},{10,8},{12,... | collective-permute-start | bytes 1966088 | tf_op jit(solution)/shard_map/ppermute | solution.py:34
  37.0 28.5 %collective-permute-start.6 = (bf16[128,2560]{1,0:T(8,128)(2,1)S(1)}, bf16[128,2560]{1,0:T(8,128)(2,1)S(1)}, u32[]{:S(2)}, u32[]{:S(2)}) collective-permute-start(bf16[128,2560]{1,0:T(8,128)(2,1)S(1)} %bitcast.30), channel_id=1, source_target_pairs={{0,4},{2,6},{4,0},{6,2},{1,5},{3,7},{5,1},{7,3},{8,12},{10,14},{12... | collective-permute-start | bytes 1966088 | tf_op jit(solution)/shard_map/ppermute | solution.py:34
  37.8 36.9 %collective-permute-start.8 = (bf16[432,640]{1,0:T(8,128)(2,1)S(1)}, bf16[432,640]{1,0:T(8,128)(2,1)}, u32[]{:S(2)}, u32[]{:S(2)}) collective-permute-start(bf16[432,640]{1,0:T(8,128)(2,1)S(1)} %bitcast.18), channel_id=1, source_target_pairs={{0,1},{1,0},{2,3},{3,2},{4,5},{5,4},{6,7},{7,6},{8,9},{9,8},{10,11... | collective-permute-start | bytes 1658888 | tf_op jit(solution)/shard_map/ppermute | solution.py:38
  46.7 28.0 %collective-permute-start.10 = (bf16[432,640]{1,0:T(8,128)(2,1)S(1)}, bf16[432,640]{1,0:T(8,128)(2,1)}, u32[]{:S(2)}, u32[]{:S(2)}) collective-permute-start(bf16[432,640]{1,0:T(8,128)(2,1)S(1)} %collective-permute-done.2.refs_4_), channel_id=1, source_target_pairs={{0,1},{1,0},{2,3},{3,2},{4,5},{5,4},{6,7},{7,6},{8,9},{9,8},{10,11... | collective-permute-start | bytes 1658888 | tf_op jit(solution)/shard_map/ppermute | solution.py:38
  46.7 28.0 %collective-permute-start.9 = (bf16[432,640]{1,0:T(8,128)(2,1)S(1)}, bf16[432,640]{1,0:T(8,128)(2,1)}, u32[]{:S(2)}, u32[]{:S(2)}) collective-permute-start(bf16[432,640]{1,0:T(8,128)(2,1)S(1)} %collective-permute-done.refs_2_), channel_id=1, source_target_pairs={{0,1},{1,0},{2,3},{3,2},{4,5},{5,4},{6,7},{7,6},{8,9},{9,8},{10,11... | collective-permute-start | bytes 1658888 | tf_op jit(solution)/shard_map/ppermute | solution.py:38
  64.7 0.8 copy-start.9
  65.6 0.8 copy-start.11
  66.5 6.6 %collective-permute-start.7 = (bf16[16,2560]{1,0:T(8,128)(2,1)S(1)}, bf16[16,2560]{1,0:T(8,128)(2,1)S(1)}, u32[]{:S(2)}, u32[]{:S(2)}) collective-permute-start(bf16[16,2560]{1,0:T(8,128)(2,1)S(1)} %concatenate.6), channel_id=1, source_target_pairs={{0,8},{8,16},{16,24},{24,32},{32,40},{40,48},{48,56},{56,64},{64,7... | collective-permute-start | bytes 245768 | tf_op jit(solution)/shard_map/ppermute | solution.py:34
  66.6 16.0 %collective-permute-start.3 = (bf16[224,640]{1,0:T(8,128)(2,1)S(1)}, bf16[224,640]{1,0:T(8,128)(2,1)S(1)}, u32[]{:S(2)}, u32[]{:S(2)}) collective-permute-start(bf16[224,640]{1,0:T(8,128)(2,1)S(1)} %slice.74), channel_id=1, source_target_pairs={{0,192},{64,0},{128,64},{192,128},{1,193},{65,1},{129,65},{193,129... | collective-permute-start | bytes 860168 | tf_op jit(solution)/shard_map/ppermute | solution.py:34
  73.1 9.5 %collective-permute-start.1 = (bf16[208,640]{1,0:T(8,128)(2,1)S(1)}, bf16[208,640]{1,0:T(8,128)(2,1)S(1)}, u32[]{:S(2)}, u32[]{:S(2)}) collective-permute-start(bf16[208,640]{1,0:T(8,128)(2,1)S(1)} %slice.73), channel_id=1, source_target_pairs={{0,64},{64,128},{128,192},{192,0},{1,65},{65,129},{129,193},{193,1... | collective-permute-start | bytes 798728 | tf_op jit(solution)/shard_map/ppermute | solution.py:34
  74.7 1.1 copy-start.10
  75.8 1.1 copy-start.12
  82.6 2.0 %collective-permute-start.12 = (bf16[224,640]{1,0:T(8,128)(2,1)S(1)}, bf16[224,640]{1,0:T(8,128)(2,1)S(1)}, u32[]{:S(2)}, u32[]{:S(2)}) collective-permute-start(bf16[224,640]{1,0:T(8,128)(2,1)S(1)} %collective-permute-done.3.refs_2_), channel_id=1, source_target_pairs={{0,1},{1,0},{2,3},{3,2},{4,5},{5,4},{6,7},{7,6},{8,9},{9,8},{10,11... | collective-permute-start | bytes 860168 | tf_op jit(solution)/shard_map/ppermute | solution.py:38
  82.7 1.9 %collective-permute-start.11 = (bf16[208,640]{1,0:T(8,128)(2,1)S(1)}, bf16[208,640]{1,0:T(8,128)(2,1)S(1)}, u32[]{:S(2)}, u32[]{:S(2)}) collective-permute-start(bf16[208,640]{1,0:T(8,128)(2,1)S(1)} %collective-permute-done.1.refs_0_), channel_id=1, source_target_pairs={{0,1},{1,0},{2,3},{3,2},{4,5},{5,4},{6,7},{7,6},{8,9},{9,8},{10,11... | collective-permute-start | bytes 798728 | tf_op jit(solution)/shard_map/ppermute | solution.py:38
  84.7 7.2 %copy-start.2 = (bf16[1,128,3456]{2,1,0:T(8,128)(2,1)S(1)}, bf16[1,128,3456]{2,1,0:T(8,128)(2,1)}, u32[]{:S(2)}) copy-start(bf16[1,128,3456]{2,1,0:T(8,128)(2,1)} %param.12) | copy-start | bytes 2654212
  84.7 16.3 %copy-start = (bf16[27,128,128]{2,1,0:T(8,128)(2,1)S(1)}, bf16[27,128,128]{2,1,0:T(8,128)(2,1)}, u32[]{:S(2)}) copy-start(bf16[27,128,128]{2,1,0:T(8,128)(2,1)} %refs_11_.3) | copy-start | bytes 2654212
  84.7 16.3 %copy-start.1 = (bf16[27,128,128]{2,1,0:T(8,128)(2,1)S(1)}, bf16[27,128,128]{2,1,0:T(8,128)(2,1)}, u32[]{:S(2)}) copy-start(bf16[27,128,128]{2,1,0:T(8,128)(2,1)} %refs_12_.1) | copy-start | bytes 2654212
  84.7 16.3 %copy-start.3 = (f32[4,3456]{1,0:T(4,128)S(1)}, f32[4,3456]{1,0:T(4,128)}, u32[]{:S(2)}) copy-start(f32[4,3456]{1,0:T(4,128)} %refs_6_.1) | copy-start | bytes 165892
  84.7 16.3 %copy-start.4 = (f32[3456]{0:T(1024)S(1)}, f32[3456]{0:T(1024)}, u32[]{:S(2)}) copy-start(f32[3456]{0:T(1024)} %param.16) | copy-start | bytes 41476
  84.7 16.3 %copy-start.5 = (f32[3456]{0:T(1024)S(1)}, f32[3456]{0:T(1024)}, u32[]{:S(2)}) copy-start(f32[3456]{0:T(1024)} %param.19) | copy-start | bytes 41476
  84.7 16.3 %copy-start.6 = (f32[3456]{0:T(1024)S(1)}, f32[3456]{0:T(1024)}, u32[]{:S(2)}) copy-start(f32[3456]{0:T(1024)} %param.20) | copy-start | bytes 41476
  84.7 16.3 %copy-start.7 = (f32[3456]{0:T(1024)S(1)}, f32[3456]{0:T(1024)}, u32[]{:S(2)}) copy-start(f32[3456]{0:T(1024)} %param.21) | copy-start | bytes 41476
  86.7 9.9 %collective-permute-start.13 = (bf16[928,128]{1,0:T(8,128)(2,1)S(1)}, bf16[928,128]{1,0:T(8,128)(2,1)S(1)}, u32[]{:S(2)}, u32[]{:S(2)}) collective-permute-start(bf16[928,128]{1,0:T(8,128)(2,1)S(1)} %get-tuple-element.28), channel_id=1, source_target_pairs={{0,2},{2,4},{4,6},{6,0},{1,3},{3,5},{5,7},{7,1},{8,10},{10,12},{12... | collective-permute-start | bytes 712712 | tf_op jit(solution)/shard_map/ppermute | solution.py:34
  88.0 13.0 %collective-permute-start.14 = (bf16[928,128]{1,0:T(8,128)(2,1)S(1)}, bf16[928,128]{1,0:T(8,128)(2,1)S(1)}, u32[]{:S(2)}, u32[]{:S(2)}) collective-permute-start(bf16[928,128]{1,0:T(8,128)(2,1)S(1)} %get-tuple-element.29), channel_id=1, source_target_pairs={{0,6},{2,0},{4,2},{6,4},{1,7},{3,1},{5,3},{7,5},{8,14},{10,8},{12,... | collective-permute-start | bytes 712712 | tf_op jit(solution)/shard_map/ppermute | solution.py:34
  90.5 17.8 %collective-permute-start.15 = (bf16[928,128]{1,0:T(8,128)(2,1)S(1)}, bf16[928,128]{1,0:T(8,128)(2,1)S(1)}, u32[]{:S(2)}, u32[]{:S(2)}) collective-permute-start(bf16[928,128]{1,0:T(8,128)(2,1)S(1)} %get-tuple-element.34), channel_id=1, source_target_pairs={{0,4},{2,6},{4,0},{6,2},{1,5},{3,7},{5,1},{7,3},{8,12},{10,14},{12... | collective-permute-start | bytes 712712 | tf_op jit(solution)/shard_map/ppermute | solution.py:34
  112.7 6.0 %collective-permute-start.16 = (f32[2,3456]{1,0:T(2,128)S(1)}, f32[2,3456]{1,0:T(2,128)S(1)}, u32[]{:S(2)}, u32[]{:S(2)}) collective-permute-start(f32[2,3456]{1,0:T(2,128)S(1)} %get-tuple-element.38), channel_id=1, source_target_pairs={{0,8},{8,16},{16,24},{24,32},{32,40},{40,48},{48,56},{56,64},{64,7... | collective-permute-start | bytes 82952 | tf_op jit(solution)/shard_map/ppermute | solution.py:34
  118.8 6.7 %collective-permute-start.17 = (f32[2,3456]{1,0:T(2,128)S(1)}, f32[2,3456]{1,0:T(2,128)S(1)}, u32[]{:S(2)}, u32[]{:S(2)}) collective-permute-start(f32[2,3456]{1,0:T(2,128)S(1)} %pad_maximum_fusion), channel_id=1, source_target_pairs={{0,8},{8,16},{16,24},{24,32},{32,40},{40,48},{48,56},{56,64},{64,7... | collective-permute-start | bytes 82952 | tf_op jit(solution)/shard_map/ppermute | solution.py:34
  118.9 7.8 %collective-permute-start.18 = (f32[2,3456]{1,0:T(2,128)S(1)}, f32[2,3456]{1,0:T(2,128)S(1)}, u32[]{:S(2)}, u32[]{:S(2)}) collective-permute-start(f32[2,3456]{1,0:T(2,128)S(1)} %pad_maximum_fusion), channel_id=1, source_target_pairs={{0,24},{8,32},{16,40},{24,48},{32,56},{40,64},{48,72},{56,80},{64,... | collective-permute-start | bytes 82952 | tf_op jit(solution)/shard_map/ppermute | solution.py:34
  119.0 7.8 %collective-permute-start.19 = (f32[2,3456]{1,0:T(2,128)S(1)}, f32[2,3456]{1,0:T(2,128)S(1)}, u32[]{:S(2)}, u32[]{:S(2)}) collective-permute-start(f32[2,3456]{1,0:T(2,128)S(1)} %pad_maximum_fusion), channel_id=1, source_target_pairs={{0,40},{8,48},{16,56},{24,64},{32,72},{40,80},{48,88},{56,96},{64,... | collective-permute-start | bytes 82952 | tf_op jit(solution)/shard_map/ppermute | solution.py:34
  124.7 4.8 %collective-permute-start.20 = (f32[2,3456]{1,0:T(2,128)S(1)}, f32[2,3456]{1,0:T(2,128)S(1)}, u32[]{:S(2)}, u32[]{:S(2)}) collective-permute-start(f32[2,3456]{1,0:T(2,128)S(1)} %pad_maximum_fusion), channel_id=1, source_target_pairs={{0,56},{8,64},{16,72},{24,80},{32,88},{40,96},{48,104},{56,112},{6... | collective-permute-start | bytes 82952 | tf_op jit(solution)/shard_map/ppermute | solution.py:34

commit v5 on v4

--- a/solution.py
+++ b/solution.py
@@ -25,6 +25,7 @@
 PACK = COLS + 32
 CUT = 208
 AHEAD = 16
+SIDE = 4
 NEAR, FAR = 20, 8
 ROWS = 4 * LENGTH + AHEAD
 
@@ -76,42 +77,41 @@
     )
 
 
-def project_kernel(at_ref, t0, t1, t2, t3, ahead, *refs):
-    weights, (part_ref, far_ref, rows_ref, sems) = refs[:6], refs[6:]
+def project_kernel(at_ref, *refs):
+    tokens, weights, (part_ref, far_ref, rows_ref, sems) = refs[:12], refs[12:15], refs[15:]
     y = at_ref[2]
-    pairs = [
-        (ref, rows_ref.at[pl.ds(i * LENGTH, LENGTH)]) for i, ref in enumerate((t0, t1, t2, t3))
-    ] + [(ahead, rows_ref.at[pl.ds(4 * LENGTH, AHEAD)])]
+    pairs, start = [], 0
+    for ref in tokens:
+        pairs.append((ref, rows_ref.at[pl.ds(start, ref.shape[0])]))
+        start += ref.shape[0]
     for copy in copies(pairs, sems):
         copy.wait()
     for half in range(2):
         total = None
-        for j, back in enumerate((0, 3, 1)):
-            start = pl.multiple_of(lax.rem(y + back, 4) * 640, 128)
-            part = across(weights[2 * j + half][...], rows_ref[:, pl.ds(start, 640)])
+        for w_ref, back in zip(weights, (0, 3, 1)):
+            at = pl.ds(pl.multiple_of(lax.rem(y + back, 4) * 640, 128), 640)
+            part = across(w_ref[...], rows_ref[half * ROWS : (half + 1) * ROWS, at])
             total = part if total is None else total + part
         part_ref[half] = total
     far_ref[...] = rows_ref[:, pl.ds(pl.multiple_of(lax.rem(y + 2, 4) * 640, 128), 640)]
 
 
-def pack_kernel(at_ref, part_ref, far_ref, *refs):
-    weights, outs, (all_ref, wide_ref) = refs[:4], refs[4:8], refs[8:]
-    c = at_ref[1]
+def pack_kernel(part_ref, far_ref, w0_ref, w1_ref, *refs):
+    outs, (all_ref, wide_ref) = refs[:4], refs[4:]
+    all_ref[0:CUT, :] = w0_ref[...]
+    all_ref[CUT:COLS, :] = w1_ref[...]
     for half in range(2):
-        all_ref[0:CUT, :] = weights[half][...]
-        all_ref[CUT:COLS, :] = weights[2 + half][...]
-        total = part_ref[half] + across(all_ref[...], far_ref[...])
-        place = c if half == 0 else 1 - c
-        main = pl.ds(pl.multiple_of(place * COLS, 16), COLS)
+        total = part_ref[half] + across(all_ref[...], far_ref[half * ROWS : (half + 1) * ROWS, :])
         wide_ref[0:COLS, 0:AHEAD] = total[:, 4 * LENGTH :]
         turned = [wide_ref[j * 128 : (j + 1) * 128, :].T for j in range(4)]
+        top = half * PACK
         for i, out_ref in enumerate(outs):
-            out_ref[main, :] = total[:, i * LENGTH : (i + 1) * LENGTH].astype(BF16)
+            out_ref[top : top + COLS, :] = total[:, i * LENGTH : (i + 1) * LENGTH].astype(BF16)
             group = [t[8 * (i // 2) : 8 * (i // 2) + 8, :] for t in turned]
             if i % 2 == 0:
                 group = [pltpu.roll(g, 4, 0) for g in group]
             for j in range(2):
-                rest = pl.ds(pl.multiple_of(2 * COLS + 32 * place + 16 * j, 16), 16)
+                rest = slice(top + COLS + 16 * j, top + COLS + 16 * j + 16)
                 out_ref[rest, :] = jnp.concatenate(group[2 * j : 2 * j + 2], axis=0).astype(BF16)
 
 
@@ -132,18 +132,19 @@
         gate_i_ref,
     ) = refs
     x_scr, main_ref, pack_ref, ahead_ref, sems = scratch
-    x = at_ref[0]
+    x, c = at_ref[0], at_ref[1]
     pairs = []
-    for back, ref in zip((0, 1, 3, 2), got):
-        block = lax.rem(x + 4 - back, 4)
-        rows = pl.ds(pl.multiple_of(block * (2 * COLS), 16), 2 * COLS)
-        pairs.append((ref.at[pl.ds(0, 2 * COLS)], main_ref.at[rows]))
-        pairs.append((ref.at[pl.ds(2 * COLS, 64)], pack_ref.at[block]))
+    for n, ref in enumerate(got):
+        place = 2 * lax.rem(x + 4 - (0, 1, 3, 2)[n // 2], 4) + (c if n % 2 == 0 else 1 - c)
+        top = (n % 2) * PACK
+        rows = pl.ds(pl.multiple_of(place * COLS, 16), COLS)
+        pairs.append((ref.at[pl.ds(top, COLS)], main_ref.at[rows]))
+        pairs.append((ref.at[pl.ds(top + COLS, 32)], pack_ref.at[place]))
     for copy in copies(pairs, sems):
         copy.wait()
     ahead = []
     for f in range(8):
-        packed = pack_ref[f // 2, 32 * (f % 2) : 32 * (f % 2) + 32, :].astype(F32)
+        packed = pack_ref[f].astype(F32)
         ahead += [packed[8 * j : 8 * j + 8, : min(128, COLS - 128 * j)] for j in range(4)]
     ahead_ref[...] = jnp.concatenate(ahead, axis=1)
 
@@ -208,24 +209,21 @@
             state_ref[out, at, :] = (states[k] + prods[k] * in_state) * gelu
             prod_ref[out, at, :] = (prods[k] * in_prod) * gelu
 
-    def pair(i, carry):
-        for slot in range(2):
-            head(2 * i + slot, slot)
+    def several(i, carry):
+        for slot in range(SIDE):
+            head(SIDE * i + slot, slot)
         return carry
 
-    lax.fori_loop(0, (FAR if far else NEAR) // 2, pair, 0)
+    lax.fori_loop(0, (FAR if far else NEAR) // SIDE, several, 0)
 
 
 def near_kernel(at_ref, *refs):
-    state_ref, prod_ref, end_ref = refs[12:15]
-    recur(at_ref, refs[:3], refs[3:12], False, state_ref, prod_ref, end_ref, refs[15:])
+    recur(at_ref, refs[:6], refs[6:15], False, *refs[15:18], refs[18:])
 
 
 def far_kernel(at_ref, *refs):
-    ends_ref = refs[13]
-    state_ref, prod_ref, end_ref = refs[14:17]
-    end_ref[...] = ends_ref[...]
-    recur(at_ref, refs[:4], refs[4:13], True, state_ref, prod_ref, end_ref, refs[17:])
+    refs[20][...] = refs[17][...]
+    recur(at_ref, refs[:8], refs[8:17], True, *refs[18:21], refs[21:])
 
 
 def finish_kernel(at_ref, state_ref, prod_ref, far_state_ref, far_prod_ref, in_ref, out_ref):
@@ -285,39 +283,42 @@
 
     copied = jnp.broadcast_to(in_weight[None], (8,) + in_weight.shape)
     column = lax.all_to_all(copied, "z", 0, 0, tiled=True).reshape(-1, COLS).T
-    streams = [own, shift(own, "x", 1), shift(own, "x", -1), shift(own, "x", 2)]
+    one_back, one_ahead = shift(own, "x", 1), shift(own, "x", -1)
+    column, one_back, one_ahead = lax.optimization_barrier((column, one_back, one_ahead))
+    upper = shift(one_back[: LENGTH // 2], "x", 1)
+    lower = shift(one_ahead[LENGTH // 2 :], "x", -1)
+    streams = [own, one_back, one_ahead, upper, lower]
     from_back = shift(column, "y", 1)
     from_ahead = shift(column, "y", -1)
-    near = [column, flip(column), from_back, flip(from_back), from_ahead, flip(from_ahead)]
     first = shift(from_back[:CUT], "y", 1)
     second = shift(from_ahead[CUT:], "y", -1)
 
     documents = jnp.pad(segment_ids.astype(BF16), ((0, 0), (0, DEPTH - LENGTH)))
     ahead = shift(
-        jnp.concatenate([documents, own[-3:]] + [t[-4:] for t in streams[1:]], axis=0), ctx, 1
-    )
-
+        jnp.concatenate([documents, own[-3:]] + [t[-4:] for t in (one_back, one_ahead, lower)], axis=0), ctx, 1
+    )
+
+    streams.append(ahead)
+    streams += [flip(t) for t in streams]
     part, rows_far = call(
         project_kernel,
         (
             jax.ShapeDtypeStruct((2, COLS, ROWS), F32),
-            jax.ShapeDtypeStruct((ROWS, 640), BF16),
+            jax.ShapeDtypeStruct((2 * ROWS, 640), BF16),
         ),
-        [SMEM] + [ANY] * 5 + [VMEM] * 6,
-        [pltpu.VMEM((ROWS, DEPTH), BF16), pltpu.SemaphoreType.DMA((5,))],
-        flops=2 * 560 * 1920 * 864,
+        [SMEM] + [ANY] * 12 + [VMEM] * 3,
+        [pltpu.VMEM((2 * ROWS, DEPTH), BF16), pltpu.SemaphoreType.DMA((12,))],
+        flops=2 * 1056 * 1920 * 432,
         moved=9_000_000,
-    )(at, *streams, ahead, *near)
-    first, second, part = lax.optimization_barrier((first, second, part))
-    far = [first, flip(first), second, flip(second)]
+    )(at, *streams, column, from_back, from_ahead)
     sent = call(
         pack_kernel,
         [jax.ShapeDtypeStruct((2 * PACK, 128), BF16)] * 4,
-        [SMEM] + [VMEM] * 6,
+        [VMEM] * 4,
         [pltpu.VMEM((COLS, 640), BF16), pltpu.VMEM((512, 128), F32)],
-        flops=2 * 560 * 640 * 864,
+        flops=2 * 1056 * 640 * 432,
         moved=5_000_000,
-    )(at, part, rows_far, *far)
+    )(part, rows_far, first, second)
     gelu, masks = call(
         prepare_kernel,
         (
@@ -334,6 +335,7 @@
         shift(sent[1], "x", -1),
         shift(sent[3], "x", 2),
     ]
+    near = [v for block in got[:3] for v in (block, flip(block))]
     shared = (
         masks,
         gelu,
@@ -343,11 +345,11 @@
         gate_i,
     )
     scratch = [
-        pltpu.VMEM((2, LENGTH + HALO, HEAD), F32),
+        pltpu.VMEM((SIDE, LENGTH + HALO, HEAD), F32),
         pltpu.VMEM((WIDTH, LENGTH), BF16),
-        pltpu.VMEM((4, 64, 128), BF16),
+        pltpu.VMEM((8, 32, 128), BF16),
         pltpu.VMEM((HALO, WIDTH), F32),
-        pltpu.SemaphoreType.DMA((8,)),
+        pltpu.SemaphoreType.DMA((16,)),
     ]
 
     def walked(heads):
@@ -360,19 +362,20 @@
     states, prods, ends = call(
         near_kernel,
         walked(HEADS),
-        [SMEM] + [ANY] * 3 + [VMEM] * 9,
+        [SMEM] + [ANY] * 6 + [VMEM] * 9,
         scratch,
         flops=2 * 128 * 2560 * 256,
         moved=20_000_000,
-    )(at, *got[:3], *shared)
+    )(at, *near, *shared)
+    last, ends = lax.optimization_barrier((got[3], ends))
     far_states, far_prods, ends = call(
         far_kernel,
         walked(FAR),
-        [SMEM] + [ANY] * 4 + [VMEM] * 10,
+        [SMEM] + [ANY] * 8 + [VMEM] * 10,
         scratch,
         flops=2 * 128 * 1024 * 256,
         moved=8_000_000,
-    )(at, *got, *shared, ends)
+    )(at, *near, last, flip(last), *shared, ends)
 
     two = joined(shift(ends, ctx, 1), ends)
     pairs = [shift(two, ctx, by) for by in (7, 5, 3, 1)]

time: 133 us -> 120 us (0.902)
  waiting for transfers between devices: 70.1 us -> 55 us
  starting transfers between devices: 31.8 us -> 35.9 us
  local copies, waits for them, and re-layouts: 6.23 us -> 4.57 us
    ppermute x16 -> x17, waiting for transfers between devices: 49.9 us -> 35.3 us  [shift(): lax.ppermute(value, axis, [(i, (i + by) % count) for i in range(count)])]
    unnamed x28 -> x18, local copies, waits for them, and re-layouts: 3.89 us -> 0.04 us
    ppermute x16 -> x17, starting transfers between devices: 22.1 us -> 25.4 us  [shift(): lax.ppermute(value, axis, [(i, (i + by) % count) for i in range(count)])]
    all_to_all x1, waiting for transfers between devices: 18.7 us -> 17.1 us  [body(): column = lax.all_to_all(copied, 'z', 0, 0, tiled=True).reshape(-1, COLS).T]
  transfers between devices with their start and end apart: 22 -> 28, of which waited for: 10 -> 11; matrix products, arithmetic and copies ran while one was open for 0% -> 2% of each run, Pallas kernels for 11% -> 12%
where the time goes in v5:
time: 120 us; the launch traced here: 119 us
  waiting for transfers between devices  55 us (46%)
  starting transfers between devices  35.9 us (30%)
  Pallas kernels  22.8 us (19%)
  local copies, waits for them, and re-layouts  4.57 us (4%)
    ppermute x17, waiting for transfers between devices, shift(): lax.ppermute(value, axis, [(i, (i + by) % count) for i in range(count)])  35.3 us
    ppermute x17, starting transfers between devices, shift(): lax.ppermute(value, axis, [(i, (i + by) % count) for i in range(count)])  25.4 us
    all_to_all x1, waiting for transfers between devices, body(): column = lax.all_to_all(copied, 'z', 0, 0, tiled=True).reshape(-1, COLS).T  17.1 us
    all_to_all x1, starting transfers between devices, body(): column = lax.all_to_all(copied, 'z', 0, 0, tiled=True).reshape(-1, COLS).T  8.6 us
    pallas_call x1, Pallas kernels, body(): call(near_kernel, walked(HEADS), [SMEM] + [ANY] * 6 + [VMEM] * 9, scratch...  6.41 us
    pallas_call x1, Pallas kernels, body(): call(project_kernel, (jax.ShapeDtypeStruct((2, COLS, ROWS), F32), jax.Sha...  6.41 us
    pallas_call x1, Pallas kernels, body(): call(far_kernel, walked(FAR), [SMEM] + [ANY] * 8 + [VMEM] * 10, scratch,...  4.05 us
    ppermute x10, waiting for transfers between devices, flip(): return lax.ppermute(value, 'c', [(0, 1), (1, 0)])  2.57 us
  transfers between devices with their start and end apart: 28, of which 11 were waited for; matrix products, arithmetic and copies ran while one was open for 2% of the time, Pallas kernels for 12%

profile of v5, /device:TPU:24, one launch (start us, length us, event | category | flops | bytes accessed | tf_op | source)
XLA Modules:
  0.0 118.8 jit_solution(6981135973185564153)
XLA Ops:
  0.0 1.8 %broadcast_in_dim.4 = bf16[8,80,432]{2,1,0:T(8,128)(2,1)} broadcast(bf16[80,432]{1,0:T(8,128)(2,1)} %param.14), dimensions={1,2} | broadcast | bytes 622080 | tf_op jit(solution)/shard_map/broadcast_in_dim | solution.py:284
  1.8 8.6 %all-to-all-start = ((bf16[8,80,432]{2,1,0:T(8,128)(2,1)}), bf16[8,80,432]{2,1,0:T(8,128)(2,1)S(1)}, u32[]{:S(2)}, u32[]{:S(2)}) async-start(bf16[8,80,432]{2,1,0:T(8,128)(2,1)} %broadcast_in_dim.4), calls=%async_computation | async-start | bytes 1310720 | tf_op jit(solution)/shard_map/all_to_all | solution.py:285
  10.4 1.5 %collective-permute-start = (bf16[128,2560]{1,0:T(8,128)(2,1)}, bf16[128,2560]{1,0:T(8,128)(2,1)S(1)}, u32[]{:S(2)}, u32[]{:S(2)}) collective-permute-start(bf16[128,2560]{1,0:T(8,128)(2,1)} %bitcast.4.refs_0_), channel_id=1, source_target_pairs={{0,2},{2,4},{4,6},{6,0},{1,3},{3,5},{5,7},{7,1},{8,10},{10,12},{12... | collective-permute-start | bytes 1966088 | tf_op jit(solution)/shard_map/ppermute | solution.py:35
  11.9 1.7 %collective-permute-start.1 = (bf16[128,2560]{1,0:T(8,128)(2,1)}, bf16[128,2560]{1,0:T(8,128)(2,1)S(1)}, u32[]{:S(2)}, u32[]{:S(2)}) collective-permute-start(bf16[128,2560]{1,0:T(8,128)(2,1)} %bitcast.4.refs_0_), channel_id=1, source_target_pairs={{0,6},{2,0},{4,2},{6,4},{1,7},{3,1},{5,3},{7,5},{8,14},{10,8},{12,... | collective-permute-start | bytes 1966088 | tf_op jit(solution)/shard_map/ppermute | solution.py:35
  13.6 17.1 %all-to-all-done = bf16[8,80,432]{2,1,0:T(8,128)(2,1)S(1)} async-done(((bf16[8,80,432]{2,1,0:T(8,128)(2,1)}), bf16[8,80,432]{2,1,0:T(8,128)(2,1)S(1)}, u32[]{:S(2)}, u32[]{:S(2)}) %all-to-all-start) | async-done | bytes 552992 | tf_op jit(solution)/shard_map/all_to_all | solution.py:285
  30.7 0.3 copy.13
  31.0 2.8 %collective-permute-start.3 = (bf16[64,2560]{1,0:T(8,128)(2,1)S(1)}, bf16[64,2560]{1,0:T(8,128)(2,1)S(1)}, u32[]{:S(2)}, u32[]{:S(2)}) collective-permute-start(bf16[64,2560]{1,0:T(8,128)(2,1)S(1)} %slice.62), channel_id=1, source_target_pairs={{0,6},{2,0},{4,2},{6,4},{1,7},{3,1},{5,3},{7,5},{8,14},{10,8},{12,... | collective-permute-start | bytes 983048 | tf_op jit(solution)/shard_map/ppermute | solution.py:35
  33.9 0.7 slice.61
  34.6 0.5 collective-permute-start.7
  35.1 0.2 collective-permute-start.11
  35.3 1.8 %collective-permute-start.12 = (bf16[432,640]{1,0:T(8,128)(2,1)S(1)}, bf16[432,640]{1,0:T(8,128)(2,1)S(1)}, u32[]{:S(2)}, u32[]{:S(2)}) collective-permute-start(bf16[432,640]{1,0:T(8,128)(2,1)S(1)} %bitcast.16), channel_id=1, source_target_pairs={{0,192},{64,0},{128,64},{192,128},{1,193},{65,1},{129,65},{193,129... | collective-permute-start | bytes 1658888 | tf_op jit(solution)/shard_map/ppermute | solution.py:35
  37.2 3.9 %collective-permute-done.3.refs_4_ = bf16[64,2560]{1,0:T(8,128)(2,1)S(1)} collective-permute-done((bf16[64,2560]{1,0:T(8,128)(2,1)S(1)}, bf16[64,2560]{1,0:T(8,128)(2,1)S(1)}, u32[]{:S(2)}, u32[]{:S(2)}) %collective-permute-start.3) | collective-permute-done | bytes 327712 | tf_op jit(solution)/shard_map/ppermute | solution.py:35
  41.0 1.2 %collective-permute-start.2 = (bf16[64,2560]{1,0:T(8,128)(2,1)}, bf16[64,2560]{1,0:T(8,128)(2,1)}, u32[]{:S(2)}, u32[]{:S(2)}) collective-permute-start(bf16[64,2560]{1,0:T(8,128)(2,1)} %slice.61), channel_id=1, source_target_pairs={{0,2},{2,4},{4,6},{6,0},{1,3},{3,5},{5,7},{7,1},{8,10},{10,12},{12... | collective-permute-start | bytes 983048 | tf_op jit(solution)/shard_map/ppermute | solution.py:35
  42.2 0.8 slice_bitcast_fusion
  43.1 0.1 concatenate.6
  43.2 8.9 %collective-permute-done.2.refs_3_ = bf16[64,2560]{1,0:T(8,128)(2,1)} collective-permute-done((bf16[64,2560]{1,0:T(8,128)(2,1)}, bf16[64,2560]{1,0:T(8,128)(2,1)}, u32[]{:S(2)}, u32[]{:S(2)}) %collective-permute-start.2) | collective-permute-done | bytes 327712 | tf_op jit(solution)/shard_map/ppermute | solution.py:35
  52.1 6.5 %collective-permute-done.4.refs_5_.ahead_ref = bf16[16,2560]{1,0:T(8,128)(2,1)S(1)} collective-permute-done((bf16[16,2560]{1,0:T(8,128)(2,1)S(1)}, bf16[16,2560]{1,0:T(8,128)(2,1)S(1)}, u32[]{:S(2)}, u32[]{:S(2)}) %collective-permute-start.4) | collective-permute-done | bytes 81952 | tf_op jit(solution)/shard_map/ppermute | solution.py:35
  58.6 1.3 %collective-permute-done.10.refs_11_ = bf16[16,2560]{1,0:T(8,128)(2,1)S(1)} collective-permute-done((bf16[16,2560]{1,0:T(8,128)(2,1)S(1)}, bf16[16,2560]{1,0:T(8,128)(2,1)S(1)}, u32[]{:S(2)}, u32[]{:S(2)}) %collective-permute-start.10) | collective-permute-done | bytes 81952 | tf_op jit(solution)/shard_map/ppermute | solution.py:39
  59.9 0.2 collective-permute-start.9
  60.1 0.4 collective-permute-start.8
  60.4 0.7 slice.83
  61.2 0.7 collective-permute-start.14
  61.9 2.8 %collective-permute-start.13 = (bf16[208,640]{1,0:T(8,128)(2,1)S(1)}, bf16[208,640]{1,0:T(8,128)(2,1)S(1)}, u32[]{:S(2)}, u32[]{:S(2)}) collective-permute-start(bf16[208,640]{1,0:T(8,128)(2,1)S(1)} %slice.82), channel_id=1, source_target_pairs={{0,64},{64,128},{128,192},{192,0},{1,65},{65,129},{129,193},{193,1... | collective-permute-start | bytes 798728 | tf_op jit(solution)/shard_map/ppermute | solution.py:35
  64.7 0.1 pad_add_fusion.at_ref
  64.8 6.4 %shard_map.109 = (f32[2,432,528]{2,1,0:T(8,128)S(1)}, bf16[1056,640]{1,0:T(8,128)(2,1)S(1)}) custom-call(s32[4]{0:T(128)S(1)} %pad_add_fusion.at_ref, bf16[128,2560]{1,0:T(8,128)(2,1)} %bitcast.4.refs_0_, bf16[128,2560]{1,0:T(8,128)(2,1)S(1)} %collective-permute-done.refs_1_, bf16[128,2560]{1,0:T(8,128)(2,1)S(1)} %collective-permute-done.1.refs_2_, ...), custom_call_target="tpu_custom_call" | custom-call | flops 1751777280 | bytes 9000000 | tf_op jit(solution)/shard_map/pallas_call | solution.py:303
  71.2 0.4 collective-permute-done.14.w1_ref
  71.6 0.0 copy-start.5
  71.6 0.0 copy-start.6
  71.6 2.5 %shard_map.110 = (bf16[928,128]{1,0:T(8,128)(2,1)S(1)}, bf16[928,128]{1,0:T(8,128)(2,1)S(1)}, bf16[928,128]{1,0:T(8,128)(2,1)S(1)}, bf16[928,128]{1,0:T(8,128)(2,1)S(1)}) custom-call(f32[2,432,528]{2,1,0:T(8,128)S(1)} %get-tuple-element.27.part_ref, bf16[1056,640]{1,0:T(8,128)(2,1)S(1)} %get-tuple-element.28.far_ref, ...), custom_call_target="tpu_custom_call" | custom-call | flops 583925760 | bytes 5000000 | tf_op jit(solution)/shard_map/pallas_call | solution.py:314
  74.1 0.1 collective-permute-start.16
  74.2 3.2 %collective-permute-start.18 = (bf16[928,128]{1,0:T(8,128)(2,1)S(1)}, bf16[928,128]{1,0:T(8,128)(2,1)S(1)}, u32[]{:S(2)}, u32[]{:S(2)}) collective-permute-start(bf16[928,128]{1,0:T(8,128)(2,1)S(1)} %get-tuple-element.31), channel_id=1, source_target_pairs={{0,6},{2,0},{4,2},{6,4},{1,7},{3,1},{5,3},{7,5},{8,14},{10,8},{12,... | collective-permute-start | bytes 712712 | tf_op jit(solution)/shard_map/ppermute | solution.py:35
  77.4 5.0 %collective-permute-done.16.refs_2_ = bf16[928,128]{1,0:T(8,128)(2,1)S(1)} collective-permute-done((bf16[928,128]{1,0:T(8,128)(2,1)S(1)}, bf16[928,128]{1,0:T(8,128)(2,1)S(1)}, u32[]{:S(2)}, u32[]{:S(2)}) %collective-permute-start.16) | collective-permute-done | bytes 237600 | tf_op jit(solution)/shard_map/ppermute | solution.py:35
  82.4 0.5 collective-permute-start.19
  82.9 1.2 %collective-permute-start.20 = (bf16[928,128]{1,0:T(8,128)(2,1)S(1)}, bf16[928,128]{1,0:T(8,128)(2,1)S(1)}, u32[]{:S(2)}, u32[]{:S(2)}) collective-permute-start(bf16[928,128]{1,0:T(8,128)(2,1)S(1)} %get-tuple-element.36), channel_id=1, source_target_pairs={{0,4},{2,6},{4,0},{6,2},{1,5},{3,7},{5,1},{7,3},{8,12},{10,14},{12... | collective-permute-start | bytes 712712 | tf_op jit(solution)/shard_map/ppermute | solution.py:35
  84.1 1.5 %shard_map.111 = (f32[27,128,128]{2,1,0:T(8,128)S(1)}, f32[4,128,128]{2,1,0:T(8,128)S(1)}) custom-call(s32[4]{0:T(128)S(1)} %pad_add_fusion.at_ref, bf16[128,3456]{1,0:T(8,128)(2,1)S(1)} %bitcast.18, s32[1,128]{1,0:T(1,128)S(1)} %copy-done.8, bf16[16,2560]{1,0:T(8,128)(2,1)S(1)} %collective-permute-done.4.refs_5_.ahead_ref), custom_call_target="tpu_custom_call" | custom-call | bytes 2700000 | tf_op jit(solution)/shard_map/pallas_call | solution.py:322
  85.7 6.4 %shard_map.112 = (f32[27,128,128]{2,1,0:T(8,128)S(1)}, f32[27,128,128]{2,1,0:T(8,128)S(1)}, f32[2,3456]{1,0:T(2,128)S(1)}) custom-call(s32[4]{0:T(128)S(1)} %pad_add_fusion.at_ref, bf16[928,128]{1,0:T(8,128)(2,1)S(1)} %get-tuple-element.29.refs_0_, bf16[928,128]{1,0:T(8,128)(2,1)S(1)} %collective-permute-done.15.refs_1_, ...), custom_call_target="tpu_custom_call" | custom-call | flops 167772160 | bytes 20000000 | tf_op jit(solution)/shard_map/pallas_call | solution.py:362
  92.2 0.3 collective-permute-start.21
  92.5 1.3 %collective-permute-done.21.refs_7_ = bf16[928,128]{1,0:T(8,128)(2,1)S(1)} collective-permute-done((bf16[928,128]{1,0:T(8,128)(2,1)S(1)}, bf16[928,128]{1,0:T(8,128)(2,1)S(1)}, u32[]{:S(2)}, u32[]{:S(2)}) %collective-permute-start.21) | collective-permute-done | bytes 237600 | tf_op jit(solution)/shard_map/ppermute | solution.py:39
  93.8 4.0 %shard_map.113 = (f32[8,128,128]{2,1,0:T(8,128)S(1)}, f32[8,128,128]{2,1,0:T(8,128)S(1)}, f32[2,3456]{1,0:T(2,128)S(1)}) custom-call(s32[4]{0:T(128)S(1)} %pad_add_fusion.at_ref, bf16[928,128]{1,0:T(8,128)(2,1)S(1)} %get-tuple-element.29.refs_0_, bf16[928,128]{1,0:T(8,128)(2,1)S(1)} %collective-permute-done.15.refs_1_, ...), custom_call_target="tpu_custom_call" | custom-call | flops 67108864 | bytes 8000000 | tf_op jit(solution)/shard_map/pallas_call | solution.py:371
  97.8 0.1 collective-permute-start.22
  97.9 6.0 %collective-permute-done.22 = f32[2,3456]{1,0:T(2,128)S(1)} collective-permute-done((f32[2,3456]{1,0:T(2,128)S(1)}, f32[2,3456]{1,0:T(2,128)S(1)}, u32[]{:S(2)}, u32[]{:S(2)}) %collective-permute-start.22) | collective-permute-done | bytes 27680 | tf_op jit(solution)/shard_map/ppermute | solution.py:35
  103.9 0.1 collective-permute-start.23
  104.0 0.1 collective-permute-start.24
  104.1 7.9 %collective-permute-start.25 = (f32[2,3456]{1,0:T(2,128)S(1)}, f32[2,3456]{1,0:T(2,128)S(1)}, u32[]{:S(2)}, u32[]{:S(2)}) collective-permute-start(f32[2,3456]{1,0:T(2,128)S(1)} %pad_maximum_fusion), channel_id=1, source_target_pairs={{0,40},{8,48},{16,56},{24,64},{32,72},{40,80},{48,88},{56,96},{64,... | collective-permute-start | bytes 82952 | tf_op jit(solution)/shard_map/ppermute | solution.py:35
  112.0 1.6 %collective-permute-done.25 = f32[2,3456]{1,0:T(2,128)S(1)} collective-permute-done((f32[2,3456]{1,0:T(2,128)S(1)}, f32[2,3456]{1,0:T(2,128)S(1)}, u32[]{:S(2)}, u32[]{:S(2)}) %collective-permute-start.25) | collective-permute-done | bytes 27680 | tf_op jit(solution)/shard_map/ppermute | solution.py:35
  113.6 3.1 %collective-permute-done.26 = f32[2,3456]{1,0:T(2,128)S(1)} collective-permute-done((f32[2,3456]{1,0:T(2,128)S(1)}, f32[2,3456]{1,0:T(2,128)S(1)}, u32[]{:S(2)}, u32[]{:S(2)}) %collective-permute-start.26) | collective-permute-done | bytes 27680 | tf_op jit(solution)/shard_map/ppermute | solution.py:35
  116.7 0.1 slice_add_fusion.in_ref
  116.8 2.0 %shard_map.114 = bf16[128,3456]{1,0:T(8,128)(2,1)} custom-call(s32[4]{0:T(128)S(1)} %pad_add_fusion.at_ref, f32[27,128,128]{2,1,0:T(8,128)S(1)} %get-tuple-element.34.state_ref, f32[27,128,128]{2,1,0:T(8,128)S(1)} %get-tuple-element.35.prod_ref, f32[8,128,128]{2,1,0:T(8,128)S(1)} %get-tuple-element.40.far_state_ref, ...), custom_call_target="tpu_custom_call" | custom-call | bytes 4400000 | tf_op jit(solution)/shard_map/pallas_call | solution.py:383
  (49 shorter events, 0.3 us)
Async XLA Ops:
  1.8 41.2 %copy-start.8 = (s32[1,128]{1,0:T(1,128)S(1)}, s32[1,128]{1,0:T(1,128)}, u32[]{:S(2)}) copy-start(s32[1,128]{1,0:T(1,128)} %ids_ref.1) | copy-start | bytes 1540
  1.8 28.9 %all-to-all-start = ((bf16[8,80,432]{2,1,0:T(8,128)(2,1)}), bf16[8,80,432]{2,1,0:T(8,128)(2,1)S(1)}, u32[]{:S(2)}, u32[]{:S(2)}) async-start(bf16[8,80,432]{2,1,0:T(8,128)(2,1)} %broadcast_in_dim.4), calls=%async_computation | async-start | bytes 1310720 | tf_op jit(solution)/shard_map/all_to_all | solution.py:285
  10.4 20.6 %collective-permute-start = (bf16[128,2560]{1,0:T(8,128)(2,1)}, bf16[128,2560]{1,0:T(8,128)(2,1)S(1)}, u32[]{:S(2)}, u32[]{:S(2)}) collective-permute-start(bf16[128,2560]{1,0:T(8,128)(2,1)} %bitcast.4.refs_0_), channel_id=1, source_target_pairs={{0,2},{2,4},{4,6},{6,0},{1,3},{3,5},{5,7},{7,1},{8,10},{10,12},{12... | collective-permute-start | bytes 1966088 | tf_op jit(solution)/shard_map/ppermute | solution.py:35
  11.9 19.1 %collective-permute-start.1 = (bf16[128,2560]{1,0:T(8,128)(2,1)}, bf16[128,2560]{1,0:T(8,128)(2,1)S(1)}, u32[]{:S(2)}, u32[]{:S(2)}) collective-permute-start(bf16[128,2560]{1,0:T(8,128)(2,1)} %bitcast.4.refs_0_), channel_id=1, source_target_pairs={{0,6},{2,0},{4,2},{6,4},{1,7},{3,1},{5,3},{7,5},{8,14},{10,8},{12,... | collective-permute-start | bytes 1966088 | tf_op jit(solution)/shard_map/ppermute | solution.py:35
  13.6 21.7 %collective-permute-start.5 = (bf16[128,2560]{1,0:T(8,128)(2,1)}, bf16[128,2560]{1,0:T(8,128)(2,1)}, u32[]{:S(2)}, u32[]{:S(2)}) collective-permute-start(bf16[128,2560]{1,0:T(8,128)(2,1)} %bitcast.4.refs_0_), channel_id=1, source_target_pairs={{0,1},{1,0},{2,3},{3,2},{4,5},{5,4},{6,7},{7,6},{8,9},{9,8},{10,11... | collective-permute-start | bytes 1966088 | tf_op jit(solution)/shard_map/ppermute | solution.py:39
  31.0 10.0 %collective-permute-start.3 = (bf16[64,2560]{1,0:T(8,128)(2,1)S(1)}, bf16[64,2560]{1,0:T(8,128)(2,1)S(1)}, u32[]{:S(2)}, u32[]{:S(2)}) collective-permute-start(bf16[64,2560]{1,0:T(8,128)(2,1)S(1)} %slice.62), channel_id=1, source_target_pairs={{0,6},{2,0},{4,2},{6,4},{1,7},{3,1},{5,3},{7,5},{8,14},{10,8},{12,... | collective-permute-start | bytes 983048 | tf_op jit(solution)/shard_map/ppermute | solution.py:35
  34.6 30.2 %collective-permute-start.6 = (bf16[128,2560]{1,0:T(8,128)(2,1)S(1)}, bf16[128,2560]{1,0:T(8,128)(2,1)}, u32[]{:S(2)}, u32[]{:S(2)}) collective-permute-start(bf16[128,2560]{1,0:T(8,128)(2,1)S(1)} %collective-permute-done.refs_1_), channel_id=1, source_target_pairs={{0,1},{1,0},{2,3},{3,2},{4,5},{5,4},{6,7},{7,6},{8,9},{9,8},{10,11... | collective-permute-start | bytes 1966088 | tf_op jit(solution)/shard_map/ppermute | solution.py:39
  34.6 30.2 %collective-permute-start.7 = (bf16[128,2560]{1,0:T(8,128)(2,1)S(1)}, bf16[128,2560]{1,0:T(8,128)(2,1)}, u32[]{:S(2)}, u32[]{:S(2)}) collective-permute-start(bf16[128,2560]{1,0:T(8,128)(2,1)S(1)} %collective-permute-done.1.refs_2_), channel_id=1, source_target_pairs={{0,1},{1,0},{2,3},{3,2},{4,5},{5,4},{6,7},{7,6},{8,9},{9,8},{10,11... | collective-permute-start | bytes 1966088 | tf_op jit(solution)/shard_map/ppermute | solution.py:39
  35.1 26.0 %collective-permute-start.11 = (bf16[432,640]{1,0:T(8,128)(2,1)S(1)}, bf16[432,640]{1,0:T(8,128)(2,1)S(1)}, u32[]{:S(2)}, u32[]{:S(2)}) collective-permute-start(bf16[432,640]{1,0:T(8,128)(2,1)S(1)} %bitcast.15), channel_id=1, source_target_pairs={{0,64},{64,128},{128,192},{192,0},{1,65},{65,129},{129,193},{193,1... | collective-permute-start | bytes 1658888 | tf_op jit(solution)/shard_map/ppermute | solution.py:35
  35.3 24.7 %collective-permute-start.12 = (bf16[432,640]{1,0:T(8,128)(2,1)S(1)}, bf16[432,640]{1,0:T(8,128)(2,1)S(1)}, u32[]{:S(2)}, u32[]{:S(2)}) collective-permute-start(bf16[432,640]{1,0:T(8,128)(2,1)S(1)} %bitcast.16), channel_id=1, source_target_pairs={{0,192},{64,0},{128,64},{192,128},{1,193},{65,1},{129,65},{193,129... | collective-permute-start | bytes 1658888 | tf_op jit(solution)/shard_map/ppermute | solution.py:35
  41.0 11.1 %collective-permute-start.2 = (bf16[64,2560]{1,0:T(8,128)(2,1)}, bf16[64,2560]{1,0:T(8,128)(2,1)}, u32[]{:S(2)}, u32[]{:S(2)}) collective-permute-start(bf16[64,2560]{1,0:T(8,128)(2,1)} %slice.61), channel_id=1, source_target_pairs={{0,2},{2,4},{4,6},{6,0},{1,3},{3,5},{5,7},{7,1},{8,10},{10,12},{12... | collective-permute-start | bytes 983048 | tf_op jit(solution)/shard_map/ppermute | solution.py:35
  52.1 6.6 %collective-permute-start.4 = (bf16[16,2560]{1,0:T(8,128)(2,1)S(1)}, bf16[16,2560]{1,0:T(8,128)(2,1)S(1)}, u32[]{:S(2)}, u32[]{:S(2)}) collective-permute-start(bf16[16,2560]{1,0:T(8,128)(2,1)S(1)} %concatenate.6), channel_id=1, source_target_pairs={{0,8},{8,16},{16,24},{24,32},{32,40},{40,48},{48,56},{56,64},{64,7... | collective-permute-start | bytes 245768 | tf_op jit(solution)/shard_map/ppermute | solution.py:35
  58.6 1.3 %collective-permute-start.10 = (bf16[16,2560]{1,0:T(8,128)(2,1)S(1)}, bf16[16,2560]{1,0:T(8,128)(2,1)S(1)}, u32[]{:S(2)}, u32[]{:S(2)}) collective-permute-start(bf16[16,2560]{1,0:T(8,128)(2,1)S(1)} %collective-permute-done.4.refs_5_.ahead_ref), channel_id=1, source_target_pairs={{0,1},{1,0},{2,3},{3,2},{4,5},{5,4},{6,7},{7,6},{8,9},{9,8},{10,11... | collective-permute-start | bytes 245768 | tf_op jit(solution)/shard_map/ppermute | solution.py:39
  59.9 2.0 %collective-permute-start.9 = (bf16[64,2560]{1,0:T(8,128)(2,1)S(1)}, bf16[64,2560]{1,0:T(8,128)(2,1)}, u32[]{:S(2)}, u32[]{:S(2)}) collective-permute-start(bf16[64,2560]{1,0:T(8,128)(2,1)S(1)} %collective-permute-done.3.refs_4_), channel_id=1, source_target_pairs={{0,1},{1,0},{2,3},{3,2},{4,5},{5,4},{6,7},{7,6},{8,9},{9,8},{10,11... | collective-permute-start | bytes 983048 | tf_op jit(solution)/shard_map/ppermute | solution.py:39
  60.1 4.7 %collective-permute-start.8 = (bf16[64,2560]{1,0:T(8,128)(2,1)}, bf16[64,2560]{1,0:T(8,128)(2,1)}, u32[]{:S(2)}, u32[]{:S(2)}) collective-permute-start(bf16[64,2560]{1,0:T(8,128)(2,1)} %collective-permute-done.2.refs_3_), channel_id=1, source_target_pairs={{0,1},{1,0},{2,3},{3,2},{4,5},{5,4},{6,7},{7,6},{8,9},{9,8},{10,11... | collective-permute-start | bytes 983048 | tf_op jit(solution)/shard_map/ppermute | solution.py:39
  61.2 10.4 %collective-permute-start.14 = (bf16[224,640]{1,0:T(8,128)(2,1)}, bf16[224,640]{1,0:T(8,128)(2,1)}, u32[]{:S(2)}, u32[]{:S(2)}) collective-permute-start(bf16[224,640]{1,0:T(8,128)(2,1)} %slice.83), channel_id=1, source_target_pairs={{0,192},{64,0},{128,64},{192,128},{1,193},{65,1},{129,65},{193,129... | collective-permute-start | bytes 860168 | tf_op jit(solution)/shard_map/ppermute | solution.py:35
  61.9 9.3 %collective-permute-start.13 = (bf16[208,640]{1,0:T(8,128)(2,1)S(1)}, bf16[208,640]{1,0:T(8,128)(2,1)S(1)}, u32[]{:S(2)}, u32[]{:S(2)}) collective-permute-start(bf16[208,640]{1,0:T(8,128)(2,1)S(1)} %slice.82), channel_id=1, source_target_pairs={{0,64},{64,128},{128,192},{192,0},{1,65},{65,129},{129,193},{193,1... | collective-permute-start | bytes 798728 | tf_op jit(solution)/shard_map/ppermute | solution.py:35
  71.6 12.5 %copy-start.2 = (bf16[1,128,3456]{2,1,0:T(8,128)(2,1)S(1)}, bf16[1,128,3456]{2,1,0:T(8,128)(2,1)}, u32[]{:S(2)}) copy-start(bf16[1,128,3456]{2,1,0:T(8,128)(2,1)} %param.12) | copy-start | bytes 2654212
  71.6 14.1 %copy-start = (bf16[27,128,128]{2,1,0:T(8,128)(2,1)S(1)}, bf16[27,128,128]{2,1,0:T(8,128)(2,1)}, u32[]{:S(2)}) copy-start(bf16[27,128,128]{2,1,0:T(8,128)(2,1)} %refs_15_.1) | copy-start | bytes 2654212
  71.6 14.1 %copy-start.1 = (bf16[27,128,128]{2,1,0:T(8,128)(2,1)S(1)}, bf16[27,128,128]{2,1,0:T(8,128)(2,1)}, u32[]{:S(2)}) copy-start(bf16[27,128,128]{2,1,0:T(8,128)(2,1)} %refs_16_.1) | copy-start | bytes 2654212
  71.6 14.1 %copy-start.3 = (f32[4,3456]{1,0:T(4,128)S(1)}, f32[4,3456]{1,0:T(4,128)}, u32[]{:S(2)}) copy-start(f32[4,3456]{1,0:T(4,128)} %refs_10_.1) | copy-start | bytes 165892
  71.6 14.1 %copy-start.4 = (f32[3456]{0:T(1024)S(1)}, f32[3456]{0:T(1024)}, u32[]{:S(2)}) copy-start(f32[3456]{0:T(1024)} %param.16) | copy-start | bytes 41476
  71.6 14.1 %copy-start.5 = (f32[3456]{0:T(1024)S(1)}, f32[3456]{0:T(1024)}, u32[]{:S(2)}) copy-start(f32[3456]{0:T(1024)} %param.19) | copy-start | bytes 41476
  71.6 14.1 %copy-start.6 = (f32[3456]{0:T(1024)S(1)}, f32[3456]{0:T(1024)}, u32[]{:S(2)}) copy-start(f32[3456]{0:T(1024)} %param.20) | copy-start | bytes 41476
  71.6 14.1 %copy-start.7 = (f32[3456]{0:T(1024)S(1)}, f32[3456]{0:T(1024)}, u32[]{:S(2)}) copy-start(f32[3456]{0:T(1024)} %param.21) | copy-start | bytes 41476
  74.1 8.3 %collective-permute-start.16 = (bf16[928,128]{1,0:T(8,128)(2,1)S(1)}, bf16[928,128]{1,0:T(8,128)(2,1)S(1)}, u32[]{:S(2)}, u32[]{:S(2)}) collective-permute-start(bf16[928,128]{1,0:T(8,128)(2,1)S(1)} %get-tuple-element.30), channel_id=1, source_target_pairs={{0,2},{2,4},{4,6},{6,0},{1,3},{3,5},{5,7},{7,1},{8,10},{10,12},{12... | collective-permute-start | bytes 712712 | tf_op jit(solution)/shard_map/ppermute | solution.py:35
  74.2 8.2 %collective-permute-start.18 = (bf16[928,128]{1,0:T(8,128)(2,1)S(1)}, bf16[928,128]{1,0:T(8,128)(2,1)S(1)}, u32[]{:S(2)}, u32[]{:S(2)}) collective-permute-start(bf16[928,128]{1,0:T(8,128)(2,1)S(1)} %get-tuple-element.31), channel_id=1, source_target_pairs={{0,6},{2,0},{4,2},{6,4},{1,7},{3,1},{5,3},{7,5},{8,14},{10,8},{12,... | collective-permute-start | bytes 712712 | tf_op jit(solution)/shard_map/ppermute | solution.py:35
  77.4 8.3 %collective-permute-start.15 = (bf16[928,128]{1,0:T(8,128)(2,1)S(1)}, bf16[928,128]{1,0:T(8,128)(2,1)S(1)}, u32[]{:S(2)}, u32[]{:S(2)}) collective-permute-start(bf16[928,128]{1,0:T(8,128)(2,1)S(1)} %get-tuple-element.29.refs_0_), channel_id=1, source_target_pairs={{0,1},{1,0},{2,3},{3,2},{4,5},{5,4},{6,7},{7,6},{8,9},{9,8},{10,11... | collective-permute-start | bytes 712712 | tf_op jit(solution)/shard_map/ppermute | solution.py:39
  82.4 3.3 %collective-permute-start.17 = (bf16[928,128]{1,0:T(8,128)(2,1)S(1)}, bf16[928,128]{1,0:T(8,128)(2,1)S(1)}, u32[]{:S(2)}, u32[]{:S(2)}) collective-permute-start(bf16[928,128]{1,0:T(8,128)(2,1)S(1)} %collective-permute-done.16.refs_2_), channel_id=1, source_target_pairs={{0,1},{1,0},{2,3},{3,2},{4,5},{5,4},{6,7},{7,6},{8,9},{9,8},{10,11... | collective-permute-start | bytes 712712 | tf_op jit(solution)/shard_map/ppermute | solution.py:39
  82.4 3.3 %collective-permute-start.19 = (bf16[928,128]{1,0:T(8,128)(2,1)S(1)}, bf16[928,128]{1,0:T(8,128)(2,1)S(1)}, u32[]{:S(2)}, u32[]{:S(2)}) collective-permute-start(bf16[928,128]{1,0:T(8,128)(2,1)S(1)} %collective-permute-done.18.refs_4_), channel_id=1, source_target_pairs={{0,1},{1,0},{2,3},{3,2},{4,5},{5,4},{6,7},{7,6},{8,9},{9,8},{10,11... | collective-permute-start | bytes 712712 | tf_op jit(solution)/shard_map/ppermute | solution.py:39
  82.9 9.3 %collective-permute-start.20 = (bf16[928,128]{1,0:T(8,128)(2,1)S(1)}, bf16[928,128]{1,0:T(8,128)(2,1)S(1)}, u32[]{:S(2)}, u32[]{:S(2)}) collective-permute-start(bf16[928,128]{1,0:T(8,128)(2,1)S(1)} %get-tuple-element.36), channel_id=1, source_target_pairs={{0,4},{2,6},{4,0},{6,2},{1,5},{3,7},{5,1},{7,3},{8,12},{10,14},{12... | collective-permute-start | bytes 712712 | tf_op jit(solution)/shard_map/ppermute | solution.py:35
  92.2 1.6 %collective-permute-start.21 = (bf16[928,128]{1,0:T(8,128)(2,1)S(1)}, bf16[928,128]{1,0:T(8,128)(2,1)S(1)}, u32[]{:S(2)}, u32[]{:S(2)}) collective-permute-start(bf16[928,128]{1,0:T(8,128)(2,1)S(1)} %collective-permute-done.20.refs_6_), channel_id=1, source_target_pairs={{0,1},{1,0},{2,3},{3,2},{4,5},{5,4},{6,7},{7,6},{8,9},{9,8},{10,11... | collective-permute-start | bytes 712712 | tf_op jit(solution)/shard_map/ppermute | solution.py:39
  97.8 6.0 %collective-permute-start.22 = (f32[2,3456]{1,0:T(2,128)S(1)}, f32[2,3456]{1,0:T(2,128)S(1)}, u32[]{:S(2)}, u32[]{:S(2)}) collective-permute-start(f32[2,3456]{1,0:T(2,128)S(1)} %get-tuple-element.42), channel_id=1, source_target_pairs={{0,8},{8,16},{16,24},{24,32},{32,40},{40,48},{48,56},{56,64},{64,7... | collective-permute-start | bytes 82952 | tf_op jit(solution)/shard_map/ppermute | solution.py:35
  103.9 8.1 %collective-permute-start.23 = (f32[2,3456]{1,0:T(2,128)S(1)}, f32[2,3456]{1,0:T(2,128)S(1)}, u32[]{:S(2)}, u32[]{:S(2)}) collective-permute-start(f32[2,3456]{1,0:T(2,128)S(1)} %pad_maximum_fusion), channel_id=1, source_target_pairs={{0,8},{8,16},{16,24},{24,32},{32,40},{40,48},{48,56},{56,64},{64,7... | collective-permute-start | bytes 82952 | tf_op jit(solution)/shard_map/ppermute | solution.py:35
  104.0 8.0 %collective-permute-start.24 = (f32[2,3456]{1,0:T(2,128)S(1)}, f32[2,3456]{1,0:T(2,128)S(1)}, u32[]{:S(2)}, u32[]{:S(2)}) collective-permute-start(f32[2,3456]{1,0:T(2,128)S(1)} %pad_maximum_fusion), channel_id=1, source_target_pairs={{0,24},{8,32},{16,40},{24,48},{32,56},{40,64},{48,72},{56,80},{64,... | collective-permute-start | bytes 82952 | tf_op jit(solution)/shard_map/ppermute | solution.py:35
  104.1 9.5 %collective-permute-start.25 = (f32[2,3456]{1,0:T(2,128)S(1)}, f32[2,3456]{1,0:T(2,128)S(1)}, u32[]{:S(2)}, u32[]{:S(2)}) collective-permute-start(f32[2,3456]{1,0:T(2,128)S(1)} %pad_maximum_fusion), channel_id=1, source_target_pairs={{0,40},{8,48},{16,56},{24,64},{32,72},{40,80},{48,88},{56,96},{64,... | collective-permute-start | bytes 82952 | tf_op jit(solution)/shard_map/ppermute | solution.py:35
  112.0 4.8 %collective-permute-start.26 = (f32[2,3456]{1,0:T(2,128)S(1)}, f32[2,3456]{1,0:T(2,128)S(1)}, u32[]{:S(2)}, u32[]{:S(2)}) collective-permute-start(f32[2,3456]{1,0:T(2,128)S(1)} %pad_maximum_fusion), channel_id=1, source_target_pairs={{0,56},{8,64},{16,72},{24,80},{32,88},{40,96},{48,104},{56,112},{6... | collective-permute-start | bytes 82952 | tf_op jit(solution)/shard_map/ppermute | solution.py:35

commit v6 on v5

--- a/solution.py
+++ b/solution.py
@@ -25,9 +25,11 @@
 PACK = COLS + 32
 CUT = 208
 AHEAD = 16
+BLOCK = LENGTH + AHEAD
+SPLIT = 64
 SIDE = 4
 NEAR, FAR = 20, 8
-ROWS = 4 * LENGTH + AHEAD
+ROWS = 4 * BLOCK
 
 
 def shift(value, axis, by):
@@ -78,12 +80,20 @@
 
 
 def project_kernel(at_ref, *refs):
-    tokens, weights, (part_ref, far_ref, rows_ref, sems) = refs[:12], refs[12:15], refs[15:]
+    tokens, weights, (part_ref, far_ref, rows_ref, sems) = refs[:10], refs[10:13], refs[13:]
     y = at_ref[2]
-    pairs, start = [], 0
-    for ref in tokens:
-        pairs.append((ref, rows_ref.at[pl.ds(start, ref.shape[0])]))
-        start += ref.shape[0]
+    pairs = []
+    for n, ref in enumerate(tokens):
+        half, n = n // 5, n % 5
+        size = ref.shape[0]
+        if n == 3:
+            pairs.append((ref, rows_ref.at[pl.ds(half * ROWS + 3 * LENGTH, size)]))
+            continue
+        top = min(n, 3) * LENGTH + (SPLIT if n == 4 else 0)
+        main = size - AHEAD
+        pairs.append((ref.at[pl.ds(0, main)], rows_ref.at[pl.ds(half * ROWS + top, main)]))
+        rest = half * ROWS + 4 * LENGTH + min(n, 3) * AHEAD
+        pairs.append((ref.at[pl.ds(main, AHEAD)], rows_ref.at[pl.ds(rest, AHEAD)]))
     for copy in copies(pairs, sems):
         copy.wait()
     for half in range(2):
@@ -102,14 +112,12 @@
     all_ref[CUT:COLS, :] = w1_ref[...]
     for half in range(2):
         total = part_ref[half] + across(all_ref[...], far_ref[half * ROWS : (half + 1) * ROWS, :])
-        wide_ref[0:COLS, 0:AHEAD] = total[:, 4 * LENGTH :]
+        wide_ref[0:COLS, 0 : 4 * AHEAD] = total[:, 4 * LENGTH :]
         turned = [wide_ref[j * 128 : (j + 1) * 128, :].T for j in range(4)]
         top = half * PACK
         for i, out_ref in enumerate(outs):
             out_ref[top : top + COLS, :] = total[:, i * LENGTH : (i + 1) * LENGTH].astype(BF16)
-            group = [t[8 * (i // 2) : 8 * (i // 2) + 8, :] for t in turned]
-            if i % 2 == 0:
-                group = [pltpu.roll(g, 4, 0) for g in group]
+            group = [t[AHEAD * (i + 1) - HALO : AHEAD * (i + 1), :] for t in turned]
             for j in range(2):
                 rest = slice(top + COLS + 16 * j, top + COLS + 16 * j + 16)
                 out_ref[rest, :] = jnp.concatenate(group[2 * j : 2 * j + 2], axis=0).astype(BF16)
@@ -281,24 +289,24 @@
         jnp.int32
     )
 
-    copied = jnp.broadcast_to(in_weight[None], (8,) + in_weight.shape)
+    documents = jnp.pad(segment_ids.astype(BF16), ((0, 0), (0, DEPTH - LENGTH)))
+    last = jnp.concatenate([documents, own[1 - AHEAD :]], axis=0)
+    last, weight = lax.optimization_barrier((last, in_weight))
+    ahead = shift(last, ctx, 1)
+    copied = jnp.broadcast_to(weight[None], (8,) + weight.shape)
     column = lax.all_to_all(copied, "z", 0, 0, tiled=True).reshape(-1, COLS).T
-    one_back, one_ahead = shift(own, "x", 1), shift(own, "x", -1)
+    rows = jnp.concatenate([own, ahead], axis=0)
+    one_back, one_ahead = shift(rows, "x", 1), shift(rows, "x", -1)
     column, one_back, one_ahead = lax.optimization_barrier((column, one_back, one_ahead))
-    upper = shift(one_back[: LENGTH // 2], "x", 1)
-    lower = shift(one_ahead[LENGTH // 2 :], "x", -1)
-    streams = [own, one_back, one_ahead, upper, lower]
+    upper = shift(one_back[:SPLIT], "x", 1)
+    lower = shift(one_ahead[SPLIT:], "x", -1)
+    streams = [rows, one_back, one_ahead, upper, lower]
     from_back = shift(column, "y", 1)
     from_ahead = shift(column, "y", -1)
+    from_back, from_ahead = lax.optimization_barrier((from_back, from_ahead))
     first = shift(from_back[:CUT], "y", 1)
     second = shift(from_ahead[CUT:], "y", -1)
 
-    documents = jnp.pad(segment_ids.astype(BF16), ((0, 0), (0, DEPTH - LENGTH)))
-    ahead = shift(
-        jnp.concatenate([documents, own[-3:]] + [t[-4:] for t in (one_back, one_ahead, lower)], axis=0), ctx, 1
-    )
-
-    streams.append(ahead)
     streams += [flip(t) for t in streams]
     part, rows_far = call(
         project_kernel,
@@ -306,8 +314,8 @@
             jax.ShapeDtypeStruct((2, COLS, ROWS), F32),
             jax.ShapeDtypeStruct((2 * ROWS, 640), BF16),
         ),
-        [SMEM] + [ANY] * 12 + [VMEM] * 3,
-        [pltpu.VMEM((2 * ROWS, DEPTH), BF16), pltpu.SemaphoreType.DMA((12,))],
+        [SMEM] + [ANY] * 10 + [VMEM] * 3,
+        [pltpu.VMEM((2 * ROWS, DEPTH), BF16), pltpu.SemaphoreType.DMA((18,))],
         flops=2 * 1056 * 1920 * 432,
         moved=9_000_000,
     )(at, *streams, column, from_back, from_ahead)

time: 120 us -> 115 us (0.958)
  waiting for transfers between devices: 55 us -> 46.7 us
  local copies, waits for them, and re-layouts: 4.57 us -> 7.9 us
    ppermute x17, waiting for transfers between devices: 35.3 us -> 28.7 us  [shift(): lax.ppermute(value, axis, [(i, (i + by) % count) for i in range(count)])]
    unnamed x18 -> x28, local copies, waits for them, and re-layouts: 0.04 us -> 3.09 us
    ppermute x10 -> x9, waiting for transfers between devices: 2.57 us -> 1.29 us  [flip(): return lax.ppermute(value, 'c', [(0, 1), (1, 0)])]
  transfers between devices with their start and end apart: 28 -> 27, of which waited for: 11 -> 10; matrix products, arithmetic and copies ran while one was open for 2% -> 3% of each run, Pallas kernels for 12% -> 13%
where the time goes in v6:
time: 115 us; the launch traced here: 114 us
  waiting for transfers between devices  46.7 us (41%)
  starting transfers between devices  35.1 us (31%)
  Pallas kernels  23.4 us (20%)
  local copies, waits for them, and re-layouts  7.9 us (7%)
    ppermute x17, waiting for transfers between devices, shift(): lax.ppermute(value, axis, [(i, (i + by) % count) for i in range(count)])  28.7 us
    ppermute x17, starting transfers between devices, shift(): lax.ppermute(value, axis, [(i, (i + by) % count) for i in range(count)])  26.1 us
    all_to_all x1, waiting for transfers between devices, body(): column = lax.all_to_all(copied, 'z', 0, 0, tiled=True).reshape(-1, COLS).T  16.6 us
    all_to_all x1, starting transfers between devices, body(): column = lax.all_to_all(copied, 'z', 0, 0, tiled=True).reshape(-1, COLS).T  7.57 us
    pallas_call x1, Pallas kernels, body(): call(project_kernel, (jax.ShapeDtypeStruct((2, COLS, ROWS), F32), jax.Sha...  6.93 us
    pallas_call x1, Pallas kernels, body(): call(near_kernel, walked(HEADS), [SMEM] + [ANY] * 6 + [VMEM] * 9, scratch...  6.45 us
    pallas_call x1, Pallas kernels, body(): call(far_kernel, walked(FAR), [SMEM] + [ANY] * 8 + [VMEM] * 10, scratch,...  4.06 us
    unnamed x28, local copies, waits for them, and re-layouts  3.09 us
  transfers between devices with their start and end apart: 27, of which 10 were waited for; matrix products, arithmetic and copies ran while one was open for 3% of the time, Pallas kernels for 13%

profile of v6, /device:TPU:24, one launch (start us, length us, event | category | flops | bytes accessed | tf_op | source)
XLA Modules:
  0.0 114.3 jit_solution(5923442755454152240)
XLA Ops:
  0.0 1.0 slice_bitcast_fusion
  1.0 0.7 convert_element_type.5
  1.7 2.0 %collective-permute-start = (bf16[16,2560]{1,0:T(8,128)(2,1)S(1)}, bf16[16,2560]{1,0:T(8,128)(2,1)S(1)}, u32[]{:S(2)}, u32[]{:S(2)}) collective-permute-start(bf16[16,2560]{1,0:T(8,128)(2,1)S(1)} %fusion.1), channel_id=1, source_target_pairs={{0,8},{8,16},{16,24},{24,32},{32,40},{40,48},{48,56},{56,64},{64,7... | collective-permute-start | bytes 245768 | tf_op jit(solution)/shard_map/ppermute | solution.py:37
  3.7 1.8 %broadcast_in_dim.4 = bf16[8,80,432]{2,1,0:T(8,128)(2,1)} broadcast(bf16[80,432]{1,0:T(8,128)(2,1)} %param.14), dimensions={1,2} | broadcast | bytes 622080 | tf_op jit(solution)/shard_map/broadcast_in_dim | solution.py:296
  5.5 7.6 %all-to-all-start = ((bf16[8,80,432]{2,1,0:T(8,128)(2,1)}), bf16[8,80,432]{2,1,0:T(8,128)(2,1)S(1)}, u32[]{:S(2)}, u32[]{:S(2)}) async-start(bf16[8,80,432]{2,1,0:T(8,128)(2,1)} %broadcast_in_dim.4), calls=%async_computation | async-start | bytes 1310720 | tf_op jit(solution)/shard_map/all_to_all | solution.py:297
  13.1 1.6 %collective-permute-start.1 = (bf16[144,2560]{1,0:T(8,128)(2,1)S(1)}, bf16[144,2560]{1,0:T(8,128)(2,1)S(1)}, u32[]{:S(2)}, u32[]{:S(2)}) collective-permute-start(bf16[144,2560]{1,0:T(8,128)(2,1)S(1)} %pad_maximum_fusion.refs_0_), channel_id=1, source_target_pairs={{0,2},{2,4},{4,6},{6,0},{1,3},{3,5},{5,7},{7,1},{8,10},{10,12},{12... | collective-permute-start | bytes 2211848 | tf_op jit(solution)/shard_map/ppermute | solution.py:37
  14.7 1.7 %collective-permute-start.2 = (bf16[144,2560]{1,0:T(8,128)(2,1)S(1)}, bf16[144,2560]{1,0:T(8,128)(2,1)S(1)}, u32[]{:S(2)}, u32[]{:S(2)}) collective-permute-start(bf16[144,2560]{1,0:T(8,128)(2,1)S(1)} %pad_maximum_fusion.refs_0_), channel_id=1, source_target_pairs={{0,6},{2,0},{4,2},{6,4},{1,7},{3,1},{5,3},{7,5},{8,14},{10,8},{12,... | collective-permute-start | bytes 2211848 | tf_op jit(solution)/shard_map/ppermute | solution.py:37
  16.4 16.6 %all-to-all-done = bf16[8,80,432]{2,1,0:T(8,128)(2,1)S(1)} async-done(((bf16[8,80,432]{2,1,0:T(8,128)(2,1)}), bf16[8,80,432]{2,1,0:T(8,128)(2,1)S(1)}, u32[]{:S(2)}, u32[]{:S(2)}) %all-to-all-start) | async-done | bytes 552992 | tf_op jit(solution)/shard_map/all_to_all | solution.py:297
  33.0 0.3 copy.13
  33.4 2.8 %collective-permute-start.4 = (bf16[80,2560]{1,0:T(8,128)(2,1)S(1)}, bf16[80,2560]{1,0:T(8,128)(2,1)}, u32[]{:S(2)}, u32[]{:S(2)}) collective-permute-start(bf16[80,2560]{1,0:T(8,128)(2,1)S(1)} %slice.55), channel_id=1, source_target_pairs={{0,6},{2,0},{4,2},{6,4},{1,7},{3,1},{5,3},{7,5},{8,14},{10,8},{12,... | collective-permute-start | bytes 1228808 | tf_op jit(solution)/shard_map/ppermute | solution.py:37
  36.3 0.1 collective-permute-start.3
  36.4 0.3 collective-permute-start.10
  36.7 1.8 %collective-permute-start.11 = (bf16[432,640]{1,0:T(8,128)(2,1)S(1)}, bf16[432,640]{1,0:T(8,128)(2,1)S(1)}, u32[]{:S(2)}, u32[]{:S(2)}) collective-permute-start(bf16[432,640]{1,0:T(8,128)(2,1)S(1)} %bitcast.16), channel_id=1, source_target_pairs={{0,192},{64,0},{128,64},{192,128},{1,193},{65,1},{129,65},{193,129... | collective-permute-start | bytes 1658888 | tf_op jit(solution)/shard_map/ppermute | solution.py:37
  38.5 8.5 %collective-permute-done.3.refs_3_ = bf16[64,2560]{1,0:T(8,128)(2,1)} collective-permute-done((bf16[64,2560]{1,0:T(8,128)(2,1)S(1)}, bf16[64,2560]{1,0:T(8,128)(2,1)}, u32[]{:S(2)}, u32[]{:S(2)}) %collective-permute-start.3) | collective-permute-done | bytes 327712 | tf_op jit(solution)/shard_map/ppermute | solution.py:37
  47.0 0.5 collective-permute-start.7
  47.5 3.1 %collective-permute-done.10.refs_11_ = bf16[432,640]{1,0:T(8,128)(2,1)S(1)} collective-permute-done((bf16[432,640]{1,0:T(8,128)(2,1)S(1)}, bf16[432,640]{1,0:T(8,128)(2,1)S(1)}, u32[]{:S(2)}, u32[]{:S(2)}) %collective-permute-start.10) | collective-permute-done | bytes 552992 | tf_op jit(solution)/shard_map/ppermute | solution.py:37
  50.6 1.3 %collective-permute-done.11.refs_12_ = bf16[432,640]{1,0:T(8,128)(2,1)S(1)} collective-permute-done((bf16[432,640]{1,0:T(8,128)(2,1)S(1)}, bf16[432,640]{1,0:T(8,128)(2,1)S(1)}, u32[]{:S(2)}, u32[]{:S(2)}) %collective-permute-start.11) | collective-permute-done | bytes 552992 | tf_op jit(solution)/shard_map/ppermute | solution.py:37
  51.9 0.7 slice.57
  52.7 0.9 copy-done.5
  53.5 0.4 collective-permute-start.13
  54.0 1.0 slice.56
  55.0 3.0 %collective-permute-start.12 = (bf16[208,640]{1,0:T(8,128)(2,1)S(1)}, bf16[208,640]{1,0:T(8,128)(2,1)S(1)}, u32[]{:S(2)}, u32[]{:S(2)}) collective-permute-start(bf16[208,640]{1,0:T(8,128)(2,1)S(1)} %slice.56), channel_id=1, source_target_pairs={{0,64},{64,128},{128,192},{192,0},{1,65},{65,129},{129,193},{193,1... | collective-permute-start | bytes 798728 | tf_op jit(solution)/shard_map/ppermute | solution.py:37
  58.0 0.1 pad_add_fusion.at_ref
  58.1 1.0 copy-done.3
  59.1 1.1 copy-done.6
  60.3 6.9 %shard_map.109 = (f32[2,432,576]{2,1,0:T(8,128)S(1)}, bf16[1152,640]{1,0:T(8,128)(2,1)S(1)}) custom-call(s32[4]{0:T(128)S(1)} %pad_add_fusion.at_ref, bf16[144,2560]{1,0:T(8,128)(2,1)S(1)} %pad_maximum_fusion.refs_0_, bf16[144,2560]{1,0:T(8,128)(2,1)S(1)} %collective-permute-done.1.refs_1_, bf16[144,2560]{1,0:T(8,128)(2,1)S(1)} %collective-permute-done.2.refs_2_, ...), custom_call_target="tpu_custom_call" | custom-call | flops 1751777280 | bytes 9000000 | tf_op jit(solution)/shard_map/pallas_call | solution.py:311
  67.3 2.5 %shard_map.110 = (bf16[928,128]{1,0:T(8,128)(2,1)S(1)}, bf16[928,128]{1,0:T(8,128)(2,1)S(1)}, bf16[928,128]{1,0:T(8,128)(2,1)S(1)}, bf16[928,128]{1,0:T(8,128)(2,1)S(1)}) custom-call(f32[2,432,576]{2,1,0:T(8,128)S(1)} %get-tuple-element.35.part_ref, bf16[1152,640]{1,0:T(8,128)(2,1)S(1)} %get-tuple-element.36.far_ref, ...), custom_call_target="tpu_custom_call" | custom-call | flops 583925760 | bytes 5000000 | tf_op jit(solution)/shard_map/pallas_call | solution.py:322
  69.8 0.4 collective-permute-start.15
  70.2 2.9 %collective-permute-start.17 = (bf16[928,128]{1,0:T(8,128)(2,1)S(1)}, bf16[928,128]{1,0:T(8,128)(2,1)S(1)}, u32[]{:S(2)}, u32[]{:S(2)}) collective-permute-start(bf16[928,128]{1,0:T(8,128)(2,1)S(1)} %get-tuple-element.39), channel_id=1, source_target_pairs={{0,6},{2,0},{4,2},{6,4},{1,7},{3,1},{5,3},{7,5},{8,14},{10,8},{12,... | collective-permute-start | bytes 712712 | tf_op jit(solution)/shard_map/ppermute | solution.py:37
  73.1 5.6 %collective-permute-done.15.refs_2_ = bf16[928,128]{1,0:T(8,128)(2,1)S(1)} collective-permute-done((bf16[928,128]{1,0:T(8,128)(2,1)S(1)}, bf16[928,128]{1,0:T(8,128)(2,1)S(1)}, u32[]{:S(2)}, u32[]{:S(2)}) %collective-permute-start.15) | collective-permute-done | bytes 237600 | tf_op jit(solution)/shard_map/ppermute | solution.py:37
  78.7 0.5 collective-permute-start.18
  79.2 2.2 %collective-permute-start.19 = (bf16[928,128]{1,0:T(8,128)(2,1)S(1)}, bf16[928,128]{1,0:T(8,128)(2,1)S(1)}, u32[]{:S(2)}, u32[]{:S(2)}) collective-permute-start(bf16[928,128]{1,0:T(8,128)(2,1)S(1)} %get-tuple-element.44), channel_id=1, source_target_pairs={{0,4},{2,6},{4,0},{6,2},{1,5},{3,7},{5,1},{7,3},{8,12},{10,14},{12... | collective-permute-start | bytes 712712 | tf_op jit(solution)/shard_map/ppermute | solution.py:37
  81.5 1.5 %shard_map.111 = (f32[27,128,128]{2,1,0:T(8,128)S(1)}, f32[4,128,128]{2,1,0:T(8,128)S(1)}) custom-call(s32[4]{0:T(128)S(1)} %pad_add_fusion.at_ref, bf16[128,3456]{1,0:T(8,128)(2,1)S(1)} %bitcast.18, s32[1,128]{1,0:T(1,128)S(1)} %copy-done.12, bf16[16,2560]{1,0:T(8,128)(2,1)S(1)} %collective-permute-done.ahead_ref), custom_call_target="tpu_custom_call" | custom-call | bytes 2700000 | tf_op jit(solution)/shard_map/pallas_call | solution.py:330
  83.1 6.5 %shard_map.112 = (f32[27,128,128]{2,1,0:T(8,128)S(1)}, f32[27,128,128]{2,1,0:T(8,128)S(1)}, f32[2,3456]{1,0:T(2,128)S(1)}) custom-call(s32[4]{0:T(128)S(1)} %pad_add_fusion.at_ref, bf16[928,128]{1,0:T(8,128)(2,1)S(1)} %get-tuple-element.37.refs_0_, bf16[928,128]{1,0:T(8,128)(2,1)S(1)} %collective-permute-done.14.refs_1_, ...), custom_call_target="tpu_custom_call" | custom-call | flops 167772160 | bytes 20000000 | tf_op jit(solution)/shard_map/pallas_call | solution.py:370
  89.6 0.3 collective-permute-start.20
  89.9 1.3 %collective-permute-done.20.refs_7_ = bf16[928,128]{1,0:T(8,128)(2,1)S(1)} collective-permute-done((bf16[928,128]{1,0:T(8,128)(2,1)S(1)}, bf16[928,128]{1,0:T(8,128)(2,1)S(1)}, u32[]{:S(2)}, u32[]{:S(2)}) %collective-permute-start.20) | collective-permute-done | bytes 237600 | tf_op jit(solution)/shard_map/ppermute | solution.py:41
  91.2 4.1 %shard_map.113 = (f32[8,128,128]{2,1,0:T(8,128)S(1)}, f32[8,128,128]{2,1,0:T(8,128)S(1)}, f32[2,3456]{1,0:T(2,128)S(1)}) custom-call(s32[4]{0:T(128)S(1)} %pad_add_fusion.at_ref, bf16[928,128]{1,0:T(8,128)(2,1)S(1)} %get-tuple-element.37.refs_0_, bf16[928,128]{1,0:T(8,128)(2,1)S(1)} %collective-permute-done.14.refs_1_, ...), custom_call_target="tpu_custom_call" | custom-call | flops 67108864 | bytes 8000000 | tf_op jit(solution)/shard_map/pallas_call | solution.py:379
  95.3 0.1 collective-permute-start.21
  95.4 6.0 %collective-permute-done.21 = f32[2,3456]{1,0:T(2,128)S(1)} collective-permute-done((f32[2,3456]{1,0:T(2,128)S(1)}, f32[2,3456]{1,0:T(2,128)S(1)}, u32[]{:S(2)}, u32[]{:S(2)}) %collective-permute-start.21) | collective-permute-done | bytes 27680 | tf_op jit(solution)/shard_map/ppermute | solution.py:37
  101.4 0.1 collective-permute-start.22
  101.5 2.0 %collective-permute-start.23 = (f32[2,3456]{1,0:T(2,128)S(1)}, f32[2,3456]{1,0:T(2,128)S(1)}, u32[]{:S(2)}, u32[]{:S(2)}) collective-permute-start(f32[2,3456]{1,0:T(2,128)S(1)} %pad_maximum_fusion.1), channel_id=1, source_target_pairs={{0,24},{8,32},{16,40},{24,48},{32,56},{40,64},{48,72},{56,80},{64,... | collective-permute-start | bytes 82952 | tf_op jit(solution)/shard_map/ppermute | solution.py:37
  103.4 4.1 %collective-permute-start.24 = (f32[2,3456]{1,0:T(2,128)S(1)}, f32[2,3456]{1,0:T(2,128)S(1)}, u32[]{:S(2)}, u32[]{:S(2)}) collective-permute-start(f32[2,3456]{1,0:T(2,128)S(1)} %pad_maximum_fusion.1), channel_id=1, source_target_pairs={{0,40},{8,48},{16,56},{24,64},{32,72},{40,80},{48,88},{56,96},{64,... | collective-permute-start | bytes 82952 | tf_op jit(solution)/shard_map/ppermute | solution.py:37
  107.5 0.5 collective-permute-start.25
  108.1 1.2 %collective-permute-done.23 = f32[2,3456]{1,0:T(2,128)S(1)} collective-permute-done((f32[2,3456]{1,0:T(2,128)S(1)}, f32[2,3456]{1,0:T(2,128)S(1)}, u32[]{:S(2)}, u32[]{:S(2)}) %collective-permute-start.23) | collective-permute-done | bytes 27680 | tf_op jit(solution)/shard_map/ppermute | solution.py:37
  109.3 1.0 collective-permute-done.24
  110.4 1.9 %collective-permute-done.25 = f32[2,3456]{1,0:T(2,128)S(1)} collective-permute-done((f32[2,3456]{1,0:T(2,128)S(1)}, f32[2,3456]{1,0:T(2,128)S(1)}, u32[]{:S(2)}, u32[]{:S(2)}) %collective-permute-start.25) | collective-permute-done | bytes 27680 | tf_op jit(solution)/shard_map/ppermute | solution.py:37
  112.3 0.1 slice_add_fusion.in_ref
  112.4 2.0 %shard_map.114 = bf16[128,3456]{1,0:T(8,128)(2,1)} custom-call(s32[4]{0:T(128)S(1)} %pad_add_fusion.at_ref, f32[27,128,128]{2,1,0:T(8,128)S(1)} %get-tuple-element.42.state_ref, f32[27,128,128]{2,1,0:T(8,128)S(1)} %get-tuple-element.43.prod_ref, f32[8,128,128]{2,1,0:T(8,128)S(1)} %get-tuple-element.48.far_state_ref, ...), custom_call_target="tpu_custom_call" | custom-call | bytes 4400000 | tf_op jit(solution)/shard_map/pallas_call | solution.py:391
  (54 shorter events, 0.3 us)
Async XLA Ops:
  0.0 13.0 %copy-start.13 = (bf16[1,128,2560]{2,1,0:T(8,128)(2,1)S(1)}, bf16[1,128,2560]{2,1,0:T(8,128)(2,1)}, u32[]{:S(2)}) copy-start(bf16[1,128,2560]{2,1,0:T(8,128)(2,1)} %param.11) | copy-start | bytes 1966084
  1.7 11.3 %collective-permute-start = (bf16[16,2560]{1,0:T(8,128)(2,1)S(1)}, bf16[16,2560]{1,0:T(8,128)(2,1)S(1)}, u32[]{:S(2)}, u32[]{:S(2)}) collective-permute-start(bf16[16,2560]{1,0:T(8,128)(2,1)S(1)} %fusion.1), channel_id=1, source_target_pairs={{0,8},{8,16},{16,24},{24,32},{32,40},{40,48},{48,56},{56,64},{64,7... | collective-permute-start | bytes 245768 | tf_op jit(solution)/shard_map/ppermute | solution.py:37
  5.5 27.6 %all-to-all-start = ((bf16[8,80,432]{2,1,0:T(8,128)(2,1)}), bf16[8,80,432]{2,1,0:T(8,128)(2,1)S(1)}, u32[]{:S(2)}, u32[]{:S(2)}) async-start(bf16[8,80,432]{2,1,0:T(8,128)(2,1)} %broadcast_in_dim.4), calls=%async_computation | async-start | bytes 1310720 | tf_op jit(solution)/shard_map/all_to_all | solution.py:297
  13.1 20.2 %collective-permute-start.1 = (bf16[144,2560]{1,0:T(8,128)(2,1)S(1)}, bf16[144,2560]{1,0:T(8,128)(2,1)S(1)}, u32[]{:S(2)}, u32[]{:S(2)}) collective-permute-start(bf16[144,2560]{1,0:T(8,128)(2,1)S(1)} %pad_maximum_fusion.refs_0_), channel_id=1, source_target_pairs={{0,2},{2,4},{4,6},{6,0},{1,3},{3,5},{5,7},{7,1},{8,10},{10,12},{12... | collective-permute-start | bytes 2211848 | tf_op jit(solution)/shard_map/ppermute | solution.py:37
  14.7 18.7 %collective-permute-start.2 = (bf16[144,2560]{1,0:T(8,128)(2,1)S(1)}, bf16[144,2560]{1,0:T(8,128)(2,1)S(1)}, u32[]{:S(2)}, u32[]{:S(2)}) collective-permute-start(bf16[144,2560]{1,0:T(8,128)(2,1)S(1)} %pad_maximum_fusion.refs_0_), channel_id=1, source_target_pairs={{0,6},{2,0},{4,2},{6,4},{1,7},{3,1},{5,3},{7,5},{8,14},{10,8},{12,... | collective-permute-start | bytes 2211848 | tf_op jit(solution)/shard_map/ppermute | solution.py:37
  33.4 13.6 %collective-permute-start.4 = (bf16[80,2560]{1,0:T(8,128)(2,1)S(1)}, bf16[80,2560]{1,0:T(8,128)(2,1)}, u32[]{:S(2)}, u32[]{:S(2)}) collective-permute-start(bf16[80,2560]{1,0:T(8,128)(2,1)S(1)} %slice.55), channel_id=1, source_target_pairs={{0,6},{2,0},{4,2},{6,4},{1,7},{3,1},{5,3},{7,5},{8,14},{10,8},{12,... | collective-permute-start | bytes 1228808 | tf_op jit(solution)/shard_map/ppermute | solution.py:37
  36.3 10.7 %collective-permute-start.3 = (bf16[64,2560]{1,0:T(8,128)(2,1)S(1)}, bf16[64,2560]{1,0:T(8,128)(2,1)}, u32[]{:S(2)}, u32[]{:S(2)}) collective-permute-start(bf16[64,2560]{1,0:T(8,128)(2,1)S(1)} %slice.54), channel_id=1, source_target_pairs={{0,2},{2,4},{4,6},{6,0},{1,3},{3,5},{5,7},{7,1},{8,10},{10,12},{12... | collective-permute-start | bytes 983048 | tf_op jit(solution)/shard_map/ppermute | solution.py:37
  36.4 14.3 %collective-permute-start.10 = (bf16[432,640]{1,0:T(8,128)(2,1)S(1)}, bf16[432,640]{1,0:T(8,128)(2,1)S(1)}, u32[]{:S(2)}, u32[]{:S(2)}) collective-permute-start(bf16[432,640]{1,0:T(8,128)(2,1)S(1)} %bitcast.15), channel_id=1, source_target_pairs={{0,64},{64,128},{128,192},{192,0},{1,65},{65,129},{129,193},{193,1... | collective-permute-start | bytes 1658888 | tf_op jit(solution)/shard_map/ppermute | solution.py:37
  36.7 15.3 %collective-permute-start.11 = (bf16[432,640]{1,0:T(8,128)(2,1)S(1)}, bf16[432,640]{1,0:T(8,128)(2,1)S(1)}, u32[]{:S(2)}, u32[]{:S(2)}) collective-permute-start(bf16[432,640]{1,0:T(8,128)(2,1)S(1)} %bitcast.16), channel_id=1, source_target_pairs={{0,192},{64,0},{128,64},{192,128},{1,193},{65,1},{129,65},{193,129... | collective-permute-start | bytes 1658888 | tf_op jit(solution)/shard_map/ppermute | solution.py:37
  38.5 14.2 %collective-permute-start.5 = (bf16[144,2560]{1,0:T(8,128)(2,1)S(1)}, bf16[144,2560]{1,0:T(8,128)(2,1)S(1)}, u32[]{:S(2)}, u32[]{:S(2)}) collective-permute-start(bf16[144,2560]{1,0:T(8,128)(2,1)S(1)} %pad_maximum_fusion.refs_0_), channel_id=1, source_target_pairs={{0,1},{1,0},{2,3},{3,2},{4,5},{5,4},{6,7},{7,6},{8,9},{9,8},{10,11... | collective-permute-start | bytes 2211848 | tf_op jit(solution)/shard_map/ppermute | solution.py:41
  47.0 11.1 %collective-permute-start.6 = (bf16[144,2560]{1,0:T(8,128)(2,1)S(1)}, bf16[144,2560]{1,0:T(8,128)(2,1)}, u32[]{:S(2)}, u32[]{:S(2)}) collective-permute-start(bf16[144,2560]{1,0:T(8,128)(2,1)S(1)} %collective-permute-done.1.refs_1_), channel_id=1, source_target_pairs={{0,1},{1,0},{2,3},{3,2},{4,5},{5,4},{6,7},{7,6},{8,9},{9,8},{10,11... | collective-permute-start | bytes 2211848 | tf_op jit(solution)/shard_map/ppermute | solution.py:41
  47.0 11.1 %collective-permute-start.7 = (bf16[144,2560]{1,0:T(8,128)(2,1)S(1)}, bf16[144,2560]{1,0:T(8,128)(2,1)}, u32[]{:S(2)}, u32[]{:S(2)}) collective-permute-start(bf16[144,2560]{1,0:T(8,128)(2,1)S(1)} %collective-permute-done.2.refs_2_), channel_id=1, source_target_pairs={{0,1},{1,0},{2,3},{3,2},{4,5},{5,4},{6,7},{7,6},{8,9},{9,8},{10,11... | collective-permute-start | bytes 2211848 | tf_op jit(solution)/shard_map/ppermute | solution.py:41
  50.6 1.3 %copy-start.2 = (bf16[432,640]{1,0:T(8,128)(2,1)}, bf16[432,640]{1,0:T(8,128)(2,1)S(1)}, u32[]{:S(2)}) copy-start(bf16[432,640]{1,0:T(8,128)(2,1)S(1)} %collective-permute-done.10.refs_11_) | copy-start | bytes 1658884
  50.6 4.3 %collective-permute-start.8 = (bf16[64,2560]{1,0:T(8,128)(2,1)}, bf16[64,2560]{1,0:T(8,128)(2,1)}, u32[]{:S(2)}, u32[]{:S(2)}) collective-permute-start(bf16[64,2560]{1,0:T(8,128)(2,1)} %collective-permute-done.3.refs_3_), channel_id=1, source_target_pairs={{0,1},{1,0},{2,3},{3,2},{4,5},{5,4},{6,7},{7,6},{8,9},{9,8},{10,11... | collective-permute-start | bytes 983048 | tf_op jit(solution)/shard_map/ppermute | solution.py:41
  51.9 6.2 %collective-permute-start.9 = (bf16[80,2560]{1,0:T(8,128)(2,1)}, bf16[80,2560]{1,0:T(8,128)(2,1)}, u32[]{:S(2)}, u32[]{:S(2)}) collective-permute-start(bf16[80,2560]{1,0:T(8,128)(2,1)} %collective-permute-done.4.refs_4_), channel_id=1, source_target_pairs={{0,1},{1,0},{2,3},{3,2},{4,5},{5,4},{6,7},{7,6},{8,9},{9,8},{10,11... | collective-permute-start | bytes 1228808 | tf_op jit(solution)/shard_map/ppermute | solution.py:41
  52.7 0.9 copy-start.5
  53.5 13.7 %collective-permute-start.13 = (bf16[224,640]{1,0:T(8,128)(2,1)}, bf16[224,640]{1,0:T(8,128)(2,1)}, u32[]{:S(2)}, u32[]{:S(2)}) collective-permute-start(bf16[224,640]{1,0:T(8,128)(2,1)} %slice.57), channel_id=1, source_target_pairs={{0,192},{64,0},{128,64},{192,128},{1,193},{65,1},{129,65},{193,129... | collective-permute-start | bytes 860168 | tf_op jit(solution)/shard_map/ppermute | solution.py:37
  55.0 12.2 %collective-permute-start.12 = (bf16[208,640]{1,0:T(8,128)(2,1)S(1)}, bf16[208,640]{1,0:T(8,128)(2,1)S(1)}, u32[]{:S(2)}, u32[]{:S(2)}) collective-permute-start(bf16[208,640]{1,0:T(8,128)(2,1)S(1)} %slice.56), channel_id=1, source_target_pairs={{0,64},{64,128},{128,192},{192,0},{1,65},{65,129},{129,193},{193,1... | collective-permute-start | bytes 798728 | tf_op jit(solution)/shard_map/ppermute | solution.py:37
  58.1 1.1 copy-start.3
  59.1 1.1 copy-start.6
  67.2 14.3 %copy-start.4 = (bf16[1,128,3456]{2,1,0:T(8,128)(2,1)S(1)}, bf16[1,128,3456]{2,1,0:T(8,128)(2,1)}, u32[]{:S(2)}) copy-start(bf16[1,128,3456]{2,1,0:T(8,128)(2,1)} %param.12) | copy-start | bytes 2654212
  67.2 14.3 %copy-start.12 = (s32[1,128]{1,0:T(1,128)S(1)}, s32[1,128]{1,0:T(1,128)}, u32[]{:S(2)}) copy-start(s32[1,128]{1,0:T(1,128)} %ids_ref.1) | copy-start | bytes 1540
  67.2 15.8 %copy-start = (bf16[27,128,128]{2,1,0:T(8,128)(2,1)S(1)}, bf16[27,128,128]{2,1,0:T(8,128)(2,1)}, u32[]{:S(2)}) copy-start(bf16[27,128,128]{2,1,0:T(8,128)(2,1)} %refs_15_.1) | copy-start | bytes 2654212
  67.3 15.8 %copy-start.1 = (bf16[27,128,128]{2,1,0:T(8,128)(2,1)S(1)}, bf16[27,128,128]{2,1,0:T(8,128)(2,1)}, u32[]{:S(2)}) copy-start(bf16[27,128,128]{2,1,0:T(8,128)(2,1)} %refs_16_.1) | copy-start | bytes 2654212
  67.3 15.8 %copy-start.7 = (f32[4,3456]{1,0:T(4,128)S(1)}, f32[4,3456]{1,0:T(4,128)}, u32[]{:S(2)}) copy-start(f32[4,3456]{1,0:T(4,128)} %refs_10_.1) | copy-start | bytes 165892
  67.3 15.8 %copy-start.8 = (f32[3456]{0:T(1024)S(1)}, f32[3456]{0:T(1024)}, u32[]{:S(2)}) copy-start(f32[3456]{0:T(1024)} %param.16) | copy-start | bytes 41476
  67.3 15.8 %copy-start.9 = (f32[3456]{0:T(1024)S(1)}, f32[3456]{0:T(1024)}, u32[]{:S(2)}) copy-start(f32[3456]{0:T(1024)} %param.19) | copy-start | bytes 41476
  67.3 15.8 %copy-start.10 = (f32[3456]{0:T(1024)S(1)}, f32[3456]{0:T(1024)}, u32[]{:S(2)}) copy-start(f32[3456]{0:T(1024)} %param.20) | copy-start | bytes 41476
  67.3 15.8 %copy-start.11 = (f32[3456]{0:T(1024)S(1)}, f32[3456]{0:T(1024)}, u32[]{:S(2)}) copy-start(f32[3456]{0:T(1024)} %param.21) | copy-start | bytes 41476
  69.8 8.9 %collective-permute-start.15 = (bf16[928,128]{1,0:T(8,128)(2,1)S(1)}, bf16[928,128]{1,0:T(8,128)(2,1)S(1)}, u32[]{:S(2)}, u32[]{:S(2)}) collective-permute-start(bf16[928,128]{1,0:T(8,128)(2,1)S(1)} %get-tuple-element.38), channel_id=1, source_target_pairs={{0,2},{2,4},{4,6},{6,0},{1,3},{3,5},{5,7},{7,1},{8,10},{10,12},{12... | collective-permute-start | bytes 712712 | tf_op jit(solution)/shard_map/ppermute | solution.py:37
  70.2 8.5 %collective-permute-start.17 = (bf16[928,128]{1,0:T(8,128)(2,1)S(1)}, bf16[928,128]{1,0:T(8,128)(2,1)S(1)}, u32[]{:S(2)}, u32[]{:S(2)}) collective-permute-start(bf16[928,128]{1,0:T(8,128)(2,1)S(1)} %get-tuple-element.39), channel_id=1, source_target_pairs={{0,6},{2,0},{4,2},{6,4},{1,7},{3,1},{5,3},{7,5},{8,14},{10,8},{12,... | collective-permute-start | bytes 712712 | tf_op jit(solution)/shard_map/ppermute | solution.py:37
  73.1 9.9 %collective-permute-start.14 = (bf16[928,128]{1,0:T(8,128)(2,1)S(1)}, bf16[928,128]{1,0:T(8,128)(2,1)S(1)}, u32[]{:S(2)}, u32[]{:S(2)}) collective-permute-start(bf16[928,128]{1,0:T(8,128)(2,1)S(1)} %get-tuple-element.37.refs_0_), channel_id=1, source_target_pairs={{0,1},{1,0},{2,3},{3,2},{4,5},{5,4},{6,7},{7,6},{8,9},{9,8},{10,11... | collective-permute-start | bytes 712712 | tf_op jit(solution)/shard_map/ppermute | solution.py:41
  78.7 4.3 %collective-permute-start.16 = (bf16[928,128]{1,0:T(8,128)(2,1)S(1)}, bf16[928,128]{1,0:T(8,128)(2,1)S(1)}, u32[]{:S(2)}, u32[]{:S(2)}) collective-permute-start(bf16[928,128]{1,0:T(8,128)(2,1)S(1)} %collective-permute-done.15.refs_2_), channel_id=1, source_target_pairs={{0,1},{1,0},{2,3},{3,2},{4,5},{5,4},{6,7},{7,6},{8,9},{9,8},{10,11... | collective-permute-start | bytes 712712 | tf_op jit(solution)/shard_map/ppermute | solution.py:41
  78.7 4.3 %collective-permute-start.18 = (bf16[928,128]{1,0:T(8,128)(2,1)S(1)}, bf16[928,128]{1,0:T(8,128)(2,1)S(1)}, u32[]{:S(2)}, u32[]{:S(2)}) collective-permute-start(bf16[928,128]{1,0:T(8,128)(2,1)S(1)} %collective-permute-done.17.refs_4_), channel_id=1, source_target_pairs={{0,1},{1,0},{2,3},{3,2},{4,5},{5,4},{6,7},{7,6},{8,9},{9,8},{10,11... | collective-permute-start | bytes 712712 | tf_op jit(solution)/shard_map/ppermute | solution.py:41
  79.2 10.4 %collective-permute-start.19 = (bf16[928,128]{1,0:T(8,128)(2,1)S(1)}, bf16[928,128]{1,0:T(8,128)(2,1)S(1)}, u32[]{:S(2)}, u32[]{:S(2)}) collective-permute-start(bf16[928,128]{1,0:T(8,128)(2,1)S(1)} %get-tuple-element.44), channel_id=1, source_target_pairs={{0,4},{2,6},{4,0},{6,2},{1,5},{3,7},{5,1},{7,3},{8,12},{10,14},{12... | collective-permute-start | bytes 712712 | tf_op jit(solution)/shard_map/ppermute | solution.py:37
  89.6 1.6 %collective-permute-start.20 = (bf16[928,128]{1,0:T(8,128)(2,1)S(1)}, bf16[928,128]{1,0:T(8,128)(2,1)S(1)}, u32[]{:S(2)}, u32[]{:S(2)}) collective-permute-start(bf16[928,128]{1,0:T(8,128)(2,1)S(1)} %collective-permute-done.19.refs_6_), channel_id=1, source_target_pairs={{0,1},{1,0},{2,3},{3,2},{4,5},{5,4},{6,7},{7,6},{8,9},{9,8},{10,11... | collective-permute-start | bytes 712712 | tf_op jit(solution)/shard_map/ppermute | solution.py:41
  95.3 6.0 %collective-permute-start.21 = (f32[2,3456]{1,0:T(2,128)S(1)}, f32[2,3456]{1,0:T(2,128)S(1)}, u32[]{:S(2)}, u32[]{:S(2)}) collective-permute-start(f32[2,3456]{1,0:T(2,128)S(1)} %get-tuple-element.50), channel_id=1, source_target_pairs={{0,8},{8,16},{16,24},{24,32},{32,40},{40,48},{48,56},{56,64},{64,7... | collective-permute-start | bytes 82952 | tf_op jit(solution)/shard_map/ppermute | solution.py:37
  101.4 6.7 %collective-permute-start.22 = (f32[2,3456]{1,0:T(2,128)S(1)}, f32[2,3456]{1,0:T(2,128)S(1)}, u32[]{:S(2)}, u32[]{:S(2)}) collective-permute-start(f32[2,3456]{1,0:T(2,128)S(1)} %pad_maximum_fusion.1), channel_id=1, source_target_pairs={{0,8},{8,16},{16,24},{24,32},{32,40},{40,48},{48,56},{56,64},{64,7... | collective-permute-start | bytes 82952 | tf_op jit(solution)/shard_map/ppermute | solution.py:37
  101.5 7.8 %collective-permute-start.23 = (f32[2,3456]{1,0:T(2,128)S(1)}, f32[2,3456]{1,0:T(2,128)S(1)}, u32[]{:S(2)}, u32[]{:S(2)}) collective-permute-start(f32[2,3456]{1,0:T(2,128)S(1)} %pad_maximum_fusion.1), channel_id=1, source_target_pairs={{0,24},{8,32},{16,40},{24,48},{32,56},{40,64},{48,72},{56,80},{64,... | collective-permute-start | bytes 82952 | tf_op jit(solution)/shard_map/ppermute | solution.py:37
  103.4 6.9 %collective-permute-start.24 = (f32[2,3456]{1,0:T(2,128)S(1)}, f32[2,3456]{1,0:T(2,128)S(1)}, u32[]{:S(2)}, u32[]{:S(2)}) collective-permute-start(f32[2,3456]{1,0:T(2,128)S(1)} %pad_maximum_fusion.1), channel_id=1, source_target_pairs={{0,40},{8,48},{16,56},{24,64},{32,72},{40,80},{48,88},{56,96},{64,... | collective-permute-start | bytes 82952 | tf_op jit(solution)/shard_map/ppermute | solution.py:37
  107.5 4.8 %collective-permute-start.25 = (f32[2,3456]{1,0:T(2,128)S(1)}, f32[2,3456]{1,0:T(2,128)S(1)}, u32[]{:S(2)}, u32[]{:S(2)}) collective-permute-start(f32[2,3456]{1,0:T(2,128)S(1)} %pad_maximum_fusion.1), channel_id=1, source_target_pairs={{0,56},{8,64},{16,72},{24,80},{32,88},{40,96},{48,104},{56,112},{6... | collective-permute-start | bytes 82952 | tf_op jit(solution)/shard_map/ppermute | solution.py:37

commit v7 on v6

--- a/solution.py
+++ b/solution.py
@@ -12,6 +12,7 @@
 BF16 = jnp.bfloat16
 VMEM = pl.BlockSpec(memory_space=pltpu.VMEM)
 ANY = pl.BlockSpec(memory_space=pl.ANY)
+HBM = pl.BlockSpec(memory_space=pltpu.HBM)
 SMEM = pl.BlockSpec(memory_space=pltpu.SMEM)
 
 LENGTH = 128
@@ -94,16 +95,19 @@
         pairs.append((ref.at[pl.ds(0, main)], rows_ref.at[pl.ds(half * ROWS + top, main)]))
         rest = half * ROWS + 4 * LENGTH + min(n, 3) * AHEAD
         pairs.append((ref.at[pl.ds(main, AHEAD)], rows_ref.at[pl.ds(rest, AHEAD)]))
-    for copy in copies(pairs, sems):
-        copy.wait()
+    made = copies(pairs, sems)
+    far = pl.ds(pl.multiple_of(lax.rem(y + 2, 4) * 640, 128), 640)
     for half in range(2):
+        for copy in made[9 * half : 9 * half + 9]:
+            copy.wait()
+        mine = slice(half * ROWS, (half + 1) * ROWS)
         total = None
         for w_ref, back in zip(weights, (0, 3, 1)):
             at = pl.ds(pl.multiple_of(lax.rem(y + back, 4) * 640, 128), 640)
-            part = across(w_ref[...], rows_ref[half * ROWS : (half + 1) * ROWS, at])
+            part = across(w_ref[...], rows_ref[mine, at])
             total = part if total is None else total + part
         part_ref[half] = total
-    far_ref[...] = rows_ref[:, pl.ds(pl.multiple_of(lax.rem(y + 2, 4) * 640, 128), 640)]
+        far_ref[mine, :] = rows_ref[mine, far]
 
 
 def pack_kernel(part_ref, far_ref, w0_ref, w1_ref, *refs):
@@ -238,18 +242,23 @@
     start = far_head(at_ref[0])
 
     def near(i, carry):
-        h = lax.rem(start + FAR + i, HEADS)
-        lanes = pl.ds(pl.multiple_of(h * HEAD, HEAD), HEAD)
-        out_ref[:, lanes] = (state_ref[h] + prod_ref[h] * in_ref[:, lanes]).astype(BF16)
+        for side in range(4):
+            h = lax.rem(start + FAR + 4 * i + side, HEADS)
+            lanes = pl.ds(pl.multiple_of(h * HEAD, HEAD), HEAD)
+            out_ref[:, lanes] = (state_ref[h] + prod_ref[h] * in_ref[:, lanes]).astype(BF16)
         return carry
 
     def far(i, carry):
-        lanes = pl.ds(pl.multiple_of((start + i) * HEAD, HEAD), HEAD)
-        out_ref[:, lanes] = (far_state_ref[i] + far_prod_ref[i] * in_ref[:, lanes]).astype(BF16)
+        for side in range(4):
+            n = 4 * i + side
+            lanes = pl.ds(pl.multiple_of((start + n) * HEAD, HEAD), HEAD)
+            out_ref[:, lanes] = (far_state_ref[n] + far_prod_ref[n] * in_ref[:, lanes]).astype(
+                BF16
+            )
         return carry
 
-    lax.fori_loop(0, HEADS - FAR, near, 0)
-    lax.fori_loop(0, FAR, far, 0)
+    lax.fori_loop(0, NEAR // 4, near, 0)
+    lax.fori_loop(0, FAR // 4, far, 0)
 
 
 def call(kernel, outs, ins, scratch=(), room=16, flops=0, moved=0):
@@ -297,7 +306,17 @@
     column = lax.all_to_all(copied, "z", 0, 0, tiled=True).reshape(-1, COLS).T
     rows = jnp.concatenate([own, ahead], axis=0)
     one_back, one_ahead = shift(rows, "x", 1), shift(rows, "x", -1)
-    column, one_back, one_ahead = lax.optimization_barrier((column, one_back, one_ahead))
+    gelu, masks = call(
+        prepare_kernel,
+        (
+            jax.ShapeDtypeStruct((HEADS, LENGTH, HEAD), F32),
+            jax.ShapeDtypeStruct((4, LENGTH, HEAD), F32),
+        ),
+        [SMEM] + [VMEM] * 3,
+        [pltpu.VMEM((LENGTH + HALO, HEAD), F32)],
+        moved=2_700_000,
+    )(at, gate_input[0], segment_ids, ahead)
+    column, one_back, one_ahead, gelu, masks = lax.optimization_barrier((column, one_back, one_ahead, gelu, masks))
     upper = shift(one_back[:SPLIT], "x", 1)
     lower = shift(one_ahead[SPLIT:], "x", -1)
     streams = [rows, one_back, one_ahead, upper, lower]
@@ -314,7 +333,7 @@
             jax.ShapeDtypeStruct((2, COLS, ROWS), F32),
             jax.ShapeDtypeStruct((2 * ROWS, 640), BF16),
         ),
-        [SMEM] + [ANY] * 10 + [VMEM] * 3,
+        [SMEM] + [ANY] * 5 + [HBM] * 5 + [VMEM] * 3,
         [pltpu.VMEM((2 * ROWS, DEPTH), BF16), pltpu.SemaphoreType.DMA((18,))],
         flops=2 * 1056 * 1920 * 432,
         moved=9_000_000,
@@ -327,16 +346,6 @@
         flops=2 * 1056 * 640 * 432,
         moved=5_000_000,
     )(part, rows_far, first, second)
-    gelu, masks = call(
-        prepare_kernel,
-        (
-            jax.ShapeDtypeStruct((HEADS, LENGTH, HEAD), F32),
-            jax.ShapeDtypeStruct((4, LENGTH, HEAD), F32),
-        ),
-        [SMEM] + [VMEM] * 3,
-        [pltpu.VMEM((LENGTH + HALO, HEAD), F32)],
-        moved=2_700_000,
-    )(at, gate_input[0], segment_ids, ahead)
     got = [
         sent[0],
         shift(sent[2], "x", 1),

time: 115 us -> 113 us (0.983)
  waiting for transfers between devices: 46.7 us -> 44.7 us
    all_to_all x1, waiting for transfers between devices: 16.6 us -> 13.9 us  [body(): column = lax.all_to_all(copied, 'z', 0, 0, tiled=True).reshape(-1, COLS).T]
    pallas_call x1, Pallas kernels: 6.93 us -> 9.06 us  [body(): call(project_kernel, (jax.ShapeDtypeStruct((2, COLS, ROWS), F32), jax.Sha...]
    unnamed x28 -> x20, local copies, waits for them, and re-layouts: 3.09 us -> 1.22 us
  transfers between devices with their start and end apart: 27 -> 27, of which waited for: 10 -> 10; matrix products, arithmetic and copies ran while one was open for 3% -> 4% of each run, Pallas kernels for 13% -> 15%
where the time goes in v7:
time: 113 us
  waiting for transfers between devices  44.7 us (40%)
  starting transfers between devices  34.9 us (31%)
  Pallas kernels  24.2 us (21%)
  local copies, waits for them, and re-layouts  7.43 us (7%)
    ppermute x17, waiting for transfers between devices, shift(): lax.ppermute(value, axis, [(i, (i + by) % count) for i in range(count)])  29.3 us
    ppermute x17, starting transfers between devices, shift(): lax.ppermute(value, axis, [(i, (i + by) % count) for i in range(count)])  26.3 us
    all_to_all x1, waiting for transfers between devices, body(): column = lax.all_to_all(copied, 'z', 0, 0, tiled=True).reshape(-1, COLS).T  13.9 us
    pallas_call x1, Pallas kernels, body(): call(project_kernel, (jax.ShapeDtypeStruct((2, COLS, ROWS), F32), jax.Sha...  9.06 us
    all_to_all x1, starting transfers between devices, body(): column = lax.all_to_all(copied, 'z', 0, 0, tiled=True).reshape(-1, COLS).T  7.57 us
    pallas_call x1, Pallas kernels, body(): call(near_kernel, walked(HEADS), [SMEM] + [ANY] * 6 + [VMEM] * 9, scratch...  6.41 us
    pallas_call x1, Pallas kernels, body(): call(far_kernel, walked(FAR), [SMEM] + [ANY] * 8 + [VMEM] * 10, scratch,...  4.05 us
  transfers between devices with their start and end apart: 27, of which 10 were waited for; matrix products, arithmetic and copies ran while one was open for 4% of the time, Pallas kernels for 15%

profile of v7, /device:TPU:24, one launch (start us, length us, event | category | flops | bytes accessed | tf_op | source)
XLA Modules:
  0.0 112.6 jit_solution(17050697627694847052)
XLA Ops:
  0.0 1.0 slice_bitcast_fusion
  1.0 0.7 convert_element_type.5
  1.7 2.0 %collective-permute-start = (bf16[16,2560]{1,0:T(8,128)(2,1)S(1)}, bf16[16,2560]{1,0:T(8,128)(2,1)S(1)}, u32[]{:S(2)}, u32[]{:S(2)}) collective-permute-start(bf16[16,2560]{1,0:T(8,128)(2,1)S(1)} %fusion.1), channel_id=1, source_target_pairs={{0,8},{8,16},{16,24},{24,32},{32,40},{40,48},{48,56},{56,64},{64,7... | collective-permute-start | bytes 245768 | tf_op jit(solution)/shard_map/ppermute | solution.py:38
  3.7 1.8 %broadcast_in_dim.4 = bf16[8,80,432]{2,1,0:T(8,128)(2,1)} broadcast(bf16[80,432]{1,0:T(8,128)(2,1)} %param.14), dimensions={1,2} | broadcast | bytes 622080 | tf_op jit(solution)/shard_map/broadcast_in_dim | solution.py:305
  5.5 7.6 %all-to-all-start = ((bf16[8,80,432]{2,1,0:T(8,128)(2,1)}), bf16[8,80,432]{2,1,0:T(8,128)(2,1)}, u32[]{:S(2)}, u32[]{:S(2)}) async-start(bf16[8,80,432]{2,1,0:T(8,128)(2,1)} %broadcast_in_dim.4), calls=%async_computation | async-start | bytes 1310720 | tf_op jit(solution)/shard_map/all_to_all | solution.py:306
  13.0 0.1 pad_maximum_fusion.refs_0_
  13.1 1.6 %collective-permute-start.1 = (bf16[144,2560]{1,0:T(8,128)(2,1)S(1)}, bf16[144,2560]{1,0:T(8,128)(2,1)}, u32[]{:S(2)}, u32[]{:S(2)}) collective-permute-start(bf16[144,2560]{1,0:T(8,128)(2,1)S(1)} %pad_maximum_fusion.refs_0_), channel_id=1, source_target_pairs={{0,2},{2,4},{4,6},{6,0},{1,3},{3,5},{5,7},{7,1},{8,10},{10,12},{12... | collective-permute-start | bytes 2211848 | tf_op jit(solution)/shard_map/ppermute | solution.py:38
  14.7 1.7 %collective-permute-start.2 = (bf16[144,2560]{1,0:T(8,128)(2,1)S(1)}, bf16[144,2560]{1,0:T(8,128)(2,1)}, u32[]{:S(2)}, u32[]{:S(2)}) collective-permute-start(bf16[144,2560]{1,0:T(8,128)(2,1)S(1)} %pad_maximum_fusion.refs_0_), channel_id=1, source_target_pairs={{0,6},{2,0},{4,2},{6,4},{1,7},{3,1},{5,3},{7,5},{8,14},{10,8},{12,... | collective-permute-start | bytes 2211848 | tf_op jit(solution)/shard_map/ppermute | solution.py:38
  16.4 0.1 pad_add_fusion.at_ref
  16.5 1.2 %copy-done.2 = bf16[1,128,3456]{2,1,0:T(8,128)(2,1)S(1)} copy-done((bf16[1,128,3456]{2,1,0:T(8,128)(2,1)S(1)}, bf16[1,128,3456]{2,1,0:T(8,128)(2,1)}, u32[]{:S(2)}) %copy-start.2) | copy-done | bytes 884760
  17.7 1.5 %shard_map.109 = (f32[27,128,128]{2,1,0:T(8,128)S(1)}, f32[4,128,128]{2,1,0:T(8,128)S(1)}) custom-call(s32[4]{0:T(128)S(1)} %pad_add_fusion.at_ref, bf16[128,3456]{1,0:T(8,128)(2,1)S(1)} %bitcast.18, s32[1,128]{1,0:T(1,128)S(1)} %copy-done.8, bf16[16,2560]{1,0:T(8,128)(2,1)S(1)} %collective-permute-done.ahead_ref), custom_call_target="tpu_custom_call" | custom-call | bytes 2700000 | tf_op jit(solution)/shard_map/pallas_call | solution.py:309
  19.2 13.9 %all-to-all-done = bf16[8,80,432]{2,1,0:T(8,128)(2,1)} async-done(((bf16[8,80,432]{2,1,0:T(8,128)(2,1)}), bf16[8,80,432]{2,1,0:T(8,128)(2,1)}, u32[]{:S(2)}, u32[]{:S(2)}) %all-to-all-start) | async-done | bytes 552992 | tf_op jit(solution)/shard_map/all_to_all | solution.py:306
  33.2 1.4 %copy.13 = bf16[640,432]{0,1:T(8,128)(2,1)S(1)} copy(bf16[640,432]{1,0:T(8,128)(2,1)} %bitcast.6) | data formatting | bytes 1105920 | tf_op jit(solution)/shard_map/reshape | solution.py:306
  34.6 1.0 slice.55
  35.6 2.8 %collective-permute-start.4 = (bf16[80,2560]{1,0:T(8,128)(2,1)S(1)}, bf16[80,2560]{1,0:T(8,128)(2,1)S(1)}, u32[]{:S(2)}, u32[]{:S(2)}) collective-permute-start(bf16[80,2560]{1,0:T(8,128)(2,1)S(1)} %slice.55), channel_id=1, source_target_pairs={{0,6},{2,0},{4,2},{6,4},{1,7},{3,1},{5,3},{7,5},{8,14},{10,8},{12,... | collective-permute-start | bytes 1228808 | tf_op jit(solution)/shard_map/ppermute | solution.py:38
  38.4 1.0 slice.54
  39.4 0.1 collective-permute-start.3
  39.5 0.3 collective-permute-start.10
  39.8 1.8 %collective-permute-start.11 = (bf16[432,640]{1,0:T(8,128)(2,1)S(1)}, bf16[432,640]{1,0:T(8,128)(2,1)S(1)}, u32[]{:S(2)}, u32[]{:S(2)}) collective-permute-start(bf16[432,640]{1,0:T(8,128)(2,1)S(1)} %bitcast.16), channel_id=1, source_target_pairs={{0,192},{64,0},{128,64},{192,128},{1,193},{65,1},{129,65},{193,129... | collective-permute-start | bytes 1658888 | tf_op jit(solution)/shard_map/ppermute | solution.py:38
  41.6 8.4 %collective-permute-done.3.refs_3_ = bf16[64,2560]{1,0:T(8,128)(2,1)S(1)} collective-permute-done((bf16[64,2560]{1,0:T(8,128)(2,1)S(1)}, bf16[64,2560]{1,0:T(8,128)(2,1)S(1)}, u32[]{:S(2)}, u32[]{:S(2)}) %collective-permute-start.3) | collective-permute-done | bytes 327712 | tf_op jit(solution)/shard_map/ppermute | solution.py:38
  50.1 0.5 collective-permute-start.7
  50.6 3.2 %collective-permute-done.10.refs_11_ = bf16[432,640]{1,0:T(8,128)(2,1)S(1)} collective-permute-done((bf16[432,640]{1,0:T(8,128)(2,1)S(1)}, bf16[432,640]{1,0:T(8,128)(2,1)S(1)}, u32[]{:S(2)}, u32[]{:S(2)}) %collective-permute-start.10) | collective-permute-done | bytes 552992 | tf_op jit(solution)/shard_map/ppermute | solution.py:38
  53.8 1.3 %collective-permute-done.11.refs_12_ = bf16[432,640]{1,0:T(8,128)(2,1)S(1)} collective-permute-done((bf16[432,640]{1,0:T(8,128)(2,1)S(1)}, bf16[432,640]{1,0:T(8,128)(2,1)S(1)}, u32[]{:S(2)}, u32[]{:S(2)}) %collective-permute-start.11) | collective-permute-done | bytes 552992 | tf_op jit(solution)/shard_map/ppermute | solution.py:38
  55.1 0.5 collective-permute-start.13
  55.7 3.0 %collective-permute-start.12 = (bf16[208,640]{1,0:T(8,128)(2,1)S(1)}, bf16[208,640]{1,0:T(8,128)(2,1)S(1)}, u32[]{:S(2)}, u32[]{:S(2)}) collective-permute-start(bf16[208,640]{1,0:T(8,128)(2,1)S(1)} %slice.56), channel_id=1, source_target_pairs={{0,64},{64,128},{128,192},{192,0},{1,65},{65,129},{129,193},{193,1... | collective-permute-start | bytes 798728 | tf_op jit(solution)/shard_map/ppermute | solution.py:38
  58.7 9.1 %shard_map.110 = (f32[2,432,576]{2,1,0:T(8,128)S(1)}, bf16[1152,640]{1,0:T(8,128)(2,1)S(1)}) custom-call(s32[4]{0:T(128)S(1)} %pad_add_fusion.at_ref, bf16[144,2560]{1,0:T(8,128)(2,1)S(1)} %pad_maximum_fusion.refs_0_, bf16[144,2560]{1,0:T(8,128)(2,1)} %collective-permute-done.1.refs_1_, bf16[144,2560]{1,0:T(8,128)(2,1)} %collective-permute-done.2.refs_2_, ...), custom_call_target="tpu_custom_call" | custom-call | flops 1751777280 | bytes 9000000 | tf_op jit(solution)/shard_map/pallas_call | solution.py:330
  67.8 0.0 copy-start.1
  67.9 0.0 copy-start.3
  67.9 1.4 %shard_map.111 = (bf16[928,128]{1,0:T(8,128)(2,1)S(1)}, bf16[928,128]{1,0:T(8,128)(2,1)S(1)}, bf16[928,128]{1,0:T(8,128)(2,1)S(1)}, bf16[928,128]{1,0:T(8,128)(2,1)S(1)}) custom-call(f32[2,432,576]{2,1,0:T(8,128)S(1)} %get-tuple-element.39.part_ref, bf16[1152,640]{1,0:T(8,128)(2,1)S(1)} %get-tuple-element.40.far_ref, ...), custom_call_target="tpu_custom_call" | custom-call | flops 583925760 | bytes 5000000 | tf_op jit(solution)/shard_map/pallas_call | solution.py:341
  69.3 0.4 collective-permute-start.15
  69.7 2.9 %collective-permute-start.17 = (bf16[928,128]{1,0:T(8,128)(2,1)S(1)}, bf16[928,128]{1,0:T(8,128)(2,1)S(1)}, u32[]{:S(2)}, u32[]{:S(2)}) collective-permute-start(bf16[928,128]{1,0:T(8,128)(2,1)S(1)} %get-tuple-element.43), channel_id=1, source_target_pairs={{0,6},{2,0},{4,2},{6,4},{1,7},{3,1},{5,3},{7,5},{8,14},{10,8},{12,... | collective-permute-start | bytes 712712 | tf_op jit(solution)/shard_map/ppermute | solution.py:38
  72.6 5.6 %collective-permute-done.15.refs_2_ = bf16[928,128]{1,0:T(8,128)(2,1)S(1)} collective-permute-done((bf16[928,128]{1,0:T(8,128)(2,1)S(1)}, bf16[928,128]{1,0:T(8,128)(2,1)S(1)}, u32[]{:S(2)}, u32[]{:S(2)}) %collective-permute-start.15) | collective-permute-done | bytes 237600 | tf_op jit(solution)/shard_map/ppermute | solution.py:38
  78.2 0.5 collective-permute-start.18
  78.7 2.2 %collective-permute-start.19 = (bf16[928,128]{1,0:T(8,128)(2,1)S(1)}, bf16[928,128]{1,0:T(8,128)(2,1)S(1)}, u32[]{:S(2)}, u32[]{:S(2)}) collective-permute-start(bf16[928,128]{1,0:T(8,128)(2,1)S(1)} %get-tuple-element.48), channel_id=1, source_target_pairs={{0,4},{2,6},{4,0},{6,2},{1,5},{3,7},{5,1},{7,3},{8,12},{10,14},{12... | collective-permute-start | bytes 712712 | tf_op jit(solution)/shard_map/ppermute | solution.py:38
  81.0 6.4 %shard_map.112 = (f32[27,128,128]{2,1,0:T(8,128)S(1)}, f32[27,128,128]{2,1,0:T(8,128)S(1)}, f32[2,3456]{1,0:T(2,128)S(1)}) custom-call(s32[4]{0:T(128)S(1)} %pad_add_fusion.at_ref, bf16[928,128]{1,0:T(8,128)(2,1)S(1)} %get-tuple-element.41.refs_0_, bf16[928,128]{1,0:T(8,128)(2,1)S(1)} %collective-permute-done.14.refs_1_, ...), custom_call_target="tpu_custom_call" | custom-call | flops 167772160 | bytes 20000000 | tf_op jit(solution)/shard_map/pallas_call | solution.py:379
  87.5 0.4 collective-permute-done.19.refs_6_
  87.9 1.5 %collective-permute-done.20.refs_7_ = bf16[928,128]{1,0:T(8,128)(2,1)S(1)} collective-permute-done((bf16[928,128]{1,0:T(8,128)(2,1)S(1)}, bf16[928,128]{1,0:T(8,128)(2,1)S(1)}, u32[]{:S(2)}, u32[]{:S(2)}) %collective-permute-start.20) | collective-permute-done | bytes 237600 | tf_op jit(solution)/shard_map/ppermute | solution.py:42
  89.4 4.0 %shard_map.113 = (f32[8,128,128]{2,1,0:T(8,128)S(1)}, f32[8,128,128]{2,1,0:T(8,128)S(1)}, f32[2,3456]{1,0:T(2,128)S(1)}) custom-call(s32[4]{0:T(128)S(1)} %pad_add_fusion.at_ref, bf16[928,128]{1,0:T(8,128)(2,1)S(1)} %get-tuple-element.41.refs_0_, bf16[928,128]{1,0:T(8,128)(2,1)S(1)} %collective-permute-done.14.refs_1_, ...), custom_call_target="tpu_custom_call" | custom-call | flops 67108864 | bytes 8000000 | tf_op jit(solution)/shard_map/pallas_call | solution.py:388
  93.5 0.1 collective-permute-start.21
  93.6 6.0 %collective-permute-done.21 = f32[2,3456]{1,0:T(2,128)S(1)} collective-permute-done((f32[2,3456]{1,0:T(2,128)S(1)}, f32[2,3456]{1,0:T(2,128)S(1)}, u32[]{:S(2)}, u32[]{:S(2)}) %collective-permute-start.21) | collective-permute-done | bytes 27680 | tf_op jit(solution)/shard_map/ppermute | solution.py:38
  99.6 0.3 collective-permute-start.22
  99.9 0.9 collective-permute-start.23
  100.8 5.2 %collective-permute-start.24 = (f32[2,3456]{1,0:T(2,128)S(1)}, f32[2,3456]{1,0:T(2,128)S(1)}, u32[]{:S(2)}, u32[]{:S(2)}) collective-permute-start(f32[2,3456]{1,0:T(2,128)S(1)} %pad_maximum_fusion.1), channel_id=1, source_target_pairs={{0,40},{8,48},{16,56},{24,64},{32,72},{40,80},{48,88},{56,96},{64,... | collective-permute-start | bytes 82952 | tf_op jit(solution)/shard_map/ppermute | solution.py:38
  106.0 0.4 collective-permute-start.25
  106.4 1.3 %collective-permute-done.23 = f32[2,3456]{1,0:T(2,128)S(1)} collective-permute-done((f32[2,3456]{1,0:T(2,128)S(1)}, f32[2,3456]{1,0:T(2,128)S(1)}, u32[]{:S(2)}, u32[]{:S(2)}) %collective-permute-start.23) | collective-permute-done | bytes 27680 | tf_op jit(solution)/shard_map/ppermute | solution.py:38
  107.8 3.0 %collective-permute-done.25 = f32[2,3456]{1,0:T(2,128)S(1)} collective-permute-done((f32[2,3456]{1,0:T(2,128)S(1)}, f32[2,3456]{1,0:T(2,128)S(1)}, u32[]{:S(2)}, u32[]{:S(2)}) %collective-permute-start.25) | collective-permute-done | bytes 27680 | tf_op jit(solution)/shard_map/ppermute | solution.py:38
  110.7 0.1 slice_add_fusion.in_ref
  110.8 1.8 %shard_map.114 = bf16[128,3456]{1,0:T(8,128)(2,1)} custom-call(s32[4]{0:T(128)S(1)} %pad_add_fusion.at_ref, f32[27,128,128]{2,1,0:T(8,128)S(1)} %get-tuple-element.46.state_ref, f32[27,128,128]{2,1,0:T(8,128)S(1)} %get-tuple-element.47.prod_ref, f32[8,128,128]{2,1,0:T(8,128)S(1)} %get-tuple-element.52.far_state_ref, ...), custom_call_target="tpu_custom_call" | custom-call | bytes 4400000 | tf_op jit(solution)/shard_map/pallas_call | solution.py:400
  (46 shorter events, 0.3 us)
Async XLA Ops:
  0.0 13.0 %copy-start.9 = (bf16[1,128,2560]{2,1,0:T(8,128)(2,1)S(1)}, bf16[1,128,2560]{2,1,0:T(8,128)(2,1)}, u32[]{:S(2)}) copy-start(bf16[1,128,2560]{2,1,0:T(8,128)(2,1)} %param.11) | copy-start | bytes 1966084
  1.7 14.8 %copy-start.8 = (s32[1,128]{1,0:T(1,128)S(1)}, s32[1,128]{1,0:T(1,128)}, u32[]{:S(2)}) copy-start(s32[1,128]{1,0:T(1,128)} %ids_ref.1) | copy-start | bytes 1540
  1.7 11.3 %collective-permute-start = (bf16[16,2560]{1,0:T(8,128)(2,1)S(1)}, bf16[16,2560]{1,0:T(8,128)(2,1)S(1)}, u32[]{:S(2)}, u32[]{:S(2)}) collective-permute-start(bf16[16,2560]{1,0:T(8,128)(2,1)S(1)} %fusion.1), channel_id=1, source_target_pairs={{0,8},{8,16},{16,24},{24,32},{32,40},{40,48},{48,56},{56,64},{64,7... | collective-permute-start | bytes 245768 | tf_op jit(solution)/shard_map/ppermute | solution.py:38
  5.5 27.7 %all-to-all-start = ((bf16[8,80,432]{2,1,0:T(8,128)(2,1)}), bf16[8,80,432]{2,1,0:T(8,128)(2,1)}, u32[]{:S(2)}, u32[]{:S(2)}) async-start(bf16[8,80,432]{2,1,0:T(8,128)(2,1)} %broadcast_in_dim.4), calls=%async_computation | async-start | bytes 1310720 | tf_op jit(solution)/shard_map/all_to_all | solution.py:306
  13.1 21.4 %collective-permute-start.1 = (bf16[144,2560]{1,0:T(8,128)(2,1)S(1)}, bf16[144,2560]{1,0:T(8,128)(2,1)}, u32[]{:S(2)}, u32[]{:S(2)}) collective-permute-start(bf16[144,2560]{1,0:T(8,128)(2,1)S(1)} %pad_maximum_fusion.refs_0_), channel_id=1, source_target_pairs={{0,2},{2,4},{4,6},{6,0},{1,3},{3,5},{5,7},{7,1},{8,10},{10,12},{12... | collective-permute-start | bytes 2211848 | tf_op jit(solution)/shard_map/ppermute | solution.py:38
  14.7 19.9 %collective-permute-start.2 = (bf16[144,2560]{1,0:T(8,128)(2,1)S(1)}, bf16[144,2560]{1,0:T(8,128)(2,1)}, u32[]{:S(2)}, u32[]{:S(2)}) collective-permute-start(bf16[144,2560]{1,0:T(8,128)(2,1)S(1)} %pad_maximum_fusion.refs_0_), channel_id=1, source_target_pairs={{0,6},{2,0},{4,2},{6,4},{1,7},{3,1},{5,3},{7,5},{8,14},{10,8},{12,... | collective-permute-start | bytes 2211848 | tf_op jit(solution)/shard_map/ppermute | solution.py:38
  16.5 1.2 %copy-start.2 = (bf16[1,128,3456]{2,1,0:T(8,128)(2,1)S(1)}, bf16[1,128,3456]{2,1,0:T(8,128)(2,1)}, u32[]{:S(2)}) copy-start(bf16[1,128,3456]{2,1,0:T(8,128)(2,1)} %param.12) | copy-start | bytes 2654212
  35.6 14.5 %collective-permute-start.4 = (bf16[80,2560]{1,0:T(8,128)(2,1)S(1)}, bf16[80,2560]{1,0:T(8,128)(2,1)S(1)}, u32[]{:S(2)}, u32[]{:S(2)}) collective-permute-start(bf16[80,2560]{1,0:T(8,128)(2,1)S(1)} %slice.55), channel_id=1, source_target_pairs={{0,6},{2,0},{4,2},{6,4},{1,7},{3,1},{5,3},{7,5},{8,14},{10,8},{12,... | collective-permute-start | bytes 1228808 | tf_op jit(solution)/shard_map/ppermute | solution.py:38
  39.4 10.6 %collective-permute-start.3 = (bf16[64,2560]{1,0:T(8,128)(2,1)S(1)}, bf16[64,2560]{1,0:T(8,128)(2,1)S(1)}, u32[]{:S(2)}, u32[]{:S(2)}) collective-permute-start(bf16[64,2560]{1,0:T(8,128)(2,1)S(1)} %slice.54), channel_id=1, source_target_pairs={{0,2},{2,4},{4,6},{6,0},{1,3},{3,5},{5,7},{7,1},{8,10},{10,12},{12... | collective-permute-start | bytes 983048 | tf_op jit(solution)/shard_map/ppermute | solution.py:38
  39.5 14.3 %collective-permute-start.10 = (bf16[432,640]{1,0:T(8,128)(2,1)S(1)}, bf16[432,640]{1,0:T(8,128)(2,1)S(1)}, u32[]{:S(2)}, u32[]{:S(2)}) collective-permute-start(bf16[432,640]{1,0:T(8,128)(2,1)S(1)} %bitcast.15), channel_id=1, source_target_pairs={{0,64},{64,128},{128,192},{192,0},{1,65},{65,129},{129,193},{193,1... | collective-permute-start | bytes 1658888 | tf_op jit(solution)/shard_map/ppermute | solution.py:38
  39.8 15.3 %collective-permute-start.11 = (bf16[432,640]{1,0:T(8,128)(2,1)S(1)}, bf16[432,640]{1,0:T(8,128)(2,1)S(1)}, u32[]{:S(2)}, u32[]{:S(2)}) collective-permute-start(bf16[432,640]{1,0:T(8,128)(2,1)S(1)} %bitcast.16), channel_id=1, source_target_pairs={{0,192},{64,0},{128,64},{192,128},{1,193},{65,1},{129,65},{193,129... | collective-permute-start | bytes 1658888 | tf_op jit(solution)/shard_map/ppermute | solution.py:38
  41.6 13.5 %collective-permute-start.5 = (bf16[144,2560]{1,0:T(8,128)(2,1)S(1)}, bf16[144,2560]{1,0:T(8,128)(2,1)S(1)}, u32[]{:S(2)}, u32[]{:S(2)}) collective-permute-start(bf16[144,2560]{1,0:T(8,128)(2,1)S(1)} %pad_maximum_fusion.refs_0_), channel_id=1, source_target_pairs={{0,1},{1,0},{2,3},{3,2},{4,5},{5,4},{6,7},{7,6},{8,9},{9,8},{10,11... | collective-permute-start | bytes 2211848 | tf_op jit(solution)/shard_map/ppermute | solution.py:42
  50.1 8.7 %collective-permute-start.6 = (bf16[144,2560]{1,0:T(8,128)(2,1)}, bf16[144,2560]{1,0:T(8,128)(2,1)S(1)}, u32[]{:S(2)}, u32[]{:S(2)}) collective-permute-start(bf16[144,2560]{1,0:T(8,128)(2,1)} %collective-permute-done.1.refs_1_), channel_id=1, source_target_pairs={{0,1},{1,0},{2,3},{3,2},{4,5},{5,4},{6,7},{7,6},{8,9},{9,8},{10,11... | collective-permute-start | bytes 2211848 | tf_op jit(solution)/shard_map/ppermute | solution.py:42
  50.1 8.7 %collective-permute-start.7 = (bf16[144,2560]{1,0:T(8,128)(2,1)}, bf16[144,2560]{1,0:T(8,128)(2,1)S(1)}, u32[]{:S(2)}, u32[]{:S(2)}) collective-permute-start(bf16[144,2560]{1,0:T(8,128)(2,1)} %collective-permute-done.2.refs_2_), channel_id=1, source_target_pairs={{0,1},{1,0},{2,3},{3,2},{4,5},{5,4},{6,7},{7,6},{8,9},{9,8},{10,11... | collective-permute-start | bytes 2211848 | tf_op jit(solution)/shard_map/ppermute | solution.py:42
  53.8 1.9 %collective-permute-start.8 = (bf16[64,2560]{1,0:T(8,128)(2,1)S(1)}, bf16[64,2560]{1,0:T(8,128)(2,1)S(1)}, u32[]{:S(2)}, u32[]{:S(2)}) collective-permute-start(bf16[64,2560]{1,0:T(8,128)(2,1)S(1)} %collective-permute-done.3.refs_3_), channel_id=1, source_target_pairs={{0,1},{1,0},{2,3},{3,2},{4,5},{5,4},{6,7},{7,6},{8,9},{9,8},{10,11... | collective-permute-start | bytes 983048 | tf_op jit(solution)/shard_map/ppermute | solution.py:42
  55.1 3.7 %collective-permute-start.9 = (bf16[80,2560]{1,0:T(8,128)(2,1)S(1)}, bf16[80,2560]{1,0:T(8,128)(2,1)S(1)}, u32[]{:S(2)}, u32[]{:S(2)}) collective-permute-start(bf16[80,2560]{1,0:T(8,128)(2,1)S(1)} %collective-permute-done.4.refs_4_), channel_id=1, source_target_pairs={{0,1},{1,0},{2,3},{3,2},{4,5},{5,4},{6,7},{7,6},{8,9},{9,8},{10,11... | collective-permute-start | bytes 1228808 | tf_op jit(solution)/shard_map/ppermute | solution.py:42
  55.1 12.7 %collective-permute-start.13 = (bf16[224,640]{1,0:T(8,128)(2,1)S(1)}, bf16[224,640]{1,0:T(8,128)(2,1)S(1)}, u32[]{:S(2)}, u32[]{:S(2)}) collective-permute-start(bf16[224,640]{1,0:T(8,128)(2,1)S(1)} %slice.57), channel_id=1, source_target_pairs={{0,192},{64,0},{128,64},{192,128},{1,193},{65,1},{129,65},{193,129... | collective-permute-start | bytes 860168 | tf_op jit(solution)/shard_map/ppermute | solution.py:38
  55.7 12.1 %collective-permute-start.12 = (bf16[208,640]{1,0:T(8,128)(2,1)S(1)}, bf16[208,640]{1,0:T(8,128)(2,1)S(1)}, u32[]{:S(2)}, u32[]{:S(2)}) collective-permute-start(bf16[208,640]{1,0:T(8,128)(2,1)S(1)} %slice.56), channel_id=1, source_target_pairs={{0,64},{64,128},{128,192},{192,0},{1,65},{65,129},{129,193},{193,1... | collective-permute-start | bytes 798728 | tf_op jit(solution)/shard_map/ppermute | solution.py:38
  67.8 13.1 %copy-start = (bf16[27,128,128]{2,1,0:T(8,128)(2,1)S(1)}, bf16[27,128,128]{2,1,0:T(8,128)(2,1)}, u32[]{:S(2)}) copy-start(bf16[27,128,128]{2,1,0:T(8,128)(2,1)} %refs_15_.1) | copy-start | bytes 2654212
  67.8 13.1 %copy-start.1 = (bf16[27,128,128]{2,1,0:T(8,128)(2,1)S(1)}, bf16[27,128,128]{2,1,0:T(8,128)(2,1)}, u32[]{:S(2)}) copy-start(bf16[27,128,128]{2,1,0:T(8,128)(2,1)} %refs_16_.1) | copy-start | bytes 2654212
  67.9 13.1 %copy-start.3 = (f32[4,3456]{1,0:T(4,128)S(1)}, f32[4,3456]{1,0:T(4,128)}, u32[]{:S(2)}) copy-start(f32[4,3456]{1,0:T(4,128)} %refs_10_.1) | copy-start | bytes 165892
  67.9 13.1 %copy-start.4 = (f32[3456]{0:T(1024)S(1)}, f32[3456]{0:T(1024)}, u32[]{:S(2)}) copy-start(f32[3456]{0:T(1024)} %param.16) | copy-start | bytes 41476
  67.9 13.1 %copy-start.5 = (f32[3456]{0:T(1024)S(1)}, f32[3456]{0:T(1024)}, u32[]{:S(2)}) copy-start(f32[3456]{0:T(1024)} %param.19) | copy-start | bytes 41476
  67.9 13.1 %copy-start.6 = (f32[3456]{0:T(1024)S(1)}, f32[3456]{0:T(1024)}, u32[]{:S(2)}) copy-start(f32[3456]{0:T(1024)} %param.20) | copy-start | bytes 41476
  67.9 13.1 %copy-start.7 = (f32[3456]{0:T(1024)S(1)}, f32[3456]{0:T(1024)}, u32[]{:S(2)}) copy-start(f32[3456]{0:T(1024)} %param.21) | copy-start | bytes 41476
  69.3 8.9 %collective-permute-start.15 = (bf16[928,128]{1,0:T(8,128)(2,1)S(1)}, bf16[928,128]{1,0:T(8,128)(2,1)S(1)}, u32[]{:S(2)}, u32[]{:S(2)}) collective-permute-start(bf16[928,128]{1,0:T(8,128)(2,1)S(1)} %get-tuple-element.42), channel_id=1, source_target_pairs={{0,2},{2,4},{4,6},{6,0},{1,3},{3,5},{5,7},{7,1},{8,10},{10,12},{12... | collective-permute-start | bytes 712712 | tf_op jit(solution)/shard_map/ppermute | solution.py:38
  69.7 8.5 %collective-permute-start.17 = (bf16[928,128]{1,0:T(8,128)(2,1)S(1)}, bf16[928,128]{1,0:T(8,128)(2,1)S(1)}, u32[]{:S(2)}, u32[]{:S(2)}) collective-permute-start(bf16[928,128]{1,0:T(8,128)(2,1)S(1)} %get-tuple-element.43), channel_id=1, source_target_pairs={{0,6},{2,0},{4,2},{6,4},{1,7},{3,1},{5,3},{7,5},{8,14},{10,8},{12,... | collective-permute-start | bytes 712712 | tf_op jit(solution)/shard_map/ppermute | solution.py:38
  72.6 8.4 %collective-permute-start.14 = (bf16[928,128]{1,0:T(8,128)(2,1)S(1)}, bf16[928,128]{1,0:T(8,128)(2,1)S(1)}, u32[]{:S(2)}, u32[]{:S(2)}) collective-permute-start(bf16[928,128]{1,0:T(8,128)(2,1)S(1)} %get-tuple-element.41.refs_0_), channel_id=1, source_target_pairs={{0,1},{1,0},{2,3},{3,2},{4,5},{5,4},{6,7},{7,6},{8,9},{9,8},{10,11... | collective-permute-start | bytes 712712 | tf_op jit(solution)/shard_map/ppermute | solution.py:42
  78.2 2.8 %collective-permute-start.16 = (bf16[928,128]{1,0:T(8,128)(2,1)S(1)}, bf16[928,128]{1,0:T(8,128)(2,1)S(1)}, u32[]{:S(2)}, u32[]{:S(2)}) collective-permute-start(bf16[928,128]{1,0:T(8,128)(2,1)S(1)} %collective-permute-done.15.refs_2_), channel_id=1, source_target_pairs={{0,1},{1,0},{2,3},{3,2},{4,5},{5,4},{6,7},{7,6},{8,9},{9,8},{10,11... | collective-permute-start | bytes 712712 | tf_op jit(solution)/shard_map/ppermute | solution.py:42
  78.2 2.8 %collective-permute-start.18 = (bf16[928,128]{1,0:T(8,128)(2,1)S(1)}, bf16[928,128]{1,0:T(8,128)(2,1)S(1)}, u32[]{:S(2)}, u32[]{:S(2)}) collective-permute-start(bf16[928,128]{1,0:T(8,128)(2,1)S(1)} %collective-permute-done.17.refs_4_), channel_id=1, source_target_pairs={{0,1},{1,0},{2,3},{3,2},{4,5},{5,4},{6,7},{7,6},{8,9},{9,8},{10,11... | collective-permute-start | bytes 712712 | tf_op jit(solution)/shard_map/ppermute | solution.py:42
  78.7 9.2 %collective-permute-start.19 = (bf16[928,128]{1,0:T(8,128)(2,1)S(1)}, bf16[928,128]{1,0:T(8,128)(2,1)S(1)}, u32[]{:S(2)}, u32[]{:S(2)}) collective-permute-start(bf16[928,128]{1,0:T(8,128)(2,1)S(1)} %get-tuple-element.48), channel_id=1, source_target_pairs={{0,4},{2,6},{4,0},{6,2},{1,5},{3,7},{5,1},{7,3},{8,12},{10,14},{12... | collective-permute-start | bytes 712712 | tf_op jit(solution)/shard_map/ppermute | solution.py:38
  87.9 1.5 %collective-permute-start.20 = (bf16[928,128]{1,0:T(8,128)(2,1)S(1)}, bf16[928,128]{1,0:T(8,128)(2,1)S(1)}, u32[]{:S(2)}, u32[]{:S(2)}) collective-permute-start(bf16[928,128]{1,0:T(8,128)(2,1)S(1)} %collective-permute-done.19.refs_6_), channel_id=1, source_target_pairs={{0,1},{1,0},{2,3},{3,2},{4,5},{5,4},{6,7},{7,6},{8,9},{9,8},{10,11... | collective-permute-start | bytes 712712 | tf_op jit(solution)/shard_map/ppermute | solution.py:42
  93.5 6.0 %collective-permute-start.21 = (f32[2,3456]{1,0:T(2,128)S(1)}, f32[2,3456]{1,0:T(2,128)S(1)}, u32[]{:S(2)}, u32[]{:S(2)}) collective-permute-start(f32[2,3456]{1,0:T(2,128)S(1)} %get-tuple-element.54), channel_id=1, source_target_pairs={{0,8},{8,16},{16,24},{24,32},{32,40},{40,48},{48,56},{56,64},{64,7... | collective-permute-start | bytes 82952 | tf_op jit(solution)/shard_map/ppermute | solution.py:38
  99.6 6.8 %collective-permute-start.22 = (f32[2,3456]{1,0:T(2,128)S(1)}, f32[2,3456]{1,0:T(2,128)S(1)}, u32[]{:S(2)}, u32[]{:S(2)}) collective-permute-start(f32[2,3456]{1,0:T(2,128)S(1)} %pad_maximum_fusion.1), channel_id=1, source_target_pairs={{0,8},{8,16},{16,24},{24,32},{32,40},{40,48},{48,56},{56,64},{64,7... | collective-permute-start | bytes 82952 | tf_op jit(solution)/shard_map/ppermute | solution.py:38
  99.9 7.8 %collective-permute-start.23 = (f32[2,3456]{1,0:T(2,128)S(1)}, f32[2,3456]{1,0:T(2,128)S(1)}, u32[]{:S(2)}, u32[]{:S(2)}) collective-permute-start(f32[2,3456]{1,0:T(2,128)S(1)} %pad_maximum_fusion.1), channel_id=1, source_target_pairs={{0,24},{8,32},{16,40},{24,48},{32,56},{40,64},{48,72},{56,80},{64,... | collective-permute-start | bytes 82952 | tf_op jit(solution)/shard_map/ppermute | solution.py:38
  100.8 7.0 %collective-permute-start.24 = (f32[2,3456]{1,0:T(2,128)S(1)}, f32[2,3456]{1,0:T(2,128)S(1)}, u32[]{:S(2)}, u32[]{:S(2)}) collective-permute-start(f32[2,3456]{1,0:T(2,128)S(1)} %pad_maximum_fusion.1), channel_id=1, source_target_pairs={{0,40},{8,48},{16,56},{24,64},{32,72},{40,80},{48,88},{56,96},{64,... | collective-permute-start | bytes 82952 | tf_op jit(solution)/shard_map/ppermute | solution.py:38
  106.0 4.8 %collective-permute-start.25 = (f32[2,3456]{1,0:T(2,128)S(1)}, f32[2,3456]{1,0:T(2,128)S(1)}, u32[]{:S(2)}, u32[]{:S(2)}) collective-permute-start(f32[2,3456]{1,0:T(2,128)S(1)} %pad_maximum_fusion.1), channel_id=1, source_target_pairs={{0,56},{8,64},{16,72},{24,80},{32,88},{40,96},{48,104},{56,112},{6... | collective-permute-start | bytes 82952 | tf_op jit(solution)/shard_map/ppermute | solution.py:38

commit v8 on v7

--- a/solution.py
+++ b/solution.py
@@ -12,7 +12,6 @@
 BF16 = jnp.bfloat16
 VMEM = pl.BlockSpec(memory_space=pltpu.VMEM)
 ANY = pl.BlockSpec(memory_space=pl.ANY)
-HBM = pl.BlockSpec(memory_space=pltpu.HBM)
 SMEM = pl.BlockSpec(memory_space=pltpu.SMEM)
 
 LENGTH = 128
@@ -81,33 +80,24 @@
 
 
 def project_kernel(at_ref, *refs):
-    tokens, weights, (part_ref, far_ref, rows_ref, sems) = refs[:10], refs[10:13], refs[13:]
+    tokens, weights, (part_ref, far_ref) = refs[:10], refs[10:13], refs[13:]
     y = at_ref[2]
-    pairs = []
-    for n, ref in enumerate(tokens):
-        half, n = n // 5, n % 5
-        size = ref.shape[0]
-        if n == 3:
-            pairs.append((ref, rows_ref.at[pl.ds(half * ROWS + 3 * LENGTH, size)]))
-            continue
-        top = min(n, 3) * LENGTH + (SPLIT if n == 4 else 0)
-        main = size - AHEAD
-        pairs.append((ref.at[pl.ds(0, main)], rows_ref.at[pl.ds(half * ROWS + top, main)]))
-        rest = half * ROWS + 4 * LENGTH + min(n, 3) * AHEAD
-        pairs.append((ref.at[pl.ds(main, AHEAD)], rows_ref.at[pl.ds(rest, AHEAD)]))
-    made = copies(pairs, sems)
+
+    def rows_of(half, at):
+        t0, t1, t2, t3, t4 = tokens[5 * half : 5 * half + 5]
+        main = [t[0:LENGTH, at] for t in (t0, t1, t2)] + [t3[:, at], t4[0:SPLIT, at]]
+        rest = [t[LENGTH:BLOCK, at] for t in (t0, t1, t2)] + [t4[SPLIT:, at]]
+        return jnp.concatenate(main + rest, axis=0)
+
     far = pl.ds(pl.multiple_of(lax.rem(y + 2, 4) * 640, 128), 640)
     for half in range(2):
-        for copy in made[9 * half : 9 * half + 9]:
-            copy.wait()
-        mine = slice(half * ROWS, (half + 1) * ROWS)
         total = None
         for w_ref, back in zip(weights, (0, 3, 1)):
             at = pl.ds(pl.multiple_of(lax.rem(y + back, 4) * 640, 128), 640)
-            part = across(w_ref[...], rows_ref[mine, at])
+            part = across(w_ref[...], rows_of(half, at))
             total = part if total is None else total + part
         part_ref[half] = total
-        far_ref[mine, :] = rows_ref[mine, far]
+        far_ref[half * ROWS : (half + 1) * ROWS, :] = rows_of(half, far)
 
 
 def pack_kernel(part_ref, far_ref, w0_ref, w1_ref, *refs):
@@ -314,9 +304,11 @@
         ),
         [SMEM] + [VMEM] * 3,
         [pltpu.VMEM((LENGTH + HALO, HEAD), F32)],
+        room=6,
         moved=2_700_000,
     )(at, gate_input[0], segment_ids, ahead)
-    column, one_back, one_ahead, gelu, masks = lax.optimization_barrier((column, one_back, one_ahead, gelu, masks))
+    column, one_back, one_ahead = lax.optimization_barrier((column, one_back, one_ahead))
+    one_back, gelu, masks = lax.optimization_barrier((one_back, gelu, masks))
     upper = shift(one_back[:SPLIT], "x", 1)
     lower = shift(one_ahead[SPLIT:], "x", -1)
     streams = [rows, one_back, one_ahead, upper, lower]
@@ -333,8 +325,7 @@
             jax.ShapeDtypeStruct((2, COLS, ROWS), F32),
             jax.ShapeDtypeStruct((2 * ROWS, 640), BF16),
         ),
-        [SMEM] + [ANY] * 5 + [HBM] * 5 + [VMEM] * 3,
-        [pltpu.VMEM((2 * ROWS, DEPTH), BF16), pltpu.SemaphoreType.DMA((18,))],
+        [SMEM] + [VMEM] * 13,
         flops=2 * 1056 * 1920 * 432,
         moved=9_000_000,
     )(at, *streams, column, from_back, from_ahead)

time: 113 us -> 112 us (level)
  waiting for transfers between devices: 44.7 us -> 50.7 us
  Pallas kernels: 24.2 us -> 19 us
  local copies, waits for them, and re-layouts: 7.43 us -> 4.36 us
  starting transfers between devices: 34.9 us -> 36.5 us
    pallas_call x1, Pallas kernels: 9.06 us -> 3.96 us  [body(): call(project_kernel, (jax.ShapeDtypeStruct((2, COLS, ROWS), F32), jax.Sha...]
    ppermute x17, waiting for transfers between devices: 29.3 us -> 32.5 us  [shift(): lax.ppermute(value, axis, [(i, (i + by) % count) for i in range(count)])]
    all_to_all x1, waiting for transfers between devices: 13.9 us -> 16.6 us  [body(): column = lax.all_to_all(copied, 'z', 0, 0, tiled=True).reshape(-1, COLS).T]
    ppermute x17, starting transfers between devices: 26.3 us -> 27.9 us  [shift(): lax.ppermute(value, axis, [(i, (i + by) % count) for i in range(count)])]
  transfers between devices with their start and end apart: 27 -> 27, of which waited for: 10 -> 12; matrix products, arithmetic and copies ran while one was open for 4% -> 2% of each run, Pallas kernels for 15% -> 11%
where the time goes in v8:
time: 112 us
  waiting for transfers between devices  50.7 us (45%)
  starting transfers between devices  36.5 us (33%)
  Pallas kernels  19 us (17%)
  local copies, waits for them, and re-layouts  4.36 us (4%)
    ppermute x17, waiting for transfers between devices, shift(): lax.ppermute(value, axis, [(i, (i + by) % count) for i in range(count)])  32.5 us
    ppermute x17, starting transfers between devices, shift(): lax.ppermute(value, axis, [(i, (i + by) % count) for i in range(count)])  27.9 us
    all_to_all x1, waiting for transfers between devices, body(): column = lax.all_to_all(copied, 'z', 0, 0, tiled=True).reshape(-1, COLS).T  16.6 us
    all_to_all x1, starting transfers between devices, body(): column = lax.all_to_all(copied, 'z', 0, 0, tiled=True).reshape(-1, COLS).T  7.57 us
    pallas_call x1, Pallas kernels, body(): call(near_kernel, walked(HEADS), [SMEM] + [ANY] * 6 + [VMEM] * 9, scratch...  6.31 us
    pallas_call x1, Pallas kernels, body(): call(far_kernel, walked(FAR), [SMEM] + [ANY] * 8 + [VMEM] * 10, scratch,...  4.02 us
    pallas_call x1, Pallas kernels, body(): call(project_kernel, (jax.ShapeDtypeStruct((2, COLS, ROWS), F32), jax.Sha...  3.96 us
  transfers between devices with their start and end apart: 27, of which 12 were waited for; matrix products, arithmetic and copies ran while one was open for 2% of the time, Pallas kernels for 11%

profile of v8, /device:TPU:24, one launch (start us, length us, event | category | flops | bytes accessed | tf_op | source)
XLA Modules:
  0.0 111.7 jit_solution(16569014436941375746)
XLA Ops:
  0.0 1.0 slice_bitcast_fusion
  1.0 0.7 convert_element_type.5
  1.7 2.0 %collective-permute-start = (bf16[16,2560]{1,0:T(8,128)(2,1)S(1)}, bf16[16,2560]{1,0:T(8,128)(2,1)S(1)}, u32[]{:S(2)}, u32[]{:S(2)}) collective-permute-start(bf16[16,2560]{1,0:T(8,128)(2,1)S(1)} %fusion.1), channel_id=1, source_target_pairs={{0,8},{8,16},{16,24},{24,32},{32,40},{40,48},{48,56},{56,64},{64,7... | collective-permute-start | bytes 245768 | tf_op jit(solution)/shard_map/ppermute | solution.py:37
  3.7 1.8 %broadcast_in_dim.4 = bf16[8,80,432]{2,1,0:T(8,128)(2,1)} broadcast(bf16[80,432]{1,0:T(8,128)(2,1)} %param.14), dimensions={1,2} | broadcast | bytes 622080 | tf_op jit(solution)/shard_map/broadcast_in_dim | solution.py:295
  5.5 7.6 %all-to-all-start = ((bf16[8,80,432]{2,1,0:T(8,128)(2,1)}), bf16[8,80,432]{2,1,0:T(8,128)(2,1)S(1)}, u32[]{:S(2)}, u32[]{:S(2)}) async-start(bf16[8,80,432]{2,1,0:T(8,128)(2,1)} %broadcast_in_dim.4), calls=%async_computation | async-start | bytes 1310720 | tf_op jit(solution)/shard_map/all_to_all | solution.py:296
  13.0 0.0 copy-start.8
  13.0 0.1 pad_maximum_fusion.refs_0_
  13.1 1.6 %collective-permute-start.1 = (bf16[144,2560]{1,0:T(8,128)(2,1)S(1)}, bf16[144,2560]{1,0:T(8,128)(2,1)S(1)}, u32[]{:S(2)}, u32[]{:S(2)}) collective-permute-start(bf16[144,2560]{1,0:T(8,128)(2,1)S(1)} %pad_maximum_fusion.refs_0_), channel_id=1, source_target_pairs={{0,2},{2,4},{4,6},{6,0},{1,3},{3,5},{5,7},{7,1},{8,10},{10,12},{12... | collective-permute-start | bytes 2211848 | tf_op jit(solution)/shard_map/ppermute | solution.py:37
  14.7 1.7 %collective-permute-start.2 = (bf16[144,2560]{1,0:T(8,128)(2,1)S(1)}, bf16[144,2560]{1,0:T(8,128)(2,1)S(1)}, u32[]{:S(2)}, u32[]{:S(2)}) collective-permute-start(bf16[144,2560]{1,0:T(8,128)(2,1)S(1)} %pad_maximum_fusion.refs_0_), channel_id=1, source_target_pairs={{0,6},{2,0},{4,2},{6,4},{1,7},{3,1},{5,3},{7,5},{8,14},{10,8},{12,... | collective-permute-start | bytes 2211848 | tf_op jit(solution)/shard_map/ppermute | solution.py:37
  16.4 16.6 %all-to-all-done = bf16[8,80,432]{2,1,0:T(8,128)(2,1)S(1)} async-done(((bf16[8,80,432]{2,1,0:T(8,128)(2,1)}), bf16[8,80,432]{2,1,0:T(8,128)(2,1)S(1)}, u32[]{:S(2)}, u32[]{:S(2)}) %all-to-all-start) | async-done | bytes 552992 | tf_op jit(solution)/shard_map/all_to_all | solution.py:296
  33.0 0.3 copy.13
  33.4 2.8 %collective-permute-start.4 = (bf16[80,2560]{1,0:T(8,128)(2,1)S(1)}, bf16[80,2560]{1,0:T(8,128)(2,1)S(1)}, u32[]{:S(2)}, u32[]{:S(2)}) collective-permute-start(bf16[80,2560]{1,0:T(8,128)(2,1)S(1)} %slice.55), channel_id=1, source_target_pairs={{0,6},{2,0},{4,2},{6,4},{1,7},{3,1},{5,3},{7,5},{8,14},{10,8},{12,... | collective-permute-start | bytes 1228808 | tf_op jit(solution)/shard_map/ppermute | solution.py:37
  36.2 0.1 pad_add_fusion.at_ref
  36.3 1.2 %copy-done.2 = bf16[1,128,3456]{2,1,0:T(8,128)(2,1)S(1)} copy-done((bf16[1,128,3456]{2,1,0:T(8,128)(2,1)S(1)}, bf16[1,128,3456]{2,1,0:T(8,128)(2,1)}, u32[]{:S(2)}) %copy-start.2) | copy-done | bytes 884760
  37.5 1.5 %shard_map.109 = (f32[27,128,128]{2,1,0:T(8,128)S(1)}, f32[4,128,128]{2,1,0:T(8,128)S(1)}) custom-call(s32[4]{0:T(128)S(1)} %pad_add_fusion.at_ref, bf16[128,3456]{1,0:T(8,128)(2,1)S(1)} %bitcast.18, s32[1,128]{1,0:T(1,128)S(1)} %copy-done.8, bf16[16,2560]{1,0:T(8,128)(2,1)S(1)} %collective-permute-done.ahead_ref), custom_call_target="tpu_custom_call" | custom-call | bytes 2700000 | tf_op jit(solution)/shard_map/pallas_call | solution.py:299
  39.1 0.1 collective-permute-start.3
  39.2 0.3 collective-permute-start.10
  39.5 1.8 %collective-permute-start.11 = (bf16[432,640]{1,0:T(8,128)(2,1)S(1)}, bf16[432,640]{1,0:T(8,128)(2,1)S(1)}, u32[]{:S(2)}, u32[]{:S(2)}) collective-permute-start(bf16[432,640]{1,0:T(8,128)(2,1)S(1)} %bitcast.16), channel_id=1, source_target_pairs={{0,192},{64,0},{128,64},{192,128},{1,193},{65,1},{129,65},{193,129... | collective-permute-start | bytes 1658888 | tf_op jit(solution)/shard_map/ppermute | solution.py:37
  41.3 8.4 %collective-permute-done.3.refs_3_ = bf16[64,2560]{1,0:T(8,128)(2,1)S(1)} collective-permute-done((bf16[64,2560]{1,0:T(8,128)(2,1)S(1)}, bf16[64,2560]{1,0:T(8,128)(2,1)S(1)}, u32[]{:S(2)}, u32[]{:S(2)}) %collective-permute-start.3) | collective-permute-done | bytes 327712 | tf_op jit(solution)/shard_map/ppermute | solution.py:37
  49.7 0.5 collective-permute-start.7
  50.2 3.2 %collective-permute-done.10.refs_11_ = bf16[432,640]{1,0:T(8,128)(2,1)S(1)} collective-permute-done((bf16[432,640]{1,0:T(8,128)(2,1)S(1)}, bf16[432,640]{1,0:T(8,128)(2,1)S(1)}, u32[]{:S(2)}, u32[]{:S(2)}) %collective-permute-start.10) | collective-permute-done | bytes 552992 | tf_op jit(solution)/shard_map/ppermute | solution.py:37
  53.4 1.3 %collective-permute-done.11.refs_12_ = bf16[432,640]{1,0:T(8,128)(2,1)S(1)} collective-permute-done((bf16[432,640]{1,0:T(8,128)(2,1)S(1)}, bf16[432,640]{1,0:T(8,128)(2,1)S(1)}, u32[]{:S(2)}, u32[]{:S(2)}) %collective-permute-start.11) | collective-permute-done | bytes 552992 | tf_op jit(solution)/shard_map/ppermute | solution.py:37
  54.8 0.5 collective-permute-start.13
  55.3 3.0 %collective-permute-start.12 = (bf16[208,640]{1,0:T(8,128)(2,1)S(1)}, bf16[208,640]{1,0:T(8,128)(2,1)S(1)}, u32[]{:S(2)}, u32[]{:S(2)}) collective-permute-start(bf16[208,640]{1,0:T(8,128)(2,1)S(1)} %slice.56), channel_id=1, source_target_pairs={{0,64},{64,128},{128,192},{192,0},{1,65},{65,129},{129,193},{193,1... | collective-permute-start | bytes 798728 | tf_op jit(solution)/shard_map/ppermute | solution.py:37
  58.4 4.0 %shard_map.110 = (f32[2,432,576]{2,1,0:T(8,128)S(1)}, bf16[1152,640]{1,0:T(8,128)(2,1)S(1)}) custom-call(s32[4]{0:T(128)S(1)} %pad_add_fusion.at_ref, bf16[144,2560]{1,0:T(8,128)(2,1)S(1)} %pad_maximum_fusion.refs_0_, bf16[144,2560]{1,0:T(8,128)(2,1)S(1)} %collective-permute-done.1.refs_1_, bf16[144,2560]{1,0:T(8,128)(2,1)S(1)} %collective-permute-done.2.refs_2_, ...), custom_call_target="tpu_custom_call" | custom-call | flops 1751777280 | bytes 9000000 | tf_op jit(solution)/shard_map/pallas_call | solution.py:322
  62.3 2.1 %collective-permute-done.12.w0_ref = bf16[208,640]{1,0:T(8,128)(2,1)S(1)} collective-permute-done((bf16[208,640]{1,0:T(8,128)(2,1)S(1)}, bf16[208,640]{1,0:T(8,128)(2,1)S(1)}, u32[]{:S(2)}, u32[]{:S(2)}) %collective-permute-start.12) | collective-permute-done | bytes 266272 | tf_op jit(solution)/shard_map/ppermute | solution.py:37
  64.4 0.9 collective-permute-done.13.w1_ref
  65.3 0.0 copy-start.5
  65.3 0.0 copy-start.7
  65.3 1.4 %shard_map.111 = (bf16[928,128]{1,0:T(8,128)(2,1)S(1)}, bf16[928,128]{1,0:T(8,128)(2,1)S(1)}, bf16[928,128]{1,0:T(8,128)(2,1)S(1)}, bf16[928,128]{1,0:T(8,128)(2,1)S(1)}) custom-call(f32[2,432,576]{2,1,0:T(8,128)S(1)} %get-tuple-element.41.part_ref, bf16[1152,640]{1,0:T(8,128)(2,1)S(1)} %get-tuple-element.42.far_ref, ...), custom_call_target="tpu_custom_call" | custom-call | flops 583925760 | bytes 5000000 | tf_op jit(solution)/shard_map/pallas_call | solution.py:332
  66.7 0.4 collective-permute-start.15
  67.1 2.9 %collective-permute-start.17 = (bf16[928,128]{1,0:T(8,128)(2,1)S(1)}, bf16[928,128]{1,0:T(8,128)(2,1)S(1)}, u32[]{:S(2)}, u32[]{:S(2)}) collective-permute-start(bf16[928,128]{1,0:T(8,128)(2,1)S(1)} %get-tuple-element.45), channel_id=1, source_target_pairs={{0,6},{2,0},{4,2},{6,4},{1,7},{3,1},{5,3},{7,5},{8,14},{10,8},{12,... | collective-permute-start | bytes 712712 | tf_op jit(solution)/shard_map/ppermute | solution.py:37
  70.0 5.4 %collective-permute-done.15.refs_2_ = bf16[928,128]{1,0:T(8,128)(2,1)S(1)} collective-permute-done((bf16[928,128]{1,0:T(8,128)(2,1)S(1)}, bf16[928,128]{1,0:T(8,128)(2,1)S(1)}, u32[]{:S(2)}, u32[]{:S(2)}) %collective-permute-start.15) | collective-permute-done | bytes 237600 | tf_op jit(solution)/shard_map/ppermute | solution.py:37
  75.4 0.5 collective-permute-start.18
  75.9 2.2 %collective-permute-start.19 = (bf16[928,128]{1,0:T(8,128)(2,1)S(1)}, bf16[928,128]{1,0:T(8,128)(2,1)S(1)}, u32[]{:S(2)}, u32[]{:S(2)}) collective-permute-start(bf16[928,128]{1,0:T(8,128)(2,1)S(1)} %get-tuple-element.50), channel_id=1, source_target_pairs={{0,4},{2,6},{4,0},{6,2},{1,5},{3,7},{5,1},{7,3},{8,12},{10,14},{12... | collective-permute-start | bytes 712712 | tf_op jit(solution)/shard_map/ppermute | solution.py:37
  78.3 6.3 %shard_map.112 = (f32[27,128,128]{2,1,0:T(8,128)S(1)}, f32[27,128,128]{2,1,0:T(8,128)S(1)}, f32[2,3456]{1,0:T(2,128)S(1)}) custom-call(s32[4]{0:T(128)S(1)} %pad_add_fusion.at_ref, bf16[928,128]{1,0:T(8,128)(2,1)S(1)} %get-tuple-element.43.refs_0_, bf16[928,128]{1,0:T(8,128)(2,1)S(1)} %collective-permute-done.14.refs_1_, ...), custom_call_target="tpu_custom_call" | custom-call | flops 167772160 | bytes 20000000 | tf_op jit(solution)/shard_map/pallas_call | solution.py:370
  84.6 0.6 collective-permute-done.19.refs_6_
  85.1 1.5 %collective-permute-done.20.refs_7_ = bf16[928,128]{1,0:T(8,128)(2,1)S(1)} collective-permute-done((bf16[928,128]{1,0:T(8,128)(2,1)S(1)}, bf16[928,128]{1,0:T(8,128)(2,1)S(1)}, u32[]{:S(2)}, u32[]{:S(2)}) %collective-permute-start.20) | collective-permute-done | bytes 237600 | tf_op jit(solution)/shard_map/ppermute | solution.py:41
  86.6 4.0 %shard_map.113 = (f32[8,128,128]{2,1,0:T(8,128)S(1)}, f32[8,128,128]{2,1,0:T(8,128)S(1)}, f32[2,3456]{1,0:T(2,128)S(1)}) custom-call(s32[4]{0:T(128)S(1)} %pad_add_fusion.at_ref, bf16[928,128]{1,0:T(8,128)(2,1)S(1)} %get-tuple-element.43.refs_0_, bf16[928,128]{1,0:T(8,128)(2,1)S(1)} %collective-permute-done.14.refs_1_, ...), custom_call_target="tpu_custom_call" | custom-call | flops 67108864 | bytes 8000000 | tf_op jit(solution)/shard_map/pallas_call | solution.py:379
  90.6 0.1 collective-permute-start.21
  90.7 6.0 %collective-permute-done.21 = f32[2,3456]{1,0:T(2,128)S(1)} collective-permute-done((f32[2,3456]{1,0:T(2,128)S(1)}, f32[2,3456]{1,0:T(2,128)S(1)}, u32[]{:S(2)}, u32[]{:S(2)}) %collective-permute-start.21) | collective-permute-done | bytes 27680 | tf_op jit(solution)/shard_map/ppermute | solution.py:37
  96.8 0.1 collective-permute-start.22
  96.9 2.0 %collective-permute-start.23 = (f32[2,3456]{1,0:T(2,128)S(1)}, f32[2,3456]{1,0:T(2,128)S(1)}, u32[]{:S(2)}, u32[]{:S(2)}) collective-permute-start(f32[2,3456]{1,0:T(2,128)S(1)} %pad_maximum_fusion.1), channel_id=1, source_target_pairs={{0,24},{8,32},{16,40},{24,48},{32,56},{40,64},{48,72},{56,80},{64,... | collective-permute-start | bytes 82952 | tf_op jit(solution)/shard_map/ppermute | solution.py:37
  98.8 6.3 %collective-permute-start.24 = (f32[2,3456]{1,0:T(2,128)S(1)}, f32[2,3456]{1,0:T(2,128)S(1)}, u32[]{:S(2)}, u32[]{:S(2)}) collective-permute-start(f32[2,3456]{1,0:T(2,128)S(1)} %pad_maximum_fusion.1), channel_id=1, source_target_pairs={{0,40},{8,48},{16,56},{24,64},{32,72},{40,80},{48,88},{56,96},{64,... | collective-permute-start | bytes 82952 | tf_op jit(solution)/shard_map/ppermute | solution.py:37
  105.1 1.6 %collective-permute-done.24 = f32[2,3456]{1,0:T(2,128)S(1)} collective-permute-done((f32[2,3456]{1,0:T(2,128)S(1)}, f32[2,3456]{1,0:T(2,128)S(1)}, u32[]{:S(2)}, u32[]{:S(2)}) %collective-permute-start.24) | collective-permute-done | bytes 27680 | tf_op jit(solution)/shard_map/ppermute | solution.py:37
  106.8 3.1 %collective-permute-done.25 = f32[2,3456]{1,0:T(2,128)S(1)} collective-permute-done((f32[2,3456]{1,0:T(2,128)S(1)}, f32[2,3456]{1,0:T(2,128)S(1)}, u32[]{:S(2)}, u32[]{:S(2)}) %collective-permute-start.25) | collective-permute-done | bytes 27680 | tf_op jit(solution)/shard_map/ppermute | solution.py:37
  109.9 0.1 slice_add_fusion.in_ref
  109.9 1.8 %shard_map.114 = bf16[128,3456]{1,0:T(8,128)(2,1)} custom-call(s32[4]{0:T(128)S(1)} %pad_add_fusion.at_ref, f32[27,128,128]{2,1,0:T(8,128)S(1)} %get-tuple-element.48.state_ref, f32[27,128,128]{2,1,0:T(8,128)S(1)} %get-tuple-element.49.prod_ref, f32[8,128,128]{2,1,0:T(8,128)S(1)} %get-tuple-element.54.far_state_ref, ...), custom_call_target="tpu_custom_call" | custom-call | bytes 4400000 | tf_op jit(solution)/shard_map/pallas_call | solution.py:391
  (46 shorter events, 0.3 us)
Async XLA Ops:
  0.0 13.0 %copy-start.9 = (bf16[1,128,2560]{2,1,0:T(8,128)(2,1)S(1)}, bf16[1,128,2560]{2,1,0:T(8,128)(2,1)}, u32[]{:S(2)}) copy-start(bf16[1,128,2560]{2,1,0:T(8,128)(2,1)} %param.11) | copy-start | bytes 1966084
  1.7 11.3 %collective-permute-start = (bf16[16,2560]{1,0:T(8,128)(2,1)S(1)}, bf16[16,2560]{1,0:T(8,128)(2,1)S(1)}, u32[]{:S(2)}, u32[]{:S(2)}) collective-permute-start(bf16[16,2560]{1,0:T(8,128)(2,1)S(1)} %fusion.1), channel_id=1, source_target_pairs={{0,8},{8,16},{16,24},{24,32},{32,40},{40,48},{48,56},{56,64},{64,7... | collective-permute-start | bytes 245768 | tf_op jit(solution)/shard_map/ppermute | solution.py:37
  5.5 27.6 %all-to-all-start = ((bf16[8,80,432]{2,1,0:T(8,128)(2,1)}), bf16[8,80,432]{2,1,0:T(8,128)(2,1)S(1)}, u32[]{:S(2)}, u32[]{:S(2)}) async-start(bf16[8,80,432]{2,1,0:T(8,128)(2,1)} %broadcast_in_dim.4), calls=%async_computation | async-start | bytes 1310720 | tf_op jit(solution)/shard_map/all_to_all | solution.py:296
  13.0 23.3 %copy-start.8 = (s32[1,128]{1,0:T(1,128)S(1)}, s32[1,128]{1,0:T(1,128)}, u32[]{:S(2)}) copy-start(s32[1,128]{1,0:T(1,128)} %ids_ref.1) | copy-start | bytes 1540
  13.1 20.2 %collective-permute-start.1 = (bf16[144,2560]{1,0:T(8,128)(2,1)S(1)}, bf16[144,2560]{1,0:T(8,128)(2,1)S(1)}, u32[]{:S(2)}, u32[]{:S(2)}) collective-permute-start(bf16[144,2560]{1,0:T(8,128)(2,1)S(1)} %pad_maximum_fusion.refs_0_), channel_id=1, source_target_pairs={{0,2},{2,4},{4,6},{6,0},{1,3},{3,5},{5,7},{7,1},{8,10},{10,12},{12... | collective-permute-start | bytes 2211848 | tf_op jit(solution)/shard_map/ppermute | solution.py:37
  14.7 18.7 %collective-permute-start.2 = (bf16[144,2560]{1,0:T(8,128)(2,1)S(1)}, bf16[144,2560]{1,0:T(8,128)(2,1)S(1)}, u32[]{:S(2)}, u32[]{:S(2)}) collective-permute-start(bf16[144,2560]{1,0:T(8,128)(2,1)S(1)} %pad_maximum_fusion.refs_0_), channel_id=1, source_target_pairs={{0,6},{2,0},{4,2},{6,4},{1,7},{3,1},{5,3},{7,5},{8,14},{10,8},{12,... | collective-permute-start | bytes 2211848 | tf_op jit(solution)/shard_map/ppermute | solution.py:37
  33.4 16.3 %collective-permute-start.4 = (bf16[80,2560]{1,0:T(8,128)(2,1)S(1)}, bf16[80,2560]{1,0:T(8,128)(2,1)S(1)}, u32[]{:S(2)}, u32[]{:S(2)}) collective-permute-start(bf16[80,2560]{1,0:T(8,128)(2,1)S(1)} %slice.55), channel_id=1, source_target_pairs={{0,6},{2,0},{4,2},{6,4},{1,7},{3,1},{5,3},{7,5},{8,14},{10,8},{12,... | collective-permute-start | bytes 1228808 | tf_op jit(solution)/shard_map/ppermute | solution.py:37
  36.3 1.2 %copy-start.2 = (bf16[1,128,3456]{2,1,0:T(8,128)(2,1)S(1)}, bf16[1,128,3456]{2,1,0:T(8,128)(2,1)}, u32[]{:S(2)}) copy-start(bf16[1,128,3456]{2,1,0:T(8,128)(2,1)} %param.12) | copy-start | bytes 2654212
  39.1 10.6 %collective-permute-start.3 = (bf16[64,2560]{1,0:T(8,128)(2,1)S(1)}, bf16[64,2560]{1,0:T(8,128)(2,1)S(1)}, u32[]{:S(2)}, u32[]{:S(2)}) collective-permute-start(bf16[64,2560]{1,0:T(8,128)(2,1)S(1)} %slice.54), channel_id=1, source_target_pairs={{0,2},{2,4},{4,6},{6,0},{1,3},{3,5},{5,7},{7,1},{8,10},{10,12},{12... | collective-permute-start | bytes 983048 | tf_op jit(solution)/shard_map/ppermute | solution.py:37
  39.2 14.3 %collective-permute-start.10 = (bf16[432,640]{1,0:T(8,128)(2,1)S(1)}, bf16[432,640]{1,0:T(8,128)(2,1)S(1)}, u32[]{:S(2)}, u32[]{:S(2)}) collective-permute-start(bf16[432,640]{1,0:T(8,128)(2,1)S(1)} %bitcast.15), channel_id=1, source_target_pairs={{0,64},{64,128},{128,192},{192,0},{1,65},{65,129},{129,193},{193,1... | collective-permute-start | bytes 1658888 | tf_op jit(solution)/shard_map/ppermute | solution.py:37
  39.5 15.3 %collective-permute-start.11 = (bf16[432,640]{1,0:T(8,128)(2,1)S(1)}, bf16[432,640]{1,0:T(8,128)(2,1)S(1)}, u32[]{:S(2)}, u32[]{:S(2)}) collective-permute-start(bf16[432,640]{1,0:T(8,128)(2,1)S(1)} %bitcast.16), channel_id=1, source_target_pairs={{0,192},{64,0},{128,64},{192,128},{1,193},{65,1},{129,65},{193,129... | collective-permute-start | bytes 1658888 | tf_op jit(solution)/shard_map/ppermute | solution.py:37
  41.3 13.5 %collective-permute-start.5 = (bf16[144,2560]{1,0:T(8,128)(2,1)S(1)}, bf16[144,2560]{1,0:T(8,128)(2,1)S(1)}, u32[]{:S(2)}, u32[]{:S(2)}) collective-permute-start(bf16[144,2560]{1,0:T(8,128)(2,1)S(1)} %pad_maximum_fusion.refs_0_), channel_id=1, source_target_pairs={{0,1},{1,0},{2,3},{3,2},{4,5},{5,4},{6,7},{7,6},{8,9},{9,8},{10,11... | collective-permute-start | bytes 2211848 | tf_op jit(solution)/shard_map/ppermute | solution.py:41
  49.7 8.7 %collective-permute-start.6 = (bf16[144,2560]{1,0:T(8,128)(2,1)S(1)}, bf16[144,2560]{1,0:T(8,128)(2,1)S(1)}, u32[]{:S(2)}, u32[]{:S(2)}) collective-permute-start(bf16[144,2560]{1,0:T(8,128)(2,1)S(1)} %collective-permute-done.1.refs_1_), channel_id=1, source_target_pairs={{0,1},{1,0},{2,3},{3,2},{4,5},{5,4},{6,7},{7,6},{8,9},{9,8},{10,11... | collective-permute-start | bytes 2211848 | tf_op jit(solution)/shard_map/ppermute | solution.py:41
  49.7 8.7 %collective-permute-start.7 = (bf16[144,2560]{1,0:T(8,128)(2,1)S(1)}, bf16[144,2560]{1,0:T(8,128)(2,1)S(1)}, u32[]{:S(2)}, u32[]{:S(2)}) collective-permute-start(bf16[144,2560]{1,0:T(8,128)(2,1)S(1)} %collective-permute-done.2.refs_2_), channel_id=1, source_target_pairs={{0,1},{1,0},{2,3},{3,2},{4,5},{5,4},{6,7},{7,6},{8,9},{9,8},{10,11... | collective-permute-start | bytes 2211848 | tf_op jit(solution)/shard_map/ppermute | solution.py:41
  53.4 1.9 %collective-permute-start.8 = (bf16[64,2560]{1,0:T(8,128)(2,1)S(1)}, bf16[64,2560]{1,0:T(8,128)(2,1)S(1)}, u32[]{:S(2)}, u32[]{:S(2)}) collective-permute-start(bf16[64,2560]{1,0:T(8,128)(2,1)S(1)} %collective-permute-done.3.refs_3_), channel_id=1, source_target_pairs={{0,1},{1,0},{2,3},{3,2},{4,5},{5,4},{6,7},{7,6},{8,9},{9,8},{10,11... | collective-permute-start | bytes 983048 | tf_op jit(solution)/shard_map/ppermute | solution.py:41
  54.7 3.7 %collective-permute-start.9 = (bf16[80,2560]{1,0:T(8,128)(2,1)S(1)}, bf16[80,2560]{1,0:T(8,128)(2,1)S(1)}, u32[]{:S(2)}, u32[]{:S(2)}) collective-permute-start(bf16[80,2560]{1,0:T(8,128)(2,1)S(1)} %collective-permute-done.4.refs_4_), channel_id=1, source_target_pairs={{0,1},{1,0},{2,3},{3,2},{4,5},{5,4},{6,7},{7,6},{8,9},{9,8},{10,11... | collective-permute-start | bytes 1228808 | tf_op jit(solution)/shard_map/ppermute | solution.py:41
  54.8 10.5 %collective-permute-start.13 = (bf16[224,640]{1,0:T(8,128)(2,1)S(1)}, bf16[224,640]{1,0:T(8,128)(2,1)S(1)}, u32[]{:S(2)}, u32[]{:S(2)}) collective-permute-start(bf16[224,640]{1,0:T(8,128)(2,1)S(1)} %slice.57), channel_id=1, source_target_pairs={{0,192},{64,0},{128,64},{192,128},{1,193},{65,1},{129,65},{193,129... | collective-permute-start | bytes 860168 | tf_op jit(solution)/shard_map/ppermute | solution.py:37
  55.3 9.1 %collective-permute-start.12 = (bf16[208,640]{1,0:T(8,128)(2,1)S(1)}, bf16[208,640]{1,0:T(8,128)(2,1)S(1)}, u32[]{:S(2)}, u32[]{:S(2)}) collective-permute-start(bf16[208,640]{1,0:T(8,128)(2,1)S(1)} %slice.56), channel_id=1, source_target_pairs={{0,64},{64,128},{128,192},{192,0},{1,65},{65,129},{129,193},{193,1... | collective-permute-start | bytes 798728 | tf_op jit(solution)/shard_map/ppermute | solution.py:37
  65.3 12.9 %copy-start = (bf16[27,128,128]{2,1,0:T(8,128)(2,1)S(1)}, bf16[27,128,128]{2,1,0:T(8,128)(2,1)}, u32[]{:S(2)}) copy-start(bf16[27,128,128]{2,1,0:T(8,128)(2,1)} %refs_15_.1) | copy-start | bytes 2654212
  65.3 12.9 %copy-start.1 = (bf16[27,128,128]{2,1,0:T(8,128)(2,1)S(1)}, bf16[27,128,128]{2,1,0:T(8,128)(2,1)}, u32[]{:S(2)}) copy-start(bf16[27,128,128]{2,1,0:T(8,128)(2,1)} %refs_16_.1) | copy-start | bytes 2654212
  65.3 12.9 %copy-start.3 = (f32[4,3456]{1,0:T(4,128)S(1)}, f32[4,3456]{1,0:T(4,128)}, u32[]{:S(2)}) copy-start(f32[4,3456]{1,0:T(4,128)} %refs_10_.1) | copy-start | bytes 165892
  65.3 12.9 %copy-start.4 = (f32[3456]{0:T(1024)S(1)}, f32[3456]{0:T(1024)}, u32[]{:S(2)}) copy-start(f32[3456]{0:T(1024)} %param.16) | copy-start | bytes 41476
  65.3 12.9 %copy-start.5 = (f32[3456]{0:T(1024)S(1)}, f32[3456]{0:T(1024)}, u32[]{:S(2)}) copy-start(f32[3456]{0:T(1024)} %param.19) | copy-start | bytes 41476
  65.3 12.9 %copy-start.6 = (f32[3456]{0:T(1024)S(1)}, f32[3456]{0:T(1024)}, u32[]{:S(2)}) copy-start(f32[3456]{0:T(1024)} %param.20) | copy-start | bytes 41476
  65.3 12.9 %copy-start.7 = (f32[3456]{0:T(1024)S(1)}, f32[3456]{0:T(1024)}, u32[]{:S(2)}) copy-start(f32[3456]{0:T(1024)} %param.21) | copy-start | bytes 41476
  66.7 8.7 %collective-permute-start.15 = (bf16[928,128]{1,0:T(8,128)(2,1)S(1)}, bf16[928,128]{1,0:T(8,128)(2,1)S(1)}, u32[]{:S(2)}, u32[]{:S(2)}) collective-permute-start(bf16[928,128]{1,0:T(8,128)(2,1)S(1)} %get-tuple-element.44), channel_id=1, source_target_pairs={{0,2},{2,4},{4,6},{6,0},{1,3},{3,5},{5,7},{7,1},{8,10},{10,12},{12... | collective-permute-start | bytes 712712 | tf_op jit(solution)/shard_map/ppermute | solution.py:37
  67.1 8.3 %collective-permute-start.17 = (bf16[928,128]{1,0:T(8,128)(2,1)S(1)}, bf16[928,128]{1,0:T(8,128)(2,1)S(1)}, u32[]{:S(2)}, u32[]{:S(2)}) collective-permute-start(bf16[928,128]{1,0:T(8,128)(2,1)S(1)} %get-tuple-element.45), channel_id=1, source_target_pairs={{0,6},{2,0},{4,2},{6,4},{1,7},{3,1},{5,3},{7,5},{8,14},{10,8},{12,... | collective-permute-start | bytes 712712 | tf_op jit(solution)/shard_map/ppermute | solution.py:37
  70.0 8.1 %collective-permute-start.14 = (bf16[928,128]{1,0:T(8,128)(2,1)S(1)}, bf16[928,128]{1,0:T(8,128)(2,1)S(1)}, u32[]{:S(2)}, u32[]{:S(2)}) collective-permute-start(bf16[928,128]{1,0:T(8,128)(2,1)S(1)} %get-tuple-element.43.refs_0_), channel_id=1, source_target_pairs={{0,1},{1,0},{2,3},{3,2},{4,5},{5,4},{6,7},{7,6},{8,9},{9,8},{10,11... | collective-permute-start | bytes 712712 | tf_op jit(solution)/shard_map/ppermute | solution.py:41
  75.4 2.8 %collective-permute-start.16 = (bf16[928,128]{1,0:T(8,128)(2,1)S(1)}, bf16[928,128]{1,0:T(8,128)(2,1)S(1)}, u32[]{:S(2)}, u32[]{:S(2)}) collective-permute-start(bf16[928,128]{1,0:T(8,128)(2,1)S(1)} %collective-permute-done.15.refs_2_), channel_id=1, source_target_pairs={{0,1},{1,0},{2,3},{3,2},{4,5},{5,4},{6,7},{7,6},{8,9},{9,8},{10,11... | collective-permute-start | bytes 712712 | tf_op jit(solution)/shard_map/ppermute | solution.py:41
  75.4 2.8 %collective-permute-start.18 = (bf16[928,128]{1,0:T(8,128)(2,1)S(1)}, bf16[928,128]{1,0:T(8,128)(2,1)S(1)}, u32[]{:S(2)}, u32[]{:S(2)}) collective-permute-start(bf16[928,128]{1,0:T(8,128)(2,1)S(1)} %collective-permute-done.17.refs_4_), channel_id=1, source_target_pairs={{0,1},{1,0},{2,3},{3,2},{4,5},{5,4},{6,7},{7,6},{8,9},{9,8},{10,11... | collective-permute-start | bytes 712712 | tf_op jit(solution)/shard_map/ppermute | solution.py:41
  75.9 9.2 %collective-permute-start.19 = (bf16[928,128]{1,0:T(8,128)(2,1)S(1)}, bf16[928,128]{1,0:T(8,128)(2,1)S(1)}, u32[]{:S(2)}, u32[]{:S(2)}) collective-permute-start(bf16[928,128]{1,0:T(8,128)(2,1)S(1)} %get-tuple-element.50), channel_id=1, source_target_pairs={{0,4},{2,6},{4,0},{6,2},{1,5},{3,7},{5,1},{7,3},{8,12},{10,14},{12... | collective-permute-start | bytes 712712 | tf_op jit(solution)/shard_map/ppermute | solution.py:37
  85.1 1.5 %collective-permute-start.20 = (bf16[928,128]{1,0:T(8,128)(2,1)S(1)}, bf16[928,128]{1,0:T(8,128)(2,1)S(1)}, u32[]{:S(2)}, u32[]{:S(2)}) collective-permute-start(bf16[928,128]{1,0:T(8,128)(2,1)S(1)} %collective-permute-done.19.refs_6_), channel_id=1, source_target_pairs={{0,1},{1,0},{2,3},{3,2},{4,5},{5,4},{6,7},{7,6},{8,9},{9,8},{10,11... | collective-permute-start | bytes 712712 | tf_op jit(solution)/shard_map/ppermute | solution.py:41
  90.6 6.0 %collective-permute-start.21 = (f32[2,3456]{1,0:T(2,128)S(1)}, f32[2,3456]{1,0:T(2,128)S(1)}, u32[]{:S(2)}, u32[]{:S(2)}) collective-permute-start(f32[2,3456]{1,0:T(2,128)S(1)} %get-tuple-element.56), channel_id=1, source_target_pairs={{0,8},{8,16},{16,24},{24,32},{32,40},{40,48},{48,56},{56,64},{64,7... | collective-permute-start | bytes 82952 | tf_op jit(solution)/shard_map/ppermute | solution.py:37
  96.8 8.4 %collective-permute-start.22 = (f32[2,3456]{1,0:T(2,128)S(1)}, f32[2,3456]{1,0:T(2,128)S(1)}, u32[]{:S(2)}, u32[]{:S(2)}) collective-permute-start(f32[2,3456]{1,0:T(2,128)S(1)} %pad_maximum_fusion.1), channel_id=1, source_target_pairs={{0,8},{8,16},{16,24},{24,32},{32,40},{40,48},{48,56},{56,64},{64,7... | collective-permute-start | bytes 82952 | tf_op jit(solution)/shard_map/ppermute | solution.py:37
  96.9 8.3 %collective-permute-start.23 = (f32[2,3456]{1,0:T(2,128)S(1)}, f32[2,3456]{1,0:T(2,128)S(1)}, u32[]{:S(2)}, u32[]{:S(2)}) collective-permute-start(f32[2,3456]{1,0:T(2,128)S(1)} %pad_maximum_fusion.1), channel_id=1, source_target_pairs={{0,24},{8,32},{16,40},{24,48},{32,56},{40,64},{48,72},{56,80},{64,... | collective-permute-start | bytes 82952 | tf_op jit(solution)/shard_map/ppermute | solution.py:37
  98.8 7.9 %collective-permute-start.24 = (f32[2,3456]{1,0:T(2,128)S(1)}, f32[2,3456]{1,0:T(2,128)S(1)}, u32[]{:S(2)}, u32[]{:S(2)}) collective-permute-start(f32[2,3456]{1,0:T(2,128)S(1)} %pad_maximum_fusion.1), channel_id=1, source_target_pairs={{0,40},{8,48},{16,56},{24,64},{32,72},{40,80},{48,88},{56,96},{64,... | collective-permute-start | bytes 82952 | tf_op jit(solution)/shard_map/ppermute | solution.py:37
  105.1 4.8 %collective-permute-start.25 = (f32[2,3456]{1,0:T(2,128)S(1)}, f32[2,3456]{1,0:T(2,128)S(1)}, u32[]{:S(2)}, u32[]{:S(2)}) collective-permute-start(f32[2,3456]{1,0:T(2,128)S(1)} %pad_maximum_fusion.1), channel_id=1, source_target_pairs={{0,56},{8,64},{16,72},{24,80},{32,88},{40,96},{48,104},{56,112},{6... | collective-permute-start | bytes 82952 | tf_op jit(solution)/shard_map/ppermute | solution.py:37

commit v9 on v8

--- a/solution.py
+++ b/solution.py
@@ -27,7 +27,7 @@
 AHEAD = 16
 BLOCK = LENGTH + AHEAD
 SPLIT = 64
-SIDE = 4
+NEAR_SIDE, FAR_SIDE = 5, 8
 NEAR, FAR = 20, 8
 ROWS = 4 * BLOCK
 
@@ -211,12 +211,14 @@
             state_ref[out, at, :] = (states[k] + prods[k] * in_state) * gelu
             prod_ref[out, at, :] = (prods[k] * in_prod) * gelu
 
+    side = FAR_SIDE if far else NEAR_SIDE
+
     def several(i, carry):
-        for slot in range(SIDE):
-            head(SIDE * i + slot, slot)
+        for slot in range(side):
+            head(side * i + slot, slot)
         return carry
 
-    lax.fori_loop(0, (FAR if far else NEAR) // SIDE, several, 0)
+    lax.fori_loop(0, (FAR if far else NEAR) // side, several, 0)
 
 
 def near_kernel(at_ref, *refs):
@@ -308,7 +310,6 @@
         moved=2_700_000,
     )(at, gate_input[0], segment_ids, ahead)
     column, one_back, one_ahead = lax.optimization_barrier((column, one_back, one_ahead))
-    one_back, gelu, masks = lax.optimization_barrier((one_back, gelu, masks))
     upper = shift(one_back[:SPLIT], "x", 1)
     lower = shift(one_ahead[SPLIT:], "x", -1)
     streams = [rows, one_back, one_ahead, upper, lower]
@@ -343,6 +344,7 @@
         shift(sent[1], "x", -1),
         shift(sent[3], "x", 2),
     ]
+    got[1], gelu, masks = lax.optimization_barrier((got[1], gelu, masks))
     near = [v for block in got[:3] for v in (block, flip(block))]
     shared = (
         masks,
@@ -353,7 +355,7 @@
         gate_i,
     )
     scratch = [
-        pltpu.VMEM((SIDE, LENGTH + HALO, HEAD), F32),
+        pltpu.VMEM((FAR_SIDE, LENGTH + HALO, HEAD), F32),
         pltpu.VMEM((WIDTH, LENGTH), BF16),
         pltpu.VMEM((8, 32, 128), BF16),
         pltpu.VMEM((HALO, WIDTH), F32),

time: 112 us -> 113 us (level)
  waiting for transfers between devices: 50.7 us -> 46.2 us
  local copies, waits for them, and re-layouts: 4.36 us -> 7.9 us
  Pallas kernels: 19 us -> 21.4 us
    ppermute x17, waiting for transfers between devices: 32.5 us -> 28 us  [shift(): lax.ppermute(value, axis, [(i, (i + by) % count) for i in range(count)])]
    unnamed x20 -> x28, local copies, waits for them, and re-layouts: 1.21 us -> 3.09 us
    pallas_call x1, Pallas kernels: 3.96 us -> 5.19 us  [body(): call(project_kernel, (jax.ShapeDtypeStruct((2, COLS, ROWS), F32), jax.Sha...]
  transfers between devices with their start and end apart: 27 -> 27, of which waited for: 12 -> 11; matrix products, arithmetic and copies ran while one was open for 2% -> 3% of each run, Pallas kernels for 11% -> 12%
where the time goes in v9:
time: 113 us
  waiting for transfers between devices  46.2 us (41%)
  starting transfers between devices  35.9 us (32%)
  Pallas kernels  21.4 us (19%)
  local copies, waits for them, and re-layouts  7.9 us (7%)
    ppermute x17, waiting for transfers between devices, shift(): lax.ppermute(value, axis, [(i, (i + by) % count) for i in range(count)])  28 us
    ppermute x17, starting transfers between devices, shift(): lax.ppermute(value, axis, [(i, (i + by) % count) for i in range(count)])  27.2 us
    all_to_all x1, waiting for transfers between devices, body(): column = lax.all_to_all(copied, 'z', 0, 0, tiled=True).reshape(-1, COLS).T  16.6 us
    all_to_all x1, starting transfers between devices, body(): column = lax.all_to_all(copied, 'z', 0, 0, tiled=True).reshape(-1, COLS).T  7.57 us
    pallas_call x1, Pallas kernels, body(): call(near_kernel, walked(HEADS), [SMEM] + [ANY] * 6 + [VMEM] * 9, scratch...  6.45 us
    pallas_call x1, Pallas kernels, body(): call(project_kernel, (jax.ShapeDtypeStruct((2, COLS, ROWS), F32), jax.Sha...  5.19 us
    pallas_call x1, Pallas kernels, body(): call(far_kernel, walked(FAR), [SMEM] + [ANY] * 8 + [VMEM] * 10, scratch,...  3.9 us
    unnamed x28, local copies, waits for them, and re-layouts  3.09 us
  transfers between devices with their start and end apart: 27, of which 11 were waited for; matrix products, arithmetic and copies ran while one was open for 3% of the time, Pallas kernels for 12%

profile of v9, /device:TPU:24, one launch (start us, length us, event | category | flops | bytes accessed | tf_op | source)
XLA Modules:
  0.0 112.6 jit_solution(7986641389891875768)
XLA Ops:
  0.0 1.0 slice_bitcast_fusion
  1.0 0.7 convert_element_type.5
  1.7 2.0 %collective-permute-start = (bf16[16,2560]{1,0:T(8,128)(2,1)S(1)}, bf16[16,2560]{1,0:T(8,128)(2,1)S(1)}, u32[]{:S(2)}, u32[]{:S(2)}) collective-permute-start(bf16[16,2560]{1,0:T(8,128)(2,1)S(1)} %fusion.1), channel_id=1, source_target_pairs={{0,8},{8,16},{16,24},{24,32},{32,40},{40,48},{48,56},{56,64},{64,7... | collective-permute-start | bytes 245768 | tf_op jit(solution)/shard_map/ppermute | solution.py:37
  3.7 1.8 %broadcast_in_dim.4 = bf16[8,80,432]{2,1,0:T(8,128)(2,1)} broadcast(bf16[80,432]{1,0:T(8,128)(2,1)} %param.14), dimensions={1,2} | broadcast | bytes 622080 | tf_op jit(solution)/shard_map/broadcast_in_dim | solution.py:297
  5.5 7.6 %all-to-all-start = ((bf16[8,80,432]{2,1,0:T(8,128)(2,1)}), bf16[8,80,432]{2,1,0:T(8,128)(2,1)S(1)}, u32[]{:S(2)}, u32[]{:S(2)}) async-start(bf16[8,80,432]{2,1,0:T(8,128)(2,1)} %broadcast_in_dim.4), calls=%async_computation | async-start | bytes 1310720 | tf_op jit(solution)/shard_map/all_to_all | solution.py:298
  13.1 1.6 %collective-permute-start.1 = (bf16[144,2560]{1,0:T(8,128)(2,1)S(1)}, bf16[144,2560]{1,0:T(8,128)(2,1)S(1)}, u32[]{:S(2)}, u32[]{:S(2)}) collective-permute-start(bf16[144,2560]{1,0:T(8,128)(2,1)S(1)} %pad_maximum_fusion.refs_0_), channel_id=1, source_target_pairs={{0,2},{2,4},{4,6},{6,0},{1,3},{3,5},{5,7},{7,1},{8,10},{10,12},{12... | collective-permute-start | bytes 2211848 | tf_op jit(solution)/shard_map/ppermute | solution.py:37
  14.7 1.7 %collective-permute-start.2 = (bf16[144,2560]{1,0:T(8,128)(2,1)S(1)}, bf16[144,2560]{1,0:T(8,128)(2,1)S(1)}, u32[]{:S(2)}, u32[]{:S(2)}) collective-permute-start(bf16[144,2560]{1,0:T(8,128)(2,1)S(1)} %pad_maximum_fusion.refs_0_), channel_id=1, source_target_pairs={{0,6},{2,0},{4,2},{6,4},{1,7},{3,1},{5,3},{7,5},{8,14},{10,8},{12,... | collective-permute-start | bytes 2211848 | tf_op jit(solution)/shard_map/ppermute | solution.py:37
  16.4 16.6 %all-to-all-done = bf16[8,80,432]{2,1,0:T(8,128)(2,1)S(1)} async-done(((bf16[8,80,432]{2,1,0:T(8,128)(2,1)}), bf16[8,80,432]{2,1,0:T(8,128)(2,1)S(1)}, u32[]{:S(2)}, u32[]{:S(2)}) %all-to-all-start) | async-done | bytes 552992 | tf_op jit(solution)/shard_map/all_to_all | solution.py:298
  33.0 0.3 copy.13
  33.4 2.8 %collective-permute-start.4 = (bf16[80,2560]{1,0:T(8,128)(2,1)S(1)}, bf16[80,2560]{1,0:T(8,128)(2,1)}, u32[]{:S(2)}, u32[]{:S(2)}) collective-permute-start(bf16[80,2560]{1,0:T(8,128)(2,1)S(1)} %slice.55), channel_id=1, source_target_pairs={{0,6},{2,0},{4,2},{6,4},{1,7},{3,1},{5,3},{7,5},{8,14},{10,8},{12,... | collective-permute-start | bytes 1228808 | tf_op jit(solution)/shard_map/ppermute | solution.py:37
  36.3 0.1 collective-permute-start.3
  36.4 0.3 collective-permute-start.10
  36.7 1.8 %collective-permute-start.11 = (bf16[432,640]{1,0:T(8,128)(2,1)S(1)}, bf16[432,640]{1,0:T(8,128)(2,1)S(1)}, u32[]{:S(2)}, u32[]{:S(2)}) collective-permute-start(bf16[432,640]{1,0:T(8,128)(2,1)S(1)} %bitcast.16), channel_id=1, source_target_pairs={{0,192},{64,0},{128,64},{192,128},{1,193},{65,1},{129,65},{193,129... | collective-permute-start | bytes 1658888 | tf_op jit(solution)/shard_map/ppermute | solution.py:37
  38.5 8.5 %collective-permute-done.3.refs_3_ = bf16[64,2560]{1,0:T(8,128)(2,1)} collective-permute-done((bf16[64,2560]{1,0:T(8,128)(2,1)S(1)}, bf16[64,2560]{1,0:T(8,128)(2,1)}, u32[]{:S(2)}, u32[]{:S(2)}) %collective-permute-start.3) | collective-permute-done | bytes 327712 | tf_op jit(solution)/shard_map/ppermute | solution.py:37
  47.0 0.5 collective-permute-start.7
  47.5 3.1 %collective-permute-done.10.refs_11_ = bf16[432,640]{1,0:T(8,128)(2,1)S(1)} collective-permute-done((bf16[432,640]{1,0:T(8,128)(2,1)S(1)}, bf16[432,640]{1,0:T(8,128)(2,1)S(1)}, u32[]{:S(2)}, u32[]{:S(2)}) %collective-permute-start.10) | collective-permute-done | bytes 552992 | tf_op jit(solution)/shard_map/ppermute | solution.py:37
  50.6 1.3 %collective-permute-done.11.refs_12_ = bf16[432,640]{1,0:T(8,128)(2,1)S(1)} collective-permute-done((bf16[432,640]{1,0:T(8,128)(2,1)S(1)}, bf16[432,640]{1,0:T(8,128)(2,1)S(1)}, u32[]{:S(2)}, u32[]{:S(2)}) %collective-permute-start.11) | collective-permute-done | bytes 552992 | tf_op jit(solution)/shard_map/ppermute | solution.py:37
  51.9 0.7 slice.57
  52.7 0.9 copy-done.5
  53.5 0.4 collective-permute-start.13
  54.0 1.0 slice.56
  55.0 3.0 %collective-permute-start.12 = (bf16[208,640]{1,0:T(8,128)(2,1)S(1)}, bf16[208,640]{1,0:T(8,128)(2,1)S(1)}, u32[]{:S(2)}, u32[]{:S(2)}) collective-permute-start(bf16[208,640]{1,0:T(8,128)(2,1)S(1)} %slice.56), channel_id=1, source_target_pairs={{0,64},{64,128},{128,192},{192,0},{1,65},{65,129},{129,193},{193,1... | collective-permute-start | bytes 798728 | tf_op jit(solution)/shard_map/ppermute | solution.py:37
  58.0 0.1 pad_add_fusion.at_ref
  58.1 1.0 copy-done.3
  59.1 1.1 copy-done.6
  60.3 5.2 %shard_map.109 = (f32[2,432,576]{2,1,0:T(8,128)S(1)}, bf16[1152,640]{1,0:T(8,128)(2,1)S(1)}) custom-call(s32[4]{0:T(128)S(1)} %pad_add_fusion.at_ref, bf16[144,2560]{1,0:T(8,128)(2,1)S(1)} %pad_maximum_fusion.refs_0_, bf16[144,2560]{1,0:T(8,128)(2,1)S(1)} %collective-permute-done.1.refs_1_, bf16[144,2560]{1,0:T(8,128)(2,1)S(1)} %collective-permute-done.2.refs_2_, ...), custom_call_target="tpu_custom_call" | custom-call | flops 1751777280 | bytes 9000000 | tf_op jit(solution)/shard_map/pallas_call | solution.py:323
  65.6 2.5 %shard_map.110 = (bf16[928,128]{1,0:T(8,128)(2,1)S(1)}, bf16[928,128]{1,0:T(8,128)(2,1)S(1)}, bf16[928,128]{1,0:T(8,128)(2,1)S(1)}, bf16[928,128]{1,0:T(8,128)(2,1)S(1)}) custom-call(f32[2,432,576]{2,1,0:T(8,128)S(1)} %get-tuple-element.38.part_ref, bf16[1152,640]{1,0:T(8,128)(2,1)S(1)} %get-tuple-element.39.far_ref, ...), custom_call_target="tpu_custom_call" | custom-call | flops 583925760 | bytes 5000000 | tf_op jit(solution)/shard_map/pallas_call | solution.py:333
  68.1 0.4 collective-permute-start.15
  68.5 2.9 %collective-permute-start.17 = (bf16[928,128]{1,0:T(8,128)(2,1)S(1)}, bf16[928,128]{1,0:T(8,128)(2,1)S(1)}, u32[]{:S(2)}, u32[]{:S(2)}) collective-permute-start(bf16[928,128]{1,0:T(8,128)(2,1)S(1)} %get-tuple-element.45), channel_id=1, source_target_pairs={{0,6},{2,0},{4,2},{6,4},{1,7},{3,1},{5,3},{7,5},{8,14},{10,8},{12,... | collective-permute-start | bytes 712712 | tf_op jit(solution)/shard_map/ppermute | solution.py:37
  71.4 1.5 %shard_map.111 = (f32[27,128,128]{2,1,0:T(8,128)S(1)}, f32[4,128,128]{2,1,0:T(8,128)S(1)}) custom-call(s32[4]{0:T(128)S(1)} %pad_add_fusion.at_ref, bf16[128,3456]{1,0:T(8,128)(2,1)S(1)} %bitcast.18, s32[1,128]{1,0:T(1,128)S(1)} %copy-done.12, bf16[16,2560]{1,0:T(8,128)(2,1)S(1)} %collective-permute-done.ahead_ref), custom_call_target="tpu_custom_call" | custom-call | bytes 2700000 | tf_op jit(solution)/shard_map/pallas_call | solution.py:301
  73.0 0.1 collective-permute-start.14
  73.1 3.9 %collective-permute-done.15.refs_2_ = bf16[928,128]{1,0:T(8,128)(2,1)S(1)} collective-permute-done((bf16[928,128]{1,0:T(8,128)(2,1)S(1)}, bf16[928,128]{1,0:T(8,128)(2,1)S(1)}, u32[]{:S(2)}, u32[]{:S(2)}) %collective-permute-start.15) | collective-permute-done | bytes 237600 | tf_op jit(solution)/shard_map/ppermute | solution.py:37
  77.0 0.5 collective-permute-start.18
  77.5 2.2 %collective-permute-start.19 = (bf16[928,128]{1,0:T(8,128)(2,1)S(1)}, bf16[928,128]{1,0:T(8,128)(2,1)S(1)}, u32[]{:S(2)}, u32[]{:S(2)}) collective-permute-start(bf16[928,128]{1,0:T(8,128)(2,1)S(1)} %get-tuple-element.50), channel_id=1, source_target_pairs={{0,4},{2,6},{4,0},{6,2},{1,5},{3,7},{5,1},{7,3},{8,12},{10,14},{12... | collective-permute-start | bytes 712712 | tf_op jit(solution)/shard_map/ppermute | solution.py:37
  79.8 6.4 %shard_map.112 = (f32[27,128,128]{2,1,0:T(8,128)S(1)}, f32[27,128,128]{2,1,0:T(8,128)S(1)}, f32[2,3456]{1,0:T(2,128)S(1)}) custom-call(s32[4]{0:T(128)S(1)} %pad_add_fusion.at_ref, bf16[928,128]{1,0:T(8,128)(2,1)S(1)} %get-tuple-element.40.refs_0_, bf16[928,128]{1,0:T(8,128)(2,1)S(1)} %collective-permute-done.14.refs_1_, ...), custom_call_target="tpu_custom_call" | custom-call | flops 167772160 | bytes 20000000 | tf_op jit(solution)/shard_map/pallas_call | solution.py:372
  86.3 0.4 collective-permute-done.19.refs_6_
  86.7 1.5 %collective-permute-done.20.refs_7_ = bf16[928,128]{1,0:T(8,128)(2,1)S(1)} collective-permute-done((bf16[928,128]{1,0:T(8,128)(2,1)S(1)}, bf16[928,128]{1,0:T(8,128)(2,1)S(1)}, u32[]{:S(2)}, u32[]{:S(2)}) %collective-permute-start.20) | collective-permute-done | bytes 237600 | tf_op jit(solution)/shard_map/ppermute | solution.py:41
  88.2 3.9 %shard_map.113 = (f32[8,128,128]{2,1,0:T(8,128)S(1)}, f32[8,128,128]{2,1,0:T(8,128)S(1)}, f32[2,3456]{1,0:T(2,128)S(1)}) custom-call(s32[4]{0:T(128)S(1)} %pad_add_fusion.at_ref, bf16[928,128]{1,0:T(8,128)(2,1)S(1)} %get-tuple-element.40.refs_0_, bf16[928,128]{1,0:T(8,128)(2,1)S(1)} %collective-permute-done.14.refs_1_, ...), custom_call_target="tpu_custom_call" | custom-call | flops 67108864 | bytes 8000000 | tf_op jit(solution)/shard_map/pallas_call | solution.py:381
  92.1 0.1 collective-permute-start.21
  92.2 6.0 %collective-permute-done.21 = f32[2,3456]{1,0:T(2,128)S(1)} collective-permute-done((f32[2,3456]{1,0:T(2,128)S(1)}, f32[2,3456]{1,0:T(2,128)S(1)}, u32[]{:S(2)}, u32[]{:S(2)}) %collective-permute-start.21) | collective-permute-done | bytes 27680 | tf_op jit(solution)/shard_map/ppermute | solution.py:37
  98.2 0.3 collective-permute-start.22
  98.5 2.0 %collective-permute-start.23 = (f32[2,3456]{1,0:T(2,128)S(1)}, f32[2,3456]{1,0:T(2,128)S(1)}, u32[]{:S(2)}, u32[]{:S(2)}) collective-permute-start(f32[2,3456]{1,0:T(2,128)S(1)} %pad_maximum_fusion.1), channel_id=1, source_target_pairs={{0,24},{8,32},{16,40},{24,48},{32,56},{40,64},{48,72},{56,80},{64,... | collective-permute-start | bytes 82952 | tf_op jit(solution)/shard_map/ppermute | solution.py:37
  100.5 5.5 %collective-permute-start.24 = (f32[2,3456]{1,0:T(2,128)S(1)}, f32[2,3456]{1,0:T(2,128)S(1)}, u32[]{:S(2)}, u32[]{:S(2)}) collective-permute-start(f32[2,3456]{1,0:T(2,128)S(1)} %pad_maximum_fusion.1), channel_id=1, source_target_pairs={{0,40},{8,48},{16,56},{24,64},{32,72},{40,80},{48,88},{56,96},{64,... | collective-permute-start | bytes 82952 | tf_op jit(solution)/shard_map/ppermute | solution.py:37
  106.0 0.4 collective-permute-done.23
  106.4 1.2 %collective-permute-done.24 = f32[2,3456]{1,0:T(2,128)S(1)} collective-permute-done((f32[2,3456]{1,0:T(2,128)S(1)}, f32[2,3456]{1,0:T(2,128)S(1)}, u32[]{:S(2)}, u32[]{:S(2)}) %collective-permute-start.24) | collective-permute-done | bytes 27680 | tf_op jit(solution)/shard_map/ppermute | solution.py:37
  107.6 3.1 %collective-permute-done.25 = f32[2,3456]{1,0:T(2,128)S(1)} collective-permute-done((f32[2,3456]{1,0:T(2,128)S(1)}, f32[2,3456]{1,0:T(2,128)S(1)}, u32[]{:S(2)}, u32[]{:S(2)}) %collective-permute-start.25) | collective-permute-done | bytes 27680 | tf_op jit(solution)/shard_map/ppermute | solution.py:37
  110.8 0.1 slice_add_fusion.in_ref
  110.8 1.8 %shard_map.114 = bf16[128,3456]{1,0:T(8,128)(2,1)} custom-call(s32[4]{0:T(128)S(1)} %pad_add_fusion.at_ref, f32[27,128,128]{2,1,0:T(8,128)S(1)} %get-tuple-element.48.state_ref, f32[27,128,128]{2,1,0:T(8,128)S(1)} %get-tuple-element.49.prod_ref, f32[8,128,128]{2,1,0:T(8,128)S(1)} %get-tuple-element.54.far_state_ref, ...), custom_call_target="tpu_custom_call" | custom-call | bytes 4400000 | tf_op jit(solution)/shard_map/pallas_call | solution.py:393
  (54 shorter events, 0.3 us)
Async XLA Ops:
  0.0 13.0 %copy-start.13 = (bf16[1,128,2560]{2,1,0:T(8,128)(2,1)S(1)}, bf16[1,128,2560]{2,1,0:T(8,128)(2,1)}, u32[]{:S(2)}) copy-start(bf16[1,128,2560]{2,1,0:T(8,128)(2,1)} %param.11) | copy-start | bytes 1966084
  1.7 11.3 %collective-permute-start = (bf16[16,2560]{1,0:T(8,128)(2,1)S(1)}, bf16[16,2560]{1,0:T(8,128)(2,1)S(1)}, u32[]{:S(2)}, u32[]{:S(2)}) collective-permute-start(bf16[16,2560]{1,0:T(8,128)(2,1)S(1)} %fusion.1), channel_id=1, source_target_pairs={{0,8},{8,16},{16,24},{24,32},{32,40},{40,48},{48,56},{56,64},{64,7... | collective-permute-start | bytes 245768 | tf_op jit(solution)/shard_map/ppermute | solution.py:37
  5.5 27.6 %all-to-all-start = ((bf16[8,80,432]{2,1,0:T(8,128)(2,1)}), bf16[8,80,432]{2,1,0:T(8,128)(2,1)S(1)}, u32[]{:S(2)}, u32[]{:S(2)}) async-start(bf16[8,80,432]{2,1,0:T(8,128)(2,1)} %broadcast_in_dim.4), calls=%async_computation | async-start | bytes 1310720 | tf_op jit(solution)/shard_map/all_to_all | solution.py:298
  13.1 20.2 %collective-permute-start.1 = (bf16[144,2560]{1,0:T(8,128)(2,1)S(1)}, bf16[144,2560]{1,0:T(8,128)(2,1)S(1)}, u32[]{:S(2)}, u32[]{:S(2)}) collective-permute-start(bf16[144,2560]{1,0:T(8,128)(2,1)S(1)} %pad_maximum_fusion.refs_0_), channel_id=1, source_target_pairs={{0,2},{2,4},{4,6},{6,0},{1,3},{3,5},{5,7},{7,1},{8,10},{10,12},{12... | collective-permute-start | bytes 2211848 | tf_op jit(solution)/shard_map/ppermute | solution.py:37
  14.7 18.7 %collective-permute-start.2 = (bf16[144,2560]{1,0:T(8,128)(2,1)S(1)}, bf16[144,2560]{1,0:T(8,128)(2,1)S(1)}, u32[]{:S(2)}, u32[]{:S(2)}) collective-permute-start(bf16[144,2560]{1,0:T(8,128)(2,1)S(1)} %pad_maximum_fusion.refs_0_), channel_id=1, source_target_pairs={{0,6},{2,0},{4,2},{6,4},{1,7},{3,1},{5,3},{7,5},{8,14},{10,8},{12,... | collective-permute-start | bytes 2211848 | tf_op jit(solution)/shard_map/ppermute | solution.py:37
  33.4 13.6 %collective-permute-start.4 = (bf16[80,2560]{1,0:T(8,128)(2,1)S(1)}, bf16[80,2560]{1,0:T(8,128)(2,1)}, u32[]{:S(2)}, u32[]{:S(2)}) collective-permute-start(bf16[80,2560]{1,0:T(8,128)(2,1)S(1)} %slice.55), channel_id=1, source_target_pairs={{0,6},{2,0},{4,2},{6,4},{1,7},{3,1},{5,3},{7,5},{8,14},{10,8},{12,... | collective-permute-start | bytes 1228808 | tf_op jit(solution)/shard_map/ppermute | solution.py:37
  36.3 10.7 %collective-permute-start.3 = (bf16[64,2560]{1,0:T(8,128)(2,1)S(1)}, bf16[64,2560]{1,0:T(8,128)(2,1)}, u32[]{:S(2)}, u32[]{:S(2)}) collective-permute-start(bf16[64,2560]{1,0:T(8,128)(2,1)S(1)} %slice.54), channel_id=1, source_target_pairs={{0,2},{2,4},{4,6},{6,0},{1,3},{3,5},{5,7},{7,1},{8,10},{10,12},{12... | collective-permute-start | bytes 983048 | tf_op jit(solution)/shard_map/ppermute | solution.py:37
  36.4 14.3 %collective-permute-start.10 = (bf16[432,640]{1,0:T(8,128)(2,1)S(1)}, bf16[432,640]{1,0:T(8,128)(2,1)S(1)}, u32[]{:S(2)}, u32[]{:S(2)}) collective-permute-start(bf16[432,640]{1,0:T(8,128)(2,1)S(1)} %bitcast.15), channel_id=1, source_target_pairs={{0,64},{64,128},{128,192},{192,0},{1,65},{65,129},{129,193},{193,1... | collective-permute-start | bytes 1658888 | tf_op jit(solution)/shard_map/ppermute | solution.py:37
  36.7 15.3 %collective-permute-start.11 = (bf16[432,640]{1,0:T(8,128)(2,1)S(1)}, bf16[432,640]{1,0:T(8,128)(2,1)S(1)}, u32[]{:S(2)}, u32[]{:S(2)}) collective-permute-start(bf16[432,640]{1,0:T(8,128)(2,1)S(1)} %bitcast.16), channel_id=1, source_target_pairs={{0,192},{64,0},{128,64},{192,128},{1,193},{65,1},{129,65},{193,129... | collective-permute-start | bytes 1658888 | tf_op jit(solution)/shard_map/ppermute | solution.py:37
  38.5 14.2 %collective-permute-start.5 = (bf16[144,2560]{1,0:T(8,128)(2,1)S(1)}, bf16[144,2560]{1,0:T(8,128)(2,1)S(1)}, u32[]{:S(2)}, u32[]{:S(2)}) collective-permute-start(bf16[144,2560]{1,0:T(8,128)(2,1)S(1)} %pad_maximum_fusion.refs_0_), channel_id=1, source_target_pairs={{0,1},{1,0},{2,3},{3,2},{4,5},{5,4},{6,7},{7,6},{8,9},{9,8},{10,11... | collective-permute-start | bytes 2211848 | tf_op jit(solution)/shard_map/ppermute | solution.py:41
  47.0 11.1 %collective-permute-start.6 = (bf16[144,2560]{1,0:T(8,128)(2,1)S(1)}, bf16[144,2560]{1,0:T(8,128)(2,1)}, u32[]{:S(2)}, u32[]{:S(2)}) collective-permute-start(bf16[144,2560]{1,0:T(8,128)(2,1)S(1)} %collective-permute-done.1.refs_1_), channel_id=1, source_target_pairs={{0,1},{1,0},{2,3},{3,2},{4,5},{5,4},{6,7},{7,6},{8,9},{9,8},{10,11... | collective-permute-start | bytes 2211848 | tf_op jit(solution)/shard_map/ppermute | solution.py:41
  47.0 11.1 %collective-permute-start.7 = (bf16[144,2560]{1,0:T(8,128)(2,1)S(1)}, bf16[144,2560]{1,0:T(8,128)(2,1)}, u32[]{:S(2)}, u32[]{:S(2)}) collective-permute-start(bf16[144,2560]{1,0:T(8,128)(2,1)S(1)} %collective-permute-done.2.refs_2_), channel_id=1, source_target_pairs={{0,1},{1,0},{2,3},{3,2},{4,5},{5,4},{6,7},{7,6},{8,9},{9,8},{10,11... | collective-permute-start | bytes 2211848 | tf_op jit(solution)/shard_map/ppermute | solution.py:41
  50.6 1.3 %copy-start.2 = (bf16[432,640]{1,0:T(8,128)(2,1)}, bf16[432,640]{1,0:T(8,128)(2,1)S(1)}, u32[]{:S(2)}) copy-start(bf16[432,640]{1,0:T(8,128)(2,1)S(1)} %collective-permute-done.10.refs_11_) | copy-start | bytes 1658884
  50.6 4.3 %collective-permute-start.8 = (bf16[64,2560]{1,0:T(8,128)(2,1)}, bf16[64,2560]{1,0:T(8,128)(2,1)}, u32[]{:S(2)}, u32[]{:S(2)}) collective-permute-start(bf16[64,2560]{1,0:T(8,128)(2,1)} %collective-permute-done.3.refs_3_), channel_id=1, source_target_pairs={{0,1},{1,0},{2,3},{3,2},{4,5},{5,4},{6,7},{7,6},{8,9},{9,8},{10,11... | collective-permute-start | bytes 983048 | tf_op jit(solution)/shard_map/ppermute | solution.py:41
  51.9 6.2 %collective-permute-start.9 = (bf16[80,2560]{1,0:T(8,128)(2,1)}, bf16[80,2560]{1,0:T(8,128)(2,1)}, u32[]{:S(2)}, u32[]{:S(2)}) collective-permute-start(bf16[80,2560]{1,0:T(8,128)(2,1)} %collective-permute-done.4.refs_4_), channel_id=1, source_target_pairs={{0,1},{1,0},{2,3},{3,2},{4,5},{5,4},{6,7},{7,6},{8,9},{9,8},{10,11... | collective-permute-start | bytes 1228808 | tf_op jit(solution)/shard_map/ppermute | solution.py:41
  52.7 0.9 copy-start.5
  53.5 12.0 %collective-permute-start.13 = (bf16[224,640]{1,0:T(8,128)(2,1)}, bf16[224,640]{1,0:T(8,128)(2,1)}, u32[]{:S(2)}, u32[]{:S(2)}) collective-permute-start(bf16[224,640]{1,0:T(8,128)(2,1)} %slice.57), channel_id=1, source_target_pairs={{0,192},{64,0},{128,64},{192,128},{1,193},{65,1},{129,65},{193,129... | collective-permute-start | bytes 860168 | tf_op jit(solution)/shard_map/ppermute | solution.py:37
  55.0 10.5 %collective-permute-start.12 = (bf16[208,640]{1,0:T(8,128)(2,1)S(1)}, bf16[208,640]{1,0:T(8,128)(2,1)S(1)}, u32[]{:S(2)}, u32[]{:S(2)}) collective-permute-start(bf16[208,640]{1,0:T(8,128)(2,1)S(1)} %slice.56), channel_id=1, source_target_pairs={{0,64},{64,128},{128,192},{192,0},{1,65},{65,129},{129,193},{193,1... | collective-permute-start | bytes 798728 | tf_op jit(solution)/shard_map/ppermute | solution.py:37
  58.1 1.1 copy-start.3
  59.1 1.1 copy-start.6
  65.5 5.9 %copy-start.4 = (bf16[1,128,3456]{2,1,0:T(8,128)(2,1)S(1)}, bf16[1,128,3456]{2,1,0:T(8,128)(2,1)}, u32[]{:S(2)}) copy-start(bf16[1,128,3456]{2,1,0:T(8,128)(2,1)} %param.12) | copy-start | bytes 2654212
  65.5 5.9 %copy-start.12 = (s32[1,128]{1,0:T(1,128)S(1)}, s32[1,128]{1,0:T(1,128)}, u32[]{:S(2)}) copy-start(s32[1,128]{1,0:T(1,128)} %ids_ref.1) | copy-start | bytes 1540
  65.5 14.3 %copy-start = (bf16[27,128,128]{2,1,0:T(8,128)(2,1)S(1)}, bf16[27,128,128]{2,1,0:T(8,128)(2,1)}, u32[]{:S(2)}) copy-start(bf16[27,128,128]{2,1,0:T(8,128)(2,1)} %refs_15_.1) | copy-start | bytes 2654212
  65.5 14.3 %copy-start.1 = (bf16[27,128,128]{2,1,0:T(8,128)(2,1)S(1)}, bf16[27,128,128]{2,1,0:T(8,128)(2,1)}, u32[]{:S(2)}) copy-start(bf16[27,128,128]{2,1,0:T(8,128)(2,1)} %refs_16_.1) | copy-start | bytes 2654212
  65.5 14.3 %copy-start.7 = (f32[4,3456]{1,0:T(4,128)S(1)}, f32[4,3456]{1,0:T(4,128)}, u32[]{:S(2)}) copy-start(f32[4,3456]{1,0:T(4,128)} %refs_10_.1) | copy-start | bytes 165892
  65.5 14.3 %copy-start.8 = (f32[3456]{0:T(1024)S(1)}, f32[3456]{0:T(1024)}, u32[]{:S(2)}) copy-start(f32[3456]{0:T(1024)} %param.16) | copy-start | bytes 41476
  65.6 14.3 %copy-start.9 = (f32[3456]{0:T(1024)S(1)}, f32[3456]{0:T(1024)}, u32[]{:S(2)}) copy-start(f32[3456]{0:T(1024)} %param.19) | copy-start | bytes 41476
  65.6 14.3 %copy-start.10 = (f32[3456]{0:T(1024)S(1)}, f32[3456]{0:T(1024)}, u32[]{:S(2)}) copy-start(f32[3456]{0:T(1024)} %param.20) | copy-start | bytes 41476
  65.6 14.3 %copy-start.11 = (f32[3456]{0:T(1024)S(1)}, f32[3456]{0:T(1024)}, u32[]{:S(2)}) copy-start(f32[3456]{0:T(1024)} %param.21) | copy-start | bytes 41476
  68.1 8.9 %collective-permute-start.15 = (bf16[928,128]{1,0:T(8,128)(2,1)S(1)}, bf16[928,128]{1,0:T(8,128)(2,1)S(1)}, u32[]{:S(2)}, u32[]{:S(2)}) collective-permute-start(bf16[928,128]{1,0:T(8,128)(2,1)S(1)} %get-tuple-element.41), channel_id=1, source_target_pairs={{0,2},{2,4},{4,6},{6,0},{1,3},{3,5},{5,7},{7,1},{8,10},{10,12},{12... | collective-permute-start | bytes 712712 | tf_op jit(solution)/shard_map/ppermute | solution.py:37
  68.5 8.5 %collective-permute-start.17 = (bf16[928,128]{1,0:T(8,128)(2,1)S(1)}, bf16[928,128]{1,0:T(8,128)(2,1)S(1)}, u32[]{:S(2)}, u32[]{:S(2)}) collective-permute-start(bf16[928,128]{1,0:T(8,128)(2,1)S(1)} %get-tuple-element.45), channel_id=1, source_target_pairs={{0,6},{2,0},{4,2},{6,4},{1,7},{3,1},{5,3},{7,5},{8,14},{10,8},{12,... | collective-permute-start | bytes 712712 | tf_op jit(solution)/shard_map/ppermute | solution.py:37
  73.0 6.8 %collective-permute-start.14 = (bf16[928,128]{1,0:T(8,128)(2,1)S(1)}, bf16[928,128]{1,0:T(8,128)(2,1)S(1)}, u32[]{:S(2)}, u32[]{:S(2)}) collective-permute-start(bf16[928,128]{1,0:T(8,128)(2,1)S(1)} %get-tuple-element.40.refs_0_), channel_id=1, source_target_pairs={{0,1},{1,0},{2,3},{3,2},{4,5},{5,4},{6,7},{7,6},{8,9},{9,8},{10,11... | collective-permute-start | bytes 712712 | tf_op jit(solution)/shard_map/ppermute | solution.py:41
  77.0 2.8 %collective-permute-start.16 = (bf16[928,128]{1,0:T(8,128)(2,1)S(1)}, bf16[928,128]{1,0:T(8,128)(2,1)S(1)}, u32[]{:S(2)}, u32[]{:S(2)}) collective-permute-start(bf16[928,128]{1,0:T(8,128)(2,1)S(1)} %collective-permute-done.15.refs_2_), channel_id=1, source_target_pairs={{0,1},{1,0},{2,3},{3,2},{4,5},{5,4},{6,7},{7,6},{8,9},{9,8},{10,11... | collective-permute-start | bytes 712712 | tf_op jit(solution)/shard_map/ppermute | solution.py:41
  77.0 2.8 %collective-permute-start.18 = (bf16[928,128]{1,0:T(8,128)(2,1)S(1)}, bf16[928,128]{1,0:T(8,128)(2,1)S(1)}, u32[]{:S(2)}, u32[]{:S(2)}) collective-permute-start(bf16[928,128]{1,0:T(8,128)(2,1)S(1)} %collective-permute-done.17.refs_4_), channel_id=1, source_target_pairs={{0,1},{1,0},{2,3},{3,2},{4,5},{5,4},{6,7},{7,6},{8,9},{9,8},{10,11... | collective-permute-start | bytes 712712 | tf_op jit(solution)/shard_map/ppermute | solution.py:41
  77.5 9.2 %collective-permute-start.19 = (bf16[928,128]{1,0:T(8,128)(2,1)S(1)}, bf16[928,128]{1,0:T(8,128)(2,1)S(1)}, u32[]{:S(2)}, u32[]{:S(2)}) collective-permute-start(bf16[928,128]{1,0:T(8,128)(2,1)S(1)} %get-tuple-element.50), channel_id=1, source_target_pairs={{0,4},{2,6},{4,0},{6,2},{1,5},{3,7},{5,1},{7,3},{8,12},{10,14},{12... | collective-permute-start | bytes 712712 | tf_op jit(solution)/shard_map/ppermute | solution.py:37
  86.7 1.5 %collective-permute-start.20 = (bf16[928,128]{1,0:T(8,128)(2,1)S(1)}, bf16[928,128]{1,0:T(8,128)(2,1)S(1)}, u32[]{:S(2)}, u32[]{:S(2)}) collective-permute-start(bf16[928,128]{1,0:T(8,128)(2,1)S(1)} %collective-permute-done.19.refs_6_), channel_id=1, source_target_pairs={{0,1},{1,0},{2,3},{3,2},{4,5},{5,4},{6,7},{7,6},{8,9},{9,8},{10,11... | collective-permute-start | bytes 712712 | tf_op jit(solution)/shard_map/ppermute | solution.py:41
  92.1 6.0 %collective-permute-start.21 = (f32[2,3456]{1,0:T(2,128)S(1)}, f32[2,3456]{1,0:T(2,128)S(1)}, u32[]{:S(2)}, u32[]{:S(2)}) collective-permute-start(f32[2,3456]{1,0:T(2,128)S(1)} %get-tuple-element.56), channel_id=1, source_target_pairs={{0,8},{8,16},{16,24},{24,32},{32,40},{40,48},{48,56},{56,64},{64,7... | collective-permute-start | bytes 82952 | tf_op jit(solution)/shard_map/ppermute | solution.py:37
  98.2 7.8 %collective-permute-start.22 = (f32[2,3456]{1,0:T(2,128)S(1)}, f32[2,3456]{1,0:T(2,128)S(1)}, u32[]{:S(2)}, u32[]{:S(2)}) collective-permute-start(f32[2,3456]{1,0:T(2,128)S(1)} %pad_maximum_fusion.1), channel_id=1, source_target_pairs={{0,8},{8,16},{16,24},{24,32},{32,40},{40,48},{48,56},{56,64},{64,7... | collective-permute-start | bytes 82952 | tf_op jit(solution)/shard_map/ppermute | solution.py:37
  98.5 7.8 %collective-permute-start.23 = (f32[2,3456]{1,0:T(2,128)S(1)}, f32[2,3456]{1,0:T(2,128)S(1)}, u32[]{:S(2)}, u32[]{:S(2)}) collective-permute-start(f32[2,3456]{1,0:T(2,128)S(1)} %pad_maximum_fusion.1), channel_id=1, source_target_pairs={{0,24},{8,32},{16,40},{24,48},{32,56},{40,64},{48,72},{56,80},{64,... | collective-permute-start | bytes 82952 | tf_op jit(solution)/shard_map/ppermute | solution.py:37
  100.5 7.1 %collective-permute-start.24 = (f32[2,3456]{1,0:T(2,128)S(1)}, f32[2,3456]{1,0:T(2,128)S(1)}, u32[]{:S(2)}, u32[]{:S(2)}) collective-permute-start(f32[2,3456]{1,0:T(2,128)S(1)} %pad_maximum_fusion.1), channel_id=1, source_target_pairs={{0,40},{8,48},{16,56},{24,64},{32,72},{40,80},{48,88},{56,96},{64,... | collective-permute-start | bytes 82952 | tf_op jit(solution)/shard_map/ppermute | solution.py:37
  106.0 4.8 %collective-permute-start.25 = (f32[2,3456]{1,0:T(2,128)S(1)}, f32[2,3456]{1,0:T(2,128)S(1)}, u32[]{:S(2)}, u32[]{:S(2)}) collective-permute-start(f32[2,3456]{1,0:T(2,128)S(1)} %pad_maximum_fusion.1), channel_id=1, source_target_pairs={{0,56},{8,64},{16,72},{24,80},{32,88},{40,96},{48,104},{56,112},{6... | collective-permute-start | bytes 82952 | tf_op jit(solution)/shard_map/ppermute | solution.py:37

commit v10 on v8

--- a/solution.py
+++ b/solution.py
@@ -295,7 +295,6 @@
     copied = jnp.broadcast_to(weight[None], (8,) + weight.shape)
     column = lax.all_to_all(copied, "z", 0, 0, tiled=True).reshape(-1, COLS).T
     rows = jnp.concatenate([own, ahead], axis=0)
-    one_back, one_ahead = shift(rows, "x", 1), shift(rows, "x", -1)
     gelu, masks = call(
         prepare_kernel,
         (
@@ -307,8 +306,9 @@
         room=6,
         moved=2_700_000,
     )(at, gate_input[0], segment_ids, ahead)
+    rows, gelu, masks = lax.optimization_barrier((rows, gelu, masks))
+    one_back, one_ahead = shift(rows, "x", 1), shift(rows, "x", -1)
     column, one_back, one_ahead = lax.optimization_barrier((column, one_back, one_ahead))
-    one_back, gelu, masks = lax.optimization_barrier((one_back, gelu, masks))
     upper = shift(one_back[:SPLIT], "x", 1)
     lower = shift(one_ahead[SPLIT:], "x", -1)
     streams = [rows, one_back, one_ahead, upper, lower]

time: 112 us -> 114 us (1.018); the launches traced: 112 us -> 112 us
  waiting for transfers between devices: 50.7 us -> 47 us
  local copies, waits for them, and re-layouts: 4.36 us -> 6.26 us
    all_to_all x1, waiting for transfers between devices: 16.6 us -> 14 us  [body(): column = lax.all_to_all(copied, 'z', 0, 0, tiled=True).reshape(-1, COLS).T]
    unnamed x20 -> x18, local copies, waits for them, and re-layouts: 1.21 us -> 0.04 us
  transfers between devices with their start and end apart: 27 -> 27, of which waited for: 12 -> 13; matrix products, arithmetic and copies ran while one was open for 2% -> 5% of each run, Pallas kernels for 11% -> 11%
where the time goes in v10:
time: 114 us; the launch traced here: 112 us
  waiting for transfers between devices  47 us (41%)
  starting transfers between devices  36.7 us (32%)
  Pallas kernels  20 us (18%)
  local copies, waits for them, and re-layouts  6.26 us (5%)
  other arithmetic  2.03 us (2%)
    ppermute x17, waiting for transfers between devices, shift(): lax.ppermute(value, axis, [(i, (i + by) % count) for i in range(count)])  31.4 us
    ppermute x17, starting transfers between devices, shift(): lax.ppermute(value, axis, [(i, (i + by) % count) for i in range(count)])  28.1 us
    all_to_all x1, waiting for transfers between devices, body(): column = lax.all_to_all(copied, 'z', 0, 0, tiled=True).reshape(-1, COLS).T  14 us
    all_to_all x1, starting transfers between devices, body(): column = lax.all_to_all(copied, 'z', 0, 0, tiled=True).reshape(-1, COLS).T  7.57 us
    pallas_call x1, Pallas kernels, body(): call(near_kernel, walked(HEADS), [SMEM] + [ANY] * 6 + [VMEM] * 9, scratch...  6.43 us
    pallas_call x1, Pallas kernels, body(): call(project_kernel, (jax.ShapeDtypeStruct((2, COLS, ROWS), F32), jax.Sha...  4.77 us
    pallas_call x1, Pallas kernels, body(): call(far_kernel, walked(FAR), [SMEM] + [ANY] * 8 + [VMEM] * 10, scratch,...  4.07 us
  transfers between devices with their start and end apart: 27, of which 13 were waited for; matrix products, arithmetic and copies ran while one was open for 5% of the time, Pallas kernels for 11%

profile of v10, /device:TPU:24, one launch (start us, length us, event | category | flops | bytes accessed | tf_op | source)
XLA Modules:
  0.0 112.2 jit_solution(15318377610017147765)
XLA Ops:
  0.0 1.0 slice_bitcast_fusion
  1.0 0.7 convert_element_type.5
  1.7 2.0 %collective-permute-start = (bf16[16,2560]{1,0:T(8,128)(2,1)S(1)}, bf16[16,2560]{1,0:T(8,128)(2,1)S(1)}, u32[]{:S(2)}, u32[]{:S(2)}) collective-permute-start(bf16[16,2560]{1,0:T(8,128)(2,1)S(1)} %fusion.1), channel_id=1, source_target_pairs={{0,8},{8,16},{16,24},{24,32},{32,40},{40,48},{48,56},{56,64},{64,7... | collective-permute-start | bytes 245768 | tf_op jit(solution)/shard_map/ppermute | solution.py:37
  3.7 1.8 %broadcast_in_dim.4 = bf16[8,80,432]{2,1,0:T(8,128)(2,1)} broadcast(bf16[80,432]{1,0:T(8,128)(2,1)} %param.14), dimensions={1,2} | broadcast | bytes 622080 | tf_op jit(solution)/shard_map/broadcast_in_dim | solution.py:295
  5.5 7.6 %all-to-all-start = ((bf16[8,80,432]{2,1,0:T(8,128)(2,1)}), bf16[8,80,432]{2,1,0:T(8,128)(2,1)}, u32[]{:S(2)}, u32[]{:S(2)}) async-start(bf16[8,80,432]{2,1,0:T(8,128)(2,1)} %broadcast_in_dim.4), calls=%async_computation | async-start | bytes 1310720 | tf_op jit(solution)/shard_map/all_to_all | solution.py:296
  13.0 0.1 pad_add_fusion.at_ref
  13.1 1.5 %shard_map.109 = (f32[27,128,128]{2,1,0:T(8,128)S(1)}, f32[4,128,128]{2,1,0:T(8,128)S(1)}) custom-call(s32[4]{0:T(128)S(1)} %pad_add_fusion.at_ref, bf16[128,3456]{1,0:T(8,128)(2,1)S(1)} %bitcast.18, s32[1,128]{1,0:T(1,128)S(1)} %copy-done.8, bf16[16,2560]{1,0:T(8,128)(2,1)S(1)} %collective-permute-done.ahead_ref), custom_call_target="tpu_custom_call" | custom-call | bytes 2700000 | tf_op jit(solution)/shard_map/pallas_call | solution.py:298
  14.7 1.1 %pad_maximum_fusion.refs_0_ = bf16[144,2560]{1,0:T(8,128)(2,1)S(1)} fusion(bf16[16,2560]{1,0:T(8,128)(2,1)S(1)} %collective-permute-done.ahead_ref, bf16[128,2560]{1,0:T(8,128)(2,1)} %bitcast.27), kind=kLoop, calls=%fused_computation | loop fusion | flops 1474560 | bytes 1474560 | tf_op jit(solution)/shard_map/concatenate | solution.py:297
  15.8 1.6 %collective-permute-start.1 = (bf16[144,2560]{1,0:T(8,128)(2,1)S(1)}, bf16[144,2560]{1,0:T(8,128)(2,1)}, u32[]{:S(2)}, u32[]{:S(2)}) collective-permute-start(bf16[144,2560]{1,0:T(8,128)(2,1)S(1)} %pad_maximum_fusion.refs_0_), channel_id=1, source_target_pairs={{0,2},{2,4},{4,6},{6,0},{1,3},{3,5},{5,7},{7,1},{8,10},{10,12},{12... | collective-permute-start | bytes 2211848 | tf_op jit(solution)/shard_map/ppermute | solution.py:37
  17.4 1.7 %collective-permute-start.2 = (bf16[144,2560]{1,0:T(8,128)(2,1)S(1)}, bf16[144,2560]{1,0:T(8,128)(2,1)}, u32[]{:S(2)}, u32[]{:S(2)}) collective-permute-start(bf16[144,2560]{1,0:T(8,128)(2,1)S(1)} %pad_maximum_fusion.refs_0_), channel_id=1, source_target_pairs={{0,6},{2,0},{4,2},{6,4},{1,7},{3,1},{5,3},{7,5},{8,14},{10,8},{12,... | collective-permute-start | bytes 2211848 | tf_op jit(solution)/shard_map/ppermute | solution.py:37
  19.1 14.0 %all-to-all-done = bf16[8,80,432]{2,1,0:T(8,128)(2,1)} async-done(((bf16[8,80,432]{2,1,0:T(8,128)(2,1)}), bf16[8,80,432]{2,1,0:T(8,128)(2,1)}, u32[]{:S(2)}, u32[]{:S(2)}) %all-to-all-start) | async-done | bytes 552992 | tf_op jit(solution)/shard_map/all_to_all | solution.py:296
  33.2 1.4 %copy.13 = bf16[640,432]{0,1:T(8,128)(2,1)S(1)} copy(bf16[640,432]{1,0:T(8,128)(2,1)} %bitcast.7) | data formatting | bytes 1105920 | tf_op jit(solution)/shard_map/reshape | solution.py:296
  34.5 0.3 collective-permute-done.1.refs_1_
  34.9 1.0 slice.55
  35.9 3.0 %collective-permute-start.4 = (bf16[80,2560]{1,0:T(8,128)(2,1)S(1)}, bf16[80,2560]{1,0:T(8,128)(2,1)S(1)}, u32[]{:S(2)}, u32[]{:S(2)}) collective-permute-start(bf16[80,2560]{1,0:T(8,128)(2,1)S(1)} %slice.55), channel_id=1, source_target_pairs={{0,6},{2,0},{4,2},{6,4},{1,7},{3,1},{5,3},{7,5},{8,14},{10,8},{12,... | collective-permute-start | bytes 1228808 | tf_op jit(solution)/shard_map/ppermute | solution.py:37
  38.9 1.0 slice.54
  39.9 0.1 collective-permute-start.3
  40.0 0.3 collective-permute-start.10
  40.3 1.8 %collective-permute-start.11 = (bf16[432,640]{1,0:T(8,128)(2,1)S(1)}, bf16[432,640]{1,0:T(8,128)(2,1)S(1)}, u32[]{:S(2)}, u32[]{:S(2)}) collective-permute-start(bf16[432,640]{1,0:T(8,128)(2,1)S(1)} %bitcast.16), channel_id=1, source_target_pairs={{0,192},{64,0},{128,64},{192,128},{1,193},{65,1},{129,65},{193,129... | collective-permute-start | bytes 1658888 | tf_op jit(solution)/shard_map/ppermute | solution.py:37
  42.1 7.9 %collective-permute-done.3.refs_3_ = bf16[64,2560]{1,0:T(8,128)(2,1)S(1)} collective-permute-done((bf16[64,2560]{1,0:T(8,128)(2,1)S(1)}, bf16[64,2560]{1,0:T(8,128)(2,1)S(1)}, u32[]{:S(2)}, u32[]{:S(2)}) %collective-permute-start.3) | collective-permute-done | bytes 327712 | tf_op jit(solution)/shard_map/ppermute | solution.py:37
  50.1 0.5 collective-permute-start.7
  50.6 3.2 %collective-permute-done.10.refs_11_ = bf16[432,640]{1,0:T(8,128)(2,1)S(1)} collective-permute-done((bf16[432,640]{1,0:T(8,128)(2,1)S(1)}, bf16[432,640]{1,0:T(8,128)(2,1)S(1)}, u32[]{:S(2)}, u32[]{:S(2)}) %collective-permute-start.10) | collective-permute-done | bytes 552992 | tf_op jit(solution)/shard_map/ppermute | solution.py:37
  53.8 1.3 %collective-permute-done.11.refs_12_ = bf16[432,640]{1,0:T(8,128)(2,1)S(1)} collective-permute-done((bf16[432,640]{1,0:T(8,128)(2,1)S(1)}, bf16[432,640]{1,0:T(8,128)(2,1)S(1)}, u32[]{:S(2)}, u32[]{:S(2)}) %collective-permute-start.11) | collective-permute-done | bytes 552992 | tf_op jit(solution)/shard_map/ppermute | solution.py:37
  55.1 0.5 collective-permute-start.13
  55.7 3.0 %collective-permute-start.12 = (bf16[208,640]{1,0:T(8,128)(2,1)S(1)}, bf16[208,640]{1,0:T(8,128)(2,1)S(1)}, u32[]{:S(2)}, u32[]{:S(2)}) collective-permute-start(bf16[208,640]{1,0:T(8,128)(2,1)S(1)} %slice.56), channel_id=1, source_target_pairs={{0,64},{64,128},{128,192},{192,0},{1,65},{65,129},{129,193},{193,1... | collective-permute-start | bytes 798728 | tf_op jit(solution)/shard_map/ppermute | solution.py:37
  58.7 4.8 %shard_map.110 = (f32[2,432,576]{2,1,0:T(8,128)S(1)}, bf16[1152,640]{1,0:T(8,128)(2,1)S(1)}) custom-call(s32[4]{0:T(128)S(1)} %pad_add_fusion.at_ref, bf16[144,2560]{1,0:T(8,128)(2,1)S(1)} %pad_maximum_fusion.refs_0_, bf16[144,2560]{1,0:T(8,128)(2,1)} %collective-permute-done.1.refs_1_, bf16[144,2560]{1,0:T(8,128)(2,1)} %collective-permute-done.2.refs_2_, ...), custom_call_target="tpu_custom_call" | custom-call | flops 1751777280 | bytes 9000000 | tf_op jit(solution)/shard_map/pallas_call | solution.py:322
  63.5 1.3 %collective-permute-done.12.w0_ref = bf16[208,640]{1,0:T(8,128)(2,1)S(1)} collective-permute-done((bf16[208,640]{1,0:T(8,128)(2,1)S(1)}, bf16[208,640]{1,0:T(8,128)(2,1)S(1)}, u32[]{:S(2)}, u32[]{:S(2)}) %collective-permute-start.12) | collective-permute-done | bytes 266272 | tf_op jit(solution)/shard_map/ppermute | solution.py:37
  64.8 0.9 collective-permute-done.13.w1_ref
  65.7 0.0 copy-start.7
  65.7 1.4 %shard_map.111 = (bf16[928,128]{1,0:T(8,128)(2,1)S(1)}, bf16[928,128]{1,0:T(8,128)(2,1)S(1)}, bf16[928,128]{1,0:T(8,128)(2,1)S(1)}, bf16[928,128]{1,0:T(8,128)(2,1)S(1)}) custom-call(f32[2,432,576]{2,1,0:T(8,128)S(1)} %get-tuple-element.41.part_ref, bf16[1152,640]{1,0:T(8,128)(2,1)S(1)} %get-tuple-element.42.far_ref, ...), custom_call_target="tpu_custom_call" | custom-call | flops 583925760 | bytes 5000000 | tf_op jit(solution)/shard_map/pallas_call | solution.py:332
  67.1 0.4 collective-permute-start.15
  67.5 2.9 %collective-permute-start.17 = (bf16[928,128]{1,0:T(8,128)(2,1)S(1)}, bf16[928,128]{1,0:T(8,128)(2,1)S(1)}, u32[]{:S(2)}, u32[]{:S(2)}) collective-permute-start(bf16[928,128]{1,0:T(8,128)(2,1)S(1)} %get-tuple-element.45), channel_id=1, source_target_pairs={{0,6},{2,0},{4,2},{6,4},{1,7},{3,1},{5,3},{7,5},{8,14},{10,8},{12,... | collective-permute-start | bytes 712712 | tf_op jit(solution)/shard_map/ppermute | solution.py:37
  70.4 5.4 %collective-permute-done.15.refs_2_ = bf16[928,128]{1,0:T(8,128)(2,1)S(1)} collective-permute-done((bf16[928,128]{1,0:T(8,128)(2,1)S(1)}, bf16[928,128]{1,0:T(8,128)(2,1)S(1)}, u32[]{:S(2)}, u32[]{:S(2)}) %collective-permute-start.15) | collective-permute-done | bytes 237600 | tf_op jit(solution)/shard_map/ppermute | solution.py:37
  75.8 0.5 collective-permute-start.18
  76.3 2.2 %collective-permute-start.19 = (bf16[928,128]{1,0:T(8,128)(2,1)S(1)}, bf16[928,128]{1,0:T(8,128)(2,1)S(1)}, u32[]{:S(2)}, u32[]{:S(2)}) collective-permute-start(bf16[928,128]{1,0:T(8,128)(2,1)S(1)} %get-tuple-element.50), channel_id=1, source_target_pairs={{0,4},{2,6},{4,0},{6,2},{1,5},{3,7},{5,1},{7,3},{8,12},{10,14},{12... | collective-permute-start | bytes 712712 | tf_op jit(solution)/shard_map/ppermute | solution.py:37
  78.6 6.4 %shard_map.112 = (f32[27,128,128]{2,1,0:T(8,128)S(1)}, f32[27,128,128]{2,1,0:T(8,128)S(1)}, f32[2,3456]{1,0:T(2,128)S(1)}) custom-call(s32[4]{0:T(128)S(1)} %pad_add_fusion.at_ref, bf16[928,128]{1,0:T(8,128)(2,1)S(1)} %get-tuple-element.43.refs_0_, bf16[928,128]{1,0:T(8,128)(2,1)S(1)} %collective-permute-done.14.refs_1_, ...), custom_call_target="tpu_custom_call" | custom-call | flops 167772160 | bytes 20000000 | tf_op jit(solution)/shard_map/pallas_call | solution.py:370
  85.1 0.4 collective-permute-done.19.refs_6_
  85.5 1.5 %collective-permute-done.20.refs_7_ = bf16[928,128]{1,0:T(8,128)(2,1)S(1)} collective-permute-done((bf16[928,128]{1,0:T(8,128)(2,1)S(1)}, bf16[928,128]{1,0:T(8,128)(2,1)S(1)}, u32[]{:S(2)}, u32[]{:S(2)}) %collective-permute-start.20) | collective-permute-done | bytes 237600 | tf_op jit(solution)/shard_map/ppermute | solution.py:41
  87.0 4.1 %shard_map.113 = (f32[8,128,128]{2,1,0:T(8,128)S(1)}, f32[8,128,128]{2,1,0:T(8,128)S(1)}, f32[2,3456]{1,0:T(2,128)S(1)}) custom-call(s32[4]{0:T(128)S(1)} %pad_add_fusion.at_ref, bf16[928,128]{1,0:T(8,128)(2,1)S(1)} %get-tuple-element.43.refs_0_, bf16[928,128]{1,0:T(8,128)(2,1)S(1)} %collective-permute-done.14.refs_1_, ...), custom_call_target="tpu_custom_call" | custom-call | flops 67108864 | bytes 8000000 | tf_op jit(solution)/shard_map/pallas_call | solution.py:379
  91.1 0.1 collective-permute-start.21
  91.2 6.0 %collective-permute-done.21 = f32[2,3456]{1,0:T(2,128)S(1)} collective-permute-done((f32[2,3456]{1,0:T(2,128)S(1)}, f32[2,3456]{1,0:T(2,128)S(1)}, u32[]{:S(2)}, u32[]{:S(2)}) %collective-permute-start.21) | collective-permute-done | bytes 27680 | tf_op jit(solution)/shard_map/ppermute | solution.py:37
  97.2 0.1 collective-permute-start.22
  97.3 3.6 %collective-permute-start.23 = (f32[2,3456]{1,0:T(2,128)S(1)}, f32[2,3456]{1,0:T(2,128)S(1)}, u32[]{:S(2)}, u32[]{:S(2)}) collective-permute-start(f32[2,3456]{1,0:T(2,128)S(1)} %pad_maximum_fusion.1), channel_id=1, source_target_pairs={{0,24},{8,32},{16,40},{24,48},{32,56},{40,64},{48,72},{56,80},{64,... | collective-permute-start | bytes 82952 | tf_op jit(solution)/shard_map/ppermute | solution.py:37
  100.9 4.7 %collective-permute-start.24 = (f32[2,3456]{1,0:T(2,128)S(1)}, f32[2,3456]{1,0:T(2,128)S(1)}, u32[]{:S(2)}, u32[]{:S(2)}) collective-permute-start(f32[2,3456]{1,0:T(2,128)S(1)} %pad_maximum_fusion.1), channel_id=1, source_target_pairs={{0,40},{8,48},{16,56},{24,64},{32,72},{40,80},{48,88},{56,96},{64,... | collective-permute-start | bytes 82952 | tf_op jit(solution)/shard_map/ppermute | solution.py:37
  105.6 2.8 %collective-permute-done.24 = f32[2,3456]{1,0:T(2,128)S(1)} collective-permute-done((f32[2,3456]{1,0:T(2,128)S(1)}, f32[2,3456]{1,0:T(2,128)S(1)}, u32[]{:S(2)}, u32[]{:S(2)}) %collective-permute-start.24) | collective-permute-done | bytes 27680 | tf_op jit(solution)/shard_map/ppermute | solution.py:37
  108.3 2.0 %collective-permute-done.25 = f32[2,3456]{1,0:T(2,128)S(1)} collective-permute-done((f32[2,3456]{1,0:T(2,128)S(1)}, f32[2,3456]{1,0:T(2,128)S(1)}, u32[]{:S(2)}, u32[]{:S(2)}) %collective-permute-start.25) | collective-permute-done | bytes 27680 | tf_op jit(solution)/shard_map/ppermute | solution.py:37
  110.3 0.1 slice_add_fusion.in_ref
  110.4 1.8 %shard_map.114 = bf16[128,3456]{1,0:T(8,128)(2,1)} custom-call(s32[4]{0:T(128)S(1)} %pad_add_fusion.at_ref, f32[27,128,128]{2,1,0:T(8,128)S(1)} %get-tuple-element.48.state_ref, f32[27,128,128]{2,1,0:T(8,128)S(1)} %get-tuple-element.49.prod_ref, f32[8,128,128]{2,1,0:T(8,128)S(1)} %get-tuple-element.54.far_state_ref, ...), custom_call_target="tpu_custom_call" | custom-call | bytes 4400000 | tf_op jit(solution)/shard_map/pallas_call | solution.py:391
  (44 shorter events, 0.2 us)
Async XLA Ops:
  0.0 13.1 %copy-start.8 = (s32[1,128]{1,0:T(1,128)S(1)}, s32[1,128]{1,0:T(1,128)}, u32[]{:S(2)}) copy-start(s32[1,128]{1,0:T(1,128)} %ids_ref.1) | copy-start | bytes 1540
  0.0 13.1 %copy-start.2 = (bf16[1,128,3456]{2,1,0:T(8,128)(2,1)S(1)}, bf16[1,128,3456]{2,1,0:T(8,128)(2,1)}, u32[]{:S(2)}) copy-start(bf16[1,128,3456]{2,1,0:T(8,128)(2,1)} %param.12) | copy-start | bytes 2654212
  1.7 11.4 %collective-permute-start = (bf16[16,2560]{1,0:T(8,128)(2,1)S(1)}, bf16[16,2560]{1,0:T(8,128)(2,1)S(1)}, u32[]{:S(2)}, u32[]{:S(2)}) collective-permute-start(bf16[16,2560]{1,0:T(8,128)(2,1)S(1)} %fusion.1), channel_id=1, source_target_pairs={{0,8},{8,16},{16,24},{24,32},{32,40},{40,48},{48,56},{56,64},{64,7... | collective-permute-start | bytes 245768 | tf_op jit(solution)/shard_map/ppermute | solution.py:37
  5.5 27.7 %all-to-all-start = ((bf16[8,80,432]{2,1,0:T(8,128)(2,1)}), bf16[8,80,432]{2,1,0:T(8,128)(2,1)}, u32[]{:S(2)}, u32[]{:S(2)}) async-start(bf16[8,80,432]{2,1,0:T(8,128)(2,1)} %broadcast_in_dim.4), calls=%async_computation | async-start | bytes 1310720 | tf_op jit(solution)/shard_map/all_to_all | solution.py:296
  15.8 19.1 %collective-permute-start.1 = (bf16[144,2560]{1,0:T(8,128)(2,1)S(1)}, bf16[144,2560]{1,0:T(8,128)(2,1)}, u32[]{:S(2)}, u32[]{:S(2)}) collective-permute-start(bf16[144,2560]{1,0:T(8,128)(2,1)S(1)} %pad_maximum_fusion.refs_0_), channel_id=1, source_target_pairs={{0,2},{2,4},{4,6},{6,0},{1,3},{3,5},{5,7},{7,1},{8,10},{10,12},{12... | collective-permute-start | bytes 2211848 | tf_op jit(solution)/shard_map/ppermute | solution.py:37
  17.4 17.5 %collective-permute-start.2 = (bf16[144,2560]{1,0:T(8,128)(2,1)S(1)}, bf16[144,2560]{1,0:T(8,128)(2,1)}, u32[]{:S(2)}, u32[]{:S(2)}) collective-permute-start(bf16[144,2560]{1,0:T(8,128)(2,1)S(1)} %pad_maximum_fusion.refs_0_), channel_id=1, source_target_pairs={{0,6},{2,0},{4,2},{6,4},{1,7},{3,1},{5,3},{7,5},{8,14},{10,8},{12,... | collective-permute-start | bytes 2211848 | tf_op jit(solution)/shard_map/ppermute | solution.py:37
  35.9 14.2 %collective-permute-start.4 = (bf16[80,2560]{1,0:T(8,128)(2,1)S(1)}, bf16[80,2560]{1,0:T(8,128)(2,1)S(1)}, u32[]{:S(2)}, u32[]{:S(2)}) collective-permute-start(bf16[80,2560]{1,0:T(8,128)(2,1)S(1)} %slice.55), channel_id=1, source_target_pairs={{0,6},{2,0},{4,2},{6,4},{1,7},{3,1},{5,3},{7,5},{8,14},{10,8},{12,... | collective-permute-start | bytes 1228808 | tf_op jit(solution)/shard_map/ppermute | solution.py:37
  39.9 10.1 %collective-permute-start.3 = (bf16[64,2560]{1,0:T(8,128)(2,1)S(1)}, bf16[64,2560]{1,0:T(8,128)(2,1)S(1)}, u32[]{:S(2)}, u32[]{:S(2)}) collective-permute-start(bf16[64,2560]{1,0:T(8,128)(2,1)S(1)} %slice.54), channel_id=1, source_target_pairs={{0,2},{2,4},{4,6},{6,0},{1,3},{3,5},{5,7},{7,1},{8,10},{10,12},{12... | collective-permute-start | bytes 983048 | tf_op jit(solution)/shard_map/ppermute | solution.py:37
  40.0 13.7 %collective-permute-start.10 = (bf16[432,640]{1,0:T(8,128)(2,1)S(1)}, bf16[432,640]{1,0:T(8,128)(2,1)S(1)}, u32[]{:S(2)}, u32[]{:S(2)}) collective-permute-start(bf16[432,640]{1,0:T(8,128)(2,1)S(1)} %bitcast.15), channel_id=1, source_target_pairs={{0,64},{64,128},{128,192},{192,0},{1,65},{65,129},{129,193},{193,1... | collective-permute-start | bytes 1658888 | tf_op jit(solution)/shard_map/ppermute | solution.py:37
  40.3 14.7 %collective-permute-start.11 = (bf16[432,640]{1,0:T(8,128)(2,1)S(1)}, bf16[432,640]{1,0:T(8,128)(2,1)S(1)}, u32[]{:S(2)}, u32[]{:S(2)}) collective-permute-start(bf16[432,640]{1,0:T(8,128)(2,1)S(1)} %bitcast.16), channel_id=1, source_target_pairs={{0,192},{64,0},{128,64},{192,128},{1,193},{65,1},{129,65},{193,129... | collective-permute-start | bytes 1658888 | tf_op jit(solution)/shard_map/ppermute | solution.py:37
  42.1 13.0 %collective-permute-start.5 = (bf16[144,2560]{1,0:T(8,128)(2,1)S(1)}, bf16[144,2560]{1,0:T(8,128)(2,1)S(1)}, u32[]{:S(2)}, u32[]{:S(2)}) collective-permute-start(bf16[144,2560]{1,0:T(8,128)(2,1)S(1)} %pad_maximum_fusion.refs_0_), channel_id=1, source_target_pairs={{0,1},{1,0},{2,3},{3,2},{4,5},{5,4},{6,7},{7,6},{8,9},{9,8},{10,11... | collective-permute-start | bytes 2211848 | tf_op jit(solution)/shard_map/ppermute | solution.py:41
  50.1 8.7 %collective-permute-start.6 = (bf16[144,2560]{1,0:T(8,128)(2,1)}, bf16[144,2560]{1,0:T(8,128)(2,1)S(1)}, u32[]{:S(2)}, u32[]{:S(2)}) collective-permute-start(bf16[144,2560]{1,0:T(8,128)(2,1)} %collective-permute-done.1.refs_1_), channel_id=1, source_target_pairs={{0,1},{1,0},{2,3},{3,2},{4,5},{5,4},{6,7},{7,6},{8,9},{9,8},{10,11... | collective-permute-start | bytes 2211848 | tf_op jit(solution)/shard_map/ppermute | solution.py:41
  50.1 8.7 %collective-permute-start.7 = (bf16[144,2560]{1,0:T(8,128)(2,1)}, bf16[144,2560]{1,0:T(8,128)(2,1)S(1)}, u32[]{:S(2)}, u32[]{:S(2)}) collective-permute-start(bf16[144,2560]{1,0:T(8,128)(2,1)} %collective-permute-done.2.refs_2_), channel_id=1, source_target_pairs={{0,1},{1,0},{2,3},{3,2},{4,5},{5,4},{6,7},{7,6},{8,9},{9,8},{10,11... | collective-permute-start | bytes 2211848 | tf_op jit(solution)/shard_map/ppermute | solution.py:41
  53.8 1.9 %collective-permute-start.8 = (bf16[64,2560]{1,0:T(8,128)(2,1)S(1)}, bf16[64,2560]{1,0:T(8,128)(2,1)S(1)}, u32[]{:S(2)}, u32[]{:S(2)}) collective-permute-start(bf16[64,2560]{1,0:T(8,128)(2,1)S(1)} %collective-permute-done.3.refs_3_), channel_id=1, source_target_pairs={{0,1},{1,0},{2,3},{3,2},{4,5},{5,4},{6,7},{7,6},{8,9},{9,8},{10,11... | collective-permute-start | bytes 983048 | tf_op jit(solution)/shard_map/ppermute | solution.py:41
  55.1 3.7 %collective-permute-start.9 = (bf16[80,2560]{1,0:T(8,128)(2,1)S(1)}, bf16[80,2560]{1,0:T(8,128)(2,1)S(1)}, u32[]{:S(2)}, u32[]{:S(2)}) collective-permute-start(bf16[80,2560]{1,0:T(8,128)(2,1)S(1)} %collective-permute-done.4.refs_4_), channel_id=1, source_target_pairs={{0,1},{1,0},{2,3},{3,2},{4,5},{5,4},{6,7},{7,6},{8,9},{9,8},{10,11... | collective-permute-start | bytes 1228808 | tf_op jit(solution)/shard_map/ppermute | solution.py:41
  55.1 10.5 %collective-permute-start.13 = (bf16[224,640]{1,0:T(8,128)(2,1)S(1)}, bf16[224,640]{1,0:T(8,128)(2,1)S(1)}, u32[]{:S(2)}, u32[]{:S(2)}) collective-permute-start(bf16[224,640]{1,0:T(8,128)(2,1)S(1)} %slice.57), channel_id=1, source_target_pairs={{0,192},{64,0},{128,64},{192,128},{1,193},{65,1},{129,65},{193,129... | collective-permute-start | bytes 860168 | tf_op jit(solution)/shard_map/ppermute | solution.py:37
  55.7 9.1 %collective-permute-start.12 = (bf16[208,640]{1,0:T(8,128)(2,1)S(1)}, bf16[208,640]{1,0:T(8,128)(2,1)S(1)}, u32[]{:S(2)}, u32[]{:S(2)}) collective-permute-start(bf16[208,640]{1,0:T(8,128)(2,1)S(1)} %slice.56), channel_id=1, source_target_pairs={{0,64},{64,128},{128,192},{192,0},{1,65},{65,129},{129,193},{193,1... | collective-permute-start | bytes 798728 | tf_op jit(solution)/shard_map/ppermute | solution.py:37
  65.7 12.9 %copy-start = (bf16[27,128,128]{2,1,0:T(8,128)(2,1)S(1)}, bf16[27,128,128]{2,1,0:T(8,128)(2,1)}, u32[]{:S(2)}) copy-start(bf16[27,128,128]{2,1,0:T(8,128)(2,1)} %refs_15_.1) | copy-start | bytes 2654212
  65.7 12.9 %copy-start.1 = (bf16[27,128,128]{2,1,0:T(8,128)(2,1)S(1)}, bf16[27,128,128]{2,1,0:T(8,128)(2,1)}, u32[]{:S(2)}) copy-start(bf16[27,128,128]{2,1,0:T(8,128)(2,1)} %refs_16_.1) | copy-start | bytes 2654212
  65.7 12.9 %copy-start.3 = (f32[4,3456]{1,0:T(4,128)S(1)}, f32[4,3456]{1,0:T(4,128)}, u32[]{:S(2)}) copy-start(f32[4,3456]{1,0:T(4,128)} %refs_10_.1) | copy-start | bytes 165892
  65.7 12.9 %copy-start.4 = (f32[3456]{0:T(1024)S(1)}, f32[3456]{0:T(1024)}, u32[]{:S(2)}) copy-start(f32[3456]{0:T(1024)} %param.16) | copy-start | bytes 41476
  65.7 12.9 %copy-start.5 = (f32[3456]{0:T(1024)S(1)}, f32[3456]{0:T(1024)}, u32[]{:S(2)}) copy-start(f32[3456]{0:T(1024)} %param.19) | copy-start | bytes 41476
  65.7 12.9 %copy-start.6 = (f32[3456]{0:T(1024)S(1)}, f32[3456]{0:T(1024)}, u32[]{:S(2)}) copy-start(f32[3456]{0:T(1024)} %param.20) | copy-start | bytes 41476
  65.7 12.9 %copy-start.7 = (f32[3456]{0:T(1024)S(1)}, f32[3456]{0:T(1024)}, u32[]{:S(2)}) copy-start(f32[3456]{0:T(1024)} %param.21) | copy-start | bytes 41476
  67.1 8.7 %collective-permute-start.15 = (bf16[928,128]{1,0:T(8,128)(2,1)S(1)}, bf16[928,128]{1,0:T(8,128)(2,1)S(1)}, u32[]{:S(2)}, u32[]{:S(2)}) collective-permute-start(bf16[928,128]{1,0:T(8,128)(2,1)S(1)} %get-tuple-element.44), channel_id=1, source_target_pairs={{0,2},{2,4},{4,6},{6,0},{1,3},{3,5},{5,7},{7,1},{8,10},{10,12},{12... | collective-permute-start | bytes 712712 | tf_op jit(solution)/shard_map/ppermute | solution.py:37
  67.5 8.3 %collective-permute-start.17 = (bf16[928,128]{1,0:T(8,128)(2,1)S(1)}, bf16[928,128]{1,0:T(8,128)(2,1)S(1)}, u32[]{:S(2)}, u32[]{:S(2)}) collective-permute-start(bf16[928,128]{1,0:T(8,128)(2,1)S(1)} %get-tuple-element.45), channel_id=1, source_target_pairs={{0,6},{2,0},{4,2},{6,4},{1,7},{3,1},{5,3},{7,5},{8,14},{10,8},{12,... | collective-permute-start | bytes 712712 | tf_op jit(solution)/shard_map/ppermute | solution.py:37
  70.4 8.1 %collective-permute-start.14 = (bf16[928,128]{1,0:T(8,128)(2,1)S(1)}, bf16[928,128]{1,0:T(8,128)(2,1)S(1)}, u32[]{:S(2)}, u32[]{:S(2)}) collective-permute-start(bf16[928,128]{1,0:T(8,128)(2,1)S(1)} %get-tuple-element.43.refs_0_), channel_id=1, source_target_pairs={{0,1},{1,0},{2,3},{3,2},{4,5},{5,4},{6,7},{7,6},{8,9},{9,8},{10,11... | collective-permute-start | bytes 712712 | tf_op jit(solution)/shard_map/ppermute | solution.py:41
  75.8 2.8 %collective-permute-start.16 = (bf16[928,128]{1,0:T(8,128)(2,1)S(1)}, bf16[928,128]{1,0:T(8,128)(2,1)S(1)}, u32[]{:S(2)}, u32[]{:S(2)}) collective-permute-start(bf16[928,128]{1,0:T(8,128)(2,1)S(1)} %collective-permute-done.15.refs_2_), channel_id=1, source_target_pairs={{0,1},{1,0},{2,3},{3,2},{4,5},{5,4},{6,7},{7,6},{8,9},{9,8},{10,11... | collective-permute-start | bytes 712712 | tf_op jit(solution)/shard_map/ppermute | solution.py:41
  75.8 2.8 %collective-permute-start.18 = (bf16[928,128]{1,0:T(8,128)(2,1)S(1)}, bf16[928,128]{1,0:T(8,128)(2,1)S(1)}, u32[]{:S(2)}, u32[]{:S(2)}) collective-permute-start(bf16[928,128]{1,0:T(8,128)(2,1)S(1)} %collective-permute-done.17.refs_4_), channel_id=1, source_target_pairs={{0,1},{1,0},{2,3},{3,2},{4,5},{5,4},{6,7},{7,6},{8,9},{9,8},{10,11... | collective-permute-start | bytes 712712 | tf_op jit(solution)/shard_map/ppermute | solution.py:41
  76.3 9.2 %collective-permute-start.19 = (bf16[928,128]{1,0:T(8,128)(2,1)S(1)}, bf16[928,128]{1,0:T(8,128)(2,1)S(1)}, u32[]{:S(2)}, u32[]{:S(2)}) collective-permute-start(bf16[928,128]{1,0:T(8,128)(2,1)S(1)} %get-tuple-element.50), channel_id=1, source_target_pairs={{0,4},{2,6},{4,0},{6,2},{1,5},{3,7},{5,1},{7,3},{8,12},{10,14},{12... | collective-permute-start | bytes 712712 | tf_op jit(solution)/shard_map/ppermute | solution.py:37
  85.5 1.5 %collective-permute-start.20 = (bf16[928,128]{1,0:T(8,128)(2,1)S(1)}, bf16[928,128]{1,0:T(8,128)(2,1)S(1)}, u32[]{:S(2)}, u32[]{:S(2)}) collective-permute-start(bf16[928,128]{1,0:T(8,128)(2,1)S(1)} %collective-permute-done.19.refs_6_), channel_id=1, source_target_pairs={{0,1},{1,0},{2,3},{3,2},{4,5},{5,4},{6,7},{7,6},{8,9},{9,8},{10,11... | collective-permute-start | bytes 712712 | tf_op jit(solution)/shard_map/ppermute | solution.py:41
  91.1 6.0 %collective-permute-start.21 = (f32[2,3456]{1,0:T(2,128)S(1)}, f32[2,3456]{1,0:T(2,128)S(1)}, u32[]{:S(2)}, u32[]{:S(2)}) collective-permute-start(f32[2,3456]{1,0:T(2,128)S(1)} %get-tuple-element.56), channel_id=1, source_target_pairs={{0,8},{8,16},{16,24},{24,32},{32,40},{40,48},{48,56},{56,64},{64,7... | collective-permute-start | bytes 82952 | tf_op jit(solution)/shard_map/ppermute | solution.py:37
  97.2 8.4 %collective-permute-start.22 = (f32[2,3456]{1,0:T(2,128)S(1)}, f32[2,3456]{1,0:T(2,128)S(1)}, u32[]{:S(2)}, u32[]{:S(2)}) collective-permute-start(f32[2,3456]{1,0:T(2,128)S(1)} %pad_maximum_fusion.1), channel_id=1, source_target_pairs={{0,8},{8,16},{16,24},{24,32},{32,40},{40,48},{48,56},{56,64},{64,7... | collective-permute-start | bytes 82952 | tf_op jit(solution)/shard_map/ppermute | solution.py:37
  97.3 8.3 %collective-permute-start.23 = (f32[2,3456]{1,0:T(2,128)S(1)}, f32[2,3456]{1,0:T(2,128)S(1)}, u32[]{:S(2)}, u32[]{:S(2)}) collective-permute-start(f32[2,3456]{1,0:T(2,128)S(1)} %pad_maximum_fusion.1), channel_id=1, source_target_pairs={{0,24},{8,32},{16,40},{24,48},{32,56},{40,64},{48,72},{56,80},{64,... | collective-permute-start | bytes 82952 | tf_op jit(solution)/shard_map/ppermute | solution.py:37
  100.9 7.5 %collective-permute-start.24 = (f32[2,3456]{1,0:T(2,128)S(1)}, f32[2,3456]{1,0:T(2,128)S(1)}, u32[]{:S(2)}, u32[]{:S(2)}) collective-permute-start(f32[2,3456]{1,0:T(2,128)S(1)} %pad_maximum_fusion.1), channel_id=1, source_target_pairs={{0,40},{8,48},{16,56},{24,64},{32,72},{40,80},{48,88},{56,96},{64,... | collective-permute-start | bytes 82952 | tf_op jit(solution)/shard_map/ppermute | solution.py:37
  105.6 4.8 %collective-permute-start.25 = (f32[2,3456]{1,0:T(2,128)S(1)}, f32[2,3456]{1,0:T(2,128)S(1)}, u32[]{:S(2)}, u32[]{:S(2)}) collective-permute-start(f32[2,3456]{1,0:T(2,128)S(1)} %pad_maximum_fusion.1), channel_id=1, source_target_pairs={{0,56},{8,64},{16,72},{24,80},{32,88},{40,96},{48,104},{56,112},{6... | collective-permute-start | bytes 82952 | tf_op jit(solution)/shard_map/ppermute | solution.py:37
